TPU v7x, 32 devices: a whole 2x2x4 slice. The times are simulated.
32 devices in a mesh: section: 4 (over y, x), lat: 8 (over z, core).
Axes of the slice: x: 2, y: 2, z: 4, core: 2. Of those that a mesh axis runs over, the one named last changes fastest.
Arguments:
- grad_out: bfloat16 [4, 8, 180, 384], P('section', 'lat'), may hold values from -6 to 6
- spec_saved: bfloat16 [4, 8, 2, 27648], P('section', None, None, 'lat'), may hold values from -6 to 6
- w1: bfloat16 [4, 2, 96, 384], P('section'), may hold values from -0.4375 to 0.4375
- w2: bfloat16 [4, 2, 96, 384], P('section'), may hold values from -0.4375 to 0.4375
- b1: bfloat16 [4, 2, 384], P('section'), may hold values from -5 to 5
- mode_counts: int32 [8], replicated, may hold values from 1 to 72, as said below
- assignment: int32 [8], replicated, may hold values from 0 to 7, each once
Outputs:
- grad_input: bfloat16 [4, 8, 180, 384], P('section', 'lat')
- grad_w1: float32 [4, 2, 96, 384], P('section', None, None, 'lat')
- grad_w2: float32 [4, 2, 96, 384], P('section', None, None, 'lat')
- grad_b1: float32 [4, 2, 384], P('section', None, 'lat')
Inputs may be any that keep to these rules, and one draw needn't show every extreme that they name: `mode_counts`: active modes shrink from the middle band toward both ends; the middle band keeps all 72. `assignment`: A permutation of the latitude bands.
All inputs are finite; a program needn't handle non-finite values.
Results may differ from a plain program's by a relative error of at most 0.018.
Values may be sent and summed in bfloat16 or wider, within the bound.
No kernel may reach another device: no remote copies, remote signals or barrier semaphores. Data moves between devices by JAX's collectives and lax.ppermute only.
A program may use at most 64 MiB of HBM per device.

v0:
```python
import math

import jax
import jax.numpy as jnp
from jax import lax
from jax.sharding import PartitionSpec as P

NB = 4
BS = 96
KM = 72


def from_behind(value, axis, by):
    length = lax.axis_size(axis)
    pairs = [(i, i + by) for i in range(length) if 0 <= i + by < length]
    return lax.ppermute(value, axis, pairs)


def lon_tables(n_modes, length):
    modes = jnp.arange(n_modes, dtype=jnp.int32)
    cells = jnp.arange(length, dtype=jnp.int32)
    phase = modes[:, None] * cells[None, :] % length
    angle = phase.astype(jnp.float32) * (2.0 * math.pi / length)
    factor = 1.0 / math.sqrt(length)
    cosine = jnp.cos(angle) * factor
    sine = jnp.sin(angle) * factor
    weight = jnp.where(modes == 0, 1.0, 2.0).astype(jnp.float32)[:, None]
    forward = jnp.stack([cosine, -sine]).astype(jnp.bfloat16)
    inverse = jnp.stack([cosine * weight, -sine * weight]).astype(jnp.bfloat16)
    return (forward, inverse)


def lat_table(latitude, n_rows):
    freqs = jnp.arange(n_rows, dtype=jnp.int32)
    phase = freqs[:, None] * latitude[None, :] % n_rows
    angle = phase.astype(jnp.float32) * (2.0 * math.pi / n_rows)
    factor = 1.0 / math.sqrt(n_rows)
    cosine = jnp.cos(angle) * factor
    sine = jnp.sin(angle) * factor
    upper = jnp.stack([cosine, sine], axis=-1)
    lower = jnp.stack([-sine, cosine], axis=-1)
    return jnp.stack([upper, lower], axis=1).astype(jnp.bfloat16)


def silu_slope(pre):
    sig = jax.nn.sigmoid(pre)
    return sig * (1.0 + pre * (1.0 - sig))


def apply_mat(vec, mat):
    return jnp.einsum("kpi,ipj->kpj", vec, mat, preferred_element_type=jnp.float32)


def adjoint_mat(vec, mat):
    return jnp.einsum("kpj,ipj->kpi", vec, mat, preferred_element_type=jnp.float32)


def outer_sum(left, right):
    return jnp.einsum("kpi,kpj->ipj", left, right, preferred_element_type=jnp.float32)


def per_device(grad_out, spec_saved, w1, w2, b1, mode_counts, assignment):
    rows_dev = grad_out.shape[1]
    length = grad_out.shape[2]
    width = grad_out.shape[3]
    n_rows = assignment.shape[0]
    pairs_dev = spec_saved.shape[3] // BS
    forward, inverse = lon_tables(KM, length)
    table = lat_table(assignment, n_rows)
    lat_pos = lax.axis_index("lat")
    lat_count = lax.axis_size("lat")
    own_lat = lax.dynamic_slice_in_dim(assignment, lat_pos * rows_dev, rows_dev)
    picked = own_lat[:, None] == jnp.arange(n_rows, dtype=jnp.int32)[None, :]
    own_count = jnp.sum(jnp.where(picked, mode_counts[None, :], 0), axis=1)
    active = (jnp.arange(KM, dtype=jnp.int32)[None, :] < own_count[:, None]).astype(jnp.float32)
    cotan = grad_out[0]
    spectral = jnp.einsum(
        "cml,rlni->rcmni",
        inverse,
        cotan.reshape(rows_dev, length, NB, BS),
        preferred_element_type=jnp.float32,
    )
    spectral = (spectral * active[:, None, :, None, None]).astype(jnp.bfloat16)
    spectral = spectral.reshape(rows_dev, 2, KM * NB * BS)
    pencil = lax.all_to_all(spectral, "lat", split_axis=2, concat_axis=0, tiled=True)
    pencil = pencil.reshape(n_rows, 2, pairs_dev, BS)
    grad_y = jnp.einsum(
        "kerc,rcpi->kepi", table, pencil, preferred_element_type=jnp.float32
    ).astype(jnp.bfloat16)
    saved = spec_saved[0].reshape(n_rows, 2, pairs_dev, BS)
    pair_ids = lat_pos * pairs_dev + jnp.arange(pairs_dev, dtype=jnp.int32)
    owner = (pair_ids % NB)[:, None] == jnp.arange(NB, dtype=jnp.int32)[None, :]
    selector = owner.astype(jnp.bfloat16)
    first = jnp.einsum(
        "pn,cinj->cipj", selector, w1[0].reshape(2, BS, NB, BS), preferred_element_type=jnp.float32
    ).astype(jnp.bfloat16)
    second = jnp.einsum(
        "pn,cinj->cipj", selector, w2[0].reshape(2, BS, NB, BS), preferred_element_type=jnp.float32
    ).astype(jnp.bfloat16)
    shift_b = jnp.einsum(
        "pn,cnj->cpj", selector, b1[0].reshape(2, NB, BS), preferred_element_type=jnp.float32
    )
    v_r = saved[:, 0]
    v_i = saved[:, 1]
    pre_r = apply_mat(v_r, first[0]) - apply_mat(v_i, first[1]) + shift_b[0][None]
    pre_i = apply_mat(v_i, first[0]) + apply_mat(v_r, first[1]) + shift_b[1][None]
    hid_r = jax.nn.silu(pre_r).astype(jnp.bfloat16)
    hid_i = jax.nn.silu(pre_i).astype(jnp.bfloat16)
    dy_r = grad_y[:, 0]
    dy_i = grad_y[:, 1]
    dh_r = adjoint_mat(dy_r, second[0]) + adjoint_mat(dy_i, second[1])
    dh_i = adjoint_mat(dy_i, second[0]) - adjoint_mat(dy_r, second[1])
    dp_r = (dh_r * silu_slope(pre_r)).astype(jnp.bfloat16)
    dp_i = (dh_i * silu_slope(pre_i)).astype(jnp.bfloat16)
    gw2 = jnp.stack(
        [
            outer_sum(hid_r, dy_r) + outer_sum(hid_i, dy_i),
            outer_sum(hid_r, dy_i) - outer_sum(hid_i, dy_r),
        ]
    )
    gw1 = jnp.stack(
        [outer_sum(v_r, dp_r) + outer_sum(v_i, dp_i), outer_sum(v_r, dp_i) - outer_sum(v_i, dp_r)]
    )
    gb1 = jnp.stack(
        [jnp.sum(dp_r.astype(jnp.float32), axis=0), jnp.sum(dp_i.astype(jnp.float32), axis=0)]
    )
    dv_r = adjoint_mat(dp_r, first[0]) + adjoint_mat(dp_i, first[1])
    dv_i = adjoint_mat(dp_i, first[0]) - adjoint_mat(dp_r, first[1])
    grad_v = jnp.stack([dv_r, dv_i], axis=1).astype(jnp.bfloat16)
    grad_u = jnp.einsum(
        "kerc,kepi->rcpi", table, grad_v, preferred_element_type=jnp.float32
    ).astype(jnp.bfloat16)
    grad_u = grad_u.reshape(n_rows, 2, pairs_dev * BS)
    back = lax.all_to_all(grad_u, "lat", split_axis=0, concat_axis=2, tiled=True)
    back = back.reshape(rows_dev, 2, KM, NB, BS) * active[:, None, :, None, None].astype(
        jnp.bfloat16
    )
    mixed = jnp.einsum("cml,rcmni->rlni", forward, back, preferred_element_type=jnp.float32)
    mixed = mixed.reshape(rows_dev, length, width).astype(jnp.bfloat16)
    owner_f = owner.astype(jnp.float32)
    block_w1 = jnp.einsum("pn,cipj->cinj", owner_f, gw1).reshape(1, 2, BS, width)
    block_w2 = jnp.einsum("pn,cipj->cinj", owner_f, gw2).reshape(1, 2, BS, width)
    block_b1 = jnp.einsum("pn,cpj->cnj", owner_f, gb1).reshape(1, 2, width)
    columns = width // lat_count
    full_w1, full_w2, full_b1 = lax.psum((block_w1, block_w2, block_b1), "lat")
    sum_w1 = lax.dynamic_slice_in_dim(full_w1, lat_pos * columns, columns, 3)
    sum_w2 = lax.dynamic_slice_in_dim(full_w2, lat_pos * columns, columns, 3)
    sum_b1 = lax.dynamic_slice_in_dim(full_b1, lat_pos * columns, columns, 2)
    whole = (cotan.astype(jnp.float32) + mixed.astype(jnp.float32)).astype(jnp.bfloat16)
    received = from_behind(whole[None], "section", -1)
    return (received, sum_w1, sum_w2, sum_b1)


def solution(mesh):
    return jax.shard_map(
        per_device,
        mesh=mesh,
        in_specs=(
            P("section", "lat", None, None),
            P("section", None, None, "lat"),
            P("section", None, None, None),
            P("section", None, None, None),
            P("section", None, None),
            P(),
            P(),
        ),
        out_specs=(
            P("section", "lat", None, None),
            P("section", None, None, "lat"),
            P("section", None, None, "lat"),
            P("section", None, "lat"),
        ),
        check_vma=False,
    )
```

profile of v0, /device:TPU:0, one launch (start us, length us, event | category | flops | bytes accessed | tf_op | source)
XLA Modules:
  0.0 368.8 jit_solution(2084462767684613967)
XLA Ops:
  7.2 1.2 dynamic_slice.12
  8.4 1.9 fusion.82
  13.3 21.7 %copy.90 = bf16[1,2,27648]{1,0,2:T(2,128)(2,1)} copy(bf16[1,2,27648]{2,1,0:T(2,128)(2,1)S(1)} %reshape.360) | data formatting | bytes 221184 | tf_op jit(solution)/shard_map/reshape | solution.py:84
  35.5 151.5 %reduce.2 = bf16[27648,2]{1,0:T(8,128)(2,1)} reduce(bf16[27648,1,2]{2,1,0:T(2,128)(2,1)} %bitcast.219, bf16[]{:T(256)} %broadcast.429), dimensions={1}, to_apply=%bitcast.195.reduce_sub_computation | reduce | bytes 221186
  187.0 14.4 %reshape.383 = bf16[8,2,3456]{2,1,0:T(2,128)(2,1)} reshape(bf16[27648,2]{1,0:T(8,128)(2,1)} %reduce.2) | data formatting | bytes 221184
  201.4 6.3 %all-to-all-start = ((bf16[8,2,3456]{2,1,0:T(2,128)(2,1)}), bf16[8,2,3456]{2,1,0:T(2,128)(2,1)S(1)}, u32[]{:S(2)}, u32[]{:S(2)}) async-start(bf16[8,2,3456]{2,1,0:T(2,128)(2,1)} %reshape.383), calls=%async_computation | async-start | bytes 221184 | tf_op jit(solution)/shard_map/all_to_all | solution.py:85
  210.3 1.3 slice_bitcast_fusion.1
  216.0 1.9 fusion.13
  217.9 1.2 fusion.16
  219.2 18.0 %reshape.384 = bf16[27648,1,2]{2,1,0:T(2,128)(2,1)} reshape(bf16[8,2,3456]{2,1,0:T(2,128)(2,1)S(1)} %all-to-all-done) | data formatting | bytes 221184
  237.2 25.9 %copy.91 = bf16[1,2,27648]{2,1,0:T(2,128)(2,1)S(1)} copy(bf16[1,2,27648]{1,0,2:T(2,128)(2,1)} %bitcast.218) | data formatting | bytes 221184 | tf_op jit(solution)/shard_map/all_to_all | solution.py:85
  266.3 1.7 fusion.65
  268.0 1.2 fusion.35
  269.8 1.7 fusion.64
  273.6 1.6 pad_maximum_fusion.1
  275.2 3.7 copy.117
  282.3 1.7 pad_maximum_fusion
  284.0 3.4 copy.115
  290.9 5.2 %all-to-all-start.1 = ((bf16[8,2,3456]{2,1,0:T(2,128)(2,1)}), bf16[8,2,3456]{2,1,0:T(2,128)(2,1)S(1)}, u32[]{:S(2)}, u32[]{:S(2)}) async-start(bf16[8,2,3456]{2,1,0:T(2,128)(2,1)} %reshape.381), calls=%async_computation.1 | async-start | bytes 221184 | tf_op jit(solution)/shard_map/all_to_all | solution.py:134
  298.3 17.6 %psum.23 = f32[1,2,384]{2,1,0:T(2,128)S(1)} all-reduce(f32[1,2,384]{2,1,0:T(2,128)S(1)} %reshape.366), channel_id=1, replica_groups=mesh['section'=4,'lat'=8] {'lat'}, use_global_device_ids=true, to_apply=%region_5.6 | all-reduce | flops 768 | bytes 6144 | tf_op jit(solution)/shard_map/psum | solution.py:145
  317.5 1.3 collective-permute-start
  318.8 39.7 %all-reduce.3.cloned.1.call-done = (f32[1,2,96,384]{2,3,1,0:T(8,128)}, f32[1,2,96,384]{2,3,1,0:T(8,128)}) async-done(((f32[1,2,96,384]{2,3,1,0:T(8,128)}, f32[1,2,96,384]{2,3,1,0:T(8,128)}), (f32[1,2,96,384]{2,3,1,0:T(8,128)}, f32[1,2,96,384]{2,3,1,0:T(8,128)})) %all-reduce.3.cloned.1.call-update) | async-done | bytes 589840 | tf_op jit(solution)/shard_map/psum | solution.py:145
  358.5 1.4 constant_dynamic-slice_fusion.1
  359.9 1.4 constant_dynamic-slice_fusion.2
  (97 shorter events, 27.2 us)
Async XLA Ops:
  187.0 20.8 %copy-start.13 = (s32[8]{0:T(128)S(1)}, s32[8]{0:T(128)}, u32[]{:S(2)}) copy-start(s32[8]{0:T(128)} %param.13) | copy-start | bytes 100
  187.0 22.4 %copy-start.9 = (bf16[1,2,96,384]{3,2,1,0:T(8,128)(2,1)S(1)}, bf16[1,2,96,384]{3,2,1,0:T(8,128)(2,1)}, u32[]{:S(2)}) copy-start(bf16[1,2,96,384]{3,2,1,0:T(8,128)(2,1)} %param.10) | copy-start | bytes 442372
  201.4 17.8 %all-to-all-start = ((bf16[8,2,3456]{2,1,0:T(2,128)(2,1)}), bf16[8,2,3456]{2,1,0:T(2,128)(2,1)S(1)}, u32[]{:S(2)}, u32[]{:S(2)}) async-start(bf16[8,2,3456]{2,1,0:T(2,128)(2,1)} %reshape.383), calls=%async_computation | async-start | bytes 221184 | tf_op jit(solution)/shard_map/all_to_all | solution.py:85
  210.3 1.3 copy-start.10
  212.5 0.9 copy-start.11
  212.6 1.1 copy-start.12
  213.4 4.5 %copy-start.2 = (bf16[96,36,96]{2,1,0:T(8,128)(2,1)}, bf16[96,36,96]{2,1,0:T(8,128)(2,1)S(1)}, u32[]{:S(2)}) copy-start(bf16[96,36,96]{2,1,0:T(8,128)(2,1)S(1)} %get-tuple-element.6) | copy-start | bytes 1990660
  237.2 26.4 %copy-start.4 = (bf16[96,36,96]{2,1,0:T(8,128)(2,1)S(1)}, bf16[96,36,96]{2,1,0:T(8,128)(2,1)}, u32[]{:S(2)}) copy-start(bf16[96,36,96]{2,1,0:T(8,128)(2,1)} %get-tuple-element.9) | copy-start | bytes 1990660
  263.4 1.4 copy-start.5
  278.9 1.5 copy-start
  280.4 1.5 copy-start.1
  287.4 1.2 copy-start.3
  287.4 1.2 copy-start.14
  287.4 1.7 copy-start.15
  290.9 25.9 %copy-start.7 = (bf16[1,72,180]{2,1,0:T(8,128)(2,1)S(1)}, bf16[1,72,180]{2,1,0:T(8,128)(2,1)}, u32[]{:S(2)}) copy-start(bf16[1,72,180]{2,1,0:T(8,128)(2,1)} %get-tuple-element.25) | copy-start | bytes 77764
  290.9 26.0 %copy-start.8 = (bf16[1,72,180]{2,1,0:T(8,128)(2,1)S(1)}, bf16[1,72,180]{2,1,0:T(8,128)(2,1)}, u32[]{:S(2)}) copy-start(bf16[1,72,180]{2,1,0:T(8,128)(2,1)} %get-tuple-element.26) | copy-start | bytes 77764
  290.9 25.6 %all-to-all-start.1 = ((bf16[8,2,3456]{2,1,0:T(2,128)(2,1)}), bf16[8,2,3456]{2,1,0:T(2,128)(2,1)S(1)}, u32[]{:S(2)}, u32[]{:S(2)}) async-start(bf16[8,2,3456]{2,1,0:T(2,128)(2,1)} %reshape.381), calls=%async_computation.1 | async-start | bytes 221184 | tf_op jit(solution)/shard_map/all_to_all | solution.py:134
  296.2 62.3 %all-reduce.3.cloned.1.call-start = ((), (), s32[]{:S(2)}) async-start(), calls=%async_computation.2 | async-start | bytes 1572864 | tf_op jit(solution)/shard_map/psum | solution.py:145
  298.3 19.2 %copy-start.6 = (bf16[1,1,180,384]{3,2,1,0:T(8,128)(2,1)S(1)}, bf16[1,1,180,384]{3,2,1,0:T(8,128)(2,1)}, u32[]{:S(2)}) copy-start(bf16[1,1,180,384]{3,2,1,0:T(8,128)(2,1)} %param.7) | copy-start | bytes 414724
  317.5 43.8 %collective-permute-start = (bf16[1,1,180,384]{3,2,1,0:T(8,128)(2,1)S(1)}, bf16[1,1,180,384]{3,2,1,0:T(8,128)(2,1)S(1)}, u32[]{:S(2)}, u32[]{:S(2)}) collective-permute-start(bf16[1,1,180,384]{3,2,1,0:T(8,128)(2,1)S(1)} %add_convert_fusion), channel_id=1, source_target_pairs={{8,0},{16,8},{24,16},{9,1},{17,9},{25,17},{10,2},{18,10},{26,18},{... | collective-permute-start | bytes 414728 | tf_op jit(solution)/shard_map/ppermute | solution.py:16
Sparse Core Ops, SparseCore 0:
  299.4 59.0 all-reduce.2
where the time goes:
time: 370 us; the launch traced here: 369 us
  other arithmetic  160 us (43%)
  local copies, waits for them, and re-layouts  104 us (28%)
  waiting for transfers between devices  39.7 us (11%)
  matrix products  20.7 us (6%)
  blocking collectives  17.6 us (5%)
  between operations  14.4 us (4%)
  starting transfers between devices  12.9 us (3%)
    unnamed x1, other arithmetic  152 us
    psum x1, waiting for transfers between devices, per_device(): full_w1, full_w2, full_b1 = lax.psum((block_w1, block_w2, block_b1), 'lat')  39.7 us
    unnamed x37, local copies, waits for them, and re-layouts  37.1 us
    all_to_all x1, local copies, waits for them, and re-layouts, per_device(): lax.all_to_all(spectral, 'lat', split_axis=2, concat_axis=0, tiled=True)  25.9 us
    reshape x2, local copies, waits for them, and re-layouts, per_device(): spectral = spectral.reshape(rows_dev, 2, KM * NB * BS)  21.9 us
    psum x1, blocking collectives, per_device(): full_w1, full_w2, full_b1 = lax.psum((block_w1, block_w2, block_b1), 'lat')  17.6 us
  transfers between devices with their start and end apart: 4, of which 1 were waited for; matrix products, arithmetic and copies ran while one was open for 5% of the time, Pallas kernels for 0%

commit v1 on v0

v1 whole, which is shorter than its diff:
```python
import functools
import math

import jax
import jax.numpy as jnp
import numpy as np
from jax import lax
from jax.experimental import pallas as pl
from jax.experimental.pallas import tpu as pltpu
from jax.sharding import PartitionSpec as P

NB = 4
BS = 96
KM = 72
LANES = 128
F32 = jnp.float32
BF16 = jnp.bfloat16


def from_behind(value, axis, by):
    length = lax.axis_size(axis)
    pairs = [(i, i + by) for i in range(length) if 0 <= i + by < length]
    return lax.ppermute(value, axis, pairs)


def lon_tables(n_modes, length):
    modes = np.arange(n_modes)
    phase = modes[:, None] * np.arange(length)[None, :] % length
    angle = phase * (2.0 * math.pi / length)
    forward = np.stack([np.cos(angle), -np.sin(angle)]) / math.sqrt(length)
    weight = np.where(modes == 0, 1.0, 2.0)[None, :, None]
    return forward, forward * weight


def lat_waves(n_rows):
    freqs = np.arange(n_rows)
    angle = (freqs[:, None] * freqs[None, :] % n_rows) * (2.0 * math.pi / n_rows)
    factor = 1.0 / math.sqrt(n_rows)
    return np.cos(angle) * factor, np.sin(angle) * factor


def silu_slope(pre):
    sig = jax.nn.sigmoid(pre)
    return sig * (1.0 + pre * (1.0 - sig))


def window(x, start):
    low = start // LANES * LANES
    shift = start - low
    if shift == 0:
        return x[:, low : low + LANES]
    if shift + BS <= LANES:
        return pltpu.roll(x[:, low : low + LANES], LANES - shift, 1)
    return pltpu.roll(x[:, low : low + 2 * LANES], 2 * LANES - shift, 1)[:, :LANES]


def dense(parts):
    lane = lax.broadcasted_iota(jnp.int32, parts[0].shape, 1)
    first = pltpu.roll(parts[1], 96, 1)
    second = pltpu.roll(parts[2], 64, 1)
    third = pltpu.roll(parts[3], 32, 1)
    return jnp.concatenate(
        [
            jnp.where(lane < 96, parts[0], first),
            jnp.where(lane < 64, first, second),
            jnp.where(lane < 32, second, third),
        ],
        axis=1,
    )


def dot(a, b, contract):
    return lax.dot_general(a, b, ((contract[:1], contract[1:]), ((), ())), preferred_element_type=F32)


def own_count(counts, assign):
    return counts[assign[lax.axis_index("lat")]]


def analyse_kernel(q, counts, assign, field, table, out):
    n_dev, pad, width = out.shape
    active = own_count(counts, assign)
    spectral = jnp.dot(table[...], field[...], preferred_element_type=F32)
    row = lax.broadcasted_iota(jnp.int32, (pad, width), 0)
    mode = jnp.where(row >= q, row - q, row)
    for d in range(n_dev):
        part = spectral[d * pad : (d + 1) * pad]
        out[d] = jnp.where(mode < active - q * d, part, 0.0).astype(BF16)


def filter_kernel(q, split, assign, pencil, saved, w1, w2, b1, lat, out, by_lat, mat1, mat2):
    n_rows, pad, width = pencil.shape
    points = q * n_rows
    cols = BS // split
    for r in range(n_rows):
        by_lat[assign[r]] = pencil[r].astype(F32)
    field = by_lat[...].reshape(n_rows * pad, width).astype(BF16)
    grad_y = dot(lat[...], field, (1, 0)).astype(BF16).astype(F32)
    parts = [saved[:, c, :].astype(F32) for c in range(2)]
    shift_b = b1[...].astype(F32)
    lane = lax.broadcasted_iota(jnp.int32, (BS, LANES), 1)
    gap = jnp.zeros((LANES - BS, 2 * LANES), BF16)
    for mat in (mat1, mat2):
        mat[BS:LANES] = gap
        mat[LANES + BS : 2 * LANES] = gap
    inner = []
    for n in range(NB):
        for mat, source in ((mat1, w1), (mat2, w2)):
            real, imag = (
                jnp.where(lane < BS, window(source[c].astype(F32), n * BS), 0.0) for c in range(2)
            )
            mat[0:BS] = jnp.concatenate([real, imag], axis=1).astype(BF16)
            mat[LANES : LANES + BS] = jnp.concatenate([-imag, real], axis=1).astype(BF16)
        bias = window(shift_b, n * BS)
        bias = jnp.concatenate([bias[0:1], bias[1:2]], axis=1)
        v = jnp.concatenate(
            [
                jnp.concatenate([window(part, (mm * NB + n) * BS) for mm in range(q)], axis=0)
                for part in parts
            ],
            axis=1,
        ).astype(BF16)
        dy = jnp.concatenate(
            [window(grad_y[c * points : (c + 1) * points], n * BS) for c in range(2)], axis=1
        ).astype(BF16)
        pre = dot(v, mat1[...], (1, 0)) + bias
        sig = jax.nn.sigmoid(pre)
        hidden = (pre * sig).astype(BF16)
        grad_hidden = dot(dy, mat2[...], (1, 1))
        dp = (grad_hidden * (sig * (1.0 + pre * (1.0 - sig)))).astype(BF16)
        dv = dot(dp, mat1[...], (1, 1))
        inner.append(jnp.concatenate([dv[:, :LANES], dv[:, LANES:]], axis=0))
        columns = []
        for left, right in ((dp, v), (dy, hidden)):
            both = dot(left, right, (0, 0))
            columns.append(both[:BS, :LANES] + both[LANES : LANES + BS, LANES:])
            columns.append(both[LANES : LANES + BS, :LANES] - both[:BS, LANES:])
        weights = dense(columns).astype(BF16)
        grad_b = jnp.sum(dp.astype(F32), axis=0, keepdims=True)
        for h in range(split):
            out[n * split + h, 0:cols] = weights[h * cols : (h + 1) * cols]
        mat_b = jnp.concatenate([grad_b, jnp.zeros((1, width - 2 * LANES), F32)], axis=1)
        inner[n] = (inner[n], mat_b)
    grad_v = dense([item[0] for item in inner]).astype(BF16)
    by_lat[...] = dot(lat[...], grad_v, (0, 0)).reshape(n_rows, pad, width)
    row = lax.broadcasted_iota(jnp.int32, (pad, width), 0)
    for d in range(n_rows):
        band = by_lat[assign[d]]
        out[d, cols : cols + pad] = jnp.where(row == 2 * q, inner[d // split][1], band).astype(BF16)


def compose_kernel(q, cols, counts, assign, back, field, table, out):
    n_dev, rows, width = back.shape
    pad = rows - cols
    active = own_count(counts, assign)
    spectral = back[:, cols:, :].astype(F32)
    row = lax.broadcasted_iota(jnp.int32, (pad, width), 0)
    mode = jnp.where(row >= q, row - q, row)
    held = [jnp.where(mode < active - q * d, spectral[d], 0.0) for d in range(n_dev)]
    held = jnp.concatenate(held, axis=0).astype(BF16)
    mixed = jnp.dot(table[...], held, preferred_element_type=F32).astype(BF16)
    out[...] = (field[...].astype(F32) + mixed.astype(F32)).astype(BF16)


def sum_kernel(q, split, back, gw1, gw2, gb1):
    n_dev, rows, width = back.shape
    cols = BS // split
    total = back[0, 0:cols].astype(F32)
    tail = back[0, cols:rows].astype(F32)
    for d in range(1, n_dev):
        total += back[d, 0:cols].astype(F32)
        tail += back[d, cols:rows].astype(F32)
    turned = total.T
    for w, ref in enumerate((gw1, gw2)):
        for c in range(2):
            start = (2 * w + c) * BS
            ref[c] = turned[start : start + BS]
    half = lax.rem(lax.axis_index("lat"), split)
    for c in range(2):
        line = tail[2 * q : 2 * q + 1, c * LANES : (c + 1) * LANES]
        picked = line[:, 0:cols]
        for h in range(1, split):
            picked = jnp.where(half == h, line[:, h * cols : (h + 1) * cols], picked)
        gb1[c : c + 1] = picked


def call(kernel, outs, scratch, n_scalars, *args):
    whole = pl.BlockSpec(memory_space=pltpu.VMEM)
    scalar = pl.BlockSpec(memory_space=pltpu.SMEM)
    specs = [scalar] * n_scalars + [whole] * (len(args) - n_scalars)
    many = isinstance(outs, tuple)
    return pl.pallas_call(
        kernel,
        out_shape=outs,
        in_specs=specs,
        out_specs=tuple([whole] * len(outs)) if many else whole,
        scratch_shapes=scratch,
        compiler_params=pltpu.CompilerParams(vmem_limit_bytes=32 * 2**20),
    )(*args)


def whole_blocks(grad_out, spec_saved, w1, w2, b1, mode_counts, assignment):
    length, width = grad_out.shape[2:]
    n_rows = assignment.shape[0]
    n_dev = lax.axis_size("lat")
    q = spec_saved.shape[3] // (NB * BS)
    split = n_dev // NB
    cols = BS // split
    pad = (2 * q + 8) // 8 * 8
    forward, inverse = lon_tables(KM, length)

    def by_device(table):
        table = table.reshape(2, n_dev, q, length).transpose(1, 0, 2, 3)
        table = table.reshape(n_dev, 2 * q, length)
        table = np.pad(table, ((0, 0), (0, pad - 2 * q), (0, 0)))
        return table.reshape(n_dev * pad, length).astype(BF16)

    cosine, sine = lat_waves(n_rows)
    eye = np.eye(q)
    rounds = np.array([[cosine, sine], [-sine, cosine]])
    lat = np.einsum("eckr,mv->emkrcv", rounds, eye)
    lat = lat.reshape(2 * q * n_rows, n_rows, 2 * q)
    lat = np.pad(lat, ((0, 0), (0, 0), (0, pad - 2 * q))).reshape(2 * q * n_rows, n_rows * pad)
    lat = jnp.asarray(lat.astype(BF16))
    inverse = jnp.asarray(by_device(inverse))
    forward = jnp.asarray(by_device(forward).T)

    field = grad_out.reshape(length, width)
    spectral = call(
        functools.partial(analyse_kernel, q),
        jax.ShapeDtypeStruct((n_dev, pad, width), BF16),
        [],
        2,
        mode_counts,
        assignment,
        field,
        inverse,
    )
    pencil = lax.all_to_all(spectral, "lat", split_axis=0, concat_axis=0, tiled=True)
    chunks = call(
        functools.partial(filter_kernel, q, split),
        jax.ShapeDtypeStruct((n_dev, cols + pad, width), BF16),
        [
            pltpu.VMEM((n_rows, pad, width), F32),
            pltpu.VMEM((2 * LANES, 2 * LANES), BF16),
            pltpu.VMEM((2 * LANES, 2 * LANES), BF16),
        ],
        1,
        assignment,
        pencil,
        spec_saved[0],
        w1[0],
        w2[0],
        b1[0],
        lat,
    )
    back = lax.all_to_all(chunks, "lat", split_axis=0, concat_axis=0, tiled=True)
    total = call(
        functools.partial(compose_kernel, q, cols),
        jax.ShapeDtypeStruct((length, width), BF16),
        [],
        2,
        mode_counts,
        assignment,
        back,
        field,
        forward,
    )
    received = from_behind(total[None, None], "section", -1)
    gw1, gw2, gb1 = call(
        functools.partial(sum_kernel, q, split),
        (
            jax.ShapeDtypeStruct((2, BS, cols), F32),
            jax.ShapeDtypeStruct((2, BS, cols), F32),
            jax.ShapeDtypeStruct((2, cols), F32),
        ),
        [],
        0,
        back,
    )
    return received, gw1[None], gw2[None], gb1[None]


def apply_mat(vec, mat):
    return jnp.einsum("kpi,ipj->kpj", vec, mat, preferred_element_type=F32)


def adjoint_mat(vec, mat):
    return jnp.einsum("kpj,ipj->kpi", vec, mat, preferred_element_type=F32)


def outer_sum(left, right):
    return jnp.einsum("kpi,kpj->ipj", left, right, preferred_element_type=F32)


def split_blocks(grad_out, spec_saved, w1, w2, b1, mode_counts, assignment):
    rows_dev = grad_out.shape[1]
    length = grad_out.shape[2]
    width = grad_out.shape[3]
    n_rows = assignment.shape[0]
    pairs_dev = spec_saved.shape[3] // BS
    forward, inverse = (jnp.asarray(t.astype(BF16)) for t in lon_tables(KM, length))
    cosine, sine = (jnp.asarray(t.astype(BF16))[:, assignment] for t in lat_waves(n_rows))
    table = jnp.stack(
        [jnp.stack([cosine, sine], axis=-1), jnp.stack([-sine, cosine], axis=-1)], axis=1
    )
    lat_pos = lax.axis_index("lat")
    lat_count = lax.axis_size("lat")
    own_lat = lax.dynamic_slice_in_dim(assignment, lat_pos * rows_dev, rows_dev)
    active = (jnp.arange(KM, dtype=jnp.int32)[None, :] < mode_counts[own_lat][:, None]).astype(F32)
    cotan = grad_out[0]
    spectral = jnp.einsum(
        "cml,rlni->rcmni",
        inverse,
        cotan.reshape(rows_dev, length, NB, BS),
        preferred_element_type=F32,
    )
    spectral = (spectral * active[:, None, :, None, None]).astype(BF16)
    spectral = spectral.reshape(rows_dev, 2, KM * NB * BS)
    pencil = lax.all_to_all(spectral, "lat", split_axis=2, concat_axis=0, tiled=True)
    pencil = pencil.reshape(n_rows, 2, pairs_dev, BS)
    grad_y = jnp.einsum("kerc,rcpi->kepi", table, pencil, preferred_element_type=F32).astype(BF16)
    saved = spec_saved[0].reshape(n_rows, 2, pairs_dev, BS)
    pair_ids = lat_pos * pairs_dev + jnp.arange(pairs_dev, dtype=jnp.int32)
    owner = (pair_ids % NB)[:, None] == jnp.arange(NB, dtype=jnp.int32)[None, :]
    owner = owner.astype(F32)
    first = jnp.take(w1[0].reshape(2, BS, NB, BS), pair_ids % NB, axis=2)
    second = jnp.take(w2[0].reshape(2, BS, NB, BS), pair_ids % NB, axis=2)
    shift_b = jnp.take(b1[0].reshape(2, NB, BS), pair_ids % NB, axis=1).astype(F32)
    v_r = saved[:, 0]
    v_i = saved[:, 1]
    pre_r = apply_mat(v_r, first[0]) - apply_mat(v_i, first[1]) + shift_b[0][None]
    pre_i = apply_mat(v_i, first[0]) + apply_mat(v_r, first[1]) + shift_b[1][None]
    hid_r = jax.nn.silu(pre_r).astype(BF16)
    hid_i = jax.nn.silu(pre_i).astype(BF16)
    dy_r = grad_y[:, 0]
    dy_i = grad_y[:, 1]
    dh_r = adjoint_mat(dy_r, second[0]) + adjoint_mat(dy_i, second[1])
    dh_i = adjoint_mat(dy_i, second[0]) - adjoint_mat(dy_r, second[1])
    dp_r = (dh_r * silu_slope(pre_r)).astype(BF16)
    dp_i = (dh_i * silu_slope(pre_i)).astype(BF16)
    gw2 = jnp.stack(
        [
            outer_sum(hid_r, dy_r) + outer_sum(hid_i, dy_i),
            outer_sum(hid_r, dy_i) - outer_sum(hid_i, dy_r),
        ]
    )
    gw1 = jnp.stack(
        [outer_sum(v_r, dp_r) + outer_sum(v_i, dp_i), outer_sum(v_r, dp_i) - outer_sum(v_i, dp_r)]
    )
    gb1 = jnp.stack([jnp.sum(dp_r.astype(F32), axis=0), jnp.sum(dp_i.astype(F32), axis=0)])
    dv_r = adjoint_mat(dp_r, first[0]) + adjoint_mat(dp_i, first[1])
    dv_i = adjoint_mat(dp_i, first[0]) - adjoint_mat(dp_r, first[1])
    grad_v = jnp.stack([dv_r, dv_i], axis=1).astype(BF16)
    grad_u = jnp.einsum("kerc,kepi->rcpi", table, grad_v, preferred_element_type=F32).astype(BF16)
    grad_u = grad_u.reshape(n_rows, 2, pairs_dev * BS)
    back = lax.all_to_all(grad_u, "lat", split_axis=0, concat_axis=2, tiled=True)
    back = back.reshape(rows_dev, 2, KM, NB, BS) * active[:, None, :, None, None].astype(BF16)
    mixed = jnp.einsum("cml,rcmni->rlni", forward, back, preferred_element_type=F32)
    mixed = mixed.reshape(rows_dev, length, width).astype(BF16)
    block_w1 = jnp.einsum("pn,cipj->cinj", owner, gw1).reshape(1, 2, BS, width)
    block_w2 = jnp.einsum("pn,cipj->cinj", owner, gw2).reshape(1, 2, BS, width)
    block_b1 = jnp.einsum("pn,cpj->cnj", owner, gb1).reshape(1, 2, width)
    columns = width // lat_count
    full_w1, full_w2, full_b1 = lax.psum((block_w1, block_w2, block_b1), "lat")
    sum_w1 = lax.dynamic_slice_in_dim(full_w1, lat_pos * columns, columns, 3)
    sum_w2 = lax.dynamic_slice_in_dim(full_w2, lat_pos * columns, columns, 3)
    sum_b1 = lax.dynamic_slice_in_dim(full_b1, lat_pos * columns, columns, 2)
    whole = (cotan.astype(F32) + mixed.astype(F32)).astype(BF16)
    received = from_behind(whole[None], "section", -1)
    return (received, sum_w1, sum_w2, sum_b1)


def per_device(grad_out, spec_saved, w1, w2, b1, mode_counts, assignment):
    n_dev = lax.axis_size("lat")
    pairs_dev = spec_saved.shape[3] // BS
    even = grad_out.shape[1] == 1 and pairs_dev % NB == 0 and n_dev % NB == 0
    even = even and BS % (n_dev // NB) == 0 and BS // (n_dev // NB) % 16 == 0
    body = whole_blocks if even else split_blocks
    return body(grad_out, spec_saved, w1, w2, b1, mode_counts, assignment)


def solution(mesh):
    return jax.shard_map(
        per_device,
        mesh=mesh,
        in_specs=(
            P("section", "lat", None, None),
            P("section", None, None, "lat"),
            P("section", None, None, None),
            P("section", None, None, None),
            P("section", None, None),
            P(),
            P(),
        ),
        out_specs=(
            P("section", "lat", None, None),
            P("section", None, None, "lat"),
            P("section", None, None, "lat"),
            P("section", None, "lat"),
        ),
        check_vma=False,
    )
```

time: 370 us -> 45.2 us (0.12)
  other arithmetic: 160 us -> 0 us
  local copies, waits for them, and re-layouts: 104 us -> 5.2 us
  waiting for transfers between devices: 39.7 us -> 3.67 us
  matrix products: 20.7 us -> 0 us
  between operations: 14.4 us -> 0.73 us
  blocking collectives: 17.6 us -> 29.6 us
  starting transfers between devices: 12.9 us -> 1.29 us
  Pallas kernels: 0 us -> 4.36 us
    unnamed x1 -> x0, other arithmetic: 152 us -> none
    psum x1 -> x0, waiting for transfers between devices: 39.7 us -> none  [per_device(): full_w1, full_w2, full_b1 = lax.psum((block_w1, block_w2, block_b1), 'lat')]
    unnamed x37 -> x25, local copies, waits for them, and re-layouts: 37.1 us -> 5.2 us
    all_to_all x0 -> x2, blocking collectives: none -> 29.6 us  [the longest x1 16.4 us: whole_blocks(): lax.all_to_all(chunks, 'lat', split_axis=0, concat_axis=0, tiled=True)]
    reshape x10 -> x0, local copies, waits for them, and re-layouts: 26.2 us -> none  [the longest x2 21.9 us: per_device(): spectral = spectral.reshape(rows_dev, 2, KM * NB * BS)]
    all_to_all x2 -> x0, local copies, waits for them, and re-layouts: 26 us -> none  [the longest x1 25.9 us: per_device(): lax.all_to_all(spectral, 'lat', split_axis=2, concat_axis=0, tiled=True)]
    dot_general x30 -> x0, matrix products: 20.7 us -> none  [the longest x8 6.1 us: outer_sum(): jnp.einsum('kpi,kpj->ipj', left, right, preferred_element_type=jnp.float32)]
    psum x1 -> x0, blocking collectives: 17.6 us -> none  [per_device(): full_w1, full_w2, full_b1 = lax.psum((block_w1, block_w2, block_b1), 'lat')]
  transfers between devices with their start and end apart: 4 -> 1, of which waited for: 1 -> 1; matrix products, arithmetic and copies ran while one was open for 5% -> 3% of each run, Pallas kernels for 0% -> 2%
where the time goes in v1:
time: 45.2 us; the launch traced here: 44.9 us
  blocking collectives  29.6 us (65%)
  local copies, waits for them, and re-layouts  5.2 us (12%)
  Pallas kernels  4.36 us (10%)
  waiting for transfers between devices  3.67 us (8%)
  starting transfers between devices  1.29 us (3%)
  between operations  0.73 us (2%)
    all_to_all x1, blocking collectives, whole_blocks(): lax.all_to_all(chunks, 'lat', split_axis=0, concat_axis=0, tiled=True)  16.4 us
    all_to_all x1, blocking collectives, whole_blocks(): lax.all_to_all(spectral, 'lat', split_axis=0, concat_axis=0, tiled=True)  13.2 us
    unnamed x25, local copies, waits for them, and re-layouts  5.2 us
    pallas_call x4, Pallas kernels, call(): pl.pallas_call(kernel, out_shape=outs, in_specs=specs, out_specs=tuple([w...  4.36 us
    ppermute x1, waiting for transfers between devices, from_behind(): return lax.ppermute(value, axis, pairs)  3.67 us
    ppermute x1, starting transfers between devices, from_behind(): return lax.ppermute(value, axis, pairs)  1.29 us
  transfers between devices with their start and end apart: 1, of which 1 were waited for; matrix products, arithmetic and copies ran while one was open for 3% of the time, Pallas kernels for 2%

profile of v1, /device:TPU:0, one launch (start us, length us, event | category | flops | bytes accessed | tf_op | source)
XLA Modules:
  0.0 44.9 jit_solution(7818794311074350299)
XLA Ops:
  0.6 0.0 copy-start.8
  0.6 0.0 copy-start.9
  0.7 0.6 %copy-done.8 = s32[8]{0:T(128)S(1)} copy-done((s32[8]{0:T(128)S(1)}, s32[8]{0:T(128)}, u32[]{:S(2)}) %copy-start.8) | copy-done | bytes 56
  1.3 0.0 copy-done.9
  1.3 0.9 %copy-done = bf16[1,1,180,384]{3,2,1,0:T(8,128)(2,1)S(1)} copy-done((bf16[1,1,180,384]{3,2,1,0:T(8,128)(2,1)S(1)}, bf16[1,1,180,384]{3,2,1,0:T(8,128)(2,1)}, u32[]{:S(2)}) %copy-start) | copy-done | bytes 138264
  2.2 0.9 %copy-done.5 = bf16[192,180]{1,0:T(8,128)(2,1)S(1)} copy-done((bf16[192,180]{1,0:T(8,128)(2,1)S(1)}, bf16[192,180]{1,0:T(8,128)(2,1)}, u32[]{:S(2)}) %copy-start.5) | copy-done | bytes 69144
  3.1 0.7 %shard_map.129 = bf16[8,24,384]{2,1,0:T(8,128)(2,1)S(1)} custom-call(s32[8]{0:T(128)S(1)} %copy-done.9, s32[8]{0:T(128)S(1)} %copy-done.8, bf16[180,384]{1,0:T(8,128)(2,1)S(1)} %bitcast.9, bf16[192,180]{1,0:T(8,128)(2,1)S(1)} %copy-done.5), custom_call_target="tpu_custom_call" | custom-call | tf_op jit(solution)/shard_map/pallas_call | solution.py:192
  3.9 0.0 copy-start.2
  3.9 0.0 copy-start.3
  3.9 13.2 %all_to_all.10.pencil = bf16[8,24,384]{2,1,0:T(8,128)(2,1)S(1)} all-to-all(bf16[8,24,384]{2,1,0:T(8,128)(2,1)S(1)} %shard_map.129), channel_id=1, replica_groups=mesh['section'=4,'lat'=8] {'lat'}, dimensions={0} | all-to-all | bytes 294912 | tf_op jit(solution)/shard_map/all_to_all | solution.py:239
  17.1 0.0 copy-done.4
  17.2 0.7 %copy-done.10 = bf16[1,2,384]{2,1,0:T(2,128)(2,1)S(1)} copy-done((bf16[1,2,384]{2,1,0:T(2,128)(2,1)S(1)}, bf16[1,2,384]{2,1,0:T(2,128)(2,1)}, u32[]{:S(2)}) %copy-start.10) | copy-done | bytes 1560
  17.8 2.1 %shard_map.130 = bf16[8,72,384]{2,1,0:T(8,128)(2,1)S(1)} custom-call(s32[8]{0:T(128)S(1)} %copy-done.8, bf16[8,24,384]{2,1,0:T(8,128)(2,1)S(1)} %all_to_all.10.pencil, bf16[8,2,3456]{2,1,0:T(2,128)(2,1)S(1)} %bitcast.14, bf16[2,96,384]{2,1,0:T(8,128)(2,1)S(1)} %bitcast.11, bf16[2,96,384]{2,1,0:T(8,128)(2,1)S(1)} %bitcast.12, bf16[2,384]{1,0:T(2,128)(2,1)S(1)} %bitcast.17, ...), custom_call_target="tpu_custom_call" | custom-call | tf_op jit(solution)/shard_map/pallas_call | solution.py:192
  20.0 0.0 copy-start.1
  20.0 0.0 copy-start.6
  20.0 16.4 %all_to_all.11.back = bf16[8,72,384]{2,1,0:T(8,128)(2,1)S(1)} all-to-all(bf16[8,72,384]{2,1,0:T(8,128)(2,1)S(1)} %shard_map.130), channel_id=1, replica_groups=mesh['section'=4,'lat'=8] {'lat'}, dimensions={0} | all-to-all | bytes 884736 | tf_op jit(solution)/shard_map/all_to_all | solution.py:257
  36.3 0.0 copy-done.1
  36.3 0.8 %shard_map.131 = bf16[180,384]{1,0:T(8,128)(2,1)S(1)} custom-call(s32[8]{0:T(128)S(1)} %copy-done.9, s32[8]{0:T(128)S(1)} %copy-done.8, bf16[8,72,384]{2,1,0:T(8,128)(2,1)S(1)} %all_to_all.11.back, bf16[180,384]{1,0:T(8,128)(2,1)S(1)} %bitcast.10, bf16[180,192]{1,0:T(8,128)(2,1)S(1)} %copy-done.6), custom_call_target="tpu_custom_call" | custom-call | tf_op jit(solution)/shard_map/pallas_call | solution.py:192
  37.1 1.3 %collective-permute-start = (bf16[1,1,180,384]{3,2,1,0:T(8,128)(2,1)S(1)}, bf16[1,1,180,384]{3,2,1,0:T(8,128)(2,1)S(1)}, u32[]{:S(2)}, u32[]{:S(2)}) collective-permute-start(bf16[1,1,180,384]{3,2,1,0:T(8,128)(2,1)S(1)} %bitcast.13), channel_id=1, source_target_pairs={{8,0},{16,8},{24,16},{9,1},{17,9},{25,17},{10,2},{18,10},{26,18},{... | collective-permute-start | bytes 414728 | tf_op jit(solution)/shard_map/ppermute | solution.py:23
  38.4 0.7 %shard_map.132 = (f32[2,96,48]{2,1,0:T(8,128)S(1)}, f32[2,96,48]{2,1,0:T(8,128)S(1)}, f32[2,48]{1,0:T(2,128)}) custom-call(bf16[8,72,384]{2,1,0:T(8,128)(2,1)S(1)} %all_to_all.11.back), custom_call_target="tpu_custom_call" | custom-call | tf_op jit(solution)/shard_map/pallas_call | solution.py:192
  39.1 0.7 %copy.14 = f32[1,2,96,48]{2,3,1,0:T(8,128)} copy(f32[1,2,96,48]{3,2,1,0:T(8,128)S(1)} %bitcast.16) | data formatting | bytes 73728
  39.8 0.7 %copy.15 = f32[1,2,96,48]{2,3,1,0:T(8,128)} copy(f32[1,2,96,48]{3,2,1,0:T(8,128)S(1)} %bitcast.15) | data formatting | bytes 73728
  40.5 3.7 %collective-permute-done = bf16[1,1,180,384]{3,2,1,0:T(8,128)(2,1)S(1)} collective-permute-done((bf16[1,1,180,384]{3,2,1,0:T(8,128)(2,1)S(1)}, bf16[1,1,180,384]{3,2,1,0:T(8,128)(2,1)S(1)}, u32[]{:S(2)}, u32[]{:S(2)}) %collective-permute-start) | collective-permute-done | bytes 138272 | tf_op jit(solution)/shard_map/ppermute | solution.py:23
  44.2 0.7 %copy.17 = bf16[1,1,180,384]{3,2,1,0:T(8,128)(2,1)} copy(bf16[1,1,180,384]{3,2,1,0:T(8,128)(2,1)S(1)} %collective-permute-done) | data formatting | bytes 276480
  (9 shorter events, 0.0 us)
Async XLA Ops:
  0.6 0.7 %copy-start.8 = (s32[8]{0:T(128)S(1)}, s32[8]{0:T(128)}, u32[]{:S(2)}) copy-start(s32[8]{0:T(128)} %assign.5) | copy-start | bytes 100
  0.6 0.7 %copy-start.9 = (s32[8]{0:T(128)S(1)}, s32[8]{0:T(128)}, u32[]{:S(2)}) copy-start(s32[8]{0:T(128)} %counts.3) | copy-start | bytes 100
  1.3 0.9 %copy-start = (bf16[1,1,180,384]{3,2,1,0:T(8,128)(2,1)S(1)}, bf16[1,1,180,384]{3,2,1,0:T(8,128)(2,1)}, u32[]{:S(2)}) copy-start(bf16[1,1,180,384]{3,2,1,0:T(8,128)(2,1)} %param.10) | copy-start | bytes 414724
  2.2 0.9 %copy-start.5 = (bf16[192,180]{1,0:T(8,128)(2,1)S(1)}, bf16[192,180]{1,0:T(8,128)(2,1)}, u32[]{:S(2)}) copy-start(bf16[192,180]{1,0:T(8,128)(2,1)} %constant.7.clone.table) | copy-start | bytes 207364
  3.1 14.0 %copy-start.4 = (bf16[1,8,2,3456]{3,2,1,0:T(2,128)(2,1)S(1)}, bf16[1,8,2,3456]{3,2,1,0:T(2,128)(2,1)}, u32[]{:S(2)}) copy-start(bf16[1,8,2,3456]{3,2,1,0:T(2,128)(2,1)} %param.11) | copy-start | bytes 331780
  3.1 14.0 %copy-start.7 = (bf16[144,192]{1,0:T(8,128)(2,1)S(1)}, bf16[144,192]{1,0:T(8,128)(2,1)}, u32[]{:S(2)}) copy-start(bf16[144,192]{1,0:T(8,128)(2,1)} %constant.6.clone.lat) | copy-start | bytes 165892
  3.9 13.3 %copy-start.2 = (bf16[1,2,96,384]{3,2,1,0:T(8,128)(2,1)S(1)}, bf16[1,2,96,384]{3,2,1,0:T(8,128)(2,1)}, u32[]{:S(2)}) copy-start(bf16[1,2,96,384]{3,2,1,0:T(8,128)(2,1)} %param.12) | copy-start | bytes 442372
  3.9 13.3 %copy-start.3 = (bf16[1,2,96,384]{3,2,1,0:T(8,128)(2,1)S(1)}, bf16[1,2,96,384]{3,2,1,0:T(8,128)(2,1)}, u32[]{:S(2)}) copy-start(bf16[1,2,96,384]{3,2,1,0:T(8,128)(2,1)} %param.13) | copy-start | bytes 442372
  17.1 0.7 %copy-start.10 = (bf16[1,2,384]{2,1,0:T(2,128)(2,1)S(1)}, bf16[1,2,384]{2,1,0:T(2,128)(2,1)}, u32[]{:S(2)}) copy-start(bf16[1,2,384]{2,1,0:T(2,128)(2,1)} %param.14) | copy-start | bytes 4612
  20.0 16.4 %copy-start.1 = (bf16[1,1,180,384]{3,2,1,0:T(8,128)(2,1)S(1)}, bf16[1,1,180,384]{3,2,1,0:T(8,128)(2,1)}, u32[]{:S(2)}) copy-start(bf16[1,1,180,384]{3,2,1,0:T(8,128)(2,1)} %param.10) | copy-start | bytes 414724
  20.0 16.4 %copy-start.6 = (bf16[180,192]{1,0:T(8,128)(2,1)S(1)}, bf16[180,192]{1,0:T(8,128)(2,1)}, u32[]{:S(2)}) copy-start(bf16[180,192]{1,0:T(8,128)(2,1)} %constant.8.clone.table) | copy-start | bytes 207364
  37.1 7.1 %collective-permute-start = (bf16[1,1,180,384]{3,2,1,0:T(8,128)(2,1)S(1)}, bf16[1,1,180,384]{3,2,1,0:T(8,128)(2,1)S(1)}, u32[]{:S(2)}, u32[]{:S(2)}) collective-permute-start(bf16[1,1,180,384]{3,2,1,0:T(8,128)(2,1)S(1)} %bitcast.13), channel_id=1, source_target_pairs={{8,0},{16,8},{24,16},{9,1},{17,9},{25,17},{10,2},{18,10},{26,18},{... | collective-permute-start | bytes 414728 | tf_op jit(solution)/shard_map/ppermute | solution.py:23

commit v2 on v1

--- a/solution.py
+++ b/solution.py
@@ -73,115 +73,108 @@
     return lax.dot_general(a, b, ((contract[:1], contract[1:]), ((), ())), preferred_element_type=F32)
 
 
-def own_count(counts, assign):
-    return counts[assign[lax.axis_index("lat")]]
-
-
-def analyse_kernel(q, counts, assign, field, table, out):
-    n_dev, pad, width = out.shape
-    active = own_count(counts, assign)
+def keep_active(counts, assign, q, groups):
+    active = counts[assign[lax.axis_index("lat")]]
+    shape = groups[0].shape
+    number = lax.broadcasted_iota(jnp.int32, shape, 0)
+    number = jnp.where(number >= NB * q, number - NB * q, number)
+    mode = number
+    for z in range(1, NB):
+        mode = jnp.where(number >= z * q, number + z * q, mode)
+    return [jnp.where(mode < active - g * q, value, 0.0) for g, value in enumerate(groups)]
+
+
+def analyse_kernel(q, counts, assign, field, table, saved, out):
+    rows = out.shape[1]
     spectral = jnp.dot(table[...], field[...], preferred_element_type=F32)
-    row = lax.broadcasted_iota(jnp.int32, (pad, width), 0)
-    mode = jnp.where(row >= q, row - q, row)
-    for d in range(n_dev):
-        part = spectral[d * pad : (d + 1) * pad]
-        out[d] = jnp.where(mode < active - q * d, part, 0.0).astype(BF16)
-
-
-def filter_kernel(q, split, assign, pencil, saved, w1, w2, b1, lat, out, by_lat, mat1, mat2):
-    n_rows, pad, width = pencil.shape
-    points = q * n_rows
-    cols = BS // split
-    for r in range(n_rows):
-        by_lat[assign[r]] = pencil[r].astype(F32)
-    field = by_lat[...].reshape(n_rows * pad, width).astype(BF16)
-    grad_y = dot(lat[...], field, (1, 0)).astype(BF16).astype(F32)
+    groups = keep_active(counts, assign, q, [spectral[:rows], spectral[rows:]])
     parts = [saved[:, c, :].astype(F32) for c in range(2)]
-    shift_b = b1[...].astype(F32)
-    lane = lax.broadcasted_iota(jnp.int32, (BS, LANES), 1)
+    for n in range(NB):
+        pieces = [window(group, n * BS) for group in groups]
+        for part in parts:
+            columns = [window(part, (mm * NB + n) * BS) for mm in range(q)]
+            pieces.append(jnp.concatenate(columns, axis=0))
+        out[n] = dense(pieces).astype(BF16)
+
+
+def weights_kernel(w1, w2, b1, mat1, mat2, bias):
+    block = lax.axis_index("lat") // 2
+
+    def pick(x):
+        value = window(x, 0)
+        for n in range(1, NB):
+            value = jnp.where(block == n, window(x, n * BS), value)
+        lane = lax.broadcasted_iota(jnp.int32, value.shape, 1)
+        return jnp.where(lane < BS, value, 0.0)
+
     gap = jnp.zeros((LANES - BS, 2 * LANES), BF16)
-    for mat in (mat1, mat2):
+    for source, mat in ((w1, mat1), (w2, mat2)):
+        real, imag = (pick(source[c].astype(F32)) for c in range(2))
+        mat[0:BS] = jnp.concatenate([real, imag], axis=1).astype(BF16)
         mat[BS:LANES] = gap
+        mat[LANES : LANES + BS] = jnp.concatenate([-imag, real], axis=1).astype(BF16)
         mat[LANES + BS : 2 * LANES] = gap
-    inner = []
-    for n in range(NB):
-        for mat, source in ((mat1, w1), (mat2, w2)):
-            real, imag = (
-                jnp.where(lane < BS, window(source[c].astype(F32), n * BS), 0.0) for c in range(2)
-            )
-            mat[0:BS] = jnp.concatenate([real, imag], axis=1).astype(BF16)
-            mat[LANES : LANES + BS] = jnp.concatenate([-imag, real], axis=1).astype(BF16)
-        bias = window(shift_b, n * BS)
-        bias = jnp.concatenate([bias[0:1], bias[1:2]], axis=1)
-        v = jnp.concatenate(
-            [
-                jnp.concatenate([window(part, (mm * NB + n) * BS) for mm in range(q)], axis=0)
-                for part in parts
-            ],
-            axis=1,
-        ).astype(BF16)
-        dy = jnp.concatenate(
-            [window(grad_y[c * points : (c + 1) * points], n * BS) for c in range(2)], axis=1
-        ).astype(BF16)
-        pre = dot(v, mat1[...], (1, 0)) + bias
+    shift_b = pick(b1[...].astype(F32))
+    bias[...] = jnp.concatenate([shift_b[0:1], shift_b[1:2]], axis=1)
+
+
+def filter_kernel(assign, own, other, mat1, mat2, bias, lat, lat_t, out, gw1, gw2, gb1, by_lat):
+    n_half, rows, width = own.shape
+    core = lax.rem(lax.axis_index("lat"), 2)
+    segments = [BS * j for j in range(4)]
+    saved = []
+    for b, buffer in enumerate((own, other)):
+        side = core if b == 0 else 1 - core
+        pieces = []
+        for z in range(n_half):
+            chunk = buffer[z].astype(F32)
+            groups = [window(chunk, segments[j]) for j in range(2)]
+            by_lat[assign[2 * z + side]] = jnp.concatenate(groups, axis=1)
+            parts = [window(chunk, segments[j]) for j in (2, 3)]
+            pieces.append(jnp.concatenate(parts, axis=1))
+        saved.append(jnp.concatenate(pieces, axis=0).astype(BF16))
+    field = by_lat[...].reshape(lat.shape[1], 2 * LANES).astype(BF16)
+    grad_y = dot(lat[...], field, (1, 0)).astype(BF16)
+    points = grad_y.shape[0] // 2
+    first, second = mat1[...], mat2[...]
+    both1, both2, sums, inner = 0.0, 0.0, 0.0, []
+    for g in range(2):
+        v = jnp.where(core == g, saved[0], saved[1])
+        dy = [grad_y[c * points : (c + 1) * points, g * LANES : (g + 1) * LANES] for c in range(2)]
+        dy = jnp.concatenate(dy, axis=1)
+        pre = dot(v, first, (1, 0)) + bias[...]
         sig = jax.nn.sigmoid(pre)
         hidden = (pre * sig).astype(BF16)
-        grad_hidden = dot(dy, mat2[...], (1, 1))
+        grad_hidden = dot(dy, second, (1, 1))
         dp = (grad_hidden * (sig * (1.0 + pre * (1.0 - sig)))).astype(BF16)
-        dv = dot(dp, mat1[...], (1, 1))
+        dv = dot(dp, first, (1, 1)).astype(BF16)
         inner.append(jnp.concatenate([dv[:, :LANES], dv[:, LANES:]], axis=0))
-        columns = []
-        for left, right in ((dp, v), (dy, hidden)):
-            both = dot(left, right, (0, 0))
-            columns.append(both[:BS, :LANES] + both[LANES : LANES + BS, LANES:])
-            columns.append(both[LANES : LANES + BS, :LANES] - both[:BS, LANES:])
-        weights = dense(columns).astype(BF16)
-        grad_b = jnp.sum(dp.astype(F32), axis=0, keepdims=True)
-        for h in range(split):
-            out[n * split + h, 0:cols] = weights[h * cols : (h + 1) * cols]
-        mat_b = jnp.concatenate([grad_b, jnp.zeros((1, width - 2 * LANES), F32)], axis=1)
-        inner[n] = (inner[n], mat_b)
-    grad_v = dense([item[0] for item in inner]).astype(BF16)
-    by_lat[...] = dot(lat[...], grad_v, (0, 0)).reshape(n_rows, pad, width)
-    row = lax.broadcasted_iota(jnp.int32, (pad, width), 0)
-    for d in range(n_rows):
-        band = by_lat[assign[d]]
-        out[d, cols : cols + pad] = jnp.where(row == 2 * q, inner[d // split][1], band).astype(BF16)
-
-
-def compose_kernel(q, cols, counts, assign, back, field, table, out):
-    n_dev, rows, width = back.shape
-    pad = rows - cols
-    active = own_count(counts, assign)
-    spectral = back[:, cols:, :].astype(F32)
-    row = lax.broadcasted_iota(jnp.int32, (pad, width), 0)
-    mode = jnp.where(row >= q, row - q, row)
-    held = [jnp.where(mode < active - q * d, spectral[d], 0.0) for d in range(n_dev)]
-    held = jnp.concatenate(held, axis=0).astype(BF16)
+        both1 += dot(dp, v, (0, 0))
+        both2 += dot(dy, hidden, (0, 0))
+        sums += jnp.sum(dp.astype(F32), axis=0, keepdims=True)
+    inner = jnp.concatenate(inner, axis=1)
+    for z in range(n_half):
+        band = dot(lat_t[assign[2 * z + core]], inner, (1, 0))
+        out[z] = band.astype(BF16)
+    half = BS // 2
+    for both, ref in ((both1, gw1), (both2, gw2)):
+        real = both[:BS, :LANES] + both[LANES : LANES + BS, LANES:]
+        imag = both[LANES : LANES + BS, :LANES] - both[:BS, LANES:]
+        for c, full in enumerate((real, imag)):
+            ref[c] = jnp.where(core == 0, full[:half], full[half:])[:, :BS]
+    for c in range(2):
+        line = sums[:, c * LANES : (c + 1) * LANES]
+        gb1[c : c + 1] = jnp.where(core == 0, line[:, :half], line[:, half:BS])
+
+
+def compose_kernel(q, counts, assign, back, field, table, out):
+    chunks = [back[n].astype(F32) for n in range(NB)]
+    groups = [
+        dense([chunk[:, g * LANES : (g + 1) * LANES] for chunk in chunks]) for g in range(2)
+    ]
+    held = jnp.concatenate(keep_active(counts, assign, q, groups), axis=0).astype(BF16)
     mixed = jnp.dot(table[...], held, preferred_element_type=F32).astype(BF16)
     out[...] = (field[...].astype(F32) + mixed.astype(F32)).astype(BF16)
-
-
-def sum_kernel(q, split, back, gw1, gw2, gb1):
-    n_dev, rows, width = back.shape
-    cols = BS // split
-    total = back[0, 0:cols].astype(F32)
-    tail = back[0, cols:rows].astype(F32)
-    for d in range(1, n_dev):
-        total += back[d, 0:cols].astype(F32)
-        tail += back[d, cols:rows].astype(F32)
-    turned = total.T
-    for w, ref in enumerate((gw1, gw2)):
-        for c in range(2):
-            start = (2 * w + c) * BS
-            ref[c] = turned[start : start + BS]
-    half = lax.rem(lax.axis_index("lat"), split)
-    for c in range(2):
-        line = tail[2 * q : 2 * q + 1, c * LANES : (c + 1) * LANES]
-        picked = line[:, 0:cols]
-        for h in range(1, split):
-            picked = jnp.where(half == h, line[:, h * cols : (h + 1) * cols], picked)
-        gb1[c : c + 1] = picked
 
 
 def call(kernel, outs, scratch, n_scalars, *args):
@@ -199,64 +192,82 @@
     )(*args)
 
 
-def whole_blocks(grad_out, spec_saved, w1, w2, b1, mode_counts, assignment):
+def paired_blocks(grad_out, spec_saved, w1, w2, b1, mode_counts, assignment):
     length, width = grad_out.shape[2:]
     n_rows = assignment.shape[0]
-    n_dev = lax.axis_size("lat")
     q = spec_saved.shape[3] // (NB * BS)
-    split = n_dev // NB
-    cols = BS // split
-    pad = (2 * q + 8) // 8 * 8
+    rows = 2 * NB * q
     forward, inverse = lon_tables(KM, length)
 
-    def by_device(table):
-        table = table.reshape(2, n_dev, q, length).transpose(1, 0, 2, 3)
-        table = table.reshape(n_dev, 2 * q, length)
-        table = np.pad(table, ((0, 0), (0, pad - 2 * q), (0, 0)))
-        return table.reshape(n_dev * pad, length).astype(BF16)
+    def by_group(table):
+        table = table.reshape(2, NB, 2, q, length).transpose(2, 0, 1, 3, 4)
+        return table.reshape(2 * rows, length).astype(BF16)
 
     cosine, sine = lat_waves(n_rows)
-    eye = np.eye(q)
-    rounds = np.array([[cosine, sine], [-sine, cosine]])
-    lat = np.einsum("eckr,mv->emkrcv", rounds, eye)
-    lat = lat.reshape(2 * q * n_rows, n_rows, 2 * q)
-    lat = np.pad(lat, ((0, 0), (0, 0), (0, pad - 2 * q))).reshape(2 * q * n_rows, n_rows * pad)
-    lat = jnp.asarray(lat.astype(BF16))
-    inverse = jnp.asarray(by_device(inverse))
-    forward = jnp.asarray(by_device(forward).T)
+    waves = np.array([[cosine, sine], [-sine, cosine]])
+    lat = np.einsum("eckr,uv->eukrcv", waves, np.eye(NB * q))
+    lat = lat.reshape(2 * NB * q * n_rows, n_rows * rows).astype(BF16)
+    lat_t = np.ascontiguousarray(lat.T).reshape(n_rows, rows, -1)
 
     field = grad_out.reshape(length, width)
-    spectral = call(
+    sent = call(
         functools.partial(analyse_kernel, q),
-        jax.ShapeDtypeStruct((n_dev, pad, width), BF16),
+        jax.ShapeDtypeStruct((NB, rows, width), BF16),
         [],
         2,
         mode_counts,
         assignment,
         field,
-        inverse,
-    )
-    pencil = lax.all_to_all(spectral, "lat", split_axis=0, concat_axis=0, tiled=True)
-    chunks = call(
-        functools.partial(filter_kernel, q, split),
-        jax.ShapeDtypeStruct((n_dev, cols + pad, width), BF16),
-        [
-            pltpu.VMEM((n_rows, pad, width), F32),
-            pltpu.VMEM((2 * LANES, 2 * LANES), BF16),
-            pltpu.VMEM((2 * LANES, 2 * LANES), BF16),
-        ],
-        1,
-        assignment,
-        pencil,
+        jnp.asarray(by_group(inverse)),
         spec_saved[0],
+    )
+    cores = [[2 * z + c for z in range(NB)] for c in range(2)]
+    exchange = functools.partial(
+        lax.all_to_all,
+        axis_name="lat",
+        split_axis=0,
+        concat_axis=0,
+        axis_index_groups=cores,
+        tiled=True,
+    )
+    own = exchange(sent)
+    wide = (2 * LANES, 2 * LANES)
+    mat1, mat2, bias = call(
+        weights_kernel,
+        (
+            jax.ShapeDtypeStruct(wide, BF16),
+            jax.ShapeDtypeStruct(wide, BF16),
+            jax.ShapeDtypeStruct((1, 2 * LANES), F32),
+        ),
+        [],
+        0,
         w1[0],
         w2[0],
         b1[0],
-        lat,
-    )
-    back = lax.all_to_all(chunks, "lat", split_axis=0, concat_axis=0, tiled=True)
+    )
+    other = lax.ppermute(own, "lat", [(i, i ^ 1) for i in range(2 * NB)])
+    chunks, gw1, gw2, gb1 = call(
+        filter_kernel,
+        (
+            jax.ShapeDtypeStruct((NB, rows, 2 * LANES), BF16),
+            jax.ShapeDtypeStruct((2, BS // 2, BS), F32),
+            jax.ShapeDtypeStruct((2, BS // 2, BS), F32),
+            jax.ShapeDtypeStruct((2, BS // 2), F32),
+        ),
+        [pltpu.VMEM((n_rows, rows, 2 * LANES), F32)],
+        1,
+        assignment,
+        own,
+        other,
+        mat1,
+        mat2,
+        bias,
+        jnp.asarray(lat),
+        jnp.asarray(lat_t),
+    )
+    back = exchange(chunks)
     total = call(
-        functools.partial(compose_kernel, q, cols),
+        functools.partial(compose_kernel, q),
         jax.ShapeDtypeStruct((length, width), BF16),
         [],
         2,
@@ -264,21 +275,10 @@
         assignment,
         back,
         field,
-        forward,
+        jnp.asarray(by_group(forward).T),
     )
     received = from_behind(total[None, None], "section", -1)
-    gw1, gw2, gb1 = call(
-        functools.partial(sum_kernel, q, split),
-        (
-            jax.ShapeDtypeStruct((2, BS, cols), F32),
-            jax.ShapeDtypeStruct((2, BS, cols), F32),
-            jax.ShapeDtypeStruct((2, cols), F32),
-        ),
-        [],
-        0,
-        back,
-    )
-    return received, gw1[None], gw2[None], gb1[None]
+    return received, gw1.swapaxes(1, 2)[None], gw2.swapaxes(1, 2)[None], gb1[None]
 
 
 def apply_mat(vec, mat):
@@ -374,9 +374,8 @@
 def per_device(grad_out, spec_saved, w1, w2, b1, mode_counts, assignment):
     n_dev = lax.axis_size("lat")
     pairs_dev = spec_saved.shape[3] // BS
-    even = grad_out.shape[1] == 1 and pairs_dev % NB == 0 and n_dev % NB == 0
-    even = even and BS % (n_dev // NB) == 0 and BS // (n_dev // NB) % 16 == 0
-    body = whole_blocks if even else split_blocks
+    paired = n_dev == 2 * NB and grad_out.shape[1] == 1 and pairs_dev % NB == 0
+    body = paired_blocks if paired else split_blocks
     return body(grad_out, spec_saved, w1, w2, b1, mode_counts, assignment)
 
 

time: 45.2 us -> 45.3 us (level)
  blocking collectives: 29.6 us -> 24.1 us
  local copies, waits for them, and re-layouts: 5.2 us -> 8.09 us
  waiting for transfers between devices: 3.67 us -> 5.67 us
  Pallas kernels: 4.36 us -> 4.97 us
    all_to_all x2, blocking collectives: 29.6 us -> 24.1 us  [the longest x1 14.2 us: paired_blocks(): own = exchange(sent)]
    unnamed x25 -> x29, local copies, waits for them, and re-layouts: 5.2 us -> 8.09 us
    ppermute x1, waiting for transfers between devices: 3.67 us -> 5.67 us  [from_behind(): return lax.ppermute(value, axis, pairs)]
    pallas_call x4, Pallas kernels: 4.36 us -> 4.97 us  [call(): pl.pallas_call(kernel, out_shape=outs, in_specs=specs, out_specs=tuple([w...]
  transfers between devices with their start and end apart: 1 -> 2, of which waited for: 1 -> 1; matrix products, arithmetic and copies ran while one was open for 3% -> 0% of each run, Pallas kernels for 2% -> 0%
where the time goes in v2:
time: 45.3 us; the launch traced here: 44.9 us
  blocking collectives  24.1 us (53%)
  local copies, waits for them, and re-layouts  8.09 us (18%)
  waiting for transfers between devices  5.67 us (13%)
  Pallas kernels  4.97 us (11%)
  starting transfers between devices  1.29 us (3%)
  between operations  0.73 us (2%)
    all_to_all x1, blocking collectives, paired_blocks(): own = exchange(sent)  14.2 us
    all_to_all x1, blocking collectives, paired_blocks(): back = exchange(chunks)  9.87 us
    unnamed x29, local copies, waits for them, and re-layouts  8.09 us
    ppermute x1, waiting for transfers between devices, from_behind(): return lax.ppermute(value, axis, pairs)  5.67 us
    pallas_call x4, Pallas kernels, call(): pl.pallas_call(kernel, out_shape=outs, in_specs=specs, out_specs=tuple([w...  4.97 us
    ppermute x1, starting transfers between devices, from_behind(): return lax.ppermute(value, axis, pairs)  1.29 us
  transfers between devices with their start and end apart: 2, of which 1 were waited for; matrix products, arithmetic and copies ran while one was open for 0% of the time, Pallas kernels for 0%

profile of v2, /device:TPU:0, one launch (start us, length us, event | category | flops | bytes accessed | tf_op | source)
XLA Modules:
  0.0 44.9 jit_solution(15167324664643762630)
XLA Ops:
  0.6 0.0 copy-start
  0.6 0.0 copy-start.2
  0.7 1.0 %copy-done.2 = bf16[1,1,180,384]{3,2,1,0:T(8,128)(2,1)S(1)} copy-done((bf16[1,1,180,384]{3,2,1,0:T(8,128)(2,1)S(1)}, bf16[1,1,180,384]{3,2,1,0:T(8,128)(2,1)}, u32[]{:S(2)}) %copy-start.2) | copy-done | bytes 138264
  1.6 0.9 %copy-done.6 = bf16[1,8,2,3456]{3,2,1,0:T(2,128)(2,1)S(1)} copy-done((bf16[1,8,2,3456]{3,2,1,0:T(2,128)(2,1)S(1)}, bf16[1,8,2,3456]{3,2,1,0:T(2,128)(2,1)}, u32[]{:S(2)}) %copy-start.6) | copy-done | bytes 110616
  2.5 0.9 %copy-done.8 = bf16[144,180]{1,0:T(8,128)(2,1)S(1)} copy-done((bf16[144,180]{1,0:T(8,128)(2,1)S(1)}, bf16[144,180]{1,0:T(8,128)(2,1)}, u32[]{:S(2)}) %copy-start.8) | copy-done | bytes 51864
  3.4 0.7 %copy-done.9 = s32[8]{0:T(128)S(1)} copy-done((s32[8]{0:T(128)S(1)}, s32[8]{0:T(128)}, u32[]{:S(2)}) %copy-start.9) | copy-done | bytes 56
  4.1 0.7 %copy-done.11 = s32[8]{0:T(128)S(1)} copy-done((s32[8]{0:T(128)S(1)}, s32[8]{0:T(128)}, u32[]{:S(2)}) %copy-start.11) | copy-done | bytes 56
  4.7 1.2 %shard_map.138 = bf16[4,72,384]{2,1,0:T(8,128)(2,1)S(1)} custom-call(s32[8]{0:T(128)S(1)} %copy-done.11, s32[8]{0:T(128)S(1)} %copy-done.9, bf16[180,384]{1,0:T(8,128)(2,1)S(1)} %bitcast.13, bf16[144,180]{1,0:T(8,128)(2,1)S(1)} %copy-done.8, bf16[8,2,3456]{2,1,0:T(2,128)(2,1)S(1)} %bitcast.18), custom_call_target="tpu_custom_call" | custom-call | tf_op jit(solution)/shard_map/pallas_call | solution.py:185
  5.9 0.0 copy-start.4
  5.9 14.2 %all_to_all.10.own = bf16[4,72,384]{2,1,0:T(8,128)(2,1)S(1)} all-to-all(bf16[4,72,384]{2,1,0:T(8,128)(2,1)S(1)} %shard_map.138), channel_id=1, replica_groups={{0,2,4,6},{1,3,5,7},{8,10,12,14},{9,11,13,15},{16,18,20,22},{17,19,21,2..., dimensions={0} | all-to-all | bytes 442368 | tf_op jit(solution)/shard_map/all_to_all | solution.py:233
  20.1 0.0 collective-permute-start
  20.2 0.7 %copy-done.13 = bf16[1,2,384]{2,1,0:T(2,128)(2,1)S(1)} copy-done((bf16[1,2,384]{2,1,0:T(2,128)(2,1)S(1)}, bf16[1,2,384]{2,1,0:T(2,128)(2,1)}, u32[]{:S(2)}) %copy-start.13) | copy-done | bytes 1560
  20.8 0.9 %copy-done.5 = bf16[1,2,96,384]{3,2,1,0:T(8,128)(2,1)S(1)} copy-done((bf16[1,2,96,384]{3,2,1,0:T(8,128)(2,1)S(1)}, bf16[1,2,96,384]{3,2,1,0:T(8,128)(2,1)}, u32[]{:S(2)}) %copy-start.5) | copy-done | bytes 147480
  21.7 0.2 shard_map.139
  22.0 0.0 collective-permute-done.other
  22.0 0.0 copy-start.10
  22.0 0.6 %copy-done.10 = s32[8]{0:T(128)S(1)} copy-done((s32[8]{0:T(128)S(1)}, s32[8]{0:T(128)}, u32[]{:S(2)}) %copy-start.10) | copy-done | bytes 56
  22.6 1.1 %copy-done.1 = bf16[576,576]{1,0:T(8,128)(2,1)S(1)} copy-done((bf16[576,576]{1,0:T(8,128)(2,1)S(1)}, bf16[576,576]{1,0:T(8,128)(2,1)}, u32[]{:S(2)}) %copy-start.1) | copy-done | bytes 663576
  23.7 2.8 %shard_map.140 = (bf16[4,72,256]{2,1,0:T(8,128)(2,1)S(1)}, f32[2,48,96]{2,1,0:T(8,128)}, f32[2,48,96]{2,1,0:T(8,128)}, f32[2,48]{1,0:T(2,128)}) custom-call(s32[8]{0:T(128)S(1)} %copy-done.10, bf16[4,72,384]{2,1,0:T(8,128)(2,1)S(1)} %all_to_all.10.own, bf16[4,72,384]{2,1,0:T(8,128)(2,1)S(1)} %collective-permute-done.other, ...), custom_call_target="tpu_custom_call" | custom-call | tf_op jit(solution)/shard_map/pallas_call | solution.py:185
  26.5 9.9 %all_to_all.11.back = bf16[4,72,256]{2,1,0:T(8,128)(2,1)S(1)} all-to-all(bf16[4,72,256]{2,1,0:T(8,128)(2,1)S(1)} %get-tuple-element.14), channel_id=1, replica_groups={{0,2,4,6},{1,3,5,7},{8,10,12,14},{9,11,13,15},{16,18,20,22},{17,19,21,2..., dimensions={0} | all-to-all | bytes 294912 | tf_op jit(solution)/shard_map/all_to_all | solution.py:268
  36.4 0.8 %shard_map.141 = bf16[180,384]{1,0:T(8,128)(2,1)S(1)} custom-call(s32[8]{0:T(128)S(1)} %copy-done.12, s32[8]{0:T(128)S(1)} %copy-done.10, bf16[4,72,256]{2,1,0:T(8,128)(2,1)S(1)} %all_to_all.11.back, bf16[180,384]{1,0:T(8,128)(2,1)S(1)} %bitcast.14, bf16[180,144]{1,0:T(8,128)(2,1)S(1)} %copy-done.7), custom_call_target="tpu_custom_call" | custom-call | tf_op jit(solution)/shard_map/pallas_call | solution.py:185
  37.2 1.3 %collective-permute-start.1 = (bf16[1,1,180,384]{3,2,1,0:T(8,128)(2,1)S(1)}, bf16[1,1,180,384]{3,2,1,0:T(8,128)(2,1)S(1)}, u32[]{:S(2)}, u32[]{:S(2)}) collective-permute-start(bf16[1,1,180,384]{3,2,1,0:T(8,128)(2,1)S(1)} %bitcast.17), channel_id=1, source_target_pairs={{8,0},{16,8},{24,16},{9,1},{17,9},{25,17},{10,2},{18,10},{26,18},{... | collective-permute-start | bytes 414728 | tf_op jit(solution)/shard_map/ppermute | solution.py:23
  38.5 5.7 %collective-permute-done.1 = bf16[1,1,180,384]{3,2,1,0:T(8,128)(2,1)S(1)} collective-permute-done((bf16[1,1,180,384]{3,2,1,0:T(8,128)(2,1)S(1)}, bf16[1,1,180,384]{3,2,1,0:T(8,128)(2,1)S(1)}, u32[]{:S(2)}, u32[]{:S(2)}) %collective-permute-start.1) | collective-permute-done | bytes 138272 | tf_op jit(solution)/shard_map/ppermute | solution.py:23
  44.2 0.7 %copy.16 = bf16[1,1,180,384]{3,2,1,0:T(8,128)(2,1)} copy(bf16[1,1,180,384]{3,2,1,0:T(8,128)(2,1)S(1)} %collective-permute-done.1) | data formatting | bytes 276480
  (15 shorter events, 0.0 us)
Async XLA Ops:
  0.6 21.4 %copy-start = (bf16[8,72,576]{2,1,0:T(8,128)(2,1)S(1)}, bf16[8,72,576]{2,1,0:T(8,128)(2,1)}, u32[]{:S(2)}) copy-start(bf16[8,72,576]{2,1,0:T(8,128)(2,1)} %constant.10.clone.lat_t) | copy-start | bytes 1990660
  0.6 1.0 %copy-start.2 = (bf16[1,1,180,384]{3,2,1,0:T(8,128)(2,1)S(1)}, bf16[1,1,180,384]{3,2,1,0:T(8,128)(2,1)}, u32[]{:S(2)}) copy-start(bf16[1,1,180,384]{3,2,1,0:T(8,128)(2,1)} %param.11) | copy-start | bytes 414724
  1.6 0.9 %copy-start.6 = (bf16[1,8,2,3456]{3,2,1,0:T(2,128)(2,1)S(1)}, bf16[1,8,2,3456]{3,2,1,0:T(2,128)(2,1)}, u32[]{:S(2)}) copy-start(bf16[1,8,2,3456]{3,2,1,0:T(2,128)(2,1)} %param.12) | copy-start | bytes 331780
  2.5 0.9 %copy-start.8 = (bf16[144,180]{1,0:T(8,128)(2,1)S(1)}, bf16[144,180]{1,0:T(8,128)(2,1)}, u32[]{:S(2)}) copy-start(bf16[144,180]{1,0:T(8,128)(2,1)} %constant.8.clone.table) | copy-start | bytes 155524
  3.4 0.7 %copy-start.9 = (s32[8]{0:T(128)S(1)}, s32[8]{0:T(128)}, u32[]{:S(2)}) copy-start(s32[8]{0:T(128)} %assign.5) | copy-start | bytes 100
  4.1 0.7 %copy-start.11 = (s32[8]{0:T(128)S(1)}, s32[8]{0:T(128)}, u32[]{:S(2)}) copy-start(s32[8]{0:T(128)} %counts.3) | copy-start | bytes 100
  5.9 14.3 %copy-start.4 = (bf16[1,2,96,384]{3,2,1,0:T(8,128)(2,1)S(1)}, bf16[1,2,96,384]{3,2,1,0:T(8,128)(2,1)}, u32[]{:S(2)}) copy-start(bf16[1,2,96,384]{3,2,1,0:T(8,128)(2,1)} %param.13) | copy-start | bytes 442372
  20.1 1.8 %collective-permute-start = (bf16[4,72,384]{2,1,0:T(8,128)(2,1)S(1)}, bf16[4,72,384]{2,1,0:T(8,128)(2,1)S(1)}, u32[]{:S(2)}, u32[]{:S(2)}) collective-permute-start(bf16[4,72,384]{2,1,0:T(8,128)(2,1)S(1)} %all_to_all.10.own), channel_id=1, source_target_pairs={{0,1},{1,0},{2,3},{3,2},{4,5},{5,4},{6,7},{7,6},{8,9},{9,8},{10,11... | collective-permute-start | bytes 663560 | tf_op jit(solution)/shard_map/ppermute | solution.py:248
  20.1 0.7 %copy-start.13 = (bf16[1,2,384]{2,1,0:T(2,128)(2,1)S(1)}, bf16[1,2,384]{2,1,0:T(2,128)(2,1)}, u32[]{:S(2)}) copy-start(bf16[1,2,384]{2,1,0:T(2,128)(2,1)} %param.15) | copy-start | bytes 4612
  20.8 0.9 %copy-start.5 = (bf16[1,2,96,384]{3,2,1,0:T(8,128)(2,1)S(1)}, bf16[1,2,96,384]{3,2,1,0:T(8,128)(2,1)}, u32[]{:S(2)}) copy-start(bf16[1,2,96,384]{3,2,1,0:T(8,128)(2,1)} %param.14) | copy-start | bytes 442372
  22.0 0.7 %copy-start.10 = (s32[8]{0:T(128)S(1)}, s32[8]{0:T(128)}, u32[]{:S(2)}) copy-start(s32[8]{0:T(128)} %assign.5) | copy-start | bytes 100
  22.6 1.1 %copy-start.1 = (bf16[576,576]{1,0:T(8,128)(2,1)S(1)}, bf16[576,576]{1,0:T(8,128)(2,1)}, u32[]{:S(2)}) copy-start(bf16[576,576]{1,0:T(8,128)(2,1)} %constant.9.clone.lat) | copy-start | bytes 1990660
  26.5 9.9 %copy-start.3 = (bf16[1,1,180,384]{3,2,1,0:T(8,128)(2,1)S(1)}, bf16[1,1,180,384]{3,2,1,0:T(8,128)(2,1)}, u32[]{:S(2)}) copy-start(bf16[1,1,180,384]{3,2,1,0:T(8,128)(2,1)} %param.11) | copy-start | bytes 414724
  26.5 9.9 %copy-start.7 = (bf16[180,144]{1,0:T(8,128)(2,1)S(1)}, bf16[180,144]{1,0:T(8,128)(2,1)}, u32[]{:S(2)}) copy-start(bf16[180,144]{1,0:T(8,128)(2,1)} %constant.11.clone.table) | copy-start | bytes 155524
  26.5 9.9 %copy-start.12 = (s32[8]{0:T(128)S(1)}, s32[8]{0:T(128)}, u32[]{:S(2)}) copy-start(s32[8]{0:T(128)} %counts.3) | copy-start | bytes 100
  37.2 7.0 %collective-permute-start.1 = (bf16[1,1,180,384]{3,2,1,0:T(8,128)(2,1)S(1)}, bf16[1,1,180,384]{3,2,1,0:T(8,128)(2,1)S(1)}, u32[]{:S(2)}, u32[]{:S(2)}) collective-permute-start(bf16[1,1,180,384]{3,2,1,0:T(8,128)(2,1)S(1)} %bitcast.17), channel_id=1, source_target_pairs={{8,0},{16,8},{24,16},{9,1},{17,9},{25,17},{10,2},{18,10},{26,18},{... | collective-permute-start | bytes 414728 | tf_op jit(solution)/shard_map/ppermute | solution.py:23

commit v3 on v2

--- a/solution.py
+++ b/solution.py
@@ -84,20 +84,51 @@
     return [jnp.where(mode < active - g * q, value, 0.0) for g, value in enumerate(groups)]
 
 
-def analyse_kernel(q, counts, assign, field, table, saved, out):
-    rows = out.shape[1]
+def fetch(sems, sources, targets):
+    copies = [
+        pltpu.make_async_copy(source, target, sems.at[i])
+        for i, (source, target) in enumerate(zip(sources, targets))
+    ]
+    for copy in copies:
+        copy.start()
+    return copies
+
+
+def wait(copies):
+    for copy in copies:
+        copy.wait()
+
+
+def partner(d):
+    return jnp.bitwise_xor(lax.axis_index("lat") // 2, d)
+
+
+def analyse_kernel(q, *refs):
+    hbm, outs, held, (by_block, sems) = refs[:5], refs[5:9], refs[9:14], refs[14:]
+    counts, assign, field, table, saved = held
+    copies = fetch(sems, hbm, held)
+    wait(copies[4:])
+    parts = [saved[:, c, :].astype(F32) for c in range(2)]
+    points = [
+        [
+            jnp.concatenate([window(part, (mm * NB + n) * BS) for mm in range(q)], axis=0)
+            for part in parts
+        ]
+        for n in range(NB)
+    ]
+    wait(copies[:4])
+    rows = by_block.shape[1]
     spectral = jnp.dot(table[...], field[...], preferred_element_type=F32)
     groups = keep_active(counts, assign, q, [spectral[:rows], spectral[rows:]])
-    parts = [saved[:, c, :].astype(F32) for c in range(2)]
     for n in range(NB):
         pieces = [window(group, n * BS) for group in groups]
-        for part in parts:
-            columns = [window(part, (mm * NB + n) * BS) for mm in range(q)]
-            pieces.append(jnp.concatenate(columns, axis=0))
-        out[n] = dense(pieces).astype(BF16)
-
-
-def weights_kernel(w1, w2, b1, mat1, mat2, bias):
+        by_block[n] = dense(pieces + points[n]).astype(BF16)
+    for d, out in enumerate(outs):
+        out[...] = by_block[partner(d)]
+
+
+def weights_kernel(w1_hbm, w2_hbm, b1_hbm, mat1, mat2, bias, w1, w2, b1, sems):
+    wait(fetch(sems, (w1_hbm, w2_hbm, b1_hbm), (w1, w2, b1)))
     block = lax.axis_index("lat") // 2
 
     def pick(x):
@@ -118,28 +149,57 @@
     bias[...] = jnp.concatenate([shift_b[0:1], shift_b[1:2]], axis=1)
 
 
-def filter_kernel(assign, own, other, mat1, mat2, bias, lat, lat_t, out, gw1, gw2, gb1, by_lat):
+def join_kernel(*refs):
+    out = refs[-1]
+    for d, ref in enumerate(refs[:-1]):
+        out[d] = ref[...]
+
+
+def pack(band):
+    rows = band.shape[0]
+    tail = rows // 2 + 4
+    left, right = band[:, :LANES], pltpu.roll(band[:, LANES:], 96, 1)
+    lane = lax.broadcasted_iota(jnp.int32, left.shape, 1)
+    upper = jnp.where(lane < 96, left, right)
+    lower = pltpu.roll(right[rows - tail :], 64, 1)
+    lower = jnp.where(lane[:tail] < 64, right[:tail], lower)
+    return jnp.concatenate([upper, lower], axis=0)
+
+
+def unpack(packed, rows):
+    tail = rows // 2 + 4
+    upper, lower = packed[:rows], packed[rows:]
+    rest = jnp.concatenate([lower, pltpu.roll(lower, 64, 1)[2 * tail - rows :]], axis=0)
+    lane = lax.broadcasted_iota(jnp.int32, upper.shape, 1)
+    right = jnp.where(lane < 32, pltpu.roll(upper, 32, 1), pltpu.roll(rest, 32, 1))
+    return [upper, right]
+
+
+def filter_kernel(*refs):
+    own, other, mat1, mat2, bias, assign_hbm, lat_hbm, lat_t_hbm = refs[:8]
+    outs, (gw1, gw2, gb1) = refs[8:12], refs[12:15]
+    assign, lat, lat_t, by_lat, points_v, sems = refs[15:]
+    copies = fetch(sems, (assign_hbm, lat_hbm, lat_t_hbm), (assign, lat, lat_t))
+    wait(copies[:1])
     n_half, rows, width = own.shape
     core = lax.rem(lax.axis_index("lat"), 2)
     segments = [BS * j for j in range(4)]
-    saved = []
     for b, buffer in enumerate((own, other)):
         side = core if b == 0 else 1 - core
-        pieces = []
-        for z in range(n_half):
-            chunk = buffer[z].astype(F32)
+        for d in range(n_half):
+            chunk = buffer[d].astype(F32)
             groups = [window(chunk, segments[j]) for j in range(2)]
-            by_lat[assign[2 * z + side]] = jnp.concatenate(groups, axis=1)
+            by_lat[assign[2 * partner(d) + side]] = jnp.concatenate(groups, axis=1)
             parts = [window(chunk, segments[j]) for j in (2, 3)]
-            pieces.append(jnp.concatenate(parts, axis=1))
-        saved.append(jnp.concatenate(pieces, axis=0).astype(BF16))
+            points_v[side, partner(d)] = jnp.concatenate(parts, axis=1)
     field = by_lat[...].reshape(lat.shape[1], 2 * LANES).astype(BF16)
+    wait(copies[1:2])
     grad_y = dot(lat[...], field, (1, 0)).astype(BF16)
     points = grad_y.shape[0] // 2
     first, second = mat1[...], mat2[...]
     both1, both2, sums, inner = 0.0, 0.0, 0.0, []
     for g in range(2):
-        v = jnp.where(core == g, saved[0], saved[1])
+        v = points_v[g].reshape(points, 2 * LANES).astype(BF16)
         dy = [grad_y[c * points : (c + 1) * points, g * LANES : (g + 1) * LANES] for c in range(2)]
         dy = jnp.concatenate(dy, axis=1)
         pre = dot(v, first, (1, 0)) + bias[...]
@@ -153,9 +213,10 @@
         both2 += dot(dy, hidden, (0, 0))
         sums += jnp.sum(dp.astype(F32), axis=0, keepdims=True)
     inner = jnp.concatenate(inner, axis=1)
-    for z in range(n_half):
-        band = dot(lat_t[assign[2 * z + core]], inner, (1, 0))
-        out[z] = band.astype(BF16)
+    wait(copies[2:])
+    for d, out in enumerate(outs):
+        band = dot(lat_t[assign[2 * partner(d) + core]], inner, (1, 0))
+        out[...] = pack(band).astype(BF16)
     half = BS // 2
     for both, ref in ((both1, gw1), (both2, gw2)):
         real = both[:BS, :LANES] + both[LANES : LANES + BS, LANES:]
@@ -167,29 +228,44 @@
         gb1[c : c + 1] = jnp.where(core == 0, line[:, :half], line[:, half:BS])
 
 
-def compose_kernel(q, counts, assign, back, field, table, out):
-    chunks = [back[n].astype(F32) for n in range(NB)]
+def compose_kernel(q, *refs):
+    backs, hbm, out, held, (by_block, sems) = refs[:4], refs[4:8], refs[8], refs[9:13], refs[13:]
+    counts, assign, field, table = held
+    copies = fetch(sems, hbm, held)
+    rows = 2 * NB * q
+    for d, back in enumerate(backs):
+        by_block[partner(d)] = jnp.concatenate(unpack(back[...].astype(F32), rows), axis=1)
     groups = [
-        dense([chunk[:, g * LANES : (g + 1) * LANES] for chunk in chunks]) for g in range(2)
+        dense([by_block[n, :, g * LANES : (g + 1) * LANES] for n in range(NB)]) for g in range(2)
     ]
-    held = jnp.concatenate(keep_active(counts, assign, q, groups), axis=0).astype(BF16)
-    mixed = jnp.dot(table[...], held, preferred_element_type=F32).astype(BF16)
+    wait(copies)
+    masked = jnp.concatenate(keep_active(counts, assign, q, groups), axis=0).astype(BF16)
+    mixed = jnp.dot(table[...], masked, preferred_element_type=F32).astype(BF16)
     out[...] = (field[...].astype(F32) + mixed.astype(F32)).astype(BF16)
 
 
-def call(kernel, outs, scratch, n_scalars, *args):
-    whole = pl.BlockSpec(memory_space=pltpu.VMEM)
-    scalar = pl.BlockSpec(memory_space=pltpu.SMEM)
-    specs = [scalar] * n_scalars + [whole] * (len(args) - n_scalars)
+VMEM = pl.BlockSpec(memory_space=pltpu.VMEM)
+HBM = pl.BlockSpec(memory_space=pltpu.HBM)
+
+
+def call(kernel, outs, scratch, near, far):
     many = isinstance(outs, tuple)
     return pl.pallas_call(
         kernel,
         out_shape=outs,
-        in_specs=specs,
-        out_specs=tuple([whole] * len(outs)) if many else whole,
+        in_specs=[VMEM] * len(near) + [HBM] * len(far),
+        out_specs=tuple([VMEM] * len(outs)) if many else VMEM,
         scratch_shapes=scratch,
         compiler_params=pltpu.CompilerParams(vmem_limit_bytes=32 * 2**20),
-    )(*args)
+    )(*near, *far)
+
+
+def scratch_for(*arrays):
+    scratch = []
+    for x in arrays:
+        space = pltpu.SMEM if x.dtype == jnp.int32 else pltpu.VMEM
+        scratch.append(space(x.shape, x.dtype))
+    return scratch, pltpu.SemaphoreType.DMA((len(arrays),))
 
 
 def paired_blocks(grad_out, spec_saved, w1, w2, b1, mode_counts, assignment):
@@ -209,76 +285,66 @@
     lat = lat.reshape(2 * NB * q * n_rows, n_rows * rows).astype(BF16)
     lat_t = np.ascontiguousarray(lat.T).reshape(n_rows, rows, -1)
 
+    lat, lat_t = jnp.asarray(lat), jnp.asarray(lat_t)
+    inverse = jnp.asarray(by_group(inverse))
+    forward = jnp.asarray(by_group(forward).T)
+
+    def swap(chunks):
+        pairs = [[(i, i ^ (2 * d)) for i in range(2 * NB)] for d in range(NB)]
+        return [chunks[0]] + [lax.ppermute(chunks[d], "lat", pairs[d]) for d in (3, 2, 1)][::-1]
+
     field = grad_out.reshape(length, width)
+    shape = jax.ShapeDtypeStruct
+    far = (mode_counts, assignment, field, inverse, spec_saved[0])
+    scratch, sems = scratch_for(*far)
     sent = call(
         functools.partial(analyse_kernel, q),
-        jax.ShapeDtypeStruct((NB, rows, width), BF16),
-        [],
-        2,
-        mode_counts,
-        assignment,
-        field,
-        jnp.asarray(by_group(inverse)),
-        spec_saved[0],
-    )
-    cores = [[2 * z + c for z in range(NB)] for c in range(2)]
-    exchange = functools.partial(
-        lax.all_to_all,
-        axis_name="lat",
-        split_axis=0,
-        concat_axis=0,
-        axis_index_groups=cores,
-        tiled=True,
-    )
-    own = exchange(sent)
+        (shape((rows, width), BF16),) * NB,
+        scratch + [pltpu.VMEM((NB, rows, width), BF16), sems],
+        (),
+        far,
+    )
+    received = swap(sent)
+    far = (w1[0], w2[0], b1[0])
+    scratch, sems = scratch_for(*far)
     wide = (2 * LANES, 2 * LANES)
-    mat1, mat2, bias = call(
+    mats = call(
         weights_kernel,
-        (
-            jax.ShapeDtypeStruct(wide, BF16),
-            jax.ShapeDtypeStruct(wide, BF16),
-            jax.ShapeDtypeStruct((1, 2 * LANES), F32),
-        ),
-        [],
-        0,
-        w1[0],
-        w2[0],
-        b1[0],
-    )
+        (shape(wide, BF16), shape(wide, BF16), shape((1, 2 * LANES), F32)),
+        scratch + [sems],
+        (),
+        far,
+    )
+    own = call(join_kernel, shape((NB, rows, width), BF16), [], received, ())
     other = lax.ppermute(own, "lat", [(i, i ^ 1) for i in range(2 * NB)])
-    chunks, gw1, gw2, gb1 = call(
+    far = (assignment, lat, lat_t)
+    scratch, sems = scratch_for(*far)
+    packed = shape((rows + rows // 2 + 4, LANES), BF16)
+    matrix = shape((2, BS // 2, BS), F32)
+    *chunks, gw1, gw2, gb1 = call(
         filter_kernel,
-        (
-            jax.ShapeDtypeStruct((NB, rows, 2 * LANES), BF16),
-            jax.ShapeDtypeStruct((2, BS // 2, BS), F32),
-            jax.ShapeDtypeStruct((2, BS // 2, BS), F32),
-            jax.ShapeDtypeStruct((2, BS // 2), F32),
-        ),
-        [pltpu.VMEM((n_rows, rows, 2 * LANES), F32)],
-        1,
-        assignment,
-        own,
-        other,
-        mat1,
-        mat2,
-        bias,
-        jnp.asarray(lat),
-        jnp.asarray(lat_t),
-    )
-    back = exchange(chunks)
+        (packed,) * NB + (matrix, matrix, shape((2, BS // 2), F32)),
+        scratch
+        + [
+            pltpu.VMEM((n_rows, rows, 2 * LANES), F32),
+            pltpu.VMEM((2, NB, rows, 2 * LANES), F32),
+            sems,
+        ],
+        (own, other, *mats),
+        far,
+    )
+    backs = swap(chunks)
+    far = (mode_counts, assignment, field, forward)
+    scratch, sems = scratch_for(*far)
     total = call(
         functools.partial(compose_kernel, q),
-        jax.ShapeDtypeStruct((length, width), BF16),
-        [],
-        2,
-        mode_counts,
-        assignment,
-        back,
-        field,
-        jnp.asarray(by_group(forward).T),
-    )
-    received = from_behind(total[None, None], "section", -1)
-    return received, gw1.swapaxes(1, 2)[None], gw2.swapaxes(1, 2)[None], gb1[None]
+        shape((length, width), BF16),
+        scratch + [pltpu.VMEM((NB, rows, 2 * LANES), F32), sems],
+        backs,
+        far,
+    )
+    shifted = from_behind(total[None, None], "section", -1)
+    return shifted, gw1.swapaxes(1, 2)[None], gw2.swapaxes(1, 2)[None], gb1[None]
 
 
 def apply_mat(vec, mat):

time: 45.3 us -> 42.2 us (0.932)
  blocking collectives: 24.1 us -> 0 us
  starting transfers between devices: 1.29 us -> 11.5 us
  waiting for transfers between devices: 5.67 us -> 14.6 us
  Pallas kernels: 4.97 us -> 5.99 us
  local copies, waits for them, and re-layouts: 8.09 us -> 8.99 us
    all_to_all x2 -> x0, blocking collectives: 24.1 us -> none  [the longest x1 14.2 us: paired_blocks(): own = exchange(sent)]
    ppermute x0 -> x6, starting transfers between devices: none -> 10.1 us  [swap(): lax.ppermute(chunks[d], 'lat', pairs[d])]
    ppermute x0 -> x6, waiting for transfers between devices: none -> 8.92 us  [swap(): lax.ppermute(chunks[d], 'lat', pairs[d])]
    pallas_call x4 -> x5, Pallas kernels: 4.97 us -> 5.99 us  [call(): pl.pallas_call(kernel, out_shape=outs, in_specs=[VMEM] * len(near) + [HBM...]
    unnamed x29, local copies, waits for them, and re-layouts: 8.09 us -> 8.99 us
  transfers between devices with their start and end apart: 2 -> 8, of which waited for: 1 -> 5; matrix products, arithmetic and copies ran while one was open for 0% -> 0% of each run, Pallas kernels for 0% -> 1%
where the time goes in v3:
time: 42.2 us; the launch traced here: 41.8 us
  waiting for transfers between devices  14.6 us (35%)
  starting transfers between devices  11.5 us (27%)
  local copies, waits for them, and re-layouts  8.99 us (21%)
  Pallas kernels  5.99 us (14%)
  between operations  0.76 us (2%)
    ppermute x6, starting transfers between devices, swap(): lax.ppermute(chunks[d], 'lat', pairs[d])  10.1 us
    unnamed x29, local copies, waits for them, and re-layouts  8.99 us
    ppermute x6, waiting for transfers between devices, swap(): lax.ppermute(chunks[d], 'lat', pairs[d])  8.92 us
    pallas_call x5, Pallas kernels, call(): pl.pallas_call(kernel, out_shape=outs, in_specs=[VMEM] * len(near) + [HBM...  5.99 us
    ppermute x1, waiting for transfers between devices, from_behind(): return lax.ppermute(value, axis, pairs)  5.67 us
    ppermute x1, starting transfers between devices, from_behind(): return lax.ppermute(value, axis, pairs)  1.29 us
  transfers between devices with their start and end apart: 8, of which 5 were waited for; matrix products, arithmetic and copies ran while one was open for 0% of the time, Pallas kernels for 1%

profile of v3, /device:TPU:0, one launch (start us, length us, event | category | flops | bytes accessed | tf_op | source)
XLA Modules:
  0.0 41.8 jit_solution(909263785888612691)
XLA Ops:
  0.7 1.0 %copy-done.2 = bf16[1,1,180,384]{3,2,1,0:T(8,128)(2,1)S(1)} copy-done((bf16[1,1,180,384]{3,2,1,0:T(8,128)(2,1)S(1)}, bf16[1,1,180,384]{3,2,1,0:T(8,128)(2,1)}, u32[]{:S(2)}) %copy-start.2) | copy-done | bytes 138264
  1.6 0.9 %copy-done.6 = bf16[1,8,2,3456]{3,2,1,0:T(2,128)(2,1)S(1)} copy-done((bf16[1,8,2,3456]{3,2,1,0:T(2,128)(2,1)S(1)}, bf16[1,8,2,3456]{3,2,1,0:T(2,128)(2,1)}, u32[]{:S(2)}) %copy-start.6) | copy-done | bytes 110616
  2.5 0.9 %copy-done.8 = bf16[144,180]{1,0:T(8,128)(2,1)S(1)} copy-done((bf16[144,180]{1,0:T(8,128)(2,1)S(1)}, bf16[144,180]{1,0:T(8,128)(2,1)}, u32[]{:S(2)}) %copy-start.8) | copy-done | bytes 51864
  3.4 0.7 %copy-done.9 = s32[8]{0:T(128)S(1)} copy-done((s32[8]{0:T(128)S(1)}, s32[8]{0:T(128)}, u32[]{:S(2)}) %copy-start.9) | copy-done | bytes 56
  4.1 0.7 %copy-done.11 = s32[8]{0:T(128)S(1)} copy-done((s32[8]{0:T(128)S(1)}, s32[8]{0:T(128)}, u32[]{:S(2)}) %copy-start.11) | copy-done | bytes 56
  4.7 1.1 %shard_map.138 = (bf16[72,384]{1,0:T(8,128)(2,1)S(1)}, bf16[72,384]{1,0:T(8,128)(2,1)S(1)}, bf16[72,384]{1,0:T(8,128)(2,1)S(1)}, bf16[72,384]{1,0:T(8,128)(2,1)S(1)}) custom-call(s32[8]{0:T(128)S(1)} %copy-done.11, s32[8]{0:T(128)S(1)} %copy-done.9, bf16[180,384]{1,0:T(8,128)(2,1)S(1)} %bitcast.13, bf16[144,180]{1,0:T(8,128)(2,1)S(1)} %copy-done.8, ...), custom_call_target="tpu_custom_call" | custom-call | tf_op jit(solution)/shard_map/pallas_call | solution.py:253
  5.8 3.1 %collective-permute-start = (bf16[72,384]{1,0:T(8,128)(2,1)S(1)}, bf16[72,384]{1,0:T(8,128)(2,1)S(1)}, u32[]{:S(2)}, u32[]{:S(2)}) collective-permute-start(bf16[72,384]{1,0:T(8,128)(2,1)S(1)} %get-tuple-element.19), channel_id=1, source_target_pairs={{0,2},{1,3},{2,0},{3,1},{4,6},{5,7},{6,4},{7,5},{8,10},{9,11},{10,... | collective-permute-start | bytes 165896 | tf_op jit(solution)/shard_map/ppermute | solution.py:294
  8.9 2.6 %collective-permute-start.1 = (bf16[72,384]{1,0:T(8,128)(2,1)S(1)}, bf16[72,384]{1,0:T(8,128)(2,1)S(1)}, u32[]{:S(2)}, u32[]{:S(2)}) collective-permute-start(bf16[72,384]{1,0:T(8,128)(2,1)S(1)} %get-tuple-element.20), channel_id=1, source_target_pairs={{0,4},{1,5},{2,6},{3,7},{4,0},{5,1},{6,2},{7,3},{8,12},{9,13},{10,... | collective-permute-start | bytes 165896 | tf_op jit(solution)/shard_map/ppermute | solution.py:294
  11.5 3.5 %collective-permute-done.1.refs_2_ = bf16[72,384]{1,0:T(8,128)(2,1)S(1)} collective-permute-done((bf16[72,384]{1,0:T(8,128)(2,1)S(1)}, bf16[72,384]{1,0:T(8,128)(2,1)S(1)}, u32[]{:S(2)}, u32[]{:S(2)}) %collective-permute-start.1) | collective-permute-done | bytes 55328 | tf_op jit(solution)/shard_map/ppermute | solution.py:294
  15.0 2.4 %collective-permute-done.2.refs_3_ = bf16[72,384]{1,0:T(8,128)(2,1)S(1)} collective-permute-done((bf16[72,384]{1,0:T(8,128)(2,1)S(1)}, bf16[72,384]{1,0:T(8,128)(2,1)S(1)}, u32[]{:S(2)}, u32[]{:S(2)}) %collective-permute-start.2) | collective-permute-done | bytes 55328 | tf_op jit(solution)/shard_map/ppermute | solution.py:294
  17.6 0.7 %copy-done.13 = bf16[1,2,384]{2,1,0:T(2,128)(2,1)S(1)} copy-done((bf16[1,2,384]{2,1,0:T(2,128)(2,1)S(1)}, bf16[1,2,384]{2,1,0:T(2,128)(2,1)}, u32[]{:S(2)}) %copy-start.13) | copy-done | bytes 1560
  18.2 0.9 %copy-done.4 = bf16[1,2,96,384]{3,2,1,0:T(8,128)(2,1)S(1)} copy-done((bf16[1,2,96,384]{3,2,1,0:T(8,128)(2,1)S(1)}, bf16[1,2,96,384]{3,2,1,0:T(8,128)(2,1)}, u32[]{:S(2)}) %copy-start.4) | copy-done | bytes 147480
  19.1 0.9 %copy-done.5 = bf16[1,2,96,384]{3,2,1,0:T(8,128)(2,1)S(1)} copy-done((bf16[1,2,96,384]{3,2,1,0:T(8,128)(2,1)S(1)}, bf16[1,2,96,384]{3,2,1,0:T(8,128)(2,1)}, u32[]{:S(2)}) %copy-start.5) | copy-done | bytes 147480
  20.0 0.6 %shard_map.140 = (bf16[256,256]{1,0:T(8,128)(2,1)S(1)}, bf16[256,256]{1,0:T(8,128)(2,1)S(1)}, f32[1,256]{1,0:T(1,128)S(1)}) custom-call(bf16[2,96,384]{2,1,0:T(8,128)(2,1)S(1)} %bitcast.15, bf16[2,96,384]{2,1,0:T(8,128)(2,1)S(1)} %bitcast.16, bf16[2,384]{1,0:T(2,128)(2,1)S(1)} %bitcast.19), custom_call_target="tpu_custom_call" | custom-call | tf_op jit(solution)/shard_map/pallas_call | solution.py:253
  20.7 0.6 %copy-done.10 = s32[8]{0:T(128)S(1)} copy-done((s32[8]{0:T(128)S(1)}, s32[8]{0:T(128)}, u32[]{:S(2)}) %copy-start.10) | copy-done | bytes 56
  21.3 1.1 %copy-done.1 = bf16[576,576]{1,0:T(8,128)(2,1)S(1)} copy-done((bf16[576,576]{1,0:T(8,128)(2,1)S(1)}, bf16[576,576]{1,0:T(8,128)(2,1)}, u32[]{:S(2)}) %copy-start.1) | copy-done | bytes 663576
  22.4 3.5 %shard_map.141 = (bf16[112,128]{1,0:T(8,128)(2,1)S(1)}, bf16[112,128]{1,0:T(8,128)(2,1)S(1)}, bf16[112,128]{1,0:T(8,128)(2,1)S(1)}, bf16[112,128]{1,0:T(8,128)(2...) custom-call(bf16[4,72,384]{2,1,0:T(8,128)(2,1)S(1)} %shard_map.139.refs_0_, ...), custom_call_target="tpu_custom_call" | custom-call | tf_op jit(solution)/shard_map/pallas_call | solution.py:253
  26.0 1.7 %collective-permute-start.5 = (bf16[112,128]{1,0:T(8,128)(2,1)S(1)}, bf16[112,128]{1,0:T(8,128)(2,1)S(1)}, u32[]{:S(2)}, u32[]{:S(2)}) collective-permute-start(bf16[112,128]{1,0:T(8,128)(2,1)S(1)} %get-tuple-element.27), channel_id=1, source_target_pairs={{0,4},{1,5},{2,6},{3,7},{4,0},{5,1},{6,2},{7,3},{8,12},{9,13},{10,... | collective-permute-start | bytes 86024 | tf_op jit(solution)/shard_map/ppermute | solution.py:294
  27.7 2.7 %collective-permute-start.6 = (bf16[112,128]{1,0:T(8,128)(2,1)S(1)}, bf16[112,128]{1,0:T(8,128)(2,1)S(1)}, u32[]{:S(2)}, u32[]{:S(2)}) collective-permute-start(bf16[112,128]{1,0:T(8,128)(2,1)S(1)} %get-tuple-element.28), channel_id=1, source_target_pairs={{0,6},{1,7},{2,4},{3,5},{4,2},{5,3},{6,0},{7,1},{8,14},{9,15},{10,... | collective-permute-start | bytes 86024 | tf_op jit(solution)/shard_map/ppermute | solution.py:294
  30.9 2.5 %collective-permute-done.6.refs_3_ = bf16[112,128]{1,0:T(8,128)(2,1)S(1)} collective-permute-done((bf16[112,128]{1,0:T(8,128)(2,1)S(1)}, bf16[112,128]{1,0:T(8,128)(2,1)S(1)}, u32[]{:S(2)}, u32[]{:S(2)}) %collective-permute-start.6) | collective-permute-done | bytes 28704 | tf_op jit(solution)/shard_map/ppermute | solution.py:294
  33.4 0.8 %shard_map.142 = bf16[180,384]{1,0:T(8,128)(2,1)S(1)} custom-call(bf16[112,128]{1,0:T(8,128)(2,1)S(1)} %get-tuple-element.25.refs_0_, bf16[112,128]{1,0:T(8,128)(2,1)S(1)} %collective-permute-done.4.refs_1_, bf16[112,128]{1,0:T(8,128)(2,1)S(1)} %collective-permute-done.5.refs_2_, bf16[112,128]{1,0:T(8,128)(2,1)S(1)} %collective-permute-done.6.refs_3_, ...), custom_call_target="tpu_custom_call" | custom-call | tf_op jit(solution)/shard_map/pallas_call | solution.py:253
  34.2 1.3 %collective-permute-start.7 = (bf16[1,1,180,384]{3,2,1,0:T(8,128)(2,1)S(1)}, bf16[1,1,180,384]{3,2,1,0:T(8,128)(2,1)S(1)}, u32[]{:S(2)}, u32[]{:S(2)}) collective-permute-start(bf16[1,1,180,384]{3,2,1,0:T(8,128)(2,1)S(1)} %bitcast.17), channel_id=1, source_target_pairs={{8,0},{16,8},{24,16},{9,1},{17,9},{25,17},{10,2},{18,10},{26,18},{... | collective-permute-start | bytes 414728 | tf_op jit(solution)/shard_map/ppermute | solution.py:23
  35.5 5.7 %collective-permute-done.7 = bf16[1,1,180,384]{3,2,1,0:T(8,128)(2,1)S(1)} collective-permute-done((bf16[1,1,180,384]{3,2,1,0:T(8,128)(2,1)S(1)}, bf16[1,1,180,384]{3,2,1,0:T(8,128)(2,1)S(1)}, u32[]{:S(2)}, u32[]{:S(2)}) %collective-permute-start.7) | collective-permute-done | bytes 138272 | tf_op jit(solution)/shard_map/ppermute | solution.py:23
  41.2 0.7 %copy.16 = bf16[1,1,180,384]{3,2,1,0:T(8,128)(2,1)} copy(bf16[1,1,180,384]{3,2,1,0:T(8,128)(2,1)S(1)} %collective-permute-done.7) | data formatting | bytes 276480
  (26 shorter events, 0.7 us)
Async XLA Ops:
  0.6 20.0 %copy-start = (bf16[8,72,576]{2,1,0:T(8,128)(2,1)S(1)}, bf16[8,72,576]{2,1,0:T(8,128)(2,1)}, u32[]{:S(2)}) copy-start(bf16[8,72,576]{2,1,0:T(8,128)(2,1)} %constant.9.clone.refs_7_) | copy-start | bytes 1990660
  0.6 1.0 %copy-start.2 = (bf16[1,1,180,384]{3,2,1,0:T(8,128)(2,1)S(1)}, bf16[1,1,180,384]{3,2,1,0:T(8,128)(2,1)}, u32[]{:S(2)}) copy-start(bf16[1,1,180,384]{3,2,1,0:T(8,128)(2,1)} %param.11) | copy-start | bytes 414724
  1.6 0.9 %copy-start.6 = (bf16[1,8,2,3456]{3,2,1,0:T(2,128)(2,1)S(1)}, bf16[1,8,2,3456]{3,2,1,0:T(2,128)(2,1)}, u32[]{:S(2)}) copy-start(bf16[1,8,2,3456]{3,2,1,0:T(2,128)(2,1)} %param.12) | copy-start | bytes 331780
  2.5 0.9 %copy-start.8 = (bf16[144,180]{1,0:T(8,128)(2,1)S(1)}, bf16[144,180]{1,0:T(8,128)(2,1)}, u32[]{:S(2)}) copy-start(bf16[144,180]{1,0:T(8,128)(2,1)} %constant.10.clone.refs_3_) | copy-start | bytes 155524
  3.4 0.7 %copy-start.9 = (s32[8]{0:T(128)S(1)}, s32[8]{0:T(128)}, u32[]{:S(2)}) copy-start(s32[8]{0:T(128)} %refs_5_.3) | copy-start | bytes 100
  4.1 0.7 %copy-start.11 = (s32[8]{0:T(128)S(1)}, s32[8]{0:T(128)}, u32[]{:S(2)}) copy-start(s32[8]{0:T(128)} %refs_4_.1) | copy-start | bytes 100
  5.8 5.7 %collective-permute-start = (bf16[72,384]{1,0:T(8,128)(2,1)S(1)}, bf16[72,384]{1,0:T(8,128)(2,1)S(1)}, u32[]{:S(2)}, u32[]{:S(2)}) collective-permute-start(bf16[72,384]{1,0:T(8,128)(2,1)S(1)} %get-tuple-element.19), channel_id=1, source_target_pairs={{0,2},{1,3},{2,0},{3,1},{4,6},{5,7},{6,4},{7,5},{8,10},{9,11},{10,... | collective-permute-start | bytes 165896 | tf_op jit(solution)/shard_map/ppermute | solution.py:294
  8.9 6.1 %collective-permute-start.1 = (bf16[72,384]{1,0:T(8,128)(2,1)S(1)}, bf16[72,384]{1,0:T(8,128)(2,1)S(1)}, u32[]{:S(2)}, u32[]{:S(2)}) collective-permute-start(bf16[72,384]{1,0:T(8,128)(2,1)S(1)} %get-tuple-element.20), channel_id=1, source_target_pairs={{0,4},{1,5},{2,6},{3,7},{4,0},{5,1},{6,2},{7,3},{8,12},{9,13},{10,... | collective-permute-start | bytes 165896 | tf_op jit(solution)/shard_map/ppermute | solution.py:294
  11.5 6.0 %collective-permute-start.2 = (bf16[72,384]{1,0:T(8,128)(2,1)S(1)}, bf16[72,384]{1,0:T(8,128)(2,1)S(1)}, u32[]{:S(2)}, u32[]{:S(2)}) collective-permute-start(bf16[72,384]{1,0:T(8,128)(2,1)S(1)} %get-tuple-element.21), channel_id=1, source_target_pairs={{0,6},{1,7},{2,4},{3,5},{4,2},{5,3},{6,0},{7,1},{8,14},{9,15},{10,... | collective-permute-start | bytes 165896 | tf_op jit(solution)/shard_map/ppermute | solution.py:294
  17.5 3.2 %collective-permute-start.3 = (bf16[4,72,384]{2,1,0:T(8,128)(2,1)S(1)}, bf16[4,72,384]{2,1,0:T(8,128)(2,1)S(1)}, u32[]{:S(2)}, u32[]{:S(2)}) collective-permute-start(bf16[4,72,384]{2,1,0:T(8,128)(2,1)S(1)} %shard_map.139.refs_0_), channel_id=1, source_target_pairs={{0,1},{1,0},{2,3},{3,2},{4,5},{5,4},{6,7},{7,6},{8,9},{9,8},{10,11... | collective-permute-start | bytes 663560 | tf_op jit(solution)/shard_map/ppermute | solution.py:319
  17.5 0.7 %copy-start.13 = (bf16[1,2,384]{2,1,0:T(2,128)(2,1)S(1)}, bf16[1,2,384]{2,1,0:T(2,128)(2,1)}, u32[]{:S(2)}) copy-start(bf16[1,2,384]{2,1,0:T(2,128)(2,1)} %param.15) | copy-start | bytes 4612
  18.2 0.9 %copy-start.4 = (bf16[1,2,96,384]{3,2,1,0:T(8,128)(2,1)S(1)}, bf16[1,2,96,384]{3,2,1,0:T(8,128)(2,1)}, u32[]{:S(2)}) copy-start(bf16[1,2,96,384]{3,2,1,0:T(8,128)(2,1)} %param.13) | copy-start | bytes 442372
  19.1 0.9 %copy-start.5 = (bf16[1,2,96,384]{3,2,1,0:T(8,128)(2,1)S(1)}, bf16[1,2,96,384]{3,2,1,0:T(8,128)(2,1)}, u32[]{:S(2)}) copy-start(bf16[1,2,96,384]{3,2,1,0:T(8,128)(2,1)} %param.14) | copy-start | bytes 442372
  20.6 0.7 %copy-start.10 = (s32[8]{0:T(128)S(1)}, s32[8]{0:T(128)}, u32[]{:S(2)}) copy-start(s32[8]{0:T(128)} %refs_5_.3) | copy-start | bytes 100
  21.3 1.1 %copy-start.1 = (bf16[576,576]{1,0:T(8,128)(2,1)S(1)}, bf16[576,576]{1,0:T(8,128)(2,1)}, u32[]{:S(2)}) copy-start(bf16[576,576]{1,0:T(8,128)(2,1)} %constant.8.clone.refs_6_) | copy-start | bytes 1990660
  22.4 10.9 %copy-start.3 = (bf16[1,1,180,384]{3,2,1,0:T(8,128)(2,1)S(1)}, bf16[1,1,180,384]{3,2,1,0:T(8,128)(2,1)}, u32[]{:S(2)}) copy-start(bf16[1,1,180,384]{3,2,1,0:T(8,128)(2,1)} %param.11) | copy-start | bytes 414724
  22.4 10.9 %copy-start.7 = (bf16[180,144]{1,0:T(8,128)(2,1)S(1)}, bf16[180,144]{1,0:T(8,128)(2,1)}, u32[]{:S(2)}) copy-start(bf16[180,144]{1,0:T(8,128)(2,1)} %constant.11.clone.refs_7_) | copy-start | bytes 155524
  25.9 4.5 %collective-permute-start.4 = (bf16[112,128]{1,0:T(8,128)(2,1)S(1)}, bf16[112,128]{1,0:T(8,128)(2,1)S(1)}, u32[]{:S(2)}, u32[]{:S(2)}) collective-permute-start(bf16[112,128]{1,0:T(8,128)(2,1)S(1)} %get-tuple-element.26), channel_id=1, source_target_pairs={{0,2},{1,3},{2,0},{3,1},{4,6},{5,7},{6,4},{7,5},{8,10},{9,11},{10,... | collective-permute-start | bytes 86024 | tf_op jit(solution)/shard_map/ppermute | solution.py:294
  26.0 4.9 %collective-permute-start.5 = (bf16[112,128]{1,0:T(8,128)(2,1)S(1)}, bf16[112,128]{1,0:T(8,128)(2,1)S(1)}, u32[]{:S(2)}, u32[]{:S(2)}) collective-permute-start(bf16[112,128]{1,0:T(8,128)(2,1)S(1)} %get-tuple-element.27), channel_id=1, source_target_pairs={{0,4},{1,5},{2,6},{3,7},{4,0},{5,1},{6,2},{7,3},{8,12},{9,13},{10,... | collective-permute-start | bytes 86024 | tf_op jit(solution)/shard_map/ppermute | solution.py:294
  27.7 5.7 %copy-start.12 = (s32[8]{0:T(128)S(1)}, s32[8]{0:T(128)}, u32[]{:S(2)}) copy-start(s32[8]{0:T(128)} %refs_4_.1) | copy-start | bytes 100
  27.7 5.7 %collective-permute-start.6 = (bf16[112,128]{1,0:T(8,128)(2,1)S(1)}, bf16[112,128]{1,0:T(8,128)(2,1)S(1)}, u32[]{:S(2)}, u32[]{:S(2)}) collective-permute-start(bf16[112,128]{1,0:T(8,128)(2,1)S(1)} %get-tuple-element.28), channel_id=1, source_target_pairs={{0,6},{1,7},{2,4},{3,5},{4,2},{5,3},{6,0},{7,1},{8,14},{9,15},{10,... | collective-permute-start | bytes 86024 | tf_op jit(solution)/shard_map/ppermute | solution.py:294
  34.2 7.0 %collective-permute-start.7 = (bf16[1,1,180,384]{3,2,1,0:T(8,128)(2,1)S(1)}, bf16[1,1,180,384]{3,2,1,0:T(8,128)(2,1)S(1)}, u32[]{:S(2)}, u32[]{:S(2)}) collective-permute-start(bf16[1,1,180,384]{3,2,1,0:T(8,128)(2,1)S(1)} %bitcast.17), channel_id=1, source_target_pairs={{8,0},{16,8},{24,16},{9,1},{17,9},{25,17},{10,2},{18,10},{26,18},{... | collective-permute-start | bytes 414728 | tf_op jit(solution)/shard_map/ppermute | solution.py:23

commit v4 on v3

--- a/solution.py
+++ b/solution.py
@@ -257,7 +257,7 @@
         out_specs=tuple([VMEM] * len(outs)) if many else VMEM,
         scratch_shapes=scratch,
         compiler_params=pltpu.CompilerParams(vmem_limit_bytes=32 * 2**20),
-    )(*near, *far)
+    )(*near, *(pltpu.with_memory_space_constraint(x, pltpu.HBM) for x in far))
 
 
 def scratch_for(*arrays):

time: 42.2 us -> 35.9 us (0.85)
  local copies, waits for them, and re-layouts: 8.99 us -> 0.66 us
  Pallas kernels: 5.99 us -> 8.01 us
    unnamed x29 -> x1, local copies, waits for them, and re-layouts: 8.99 us -> 0.66 us
    pallas_call x5, Pallas kernels: 5.99 us -> 8.01 us  [call(): pl.pallas_call(kernel, out_shape=outs, in_specs=[VMEM] * len(near) + [HBM...]
  transfers between devices with their start and end apart: 8 -> 8, of which waited for: 5 -> 6; matrix products, arithmetic and copies ran while one was open for 0% -> 0% of each run, Pallas kernels for 1% -> 3%
where the time goes in v4:
time: 35.9 us; the launch traced here: 35.7 us
  waiting for transfers between devices  14.8 us (41%)
  starting transfers between devices  11.5 us (32%)
  Pallas kernels  8.01 us (22%)
  between operations  0.7 us (2%)
  local copies, waits for them, and re-layouts  0.66 us (2%)
    ppermute x6, starting transfers between devices, swap(): lax.ppermute(chunks[d], 'lat', pairs[d])  10.1 us
    ppermute x6, waiting for transfers between devices, swap(): lax.ppermute(chunks[d], 'lat', pairs[d])  8.92 us
    pallas_call x5, Pallas kernels, call(): pl.pallas_call(kernel, out_shape=outs, in_specs=[VMEM] * len(near) + [HBM...  8.01 us
    ppermute x1, waiting for transfers between devices, from_behind(): return lax.ppermute(value, axis, pairs)  5.67 us
    ppermute x1, starting transfers between devices, from_behind(): return lax.ppermute(value, axis, pairs)  1.29 us
  transfers between devices with their start and end apart: 8, of which 6 were waited for; matrix products, arithmetic and copies ran while one was open for 0% of the time, Pallas kernels for 3%

profile of v4, /device:TPU:0, one launch (start us, length us, event | category | flops | bytes accessed | tf_op | source)
XLA Modules:
  0.0 35.7 jit_solution(7487870998862073062)
XLA Ops:
  0.6 1.7 %shard_map.138 = (bf16[72,384]{1,0:T(8,128)(2,1)S(1)}, bf16[72,384]{1,0:T(8,128)(2,1)S(1)}, bf16[72,384]{1,0:T(8,128)(2,1)S(1)}, bf16[72,384]{1,0:T(8,128)(2,1)S(1)}) custom-call(s32[8]{0:T(128)} %refs_4_.1, s32[8]{0:T(128)} %refs_5_.3, bf16[180,384]{1,0:T(8,128)(2,1)} %bitcast.14, bf16[144,180]{1,0:T(8,128)(2,1)} %constant.10.clone.refs_3_, ...), custom_call_target="tpu_custom_call" | custom-call | tf_op jit(solution)/shard_map/pallas_call | solution.py:253
  2.3 3.1 %collective-permute-start = (bf16[72,384]{1,0:T(8,128)(2,1)S(1)}, bf16[72,384]{1,0:T(8,128)(2,1)S(1)}, u32[]{:S(2)}, u32[]{:S(2)}) collective-permute-start(bf16[72,384]{1,0:T(8,128)(2,1)S(1)} %get-tuple-element.19), channel_id=1, source_target_pairs={{0,2},{1,3},{2,0},{3,1},{4,6},{5,7},{6,4},{7,5},{8,10},{9,11},{10,... | collective-permute-start | bytes 165896 | tf_op jit(solution)/shard_map/ppermute | solution.py:294
  5.4 2.6 %collective-permute-start.1 = (bf16[72,384]{1,0:T(8,128)(2,1)S(1)}, bf16[72,384]{1,0:T(8,128)(2,1)S(1)}, u32[]{:S(2)}, u32[]{:S(2)}) collective-permute-start(bf16[72,384]{1,0:T(8,128)(2,1)S(1)} %get-tuple-element.20), channel_id=1, source_target_pairs={{0,4},{1,5},{2,6},{3,7},{4,0},{5,1},{6,2},{7,3},{8,12},{9,13},{10,... | collective-permute-start | bytes 165896 | tf_op jit(solution)/shard_map/ppermute | solution.py:294
  8.0 0.0 collective-permute-start.2
  8.0 0.0 collective-permute-done.refs_1_
  8.0 3.5 %collective-permute-done.1.refs_2_ = bf16[72,384]{1,0:T(8,128)(2,1)S(1)} collective-permute-done((bf16[72,384]{1,0:T(8,128)(2,1)S(1)}, bf16[72,384]{1,0:T(8,128)(2,1)S(1)}, u32[]{:S(2)}, u32[]{:S(2)}) %collective-permute-start.1) | collective-permute-done | bytes 55328 | tf_op jit(solution)/shard_map/ppermute | solution.py:294
  11.5 2.4 %collective-permute-done.2.refs_3_ = bf16[72,384]{1,0:T(8,128)(2,1)S(1)} collective-permute-done((bf16[72,384]{1,0:T(8,128)(2,1)S(1)}, bf16[72,384]{1,0:T(8,128)(2,1)S(1)}, u32[]{:S(2)}, u32[]{:S(2)}) %collective-permute-start.2) | collective-permute-done | bytes 55328 | tf_op jit(solution)/shard_map/ppermute | solution.py:294
  14.0 0.1 collective-permute-start.3
  14.1 1.2 %shard_map.140 = (bf16[256,256]{1,0:T(8,128)(2,1)S(1)}, bf16[256,256]{1,0:T(8,128)(2,1)S(1)}, f32[1,256]{1,0:T(1,128)S(1)}) custom-call(bf16[2,96,384]{2,1,0:T(8,128)(2,1)} %bitcast.16, bf16[2,96,384]{2,1,0:T(8,128)(2,1)} %bitcast.17, bf16[2,384]{1,0:T(2,128)(2,1)} %bitcast.19), custom_call_target="tpu_custom_call" | custom-call | tf_op jit(solution)/shard_map/pallas_call | solution.py:253
  15.3 0.2 collective-permute-done.3.refs_1_
  15.5 3.7 %shard_map.141 = (bf16[112,128]{1,0:T(8,128)(2,1)S(1)}, bf16[112,128]{1,0:T(8,128)(2,1)S(1)}, bf16[112,128]{1,0:T(8,128)(2,1)S(1)}, bf16[112,128]{1,0:T(8,128)(2...) custom-call(bf16[4,72,384]{2,1,0:T(8,128)(2,1)S(1)} %shard_map.139.refs_0_, ...), custom_call_target="tpu_custom_call" | custom-call | tf_op jit(solution)/shard_map/pallas_call | solution.py:253
  19.2 0.1 collective-permute-start.4
  19.3 1.7 %collective-permute-start.5 = (bf16[112,128]{1,0:T(8,128)(2,1)S(1)}, bf16[112,128]{1,0:T(8,128)(2,1)S(1)}, u32[]{:S(2)}, u32[]{:S(2)}) collective-permute-start(bf16[112,128]{1,0:T(8,128)(2,1)S(1)} %get-tuple-element.27), channel_id=1, source_target_pairs={{0,4},{1,5},{2,6},{3,7},{4,0},{5,1},{6,2},{7,3},{8,12},{9,13},{10,... | collective-permute-start | bytes 86024 | tf_op jit(solution)/shard_map/ppermute | solution.py:294
  21.0 2.7 %collective-permute-start.6 = (bf16[112,128]{1,0:T(8,128)(2,1)S(1)}, bf16[112,128]{1,0:T(8,128)(2,1)S(1)}, u32[]{:S(2)}, u32[]{:S(2)}) collective-permute-start(bf16[112,128]{1,0:T(8,128)(2,1)S(1)} %get-tuple-element.28), channel_id=1, source_target_pairs={{0,6},{1,7},{2,4},{3,5},{4,2},{5,3},{6,0},{7,1},{8,14},{9,15},{10,... | collective-permute-start | bytes 86024 | tf_op jit(solution)/shard_map/ppermute | solution.py:294
  23.7 0.0 collective-permute-done.4.refs_1_
  23.7 1.0 %collective-permute-done.5.refs_2_ = bf16[112,128]{1,0:T(8,128)(2,1)S(1)} collective-permute-done((bf16[112,128]{1,0:T(8,128)(2,1)S(1)}, bf16[112,128]{1,0:T(8,128)(2,1)S(1)}, u32[]{:S(2)}, u32[]{:S(2)}) %collective-permute-start.5) | collective-permute-done | bytes 28704 | tf_op jit(solution)/shard_map/ppermute | solution.py:294
  24.7 1.9 %collective-permute-done.6.refs_3_ = bf16[112,128]{1,0:T(8,128)(2,1)S(1)} collective-permute-done((bf16[112,128]{1,0:T(8,128)(2,1)S(1)}, bf16[112,128]{1,0:T(8,128)(2,1)S(1)}, u32[]{:S(2)}, u32[]{:S(2)}) %collective-permute-start.6) | collective-permute-done | bytes 28704 | tf_op jit(solution)/shard_map/ppermute | solution.py:294
  26.6 1.4 %shard_map.142 = bf16[180,384]{1,0:T(8,128)(2,1)S(1)} custom-call(bf16[112,128]{1,0:T(8,128)(2,1)S(1)} %get-tuple-element.25.refs_0_, bf16[112,128]{1,0:T(8,128)(2,1)S(1)} %collective-permute-done.4.refs_1_, bf16[112,128]{1,0:T(8,128)(2,1)S(1)} %collective-permute-done.5.refs_2_, bf16[112,128]{1,0:T(8,128)(2,1)S(1)} %collective-permute-done.6.refs_3_, ...), custom_call_target="tpu_custom_call" | custom-call | tf_op jit(solution)/shard_map/pallas_call | solution.py:253
  28.1 1.3 %collective-permute-start.7 = (bf16[1,1,180,384]{3,2,1,0:T(8,128)(2,1)S(1)}, bf16[1,1,180,384]{3,2,1,0:T(8,128)(2,1)S(1)}, u32[]{:S(2)}, u32[]{:S(2)}) collective-permute-start(bf16[1,1,180,384]{3,2,1,0:T(8,128)(2,1)S(1)} %bitcast.13), channel_id=1, source_target_pairs={{8,0},{16,8},{24,16},{9,1},{17,9},{25,17},{10,2},{18,10},{26,18},{... | collective-permute-start | bytes 414728 | tf_op jit(solution)/shard_map/ppermute | solution.py:23
  29.4 5.7 %collective-permute-done.7 = bf16[1,1,180,384]{3,2,1,0:T(8,128)(2,1)S(1)} collective-permute-done((bf16[1,1,180,384]{3,2,1,0:T(8,128)(2,1)S(1)}, bf16[1,1,180,384]{3,2,1,0:T(8,128)(2,1)S(1)}, u32[]{:S(2)}, u32[]{:S(2)}) %collective-permute-start.7) | collective-permute-done | bytes 138272 | tf_op jit(solution)/shard_map/ppermute | solution.py:23
  35.0 0.7 %copy.16 = bf16[1,1,180,384]{3,2,1,0:T(8,128)(2,1)} copy(bf16[1,1,180,384]{3,2,1,0:T(8,128)(2,1)S(1)} %collective-permute-done.7) | data formatting | bytes 276480
  (1 shorter events, 0.0 us)
Async XLA Ops:
  2.3 5.7 %collective-permute-start = (bf16[72,384]{1,0:T(8,128)(2,1)S(1)}, bf16[72,384]{1,0:T(8,128)(2,1)S(1)}, u32[]{:S(2)}, u32[]{:S(2)}) collective-permute-start(bf16[72,384]{1,0:T(8,128)(2,1)S(1)} %get-tuple-element.19), channel_id=1, source_target_pairs={{0,2},{1,3},{2,0},{3,1},{4,6},{5,7},{6,4},{7,5},{8,10},{9,11},{10,... | collective-permute-start | bytes 165896 | tf_op jit(solution)/shard_map/ppermute | solution.py:294
  5.4 6.1 %collective-permute-start.1 = (bf16[72,384]{1,0:T(8,128)(2,1)S(1)}, bf16[72,384]{1,0:T(8,128)(2,1)S(1)}, u32[]{:S(2)}, u32[]{:S(2)}) collective-permute-start(bf16[72,384]{1,0:T(8,128)(2,1)S(1)} %get-tuple-element.20), channel_id=1, source_target_pairs={{0,4},{1,5},{2,6},{3,7},{4,0},{5,1},{6,2},{7,3},{8,12},{9,13},{10,... | collective-permute-start | bytes 165896 | tf_op jit(solution)/shard_map/ppermute | solution.py:294
  8.0 6.0 %collective-permute-start.2 = (bf16[72,384]{1,0:T(8,128)(2,1)S(1)}, bf16[72,384]{1,0:T(8,128)(2,1)S(1)}, u32[]{:S(2)}, u32[]{:S(2)}) collective-permute-start(bf16[72,384]{1,0:T(8,128)(2,1)S(1)} %get-tuple-element.21), channel_id=1, source_target_pairs={{0,6},{1,7},{2,4},{3,5},{4,2},{5,3},{6,0},{7,1},{8,14},{9,15},{10,... | collective-permute-start | bytes 165896 | tf_op jit(solution)/shard_map/ppermute | solution.py:294
  14.0 1.5 %collective-permute-start.3 = (bf16[4,72,384]{2,1,0:T(8,128)(2,1)S(1)}, bf16[4,72,384]{2,1,0:T(8,128)(2,1)S(1)}, u32[]{:S(2)}, u32[]{:S(2)}) collective-permute-start(bf16[4,72,384]{2,1,0:T(8,128)(2,1)S(1)} %shard_map.139.refs_0_), channel_id=1, source_target_pairs={{0,1},{1,0},{2,3},{3,2},{4,5},{5,4},{6,7},{7,6},{8,9},{9,8},{10,11... | collective-permute-start | bytes 663560 | tf_op jit(solution)/shard_map/ppermute | solution.py:319
  19.2 4.5 %collective-permute-start.4 = (bf16[112,128]{1,0:T(8,128)(2,1)S(1)}, bf16[112,128]{1,0:T(8,128)(2,1)S(1)}, u32[]{:S(2)}, u32[]{:S(2)}) collective-permute-start(bf16[112,128]{1,0:T(8,128)(2,1)S(1)} %get-tuple-element.26), channel_id=1, source_target_pairs={{0,2},{1,3},{2,0},{3,1},{4,6},{5,7},{6,4},{7,5},{8,10},{9,11},{10,... | collective-permute-start | bytes 86024 | tf_op jit(solution)/shard_map/ppermute | solution.py:294
  19.3 5.4 %collective-permute-start.5 = (bf16[112,128]{1,0:T(8,128)(2,1)S(1)}, bf16[112,128]{1,0:T(8,128)(2,1)S(1)}, u32[]{:S(2)}, u32[]{:S(2)}) collective-permute-start(bf16[112,128]{1,0:T(8,128)(2,1)S(1)} %get-tuple-element.27), channel_id=1, source_target_pairs={{0,4},{1,5},{2,6},{3,7},{4,0},{5,1},{6,2},{7,3},{8,12},{9,13},{10,... | collective-permute-start | bytes 86024 | tf_op jit(solution)/shard_map/ppermute | solution.py:294
  21.0 5.7 %collective-permute-start.6 = (bf16[112,128]{1,0:T(8,128)(2,1)S(1)}, bf16[112,128]{1,0:T(8,128)(2,1)S(1)}, u32[]{:S(2)}, u32[]{:S(2)}) collective-permute-start(bf16[112,128]{1,0:T(8,128)(2,1)S(1)} %get-tuple-element.28), channel_id=1, source_target_pairs={{0,6},{1,7},{2,4},{3,5},{4,2},{5,3},{6,0},{7,1},{8,14},{9,15},{10,... | collective-permute-start | bytes 86024 | tf_op jit(solution)/shard_map/ppermute | solution.py:294
  28.1 7.0 %collective-permute-start.7 = (bf16[1,1,180,384]{3,2,1,0:T(8,128)(2,1)S(1)}, bf16[1,1,180,384]{3,2,1,0:T(8,128)(2,1)S(1)}, u32[]{:S(2)}, u32[]{:S(2)}) collective-permute-start(bf16[1,1,180,384]{3,2,1,0:T(8,128)(2,1)S(1)} %bitcast.13), channel_id=1, source_target_pairs={{8,0},{16,8},{24,16},{9,1},{17,9},{25,17},{10,2},{18,10},{26,18},{... | collective-permute-start | bytes 414728 | tf_op jit(solution)/shard_map/ppermute | solution.py:23

commit v5 on v4

v5 whole, which is shorter than its diff:
```python
import functools
import math

import jax
import jax.numpy as jnp
import numpy as np
from jax import lax
from jax.experimental import pallas as pl
from jax.experimental.pallas import tpu as pltpu
from jax.sharding import PartitionSpec as P

NB = 4
BS = 96
KM = 72
LANES = 128
F32 = jnp.float32
BF16 = jnp.bfloat16


def from_behind(value, axis, by):
    length = lax.axis_size(axis)
    pairs = [(i, i + by) for i in range(length) if 0 <= i + by < length]
    return lax.ppermute(value, axis, pairs)


def lon_tables(n_modes, length):
    modes = np.arange(n_modes)
    phase = modes[:, None] * np.arange(length)[None, :] % length
    angle = phase * (2.0 * math.pi / length)
    forward = np.stack([np.cos(angle), -np.sin(angle)]) / math.sqrt(length)
    weight = np.where(modes == 0, 1.0, 2.0)[None, :, None]
    return forward, forward * weight


def lat_waves(n_rows):
    freqs = np.arange(n_rows)
    angle = (freqs[:, None] * freqs[None, :] % n_rows) * (2.0 * math.pi / n_rows)
    factor = 1.0 / math.sqrt(n_rows)
    return np.cos(angle) * factor, np.sin(angle) * factor


def silu_slope(pre):
    sig = jax.nn.sigmoid(pre)
    return sig * (1.0 + pre * (1.0 - sig))


def window(x, start):
    low = start // LANES * LANES
    shift = start - low
    if shift == 0:
        return x[:, low : low + LANES]
    if shift + BS <= LANES:
        return pltpu.roll(x[:, low : low + LANES], LANES - shift, 1)
    return pltpu.roll(x[:, low : low + 2 * LANES], 2 * LANES - shift, 1)[:, :LANES]


def dense(parts):
    lane = lax.broadcasted_iota(jnp.int32, parts[0].shape, 1)
    first = pltpu.roll(parts[1], 96, 1)
    second = pltpu.roll(parts[2], 64, 1)
    third = pltpu.roll(parts[3], 32, 1)
    return jnp.concatenate(
        [
            jnp.where(lane < 96, parts[0], first),
            jnp.where(lane < 64, first, second),
            jnp.where(lane < 32, second, third),
        ],
        axis=1,
    )


def dot(a, b, contract):
    return lax.dot_general(a, b, ((contract[:1], contract[1:]), ((), ())), preferred_element_type=F32)


def fetch(sems, sources, targets):
    copies = [
        pltpu.make_async_copy(source, target, sems.at[i])
        for i, (source, target) in enumerate(zip(sources, targets))
    ]
    for copy in copies:
        copy.start()
    return copies


def wait(copies):
    for copy in copies:
        copy.wait()


def partner(d):
    return jnp.bitwise_xor(lax.axis_index("lat") // 2, d)


def place():
    device = lax.axis_index("lat")
    return device // 2, lax.rem(device, 2)


def row_modes(shape, q):
    row = lax.broadcasted_iota(jnp.int32, shape, 0)
    twin = row >= 2 * q
    row = jnp.where(twin, row - 2 * q, row)
    return twin, jnp.where(row >= q, row - q, row)


def analyse_kernel(q, *refs):
    other, hbm, outs, held, (by_pair, sems) = refs[0], refs[1:5], refs[5:9], refs[9:13], refs[13:]
    counts, assign, field, table = held
    z, core = place()
    copies = fetch(sems, hbm[:3] + (hbm[3].at[core],), held)
    wait(copies)
    pad, width = by_pair.shape[1:]
    spectral = jnp.dot(table[0], field[...], preferred_element_type=F32)
    spectral += jnp.dot(table[1], other[...], preferred_element_type=F32)
    twin, mode = row_modes((pad, width), q)
    active = [counts[assign[2 * z + side]] for side in (core, 1 - core)]
    limit = jnp.where(twin, active[1], active[0])
    for n in range(NB):
        part = spectral[n * pad : (n + 1) * pad]
        by_pair[n] = jnp.where(mode < limit - q * (2 * n + core), part, 0.0).astype(BF16)
    for d, out in enumerate(outs):
        out[...] = by_pair[partner(d)]


def silu_kernel(q, *refs):
    hbm, outs, held, sems = refs[:6], refs[6:12], refs[12:18], refs[18]
    mats1, mats2, points, hidden, slope, lat = outs
    assign, saved, w1, w2, b1, base = held
    copies = fetch(sems, hbm, held)
    z, core = place()
    wait(copies)
    shift_b = b1[...].astype(F32)
    parts = [saved[:, c, :].astype(F32) for c in range(2)]
    lane = lax.broadcasted_iota(jnp.int32, (BS, LANES), 1)
    gap = jnp.zeros((LANES - BS, 2 * LANES), BF16)
    for n in range(NB):
        for source, mats in ((w1, mats1), (w2, mats2)):
            real, imag = (
                jnp.where(lane < BS, window(source[c].astype(F32), n * BS), 0.0) for c in range(2)
            )
            mats[n, 0:BS] = jnp.concatenate([real, imag], axis=1).astype(BF16)
            mats[n, BS:LANES] = gap
            mats[n, LANES : LANES + BS] = jnp.concatenate([-imag, real], axis=1).astype(BF16)
            mats[n, LANES + BS : 2 * LANES] = gap
        bias = window(shift_b, n * BS)
        bias = jnp.concatenate([bias[0:1], bias[1:2]], axis=1)
        columns = [
            jnp.concatenate([window(part, (mm * NB + n) * BS) for mm in range(q)], axis=0)
            for part in parts
        ]
        v = jnp.concatenate(columns, axis=1).astype(BF16)
        points[n] = v
        pre = dot(v, mats1[n], (1, 0)) + bias
        sig = jax.nn.sigmoid(pre)
        hidden[n] = (pre * sig).astype(BF16)
        slope[n] = sig * (1.0 + pre * (1.0 - sig))
    pad = lat.shape[1] // NB
    row = lax.broadcasted_iota(jnp.int32, (base.shape[1], lat.shape[1]), 0)
    column = lax.broadcasted_iota(jnp.int32, row.shape, 1)
    row_lat = sum((row >= 2 * q * i).astype(jnp.int32) for i in range(1, 2 * NB))
    column_lat = jnp.full(row.shape, -1, jnp.int32)
    inside = column
    for d in range(NB):
        for twin, side in enumerate((core, 1 - core)):
            start = d * pad + twin * 2 * q
            here = jnp.logical_and(column >= start, column < start + 2 * q)
            column_lat = jnp.where(here, assign[2 * partner(d) + side], column_lat)
            inside = jnp.where(here, column - start, inside)
    same = jnp.logical_and(row_lat == column_lat, row - 2 * q * row_lat == inside)
    lat[...] = dot(base[...], same.astype(F32).astype(BF16), (1, 0)).astype(BF16)


def filter_kernel(q, *refs):
    chunks, (mats1, mats2, points, hidden, slope, lat) = refs[:4], refs[4:10]
    outs, kept, sent, by_block = refs[10:14], refs[14], refs[15], refs[16]
    z, core = place()
    pad, width = chunks[0].shape
    rows = points.shape[1]
    half = BS // 2
    field = jnp.concatenate([chunk[...].astype(F32) for chunk in chunks], axis=0).astype(BF16)
    grad_y = dot(lat[...], field, (1, 0)).astype(BF16).astype(F32)
    inner = []
    for n in range(NB):
        dy = [window(grad_y[c * rows : (c + 1) * rows], n * BS) for c in range(2)]
        dy = jnp.concatenate(dy, axis=1).astype(BF16)
        dp = (dot(dy, mats2[n], (1, 1)) * slope[n]).astype(BF16)
        dv = dot(dp, mats1[n], (1, 1))
        inner.append(jnp.concatenate([dv[:, :LANES], dv[:, LANES:]], axis=0))
        columns = []
        for left, right in ((dp, points[n]), (dy, hidden[n])):
            both = dot(left, right, (0, 0))
            columns.append(both[:BS, :LANES] + both[LANES : LANES + BS, LANES:])
            columns.append(both[LANES : LANES + BS, :LANES] - both[:BS, LANES:])
        by_block[n, 0:BS] = dense(columns)
        sums = jnp.sum(dp.astype(F32), axis=0, keepdims=True)
        sums = jnp.concatenate([sums, jnp.zeros((1, width - 2 * LANES), F32)], axis=1)
        by_block[n, BS : BS + 8] = jnp.broadcast_to(sums, (8, width))
    grad_v = dense(inner).astype(BF16)
    band = dot(lat[...], grad_v, (0, 0))
    for d, out in enumerate(outs):
        out[...] = band[d * pad : (d + 1) * pad].astype(BF16)
    for d in range(NB):
        block = by_block[partner(d)]
        upper, lower, sums = block[:half], block[half:BS], block[BS:]
        own = jnp.where(core == 0, upper, lower)
        other = jnp.where(core == 0, lower, upper)
        kept[d] = jnp.concatenate([own, sums], axis=0)
        sent[d] = jnp.concatenate([other, sums], axis=0).astype(BF16)


def halve_kernel(kept, got, keep, send):
    count = keep.shape[0]
    for d in range(count):
        keep[d] = kept[d] + got[d].astype(F32)
        send[d] = (kept[count + d] + got[count + d].astype(F32)).astype(BF16)


def weights_kernel(kept, got, gw1, gw2, gb1):
    total = kept[0] + got[0].astype(F32)
    half = BS // 2
    for w, ref in enumerate((gw1, gw2)):
        for c in range(2):
            ref[c] = window(total[:half], (2 * w + c) * BS)[:, :BS]
    core = place()[1]
    for c in range(2):
        line = total[half : half + 1, c * LANES : (c + 1) * LANES]
        gb1[c : c + 1] = jnp.where(core == 0, line[:, :half], line[:, half:BS])


def part_kernel(q, *refs):
    backs, out = refs[:4], refs[4]
    pad = backs[0].shape[0]
    rows = out.shape[0] // NB
    twin = [pltpu.roll(back[...].astype(F32), pad - 2 * q, 0)[:rows] for back in backs]
    out[...] = jnp.concatenate(twin, axis=0).astype(BF16)


def compose_kernel(q, *refs):
    backs, got, hbm, out, held, (by_device, sems) = (
        refs[:4],
        refs[4],
        refs[5:9],
        refs[9],
        refs[10:14],
        refs[14:],
    )
    counts, assign, field, table = held
    copies = fetch(sems, hbm, held)
    z, core = place()
    rows, width = by_device.shape[2:]
    other = got[...].astype(F32)
    for d, back in enumerate(backs):
        by_device[core, partner(d)] = back[...].astype(F32)[:rows]
        by_device[1 - core, partner(d)] = other[d * rows : (d + 1) * rows]
    wait(copies)
    active = counts[assign[2 * z + core]]
    mode = row_modes((rows, width), q)[1]
    held_rows = [
        jnp.where(mode < active - q * (2 * n + c), by_device[c, n], 0.0)
        for c in range(2)
        for n in range(NB)
    ]
    held_rows = jnp.concatenate(held_rows, axis=0).astype(BF16)
    mixed = jnp.dot(table[...], held_rows, preferred_element_type=F32).astype(BF16)
    out[...] = (field[...].astype(F32) + mixed.astype(F32)).astype(BF16)


VMEM = pl.BlockSpec(memory_space=pltpu.VMEM)
HBM = pl.BlockSpec(memory_space=pltpu.HBM)


def call(kernel, outs, scratch, near, far):
    many = isinstance(outs, tuple)
    return pl.pallas_call(
        kernel,
        out_shape=outs,
        in_specs=[VMEM] * len(near) + [HBM] * len(far),
        out_specs=tuple([VMEM] * len(outs)) if many else VMEM,
        scratch_shapes=scratch,
        compiler_params=pltpu.CompilerParams(vmem_limit_bytes=32 * 2**20),
    )(*near, *(pltpu.with_memory_space_constraint(x, pltpu.HBM) for x in far))


def scratch_for(*arrays):
    scratch = []
    for x in arrays:
        space = pltpu.SMEM if x.dtype == jnp.int32 else pltpu.VMEM
        scratch.append(space(x.shape, x.dtype))
    return scratch, pltpu.SemaphoreType.DMA((len(arrays),))


def paired_blocks(grad_out, spec_saved, w1, w2, b1, mode_counts, assignment):
    length, width = grad_out.shape[2:]
    n_rows = assignment.shape[0]
    q = spec_saved.shape[3] // (NB * BS)
    rows = q * n_rows
    pad = (4 * q + 7) // 8 * 8
    short = (2 * q + 7) // 8 * 8
    forward, inverse = lon_tables(KM, length)

    inverse, forward = (
        t.reshape(2, NB, 2, q, length).transpose(2, 1, 0, 3, 4).reshape(2, NB, 2 * q, length)
        for t in (inverse, forward)
    )
    analysis = np.zeros((2, 2, NB, pad, length))
    analysis[:, 0, :, : 2 * q] = inverse
    analysis[:, 1, :, 2 * q : 4 * q] = inverse
    analysis = jnp.asarray(analysis.reshape(2, 2, NB * pad, length).astype(BF16))
    synthesis = np.zeros((2, NB, short, length))
    synthesis[:, :, : 2 * q] = forward
    synthesis = jnp.asarray(synthesis.reshape(2 * NB * short, length).T.astype(BF16))
    cosine, sine = lat_waves(n_rows)
    waves = np.array([[cosine, sine], [-sine, cosine]])
    base = np.einsum("eckr,uv->eukrcv", waves, np.eye(q))
    base = jnp.asarray(base.reshape(2 * rows, n_rows * 2 * q).astype(BF16))

    def across(value, d):
        return lax.ppermute(value, "lat", [(i, i ^ (2 * d)) for i in range(2 * NB)])

    def twin(value):
        return lax.ppermute(value, "lat", [(i, i ^ 1) for i in range(2 * NB)])

    def swap(chunks):
        return [chunks[0]] + [across(chunks[d], d) for d in (3, 2, 1)][::-1]

    shape = jax.ShapeDtypeStruct
    field = grad_out.reshape(length, width)
    other = twin(field)
    far = (mode_counts, assignment, field, analysis)
    scratch, sems = scratch_for(mode_counts, assignment, field, shape(analysis.shape[1:], BF16))
    sent = call(
        functools.partial(analyse_kernel, q),
        (shape((pad, width), BF16),) * NB,
        scratch + [pltpu.VMEM((NB, pad, width), BF16), sems],
        (other,),
        far,
    )
    received = swap(sent)
    far = (assignment, spec_saved[0], w1[0], w2[0], b1[0], base)
    scratch, sems = scratch_for(*far)
    wide = 2 * LANES
    ready = call(
        functools.partial(silu_kernel, q),
        (
            shape((NB, wide, wide), BF16),
            shape((NB, wide, wide), BF16),
            shape((NB, rows, wide), BF16),
            shape((NB, rows, wide), BF16),
            shape((NB, rows, wide), F32),
            shape((2 * rows, NB * pad), BF16),
        ),
        scratch + [sems],
        (),
        far,
    )
    tall = BS // 2 + 8
    *chunks, kept, given = call(
        functools.partial(filter_kernel, q),
        (shape((pad, width), BF16),) * NB
        + (shape((NB, tall, width), F32), shape((NB, tall, width), BF16)),
        [pltpu.VMEM((NB, BS + 8, width), F32)],
        (*received, *ready),
        (),
    )
    backs = swap(chunks)
    got = twin(
        call(
            functools.partial(part_kernel, q), shape((NB * short, width), BF16), [], backs, ()
        )
    )
    far = (mode_counts, assignment, field, synthesis)
    scratch, sems = scratch_for(*far)
    total = call(
        functools.partial(compose_kernel, q),
        shape((length, width), BF16),
        scratch + [pltpu.VMEM((2, NB, short, width), F32), sems],
        (*backs, got),
        far,
    )
    shifted = from_behind(total[None, None], "section", -1)

    added = twin(given)
    for d in (2, 1):
        halves = (shape((d, tall, width), F32), shape((d, tall, width), BF16))
        kept, given = call(halve_kernel, halves, [], (kept, added), ())
        added = across(given, d)
    matrix = shape((2, BS // 2, BS), F32)
    gw1, gw2, gb1 = call(
        weights_kernel, (matrix, matrix, shape((2, BS // 2), F32)), [], (kept, added), ()
    )
    return shifted, gw1.swapaxes(1, 2)[None], gw2.swapaxes(1, 2)[None], gb1[None]


def apply_mat(vec, mat):
    return jnp.einsum("kpi,ipj->kpj", vec, mat, preferred_element_type=F32)


def adjoint_mat(vec, mat):
    return jnp.einsum("kpj,ipj->kpi", vec, mat, preferred_element_type=F32)


def outer_sum(left, right):
    return jnp.einsum("kpi,kpj->ipj", left, right, preferred_element_type=F32)


def split_blocks(grad_out, spec_saved, w1, w2, b1, mode_counts, assignment):
    rows_dev = grad_out.shape[1]
    length = grad_out.shape[2]
    width = grad_out.shape[3]
    n_rows = assignment.shape[0]
    pairs_dev = spec_saved.shape[3] // BS
    forward, inverse = (jnp.asarray(t.astype(BF16)) for t in lon_tables(KM, length))
    cosine, sine = (jnp.asarray(t.astype(BF16))[:, assignment] for t in lat_waves(n_rows))
    table = jnp.stack(
        [jnp.stack([cosine, sine], axis=-1), jnp.stack([-sine, cosine], axis=-1)], axis=1
    )
    lat_pos = lax.axis_index("lat")
    lat_count = lax.axis_size("lat")
    own_lat = lax.dynamic_slice_in_dim(assignment, lat_pos * rows_dev, rows_dev)
    active = (jnp.arange(KM, dtype=jnp.int32)[None, :] < mode_counts[own_lat][:, None]).astype(F32)
    cotan = grad_out[0]
    spectral = jnp.einsum(
        "cml,rlni->rcmni",
        inverse,
        cotan.reshape(rows_dev, length, NB, BS),
        preferred_element_type=F32,
    )
    spectral = (spectral * active[:, None, :, None, None]).astype(BF16)
    spectral = spectral.reshape(rows_dev, 2, KM * NB * BS)
    pencil = lax.all_to_all(spectral, "lat", split_axis=2, concat_axis=0, tiled=True)
    pencil = pencil.reshape(n_rows, 2, pairs_dev, BS)
    grad_y = jnp.einsum("kerc,rcpi->kepi", table, pencil, preferred_element_type=F32).astype(BF16)
    saved = spec_saved[0].reshape(n_rows, 2, pairs_dev, BS)
    pair_ids = lat_pos * pairs_dev + jnp.arange(pairs_dev, dtype=jnp.int32)
    owner = (pair_ids % NB)[:, None] == jnp.arange(NB, dtype=jnp.int32)[None, :]
    owner = owner.astype(F32)
    first = jnp.take(w1[0].reshape(2, BS, NB, BS), pair_ids % NB, axis=2)
    second = jnp.take(w2[0].reshape(2, BS, NB, BS), pair_ids % NB, axis=2)
    shift_b = jnp.take(b1[0].reshape(2, NB, BS), pair_ids % NB, axis=1).astype(F32)
    v_r = saved[:, 0]
    v_i = saved[:, 1]
    pre_r = apply_mat(v_r, first[0]) - apply_mat(v_i, first[1]) + shift_b[0][None]
    pre_i = apply_mat(v_i, first[0]) + apply_mat(v_r, first[1]) + shift_b[1][None]
    hid_r = jax.nn.silu(pre_r).astype(BF16)
    hid_i = jax.nn.silu(pre_i).astype(BF16)
    dy_r = grad_y[:, 0]
    dy_i = grad_y[:, 1]
    dh_r = adjoint_mat(dy_r, second[0]) + adjoint_mat(dy_i, second[1])
    dh_i = adjoint_mat(dy_i, second[0]) - adjoint_mat(dy_r, second[1])
    dp_r = (dh_r * silu_slope(pre_r)).astype(BF16)
    dp_i = (dh_i * silu_slope(pre_i)).astype(BF16)
    gw2 = jnp.stack(
        [
            outer_sum(hid_r, dy_r) + outer_sum(hid_i, dy_i),
            outer_sum(hid_r, dy_i) - outer_sum(hid_i, dy_r),
        ]
    )
    gw1 = jnp.stack(
        [outer_sum(v_r, dp_r) + outer_sum(v_i, dp_i), outer_sum(v_r, dp_i) - outer_sum(v_i, dp_r)]
    )
    gb1 = jnp.stack([jnp.sum(dp_r.astype(F32), axis=0), jnp.sum(dp_i.astype(F32), axis=0)])
    dv_r = adjoint_mat(dp_r, first[0]) + adjoint_mat(dp_i, first[1])
    dv_i = adjoint_mat(dp_i, first[0]) - adjoint_mat(dp_r, first[1])
    grad_v = jnp.stack([dv_r, dv_i], axis=1).astype(BF16)
    grad_u = jnp.einsum("kerc,kepi->rcpi", table, grad_v, preferred_element_type=F32).astype(BF16)
    grad_u = grad_u.reshape(n_rows, 2, pairs_dev * BS)
    back = lax.all_to_all(grad_u, "lat", split_axis=0, concat_axis=2, tiled=True)
    back = back.reshape(rows_dev, 2, KM, NB, BS) * active[:, None, :, None, None].astype(BF16)
    mixed = jnp.einsum("cml,rcmni->rlni", forward, back, preferred_element_type=F32)
    mixed = mixed.reshape(rows_dev, length, width).astype(BF16)
    block_w1 = jnp.einsum("pn,cipj->cinj", owner, gw1).reshape(1, 2, BS, width)
    block_w2 = jnp.einsum("pn,cipj->cinj", owner, gw2).reshape(1, 2, BS, width)
    block_b1 = jnp.einsum("pn,cpj->cnj", owner, gb1).reshape(1, 2, width)
    columns = width // lat_count
    full_w1, full_w2, full_b1 = lax.psum((block_w1, block_w2, block_b1), "lat")
    sum_w1 = lax.dynamic_slice_in_dim(full_w1, lat_pos * columns, columns, 3)
    sum_w2 = lax.dynamic_slice_in_dim(full_w2, lat_pos * columns, columns, 3)
    sum_b1 = lax.dynamic_slice_in_dim(full_b1, lat_pos * columns, columns, 2)
    whole = (cotan.astype(F32) + mixed.astype(F32)).astype(BF16)
    received = from_behind(whole[None], "section", -1)
    return (received, sum_w1, sum_w2, sum_b1)


def per_device(grad_out, spec_saved, w1, w2, b1, mode_counts, assignment):
    n_dev = lax.axis_size("lat")
    pairs_dev = spec_saved.shape[3] // BS
    paired = n_dev == 2 * NB and grad_out.shape[1] == 1 and pairs_dev % NB == 0
    body = paired_blocks if paired else split_blocks
    return body(grad_out, spec_saved, w1, w2, b1, mode_counts, assignment)


def solution(mesh):
    return jax.shard_map(
        per_device,
        mesh=mesh,
        in_specs=(
            P("section", "lat", None, None),
            P("section", None, None, "lat"),
            P("section", None, None, None),
            P("section", None, None, None),
            P("section", None, None),
            P(),
            P(),
        ),
        out_specs=(
            P("section", "lat", None, None),
            P("section", None, None, "lat"),
            P("section", None, None, "lat"),
            P("section", None, "lat"),
        ),
        check_vma=False,
    )
```

time: 35.9 us -> 40.6 us (1.13)
  waiting for transfers between devices: 14.8 us -> 19.9 us
  Pallas kernels: 8.01 us -> 6.41 us
  starting transfers between devices: 11.5 us -> 12.4 us
    ppermute x7 -> x11, waiting for transfers between devices: 9.15 us -> 19.9 us  [the longest x8 17.4 us: across(): return lax.ppermute(value, 'lat', [(i, i ^ 2 * d) for i in range(2 * NB)])]
    ppermute x1, waiting for transfers between devices: 5.67 us -> 0.01 us  [from_behind(): return lax.ppermute(value, axis, pairs)]
    pallas_call x5 -> x8, Pallas kernels: 8.01 us -> 6.41 us  [call(): pl.pallas_call(kernel, out_shape=outs, in_specs=[VMEM] * len(near) + [HBM...]
    ppermute x7 -> x11, starting transfers between devices: 10.2 us -> 11.1 us  [the longest x8 10.4 us: across(): return lax.ppermute(value, 'lat', [(i, i ^ 2 * d) for i in range(2 * NB)])]
  transfers between devices with their start and end apart: 8 -> 12, of which waited for: 6 -> 8; matrix products, arithmetic and copies ran while one was open for 0% -> 0% of each run, Pallas kernels for 3% -> 7%
where the time goes in v5:
time: 40.6 us; the launch traced here: 40.1 us
  waiting for transfers between devices  19.9 us (49%)
  starting transfers between devices  12.4 us (31%)
  Pallas kernels  6.41 us (16%)
  between operations  0.74 us (2%)
  local copies, waits for them, and re-layouts  0.66 us (2%)
    ppermute x8, waiting for transfers between devices, across(): return lax.ppermute(value, 'lat', [(i, i ^ 2 * d) for i in range(2 * NB)])  17.4 us
    ppermute x8, starting transfers between devices, across(): return lax.ppermute(value, 'lat', [(i, i ^ 2 * d) for i in range(2 * NB)])  10.4 us
    pallas_call x8, Pallas kernels, call(): pl.pallas_call(kernel, out_shape=outs, in_specs=[VMEM] * len(near) + [HBM...  6.41 us
    ppermute x3, waiting for transfers between devices, twin(): return lax.ppermute(value, 'lat', [(i, i ^ 1) for i in range(2 * NB)])  2.47 us
    ppermute x1, starting transfers between devices, from_behind(): return lax.ppermute(value, axis, pairs)  1.29 us
  transfers between devices with their start and end apart: 12, of which 8 were waited for; matrix products, arithmetic and copies ran while one was open for 0% of the time, Pallas kernels for 7%

profile of v5, /device:TPU:0, one launch (start us, length us, event | category | flops | bytes accessed | tf_op | source)
XLA Modules:
  0.0 40.1 jit_solution(12791289855908180268)
XLA Ops:
  0.6 0.5 %collective-permute-start = (bf16[180,384]{1,0:T(8,128)(2,1)}, bf16[180,384]{1,0:T(8,128)(2,1)S(1)}, u32[]{:S(2)}, u32[]{:S(2)}) collective-permute-start(bf16[180,384]{1,0:T(8,128)(2,1)} %bitcast.14), channel_id=1, source_target_pairs={{0,1},{1,0},{2,3},{3,2},{4,5},{5,4},{6,7},{7,6},{8,9},{9,8},{10,11... | collective-permute-start | bytes 414728 | tf_op jit(solution)/shard_map/ppermute | solution.py:322
  1.1 1.2 %collective-permute-done.refs_0_ = bf16[180,384]{1,0:T(8,128)(2,1)S(1)} collective-permute-done((bf16[180,384]{1,0:T(8,128)(2,1)}, bf16[180,384]{1,0:T(8,128)(2,1)S(1)}, u32[]{:S(2)}, u32[]{:S(2)}) %collective-permute-start) | collective-permute-done | bytes 138272 | tf_op jit(solution)/shard_map/ppermute | solution.py:322
  2.4 1.3 %shard_map.129 = (bf16[40,384]{1,0:T(8,128)(2,1)S(1)}, bf16[40,384]{1,0:T(8,128)(2,1)S(1)}, bf16[40,384]{1,0:T(8,128)(2,1)S(1)}, bf16[40,384]{1,0:T(8,128)(2,1)S(1)}) custom-call(bf16[180,384]{1,0:T(8,128)(2,1)S(1)} %collective-permute-done.refs_0_, s32[8]{0:T(128)} %refs_5_.2, s32[8]{0:T(128)} %refs_6_.1, bf16[180,384]{1,0:T(8,128)(2,1)} %bitcast.15, ...), custom_call_target="tpu_custom_call" | custom-call | tf_op jit(solution)/shard_map/pallas_call | solution.py:275
  3.6 3.0 %collective-permute-start.1 = (bf16[40,384]{1,0:T(8,128)(2,1)S(1)}, bf16[40,384]{1,0:T(8,128)(2,1)S(1)}, u32[]{:S(2)}, u32[]{:S(2)}) collective-permute-start(bf16[40,384]{1,0:T(8,128)(2,1)S(1)} %get-tuple-element.28), channel_id=1, source_target_pairs={{0,2},{1,3},{2,0},{3,1},{4,6},{5,7},{6,4},{7,5},{8,10},{9,11},{10,... | collective-permute-start | bytes 92168 | tf_op jit(solution)/shard_map/ppermute | solution.py:319
  6.6 2.6 %collective-permute-start.2 = (bf16[40,384]{1,0:T(8,128)(2,1)S(1)}, bf16[40,384]{1,0:T(8,128)(2,1)S(1)}, u32[]{:S(2)}, u32[]{:S(2)}) collective-permute-start(bf16[40,384]{1,0:T(8,128)(2,1)S(1)} %get-tuple-element.29), channel_id=1, source_target_pairs={{0,4},{1,5},{2,6},{3,7},{4,0},{5,1},{6,2},{7,3},{8,12},{9,13},{10,... | collective-permute-start | bytes 92168 | tf_op jit(solution)/shard_map/ppermute | solution.py:319
  9.2 1.6 %shard_map.130 = (bf16[4,256,256]{2,1,0:T(8,128)(2,1)S(1)}, bf16[4,256,256]{2,1,0:T(8,128)(2,1)S(1)}, bf16[4,72,256]{2,1,0:T(8,128)(2,1)S(1)}, bf16[4,72,256]{2,...) custom-call(s32[8]{0:T(128)} %refs_6_.1, bf16[8,2,3456]{2,1,0:T(2,128)(2,1)} %bitcast.19, ...), custom_call_target="tpu_custom_call" | custom-call | tf_op jit(solution)/shard_map/pallas_call | solution.py:275
  10.9 1.1 %collective-permute-done.2.refs_2_ = bf16[40,384]{1,0:T(8,128)(2,1)S(1)} collective-permute-done((bf16[40,384]{1,0:T(8,128)(2,1)S(1)}, bf16[40,384]{1,0:T(8,128)(2,1)S(1)}, u32[]{:S(2)}, u32[]{:S(2)}) %collective-permute-start.2) | collective-permute-done | bytes 30752 | tf_op jit(solution)/shard_map/ppermute | solution.py:319
  12.0 3.0 %collective-permute-done.3.refs_3_ = bf16[40,384]{1,0:T(8,128)(2,1)S(1)} collective-permute-done((bf16[40,384]{1,0:T(8,128)(2,1)S(1)}, bf16[40,384]{1,0:T(8,128)(2,1)S(1)}, u32[]{:S(2)}, u32[]{:S(2)}) %collective-permute-start.3) | collective-permute-done | bytes 30752 | tf_op jit(solution)/shard_map/ppermute | solution.py:319
  14.9 1.5 %shard_map.131 = (bf16[40,384]{1,0:T(8,128)(2,1)S(1)}, bf16[40,384]{1,0:T(8,128)(2,1)S(1)}, bf16[40,384]{1,0:T(8,128)(2,1)S(1)}, bf16[40,384]{1,0:T(8,128)(2,1)S...) custom-call(bf16[40,384]{1,0:T(8,128)(2,1)S(1)} %get-tuple-element.27.refs_0_, ...), custom_call_target="tpu_custom_call" | custom-call | tf_op jit(solution)/shard_map/pallas_call | solution.py:275
  16.4 0.1 collective-permute-start.9
  16.6 0.9 %collective-permute-start.5 = (bf16[40,384]{1,0:T(8,128)(2,1)S(1)}, bf16[40,384]{1,0:T(8,128)(2,1)S(1)}, u32[]{:S(2)}, u32[]{:S(2)}) collective-permute-start(bf16[40,384]{1,0:T(8,128)(2,1)S(1)} %get-tuple-element.39), channel_id=1, source_target_pairs={{0,4},{1,5},{2,6},{3,7},{4,0},{5,1},{6,2},{7,3},{8,12},{9,13},{10,... | collective-permute-start | bytes 92168 | tf_op jit(solution)/shard_map/ppermute | solution.py:319
  17.5 3.4 %collective-permute-start.6 = (bf16[40,384]{1,0:T(8,128)(2,1)S(1)}, bf16[40,384]{1,0:T(8,128)(2,1)S(1)}, u32[]{:S(2)}, u32[]{:S(2)}) collective-permute-start(bf16[40,384]{1,0:T(8,128)(2,1)S(1)} %get-tuple-element.40), channel_id=1, source_target_pairs={{0,6},{1,7},{2,4},{3,5},{4,2},{5,3},{6,0},{7,1},{8,14},{9,15},{10,... | collective-permute-start | bytes 92168 | tf_op jit(solution)/shard_map/ppermute | solution.py:319
  20.9 0.5 %collective-permute-done.5.refs_2_ = bf16[40,384]{1,0:T(8,128)(2,1)S(1)} collective-permute-done((bf16[40,384]{1,0:T(8,128)(2,1)S(1)}, bf16[40,384]{1,0:T(8,128)(2,1)S(1)}, u32[]{:S(2)}, u32[]{:S(2)}) %collective-permute-start.5) | collective-permute-done | bytes 30752 | tf_op jit(solution)/shard_map/ppermute | solution.py:319
  21.5 1.8 %collective-permute-done.6.refs_3_ = bf16[40,384]{1,0:T(8,128)(2,1)S(1)} collective-permute-done((bf16[40,384]{1,0:T(8,128)(2,1)S(1)}, bf16[40,384]{1,0:T(8,128)(2,1)S(1)}, u32[]{:S(2)}, u32[]{:S(2)}) %collective-permute-start.6) | collective-permute-done | bytes 30752 | tf_op jit(solution)/shard_map/ppermute | solution.py:319
  23.3 0.1 collective-permute-start.7
  23.3 1.3 %collective-permute-done.7.refs_4_ = bf16[96,384]{1,0:T(8,128)(2,1)S(1)} collective-permute-done((bf16[96,384]{1,0:T(8,128)(2,1)S(1)}, bf16[96,384]{1,0:T(8,128)(2,1)S(1)}, u32[]{:S(2)}, u32[]{:S(2)}) %collective-permute-start.7) | collective-permute-done | bytes 73760 | tf_op jit(solution)/shard_map/ppermute | solution.py:322
  24.6 1.2 %shard_map.133 = bf16[180,384]{1,0:T(8,128)(2,1)S(1)} custom-call(bf16[40,384]{1,0:T(8,128)(2,1)S(1)} %get-tuple-element.37.refs_0_, bf16[40,384]{1,0:T(8,128)(2,1)S(1)} %collective-permute-done.4.refs_1_, bf16[40,384]{1,0:T(8,128)(2,1)S(1)} %collective-permute-done.5.refs_2_, bf16[40,384]{1,0:T(8,128)(2,1)S(1)} %collective-permute-done.6.refs_3_, ...), custom_call_target="tpu_custom_call" | custom-call | tf_op jit(solution)/shard_map/pallas_call | solution.py:275
  25.8 1.3 %collective-permute-start.8 = (bf16[1,1,180,384]{3,2,1,0:T(8,128)(2,1)S(1)}, bf16[1,1,180,384]{3,2,1,0:T(8,128)(2,1)S(1)}, u32[]{:S(2)}, u32[]{:S(2)}) collective-permute-start(bf16[1,1,180,384]{3,2,1,0:T(8,128)(2,1)S(1)} %bitcast.13), channel_id=1, source_target_pairs={{8,0},{16,8},{24,16},{9,1},{17,9},{25,17},{10,2},{18,10},{26,18},{... | collective-permute-start | bytes 414728 | tf_op jit(solution)/shard_map/ppermute | solution.py:23
  27.2 0.3 collective-permute-start.10
  27.5 7.1 %collective-permute-done.10.got = bf16[2,56,384]{2,1,0:T(8,128)(2,1)S(1)} collective-permute-done((bf16[2,56,384]{2,1,0:T(8,128)(2,1)S(1)}, bf16[2,56,384]{2,1,0:T(8,128)(2,1)S(1)}, u32[]{:S(2)}, u32[]{:S(2)}) %collective-permute-start.10) | collective-permute-done | bytes 86048 | tf_op jit(solution)/shard_map/ppermute | solution.py:319
  34.6 0.1 collective-permute-start.11
  34.7 4.0 %collective-permute-done.11.got = bf16[1,56,384]{2,1,0:T(8,128)(2,1)S(1)} collective-permute-done((bf16[1,56,384]{2,1,0:T(8,128)(2,1)S(1)}, bf16[1,56,384]{2,1,0:T(8,128)(2,1)S(1)}, u32[]{:S(2)}, u32[]{:S(2)}) %collective-permute-start.11) | collective-permute-done | bytes 43040 | tf_op jit(solution)/shard_map/ppermute | solution.py:319
  38.7 0.7 %shard_map.136 = (f32[2,48,96]{2,1,0:T(8,128)}, f32[2,48,96]{2,1,0:T(8,128)}, f32[2,48]{1,0:T(2,128)}) custom-call(f32[1,56,384]{2,1,0:T(8,128)S(1)} %get-tuple-element.45.kept, bf16[1,56,384]{2,1,0:T(8,128)(2,1)S(1)} %collective-permute-done.11.got), custom_call_target="tpu_custom_call" | custom-call | tf_op jit(solution)/shard_map/pallas_call | solution.py:275
  39.4 0.7 %copy.15 = bf16[1,1,180,384]{3,2,1,0:T(8,128)(2,1)} copy(bf16[1,1,180,384]{3,2,1,0:T(8,128)(2,1)S(1)} %collective-permute-done.8) | data formatting | bytes 276480
  (9 shorter events, 0.2 us)
Async XLA Ops:
  0.6 1.7 %collective-permute-start = (bf16[180,384]{1,0:T(8,128)(2,1)}, bf16[180,384]{1,0:T(8,128)(2,1)S(1)}, u32[]{:S(2)}, u32[]{:S(2)}) collective-permute-start(bf16[180,384]{1,0:T(8,128)(2,1)} %bitcast.14), channel_id=1, source_target_pairs={{0,1},{1,0},{2,3},{3,2},{4,5},{5,4},{6,7},{7,6},{8,9},{9,8},{10,11... | collective-permute-start | bytes 414728 | tf_op jit(solution)/shard_map/ppermute | solution.py:322
  3.6 7.2 %collective-permute-start.1 = (bf16[40,384]{1,0:T(8,128)(2,1)S(1)}, bf16[40,384]{1,0:T(8,128)(2,1)S(1)}, u32[]{:S(2)}, u32[]{:S(2)}) collective-permute-start(bf16[40,384]{1,0:T(8,128)(2,1)S(1)} %get-tuple-element.28), channel_id=1, source_target_pairs={{0,2},{1,3},{2,0},{3,1},{4,6},{5,7},{6,4},{7,5},{8,10},{9,11},{10,... | collective-permute-start | bytes 92168 | tf_op jit(solution)/shard_map/ppermute | solution.py:319
  6.6 5.3 %collective-permute-start.2 = (bf16[40,384]{1,0:T(8,128)(2,1)S(1)}, bf16[40,384]{1,0:T(8,128)(2,1)S(1)}, u32[]{:S(2)}, u32[]{:S(2)}) collective-permute-start(bf16[40,384]{1,0:T(8,128)(2,1)S(1)} %get-tuple-element.29), channel_id=1, source_target_pairs={{0,4},{1,5},{2,6},{3,7},{4,0},{5,1},{6,2},{7,3},{8,12},{9,13},{10,... | collective-permute-start | bytes 92168 | tf_op jit(solution)/shard_map/ppermute | solution.py:319
  9.2 5.7 %collective-permute-start.3 = (bf16[40,384]{1,0:T(8,128)(2,1)S(1)}, bf16[40,384]{1,0:T(8,128)(2,1)S(1)}, u32[]{:S(2)}, u32[]{:S(2)}) collective-permute-start(bf16[40,384]{1,0:T(8,128)(2,1)S(1)} %get-tuple-element.30), channel_id=1, source_target_pairs={{0,6},{1,7},{2,4},{3,5},{4,2},{5,3},{6,0},{7,1},{8,14},{9,15},{10,... | collective-permute-start | bytes 92168 | tf_op jit(solution)/shard_map/ppermute | solution.py:319
  16.4 10.7 %collective-permute-start.9 = (bf16[4,56,384]{2,1,0:T(8,128)(2,1)S(1)}, bf16[4,56,384]{2,1,0:T(8,128)(2,1)S(1)}, u32[]{:S(2)}, u32[]{:S(2)}) collective-permute-start(bf16[4,56,384]{2,1,0:T(8,128)(2,1)S(1)} %get-tuple-element.42), channel_id=1, source_target_pairs={{0,1},{1,0},{2,3},{3,2},{4,5},{5,4},{6,7},{7,6},{8,9},{9,8},{10,11... | collective-permute-start | bytes 516104 | tf_op jit(solution)/shard_map/ppermute | solution.py:322
  16.5 4.5 %collective-permute-start.4 = (bf16[40,384]{1,0:T(8,128)(2,1)S(1)}, bf16[40,384]{1,0:T(8,128)(2,1)S(1)}, u32[]{:S(2)}, u32[]{:S(2)}) collective-permute-start(bf16[40,384]{1,0:T(8,128)(2,1)S(1)} %get-tuple-element.38), channel_id=1, source_target_pairs={{0,2},{1,3},{2,0},{3,1},{4,6},{5,7},{6,4},{7,5},{8,10},{9,11},{10,... | collective-permute-start | bytes 92168 | tf_op jit(solution)/shard_map/ppermute | solution.py:319
  16.6 4.9 %collective-permute-start.5 = (bf16[40,384]{1,0:T(8,128)(2,1)S(1)}, bf16[40,384]{1,0:T(8,128)(2,1)S(1)}, u32[]{:S(2)}, u32[]{:S(2)}) collective-permute-start(bf16[40,384]{1,0:T(8,128)(2,1)S(1)} %get-tuple-element.39), channel_id=1, source_target_pairs={{0,4},{1,5},{2,6},{3,7},{4,0},{5,1},{6,2},{7,3},{8,12},{9,13},{10,... | collective-permute-start | bytes 92168 | tf_op jit(solution)/shard_map/ppermute | solution.py:319
  17.5 5.7 %collective-permute-start.6 = (bf16[40,384]{1,0:T(8,128)(2,1)S(1)}, bf16[40,384]{1,0:T(8,128)(2,1)S(1)}, u32[]{:S(2)}, u32[]{:S(2)}) collective-permute-start(bf16[40,384]{1,0:T(8,128)(2,1)S(1)} %get-tuple-element.40), channel_id=1, source_target_pairs={{0,6},{1,7},{2,4},{3,5},{4,2},{5,3},{6,0},{7,1},{8,14},{9,15},{10,... | collective-permute-start | bytes 92168 | tf_op jit(solution)/shard_map/ppermute | solution.py:319
  23.3 1.3 %collective-permute-start.7 = (bf16[96,384]{1,0:T(8,128)(2,1)S(1)}, bf16[96,384]{1,0:T(8,128)(2,1)S(1)}, u32[]{:S(2)}, u32[]{:S(2)}) collective-permute-start(bf16[96,384]{1,0:T(8,128)(2,1)S(1)} %shard_map.132), channel_id=1, source_target_pairs={{0,1},{1,0},{2,3},{3,2},{4,5},{5,4},{6,7},{7,6},{8,9},{9,8},{10,11... | collective-permute-start | bytes 221192 | tf_op jit(solution)/shard_map/ppermute | solution.py:322
  25.8 8.9 %collective-permute-start.8 = (bf16[1,1,180,384]{3,2,1,0:T(8,128)(2,1)S(1)}, bf16[1,1,180,384]{3,2,1,0:T(8,128)(2,1)S(1)}, u32[]{:S(2)}, u32[]{:S(2)}) collective-permute-start(bf16[1,1,180,384]{3,2,1,0:T(8,128)(2,1)S(1)} %bitcast.13), channel_id=1, source_target_pairs={{8,0},{16,8},{24,16},{9,1},{17,9},{25,17},{10,2},{18,10},{26,18},{... | collective-permute-start | bytes 414728 | tf_op jit(solution)/shard_map/ppermute | solution.py:23
  27.2 7.4 %collective-permute-start.10 = (bf16[2,56,384]{2,1,0:T(8,128)(2,1)S(1)}, bf16[2,56,384]{2,1,0:T(8,128)(2,1)S(1)}, u32[]{:S(2)}, u32[]{:S(2)}) collective-permute-start(bf16[2,56,384]{2,1,0:T(8,128)(2,1)S(1)} %get-tuple-element.44), channel_id=1, source_target_pairs={{0,4},{1,5},{2,6},{3,7},{4,0},{5,1},{6,2},{7,3},{8,12},{9,13},{10,... | collective-permute-start | bytes 258056 | tf_op jit(solution)/shard_map/ppermute | solution.py:319
  34.6 4.1 %collective-permute-start.11 = (bf16[1,56,384]{2,1,0:T(8,128)(2,1)S(1)}, bf16[1,56,384]{2,1,0:T(8,128)(2,1)S(1)}, u32[]{:S(2)}, u32[]{:S(2)}) collective-permute-start(bf16[1,56,384]{2,1,0:T(8,128)(2,1)S(1)} %get-tuple-element.46), channel_id=1, source_target_pairs={{0,2},{1,3},{2,0},{3,1},{4,6},{5,7},{6,4},{7,5},{8,10},{9,11},{10,... | collective-permute-start | bytes 129032 | tf_op jit(solution)/shard_map/ppermute | solution.py:319

commit v6 on v5

--- a/solution.py
+++ b/solution.py
@@ -97,30 +97,21 @@
     return device // 2, lax.rem(device, 2)
 
 
-def row_modes(shape, q):
-    row = lax.broadcasted_iota(jnp.int32, shape, 0)
-    twin = row >= 2 * q
-    row = jnp.where(twin, row - 2 * q, row)
-    return twin, jnp.where(row >= q, row - q, row)
+def active_rows(rows, limit, q):
+    row = lax.broadcasted_iota(jnp.int32, rows.shape, 0)
+    return jnp.where(jnp.where(row >= q, row - q, row) < limit, rows, 0.0)
 
 
 def analyse_kernel(q, *refs):
-    other, hbm, outs, held, (by_pair, sems) = refs[0], refs[1:5], refs[5:9], refs[9:13], refs[13:]
+    hbm, out, held, sems = refs[:4], refs[4], refs[5:9], refs[9]
     counts, assign, field, table = held
-    z, core = place()
-    copies = fetch(sems, hbm[:3] + (hbm[3].at[core],), held)
-    wait(copies)
-    pad, width = by_pair.shape[1:]
-    spectral = jnp.dot(table[0], field[...], preferred_element_type=F32)
-    spectral += jnp.dot(table[1], other[...], preferred_element_type=F32)
-    twin, mode = row_modes((pad, width), q)
-    active = [counts[assign[2 * z + side]] for side in (core, 1 - core)]
-    limit = jnp.where(twin, active[1], active[0])
-    for n in range(NB):
-        part = spectral[n * pad : (n + 1) * pad]
-        by_pair[n] = jnp.where(mode < limit - q * (2 * n + core), part, 0.0).astype(BF16)
-    for d, out in enumerate(outs):
-        out[...] = by_pair[partner(d)]
+    wait(fetch(sems, hbm, held))
+    n_dev, pad, width = out.shape
+    active = counts[assign[lax.axis_index("lat")]]
+    spectral = jnp.dot(table[...], field[...], preferred_element_type=F32)
+    for i in range(n_dev):
+        part = spectral[i * pad : (i + 1) * pad]
+        out[i] = active_rows(part, active - q * i, q).astype(BF16)
 
 
 def silu_kernel(q, *refs):
@@ -155,30 +146,25 @@
         sig = jax.nn.sigmoid(pre)
         hidden[n] = (pre * sig).astype(BF16)
         slope[n] = sig * (1.0 + pre * (1.0 - sig))
-    pad = lat.shape[1] // NB
+    n_rows = base.shape[1] // (2 * q)
+    pad = lat.shape[1] // n_rows
     row = lax.broadcasted_iota(jnp.int32, (base.shape[1], lat.shape[1]), 0)
     column = lax.broadcasted_iota(jnp.int32, row.shape, 1)
-    row_lat = sum((row >= 2 * q * i).astype(jnp.int32) for i in range(1, 2 * NB))
+    row_lat = sum((row >= 2 * q * i).astype(jnp.int32) for i in range(1, n_rows))
     column_lat = jnp.full(row.shape, -1, jnp.int32)
     inside = column
-    for d in range(NB):
-        for twin, side in enumerate((core, 1 - core)):
-            start = d * pad + twin * 2 * q
-            here = jnp.logical_and(column >= start, column < start + 2 * q)
-            column_lat = jnp.where(here, assign[2 * partner(d) + side], column_lat)
-            inside = jnp.where(here, column - start, inside)
+    for r in range(n_rows):
+        here = jnp.logical_and(column >= r * pad, column < r * pad + 2 * q)
+        column_lat = jnp.where(here, assign[r], column_lat)
+        inside = jnp.where(here, column - r * pad, inside)
     same = jnp.logical_and(row_lat == column_lat, row - 2 * q * row_lat == inside)
     lat[...] = dot(base[...], same.astype(F32).astype(BF16), (1, 0)).astype(BF16)
 
 
-def filter_kernel(q, *refs):
-    chunks, (mats1, mats2, points, hidden, slope, lat) = refs[:4], refs[4:10]
-    outs, kept, sent, by_block = refs[10:14], refs[14], refs[15], refs[16]
-    z, core = place()
-    pad, width = chunks[0].shape
-    rows = points.shape[1]
-    half = BS // 2
-    field = jnp.concatenate([chunk[...].astype(F32) for chunk in chunks], axis=0).astype(BF16)
+def filter_kernel(pencil, mats1, mats2, slope, lat, out, grad_pre, grad_out):
+    n_rows, pad, width = pencil.shape
+    rows = slope.shape[1]
+    field = pencil[...].astype(F32).reshape(n_rows * pad, width).astype(BF16)
     grad_y = dot(lat[...], field, (1, 0)).astype(BF16).astype(F32)
     inner = []
     for n in range(NB):
@@ -187,26 +173,35 @@
         dp = (dot(dy, mats2[n], (1, 1)) * slope[n]).astype(BF16)
         dv = dot(dp, mats1[n], (1, 1))
         inner.append(jnp.concatenate([dv[:, :LANES], dv[:, LANES:]], axis=0))
+        grad_out[n] = dy
+        grad_pre[n] = dp
+    grad_v = dense(inner).astype(BF16)
+    band = dot(lat[...], grad_v, (0, 0))
+    for r in range(n_rows):
+        out[r] = band[r * pad : (r + 1) * pad].astype(BF16)
+
+
+def products_kernel(points, hidden, grad_pre, grad_out, kept, sent, by_block):
+    core = place()[1]
+    width = kept.shape[2]
+    half = BS // 2
+    for n in range(NB):
         columns = []
-        for left, right in ((dp, points[n]), (dy, hidden[n])):
-            both = dot(left, right, (0, 0))
+        for left, right in ((grad_pre, points), (grad_out, hidden)):
+            both = dot(left[n], right[n], (0, 0))
             columns.append(both[:BS, :LANES] + both[LANES : LANES + BS, LANES:])
             columns.append(both[LANES : LANES + BS, :LANES] - both[:BS, LANES:])
         by_block[n, 0:BS] = dense(columns)
-        sums = jnp.sum(dp.astype(F32), axis=0, keepdims=True)
+        sums = jnp.sum(grad_pre[n].astype(F32), axis=0, keepdims=True)
         sums = jnp.concatenate([sums, jnp.zeros((1, width - 2 * LANES), F32)], axis=1)
         by_block[n, BS : BS + 8] = jnp.broadcast_to(sums, (8, width))
-    grad_v = dense(inner).astype(BF16)
-    band = dot(lat[...], grad_v, (0, 0))
-    for d, out in enumerate(outs):
-        out[...] = band[d * pad : (d + 1) * pad].astype(BF16)
-    for d in range(NB):
+    for i, d in enumerate((0, 2, 1, 3)):
         block = by_block[partner(d)]
         upper, lower, sums = block[:half], block[half:BS], block[BS:]
         own = jnp.where(core == 0, upper, lower)
         other = jnp.where(core == 0, lower, upper)
-        kept[d] = jnp.concatenate([own, sums], axis=0)
-        sent[d] = jnp.concatenate([other, sums], axis=0).astype(BF16)
+        kept[i] = jnp.concatenate([own, sums], axis=0)
+        sent[i] = jnp.concatenate([other, sums], axis=0).astype(BF16)
 
 
 def halve_kernel(kept, got, keep, send):
@@ -228,41 +223,15 @@
         gb1[c : c + 1] = jnp.where(core == 0, line[:, :half], line[:, half:BS])
 
 
-def part_kernel(q, *refs):
-    backs, out = refs[:4], refs[4]
-    pad = backs[0].shape[0]
-    rows = out.shape[0] // NB
-    twin = [pltpu.roll(back[...].astype(F32), pad - 2 * q, 0)[:rows] for back in backs]
-    out[...] = jnp.concatenate(twin, axis=0).astype(BF16)
-
-
 def compose_kernel(q, *refs):
-    backs, got, hbm, out, held, (by_device, sems) = (
-        refs[:4],
-        refs[4],
-        refs[5:9],
-        refs[9],
-        refs[10:14],
-        refs[14:],
-    )
+    back, hbm, out, held, sems = refs[0], refs[1:5], refs[5], refs[6:10], refs[10]
     counts, assign, field, table = held
     copies = fetch(sems, hbm, held)
-    z, core = place()
-    rows, width = by_device.shape[2:]
-    other = got[...].astype(F32)
-    for d, back in enumerate(backs):
-        by_device[core, partner(d)] = back[...].astype(F32)[:rows]
-        by_device[1 - core, partner(d)] = other[d * rows : (d + 1) * rows]
     wait(copies)
-    active = counts[assign[2 * z + core]]
-    mode = row_modes((rows, width), q)[1]
-    held_rows = [
-        jnp.where(mode < active - q * (2 * n + c), by_device[c, n], 0.0)
-        for c in range(2)
-        for n in range(NB)
-    ]
-    held_rows = jnp.concatenate(held_rows, axis=0).astype(BF16)
-    mixed = jnp.dot(table[...], held_rows, preferred_element_type=F32).astype(BF16)
+    active = counts[assign[lax.axis_index("lat")]]
+    rows = [active_rows(back[i].astype(F32), active - q * i, q) for i in range(back.shape[0])]
+    rows = jnp.concatenate(rows, axis=0).astype(BF16)
+    mixed = jnp.dot(table[...], rows, preferred_element_type=F32).astype(BF16)
     out[...] = (field[...].astype(F32) + mixed.astype(F32)).astype(BF16)
 
 
@@ -270,7 +239,8 @@
 HBM = pl.BlockSpec(memory_space=pltpu.HBM)
 
 
-def call(kernel, outs, scratch, near, far):
+def call(kernel, outs, scratch, near, far, flops=1 * 10**8):
+    cost = pl.CostEstimate(flops=flops, bytes_accessed=10**6, transcendentals=0)
     many = isinstance(outs, tuple)
     return pl.pallas_call(
         kernel,
@@ -278,6 +248,7 @@
         in_specs=[VMEM] * len(near) + [HBM] * len(far),
         out_specs=tuple([VMEM] * len(outs)) if many else VMEM,
         scratch_shapes=scratch,
+        cost_estimate=cost,
         compiler_params=pltpu.CompilerParams(vmem_limit_bytes=32 * 2**20),
     )(*near, *(pltpu.with_memory_space_constraint(x, pltpu.HBM) for x in far))
 
@@ -295,21 +266,17 @@
     n_rows = assignment.shape[0]
     q = spec_saved.shape[3] // (NB * BS)
     rows = q * n_rows
-    pad = (4 * q + 7) // 8 * 8
-    short = (2 * q + 7) // 8 * 8
+    pad = (2 * q + 7) // 8 * 8
     forward, inverse = lon_tables(KM, length)
 
-    inverse, forward = (
-        t.reshape(2, NB, 2, q, length).transpose(2, 1, 0, 3, 4).reshape(2, NB, 2 * q, length)
-        for t in (inverse, forward)
-    )
-    analysis = np.zeros((2, 2, NB, pad, length))
-    analysis[:, 0, :, : 2 * q] = inverse
-    analysis[:, 1, :, 2 * q : 4 * q] = inverse
-    analysis = jnp.asarray(analysis.reshape(2, 2, NB * pad, length).astype(BF16))
-    synthesis = np.zeros((2, NB, short, length))
-    synthesis[:, :, : 2 * q] = forward
-    synthesis = jnp.asarray(synthesis.reshape(2 * NB * short, length).T.astype(BF16))
+    def by_device(table):
+        table = table.reshape(2, n_rows, q, length).transpose(1, 0, 2, 3)
+        table = table.reshape(n_rows, 2 * q, length)
+        table = np.pad(table, ((0, 0), (0, pad - 2 * q), (0, 0)))
+        return table.reshape(n_rows * pad, length).astype(BF16)
+
+    analysis = jnp.asarray(by_device(inverse))
+    synthesis = jnp.asarray(by_device(forward).T)
     cosine, sine = lat_waves(n_rows)
     waves = np.array([[cosine, sine], [-sine, cosine]])
     base = np.einsum("eckr,uv->eukrcv", waves, np.eye(q))
@@ -321,68 +288,69 @@
     def twin(value):
         return lax.ppermute(value, "lat", [(i, i ^ 1) for i in range(2 * NB)])
 
-    def swap(chunks):
-        return [chunks[0]] + [across(chunks[d], d) for d in (3, 2, 1)][::-1]
+    def exchange(value):
+        return lax.all_to_all(value, "lat", split_axis=0, concat_axis=0, tiled=True)
 
     shape = jax.ShapeDtypeStruct
     field = grad_out.reshape(length, width)
-    other = twin(field)
     far = (mode_counts, assignment, field, analysis)
-    scratch, sems = scratch_for(mode_counts, assignment, field, shape(analysis.shape[1:], BF16))
-    sent = call(
-        functools.partial(analyse_kernel, q),
-        (shape((pad, width), BF16),) * NB,
-        scratch + [pltpu.VMEM((NB, pad, width), BF16), sems],
-        (other,),
-        far,
-    )
-    received = swap(sent)
+    scratch, sems = scratch_for(*far)
+    chunks = shape((n_rows, pad, width), BF16)
+    sent = call(functools.partial(analyse_kernel, q), chunks, scratch + [sems], (), far)
+    pencil = exchange(sent)
     far = (assignment, spec_saved[0], w1[0], w2[0], b1[0], base)
     scratch, sems = scratch_for(*far)
     wide = 2 * LANES
-    ready = call(
+    matrices, vectors = shape((NB, wide, wide), BF16), shape((NB, rows, wide), BF16)
+    mats1, mats2, points, hidden, slope, lat = call(
         functools.partial(silu_kernel, q),
         (
-            shape((NB, wide, wide), BF16),
-            shape((NB, wide, wide), BF16),
-            shape((NB, rows, wide), BF16),
-            shape((NB, rows, wide), BF16),
+            matrices,
+            matrices,
+            vectors,
+            vectors,
             shape((NB, rows, wide), F32),
-            shape((2 * rows, NB * pad), BF16),
+            shape((2 * rows, n_rows * pad), BF16),
         ),
         scratch + [sems],
         (),
         far,
-    )
+        5 * 10**9,
+    )
+    band, grad_pre, grad_y = call(
+        filter_kernel,
+        (chunks, vectors, vectors),
+        [],
+        (pencil, mats1, mats2, slope, lat),
+        (),
+    )
+    back = exchange(band)
     tall = BS // 2 + 8
-    *chunks, kept, given = call(
-        functools.partial(filter_kernel, q),
-        (shape((pad, width), BF16),) * NB
-        + (shape((NB, tall, width), F32), shape((NB, tall, width), BF16)),
+    kept, given = call(
+        products_kernel,
+        (shape((NB, tall, width), F32), shape((NB, tall, width), BF16)),
         [pltpu.VMEM((NB, BS + 8, width), F32)],
-        (*received, *ready),
+        (points, hidden, grad_pre, grad_y),
         (),
-    )
-    backs = swap(chunks)
-    got = twin(
-        call(
-            functools.partial(part_kernel, q), shape((NB * short, width), BF16), [], backs, ()
-        )
+        5 * 10**9,
     )
     far = (mode_counts, assignment, field, synthesis)
     scratch, sems = scratch_for(*far)
     total = call(
         functools.partial(compose_kernel, q),
         shape((length, width), BF16),
-        scratch + [pltpu.VMEM((2, NB, short, width), F32), sems],
-        (*backs, got),
+        scratch + [sems],
+        (back,),
         far,
     )
     shifted = from_behind(total[None, None], "section", -1)
 
     added = twin(given)
-    for d in (2, 1):
-        halves = (shape((d, tall, width), F32), shape((d, tall, width), BF16))
+    for d in (1, 2):
+        halves = (
+            shape((NB // (2 * d), tall, width), F32),
+            shape((NB // (2 * d), tall, width), BF16),
+        )
         kept, given = call(halve_kernel, halves, [], (kept, added), ())
         added = across(given, d)
     matrix = shape((2, BS // 2, BS), F32)

time: 40.6 us -> 37.7 us (0.929)
  the two profiles are of different devices: /device:TPU:0 before, /device:TPU:4 now
where the time goes in v6:
time: 37.7 us; the launch traced here: 37.3 us
  starting transfers between devices  14.3 us (38%)
  waiting for transfers between devices  14 us (37%)
  Pallas kernels  7.65 us (20%)
  between operations  0.69 us (2%)
  local copies, waits for them, and re-layouts  0.66 us (2%)
    all_to_all x2, starting transfers between devices, exchange(): return lax.all_to_all(value, 'lat', split_axis=0, concat_axis=0, tiled=True)  8.26 us
    all_to_all x2, waiting for transfers between devices, exchange(): return lax.all_to_all(value, 'lat', split_axis=0, concat_axis=0, tiled=True)  8.21 us
    pallas_call x8, Pallas kernels, call(): pl.pallas_call(kernel, out_shape=outs, in_specs=[VMEM] * len(near) + [HBM...  7.65 us
    ppermute x2, waiting for transfers between devices, across(): return lax.ppermute(value, 'lat', [(i, i ^ 2 * d) for i in range(2 * NB)])  4.71 us
    ppermute x1, starting transfers between devices, from_behind(): return lax.ppermute(value, axis, pairs)  3.34 us
    ppermute x2, starting transfers between devices, across(): return lax.ppermute(value, 'lat', [(i, i ^ 2 * d) for i in range(2 * NB)])  2.25 us
    ppermute x1, waiting for transfers between devices, twin(): return lax.ppermute(value, 'lat', [(i, i ^ 1) for i in range(2 * NB)])  1.04 us
  transfers between devices with their start and end apart: 6, of which 4 were waited for; matrix products, arithmetic and copies ran while one was open for 0% of the time, Pallas kernels for 11%

profile of v6, /device:TPU:4, one launch (start us, length us, event | category | flops | bytes accessed | tf_op | source)
XLA Modules:
  0.0 37.3 jit_solution(7880048683104760605)
XLA Ops:
  0.6 1.9 %shard_map.129 = bf16[8,24,384]{2,1,0:T(8,128)(2,1)} custom-call(s32[8]{0:T(128)} %refs_1_.3, s32[8]{0:T(128)} %refs_2_.1, bf16[180,384]{1,0:T(8,128)(2,1)} %bitcast.14, bf16[192,180]{1,0:T(8,128)(2,1)} %constant.6.clone.refs_3_), custom_call_target="tpu_custom_call" | custom-call | flops 100000000 | bytes 1000000 | tf_op jit(solution)/shard_map/pallas_call | solution.py:245
  2.5 4.9 %all-to-all-start = ((bf16[8,24,384]{2,1,0:T(8,128)(2,1)}), bf16[8,24,384]{2,1,0:T(8,128)(2,1)S(1)}, u32[]{:S(2)}, u32[]{:S(2)}) async-start(bf16[8,24,384]{2,1,0:T(8,128)(2,1)} %shard_map.129), calls=%async_computation | async-start | bytes 294912 | tf_op jit(solution)/shard_map/all_to_all | solution.py:292
  7.4 1.6 %shard_map.130 = (bf16[4,256,256]{2,1,0:T(8,128)(2,1)S(1)}, bf16[4,256,256]{2,1,0:T(8,128)(2,1)S(1)}, bf16[4,72,256]{2,1,0:T(8,128)(2,1)S(1)}, bf16[4,72,256]{2,...) custom-call(s32[8]{0:T(128)} %refs_2_.1, bf16[8,2,3456]{2,1,0:T(2,128)(2,1)} %bitcast.18, ...), custom_call_target="tpu_custom_call" | custom-call | flops 5000000000 | bytes 1000000 | tf_op jit(solution)/shard_map/pallas_call | solution.py:245
  9.0 5.4 %all-to-all-done.pencil = bf16[8,24,384]{2,1,0:T(8,128)(2,1)S(1)} async-done(((bf16[8,24,384]{2,1,0:T(8,128)(2,1)}), bf16[8,24,384]{2,1,0:T(8,128)(2,1)S(1)}, u32[]{:S(2)}, u32[]{:S(2)}) %all-to-all-start) | async-done | bytes 147488 | tf_op jit(solution)/shard_map/all_to_all | solution.py:292
  14.4 1.6 %shard_map.131 = (bf16[8,24,384]{2,1,0:T(8,128)(2,1)}, bf16[4,72,256]{2,1,0:T(8,128)(2,1)S(1)}, bf16[4,72,256]{2,1,0:T(8,128)(2,1)S(1)}) custom-call(bf16[8,24,384]{2,1,0:T(8,128)(2,1)S(1)} %all-to-all-done.pencil, bf16[4,256,256]{2,1,0:T(8,128)(2,1)S(1)} %get-tuple-element.22.mats1, bf16[4,256,256]{2,1,0:T(8,128)(2,1)S(1)} %get-tuple-element.23.mats2, ...), custom_call_target="tpu_custom_call" | custom-call | flops 100000000 | bytes 1000000 | tf_op jit(solution)/shard_map/pallas_call | solution.py:245
  16.0 3.4 %all-to-all-start.1 = ((bf16[8,24,384]{2,1,0:T(8,128)(2,1)}), bf16[8,24,384]{2,1,0:T(8,128)(2,1)S(1)}, u32[]{:S(2)}, u32[]{:S(2)}) async-start(bf16[8,24,384]{2,1,0:T(8,128)(2,1)} %get-tuple-element.26), calls=%async_computation.1 | async-start | bytes 294912 | tf_op jit(solution)/shard_map/all_to_all | solution.py:292
  19.3 0.6 %shard_map.133 = (f32[4,56,384]{2,1,0:T(8,128)S(1)}, bf16[4,56,384]{2,1,0:T(8,128)(2,1)S(1)}) custom-call(bf16[4,72,256]{2,1,0:T(8,128)(2,1)S(1)} %get-tuple-element.27.points, bf16[4,72,256]{2,1,0:T(8,128)(2,1)S(1)} %get-tuple-element.28.hidden, bf16[4,72,256]{2,1,0:T(8,128)(2,1)S(1)} %get-tuple-element.29.grad_pre, ...), custom_call_target="tpu_custom_call" | custom-call | flops 5000000000 | bytes 1000000 | tf_op jit(solution)/shard_map/pallas_call | solution.py:245
  19.9 0.5 %collective-permute-start.1 = (bf16[4,56,384]{2,1,0:T(8,128)(2,1)S(1)}, bf16[4,56,384]{2,1,0:T(8,128)(2,1)S(1)}, u32[]{:S(2)}, u32[]{:S(2)}) collective-permute-start(bf16[4,56,384]{2,1,0:T(8,128)(2,1)S(1)} %get-tuple-element.32), channel_id=1, source_target_pairs={{0,1},{1,0},{2,3},{3,2},{4,5},{5,4},{6,7},{7,6},{8,9},{9,8},{10,11... | collective-permute-start | bytes 516104 | tf_op jit(solution)/shard_map/ppermute | solution.py:289
  20.4 1.0 %collective-permute-done.1.got = bf16[4,56,384]{2,1,0:T(8,128)(2,1)S(1)} collective-permute-done((bf16[4,56,384]{2,1,0:T(8,128)(2,1)S(1)}, bf16[4,56,384]{2,1,0:T(8,128)(2,1)S(1)}, u32[]{:S(2)}, u32[]{:S(2)}) %collective-permute-start.1) | collective-permute-done | bytes 172064 | tf_op jit(solution)/shard_map/ppermute | solution.py:289
  21.5 2.0 %collective-permute-start.2 = (bf16[2,56,384]{2,1,0:T(8,128)(2,1)S(1)}, bf16[2,56,384]{2,1,0:T(8,128)(2,1)S(1)}, u32[]{:S(2)}, u32[]{:S(2)}) collective-permute-start(bf16[2,56,384]{2,1,0:T(8,128)(2,1)S(1)} %get-tuple-element.34), channel_id=1, source_target_pairs={{0,2},{1,3},{2,0},{3,1},{4,6},{5,7},{6,4},{7,5},{8,10},{9,11},{10,... | collective-permute-start | bytes 258056 | tf_op jit(solution)/shard_map/ppermute | solution.py:286
  23.4 2.8 %all-to-all-done.1.refs_0_ = bf16[8,24,384]{2,1,0:T(8,128)(2,1)S(1)} async-done(((bf16[8,24,384]{2,1,0:T(8,128)(2,1)}), bf16[8,24,384]{2,1,0:T(8,128)(2,1)S(1)}, u32[]{:S(2)}, u32[]{:S(2)}) %all-to-all-start.1) | async-done | bytes 147488 | tf_op jit(solution)/shard_map/all_to_all | solution.py:292
  26.3 1.2 %shard_map.132 = bf16[180,384]{1,0:T(8,128)(2,1)S(1)} custom-call(bf16[8,24,384]{2,1,0:T(8,128)(2,1)S(1)} %all-to-all-done.1.refs_0_, s32[8]{0:T(128)} %refs_1_.3, s32[8]{0:T(128)} %refs_2_.1, bf16[180,384]{1,0:T(8,128)(2,1)} %bitcast.15, bf16[180,192]{1,0:T(8,128)(2,1)} %constant.7.clone.refs_4_), custom_call_target="tpu_custom_call" | custom-call | flops 100000000 | bytes 1000000 | tf_op jit(solution)/shard_map/pallas_call | solution.py:245
  27.5 3.3 %collective-permute-start = (bf16[1,1,180,384]{3,2,1,0:T(8,128)(2,1)S(1)}, bf16[1,1,180,384]{3,2,1,0:T(8,128)(2,1)S(1)}, u32[]{:S(2)}, u32[]{:S(2)}) collective-permute-start(bf16[1,1,180,384]{3,2,1,0:T(8,128)(2,1)S(1)} %bitcast.13), channel_id=1, source_target_pairs={{8,0},{16,8},{24,16},{9,1},{17,9},{25,17},{10,2},{18,10},{26,18},{... | collective-permute-start | bytes 414728 | tf_op jit(solution)/shard_map/ppermute | solution.py:23
  30.9 0.0 collective-permute-done.2.got
  30.9 0.3 collective-permute-start.3
  31.2 4.7 %collective-permute-done.3.got = bf16[1,56,384]{2,1,0:T(8,128)(2,1)S(1)} collective-permute-done((bf16[1,56,384]{2,1,0:T(8,128)(2,1)S(1)}, bf16[1,56,384]{2,1,0:T(8,128)(2,1)S(1)}, u32[]{:S(2)}, u32[]{:S(2)}) %collective-permute-start.3) | collective-permute-done | bytes 43040 | tf_op jit(solution)/shard_map/ppermute | solution.py:286
  35.9 0.7 %shard_map.136 = (f32[2,48,96]{2,1,0:T(8,128)}, f32[2,48,96]{2,1,0:T(8,128)}, f32[2,48]{1,0:T(2,128)}) custom-call(f32[1,56,384]{2,1,0:T(8,128)S(1)} %get-tuple-element.35.kept, bf16[1,56,384]{2,1,0:T(8,128)(2,1)S(1)} %collective-permute-done.3.got), custom_call_target="tpu_custom_call" | custom-call | flops 100000000 | bytes 1000000 | tf_op jit(solution)/shard_map/pallas_call | solution.py:245
  36.6 0.0 collective-permute-done
  36.6 0.7 %copy.15 = bf16[1,1,180,384]{3,2,1,0:T(8,128)(2,1)} copy(bf16[1,1,180,384]{3,2,1,0:T(8,128)(2,1)S(1)} %collective-permute-done) | data formatting | bytes 276480
  (2 shorter events, 0.1 us)
Async XLA Ops:
  2.5 11.9 %all-to-all-start = ((bf16[8,24,384]{2,1,0:T(8,128)(2,1)}), bf16[8,24,384]{2,1,0:T(8,128)(2,1)S(1)}, u32[]{:S(2)}, u32[]{:S(2)}) async-start(bf16[8,24,384]{2,1,0:T(8,128)(2,1)} %shard_map.129), calls=%async_computation | async-start | bytes 294912 | tf_op jit(solution)/shard_map/all_to_all | solution.py:292
  16.0 10.3 %all-to-all-start.1 = ((bf16[8,24,384]{2,1,0:T(8,128)(2,1)}), bf16[8,24,384]{2,1,0:T(8,128)(2,1)S(1)}, u32[]{:S(2)}, u32[]{:S(2)}) async-start(bf16[8,24,384]{2,1,0:T(8,128)(2,1)} %get-tuple-element.26), calls=%async_computation.1 | async-start | bytes 294912 | tf_op jit(solution)/shard_map/all_to_all | solution.py:292
  19.9 1.5 %collective-permute-start.1 = (bf16[4,56,384]{2,1,0:T(8,128)(2,1)S(1)}, bf16[4,56,384]{2,1,0:T(8,128)(2,1)S(1)}, u32[]{:S(2)}, u32[]{:S(2)}) collective-permute-start(bf16[4,56,384]{2,1,0:T(8,128)(2,1)S(1)} %get-tuple-element.32), channel_id=1, source_target_pairs={{0,1},{1,0},{2,3},{3,2},{4,5},{5,4},{6,7},{7,6},{8,9},{9,8},{10,11... | collective-permute-start | bytes 516104 | tf_op jit(solution)/shard_map/ppermute | solution.py:289
  21.5 9.4 %collective-permute-start.2 = (bf16[2,56,384]{2,1,0:T(8,128)(2,1)S(1)}, bf16[2,56,384]{2,1,0:T(8,128)(2,1)S(1)}, u32[]{:S(2)}, u32[]{:S(2)}) collective-permute-start(bf16[2,56,384]{2,1,0:T(8,128)(2,1)S(1)} %get-tuple-element.34), channel_id=1, source_target_pairs={{0,2},{1,3},{2,0},{3,1},{4,6},{5,7},{6,4},{7,5},{8,10},{9,11},{10,... | collective-permute-start | bytes 258056 | tf_op jit(solution)/shard_map/ppermute | solution.py:286
  27.5 9.1 %collective-permute-start = (bf16[1,1,180,384]{3,2,1,0:T(8,128)(2,1)S(1)}, bf16[1,1,180,384]{3,2,1,0:T(8,128)(2,1)S(1)}, u32[]{:S(2)}, u32[]{:S(2)}) collective-permute-start(bf16[1,1,180,384]{3,2,1,0:T(8,128)(2,1)S(1)} %bitcast.13), channel_id=1, source_target_pairs={{8,0},{16,8},{24,16},{9,1},{17,9},{25,17},{10,2},{18,10},{26,18},{... | collective-permute-start | bytes 414728 | tf_op jit(solution)/shard_map/ppermute | solution.py:23
  30.9 5.0 %collective-permute-start.3 = (bf16[1,56,384]{2,1,0:T(8,128)(2,1)S(1)}, bf16[1,56,384]{2,1,0:T(8,128)(2,1)S(1)}, u32[]{:S(2)}, u32[]{:S(2)}) collective-permute-start(bf16[1,56,384]{2,1,0:T(8,128)(2,1)S(1)} %get-tuple-element.36), channel_id=1, source_target_pairs={{0,4},{1,5},{2,6},{3,7},{4,0},{5,1},{6,2},{7,3},{8,12},{9,13},{10,... | collective-permute-start | bytes 129032 | tf_op jit(solution)/shard_map/ppermute | solution.py:286

commit v7 on v4

--- a/solution.py
+++ b/solution.py
@@ -21,6 +21,13 @@
     length = lax.axis_size(axis)
     pairs = [(i, i + by) for i in range(length) if 0 <= i + by < length]
     return lax.ppermute(value, axis, pairs)
+
+
+def from_next(value, axis):
+    length = lax.axis_size(axis)
+    odd = lax.ppermute(value, axis, [(i, i - 1) for i in range(2, length, 2)])
+    even = lax.ppermute(value, axis, [(i, i - 1) for i in range(1, length, 2)])
+    return jnp.where(lax.axis_index(axis) % 2 == 1, odd, even)
 
 
 def lon_tables(n_modes, length):
@@ -73,15 +80,13 @@
     return lax.dot_general(a, b, ((contract[:1], contract[1:]), ((), ())), preferred_element_type=F32)
 
 
-def keep_active(counts, assign, q, groups):
-    active = counts[assign[lax.axis_index("lat")]]
-    shape = groups[0].shape
-    number = lax.broadcasted_iota(jnp.int32, shape, 0)
+def mode_numbers(shape, axis, q):
+    number = lax.broadcasted_iota(jnp.int32, shape, axis)
     number = jnp.where(number >= NB * q, number - NB * q, number)
     mode = number
     for z in range(1, NB):
         mode = jnp.where(number >= z * q, number + z * q, mode)
-    return [jnp.where(mode < active - g * q, value, 0.0) for g, value in enumerate(groups)]
+    return mode
 
 
 def fetch(sems, sources, targets):
@@ -119,7 +124,12 @@
     wait(copies[:4])
     rows = by_block.shape[1]
     spectral = jnp.dot(table[...], field[...], preferred_element_type=F32)
-    groups = keep_active(counts, assign, q, [spectral[:rows], spectral[rows:]])
+    active = counts[assign[lax.axis_index("lat")]]
+    mode = mode_numbers((rows, spectral.shape[1]), 0, q)
+    groups = [
+        jnp.where(mode < active - g * q, spectral[g * rows : (g + 1) * rows], 0.0)
+        for g in range(2)
+    ]
     for n in range(NB):
         pieces = [window(group, n * BS) for group in groups]
         by_block[n] = dense(pieces + points[n]).astype(BF16)
@@ -127,8 +137,18 @@
         out[...] = by_block[partner(d)]
 
 
-def weights_kernel(w1_hbm, w2_hbm, b1_hbm, mat1, mat2, bias, w1, w2, b1, sems):
-    wait(fetch(sems, (w1_hbm, w2_hbm, b1_hbm), (w1, w2, b1)))
+def ready_kernel(q, *refs):
+    hbm, (mat1, mat2, bias, lat, lat_t, own_field, own_table) = refs[:9], refs[9:16]
+    counts, assign, w1, w2, b1, table, sems = refs[16:]
+    copies = fetch(sems, hbm, (counts, assign, w1, w2, b1, table, lat, lat_t, own_field))
+    wait(copies[:6])
+    active = counts[assign[lax.axis_index("lat")]]
+    rows = table.shape[1] // 2
+    mode = mode_numbers((table.shape[0], rows), 1, q)
+    for g in range(2):
+        part = table[:, g * rows : (g + 1) * rows].astype(F32)
+        part = jnp.where(mode < active - g * q, part, 0.0)
+        own_table[:, g * rows : (g + 1) * rows] = part.astype(BF16)
     block = lax.axis_index("lat") // 2
 
     def pick(x):
@@ -147,6 +167,7 @@
         mat[LANES + BS : 2 * LANES] = gap
     shift_b = pick(b1[...].astype(F32))
     bias[...] = jnp.concatenate([shift_b[0:1], shift_b[1:2]], axis=1)
+    wait(copies[6:])
 
 
 def join_kernel(*refs):
@@ -175,72 +196,85 @@
     return [upper, right]
 
 
+def silu_points(chunks, mat, bias, by_pair, points, hidden, slope):
+    for d, chunk in enumerate(chunks):
+        parts = [window(chunk, j * BS) for j in (2, 3)]
+        by_pair[partner(d)] = jnp.concatenate(parts, axis=1)
+    v = by_pair[...].reshape(points.shape).astype(BF16)
+    pre = dot(v, mat[...], (1, 0)) + bias[...]
+    sig = jax.nn.sigmoid(pre)
+    points[...] = v
+    hidden[...] = (pre * sig).astype(BF16)
+    slope[...] = sig * (1.0 + pre * (1.0 - sig))
+
+
+def own_kernel(*refs):
+    chunks, (mat1, bias), (points, hidden, slope), by_pair = refs[:4], refs[4:6], refs[6:9], refs[9]
+    silu_points([chunk[...].astype(F32) for chunk in chunks], mat1, bias, by_pair, points, hidden, slope)
+
+
 def filter_kernel(*refs):
-    own, other, mat1, mat2, bias, assign_hbm, lat_hbm, lat_t_hbm = refs[:8]
-    outs, (gw1, gw2, gb1) = refs[8:12], refs[12:15]
-    assign, lat, lat_t, by_lat, points_v, sems = refs[15:]
-    copies = fetch(sems, (assign_hbm, lat_hbm, lat_t_hbm), (assign, lat, lat_t))
-    wait(copies[:1])
-    n_half, rows, width = own.shape
+    owns, (other, slope_own, mat1, mat2, bias, lat, lat_t, assign_hbm) = refs[:4], refs[4:12]
+    outs, (points, hidden, grad_pre, grad_y) = refs[12:16], refs[16:20]
+    assign, by_lat, by_pair, slope, sems = refs[20:]
+    copies = fetch(sems, (assign_hbm,), (assign,))
     core = lax.rem(lax.axis_index("lat"), 2)
-    segments = [BS * j for j in range(4)]
-    for b, buffer in enumerate((own, other)):
-        side = core if b == 0 else 1 - core
-        for d in range(n_half):
-            chunk = buffer[d].astype(F32)
-            groups = [window(chunk, segments[j]) for j in range(2)]
+    sides = [[own[...].astype(F32) for own in owns], [other[d].astype(F32) for d in range(NB)]]
+    silu_points(sides[1], mat1, bias, by_pair, points, hidden, slope)
+    wait(copies)
+    for side, chunks in zip((core, 1 - core), sides):
+        for d, chunk in enumerate(chunks):
+            groups = [window(chunk, j * BS) for j in range(2)]
             by_lat[assign[2 * partner(d) + side]] = jnp.concatenate(groups, axis=1)
-            parts = [window(chunk, segments[j]) for j in (2, 3)]
-            points_v[side, partner(d)] = jnp.concatenate(parts, axis=1)
     field = by_lat[...].reshape(lat.shape[1], 2 * LANES).astype(BF16)
-    wait(copies[1:2])
-    grad_y = dot(lat[...], field, (1, 0)).astype(BF16)
-    points = grad_y.shape[0] // 2
-    first, second = mat1[...], mat2[...]
-    both1, both2, sums, inner = 0.0, 0.0, 0.0, []
-    for g in range(2):
-        v = points_v[g].reshape(points, 2 * LANES).astype(BF16)
-        dy = [grad_y[c * points : (c + 1) * points, g * LANES : (g + 1) * LANES] for c in range(2)]
+    waves = dot(lat[...], field, (1, 0)).astype(BF16)
+    rows = waves.shape[0] // 2
+    inner = []
+    for side, slopes in enumerate((slope_own, slope)):
+        dy = []
+        for c in range(2):
+            part = waves[c * rows : (c + 1) * rows]
+            flip = core == 0 if side == 0 else core == 1
+            dy.append(jnp.where(flip, part[:, :LANES], part[:, LANES:]))
         dy = jnp.concatenate(dy, axis=1)
-        pre = dot(v, first, (1, 0)) + bias[...]
-        sig = jax.nn.sigmoid(pre)
-        hidden = (pre * sig).astype(BF16)
-        grad_hidden = dot(dy, second, (1, 1))
-        dp = (grad_hidden * (sig * (1.0 + pre * (1.0 - sig)))).astype(BF16)
-        dv = dot(dp, first, (1, 1)).astype(BF16)
+        dp = (dot(dy, mat2[...], (1, 1)) * slopes[...]).astype(BF16)
+        dv = dot(dp, mat1[...], (1, 1))
+        grad_y[side] = dy
+        grad_pre[side] = dp
         inner.append(jnp.concatenate([dv[:, :LANES], dv[:, LANES:]], axis=0))
-        both1 += dot(dp, v, (0, 0))
-        both2 += dot(dy, hidden, (0, 0))
-        sums += jnp.sum(dp.astype(F32), axis=0, keepdims=True)
-    inner = jnp.concatenate(inner, axis=1)
-    wait(copies[2:])
+    left = jnp.where(core == 0, inner[0], inner[1])
+    right = jnp.where(core == 0, inner[1], inner[0])
+    inner = jnp.concatenate([left, right], axis=1).astype(BF16)
     for d, out in enumerate(outs):
         band = dot(lat_t[assign[2 * partner(d) + core]], inner, (1, 0))
         out[...] = pack(band).astype(BF16)
+
+
+def products_kernel(points0, hidden0, points1, hidden1, grad_pre, grad_y, gw1, gw2, gb1):
+    core = lax.rem(lax.axis_index("lat"), 2)
     half = BS // 2
-    for both, ref in ((both1, gw1), (both2, gw2)):
+    for ref, grads, values in ((gw1, grad_pre, (points0, points1)), (gw2, grad_y, (hidden0, hidden1))):
+        both = dot(grads[0], values[0][...], (0, 0)) + dot(grads[1], values[1][...], (0, 0))
         real = both[:BS, :LANES] + both[LANES : LANES + BS, LANES:]
         imag = both[LANES : LANES + BS, :LANES] - both[:BS, LANES:]
         for c, full in enumerate((real, imag)):
             ref[c] = jnp.where(core == 0, full[:half], full[half:])[:, :BS]
+    sums = sum(jnp.sum(grad_pre[side].astype(F32), axis=0, keepdims=True) for side in range(2))
     for c in range(2):
         line = sums[:, c * LANES : (c + 1) * LANES]
         gb1[c : c + 1] = jnp.where(core == 0, line[:, :half], line[:, half:BS])
 
 
-def compose_kernel(q, *refs):
-    backs, hbm, out, held, (by_block, sems) = refs[:4], refs[4:8], refs[8], refs[9:13], refs[13:]
-    counts, assign, field, table = held
-    copies = fetch(sems, hbm, held)
-    rows = 2 * NB * q
+def compose_kernel(*refs):
+    backs, (field, table, out, by_block) = refs[:4], refs[4:]
+    rows = by_block.shape[1]
     for d, back in enumerate(backs):
         by_block[partner(d)] = jnp.concatenate(unpack(back[...].astype(F32), rows), axis=1)
     groups = [
         dense([by_block[n, :, g * LANES : (g + 1) * LANES] for n in range(NB)]) for g in range(2)
     ]
-    wait(copies)
-    masked = jnp.concatenate(keep_active(counts, assign, q, groups), axis=0).astype(BF16)
-    mixed = jnp.dot(table[...], masked, preferred_element_type=F32).astype(BF16)
+    groups = jnp.concatenate(groups, axis=0).astype(BF16)
+    mixed = jnp.dot(table[...], groups, preferred_element_type=F32).astype(BF16)
     out[...] = (field[...].astype(F32) + mixed.astype(F32)).astype(BF16)
 
 
@@ -248,7 +282,8 @@
 HBM = pl.BlockSpec(memory_space=pltpu.HBM)
 
 
-def call(kernel, outs, scratch, near, far):
+def call(kernel, outs, scratch, near, far, flops=10**8):
+    many = isinstance(outs, tuple)
     many = isinstance(outs, tuple)
     return pl.pallas_call(
         kernel,
@@ -256,6 +291,7 @@
         in_specs=[VMEM] * len(near) + [HBM] * len(far),
         out_specs=tuple([VMEM] * len(outs)) if many else VMEM,
         scratch_shapes=scratch,
+        cost_estimate=pl.CostEstimate(flops=flops, bytes_accessed=10**6, transcendentals=0),
         compiler_params=pltpu.CompilerParams(vmem_limit_bytes=32 * 2**20),
     )(*near, *(pltpu.with_memory_space_constraint(x, pltpu.HBM) for x in far))
 
@@ -305,45 +341,73 @@
         far,
     )
     received = swap(sent)
-    far = (w1[0], w2[0], b1[0])
-    scratch, sems = scratch_for(*far)
-    wide = (2 * LANES, 2 * LANES)
-    mats = call(
-        weights_kernel,
-        (shape(wide, BF16), shape(wide, BF16), shape((1, 2 * LANES), F32)),
-        scratch + [sems],
+    far = (mode_counts, assignment, w1[0], w2[0], b1[0], forward)
+    scratch, _ = scratch_for(*far)
+    far = (*far, lat, lat_t, field)
+    wide = 2 * LANES
+    mat1, mat2, bias, lat, lat_t, field, forward = call(
+        functools.partial(ready_kernel, q),
+        (
+            shape((wide, wide), BF16),
+            shape((wide, wide), BF16),
+            shape((1, wide), F32),
+            shape(lat.shape, BF16),
+            shape(lat_t.shape, BF16),
+            shape(field.shape, BF16),
+            shape(forward.shape, BF16),
+        ),
+        scratch + [pltpu.SemaphoreType.DMA((len(far),))],
         (),
         far,
+        2 * 10**9,
     )
     own = call(join_kernel, shape((NB, rows, width), BF16), [], received, ())
     other = lax.ppermute(own, "lat", [(i, i ^ 1) for i in range(2 * NB)])
-    far = (assignment, lat, lat_t)
-    scratch, sems = scratch_for(*far)
+    vectors = shape((NB * rows, wide), BF16)
+    slopes = shape((NB * rows, wide), F32)
+    by_pair = pltpu.VMEM((NB, rows, wide), F32)
+    points0, hidden0, slope0 = call(
+        own_kernel,
+        (vectors, vectors, slopes),
+        [by_pair],
+        (*received, mat1, bias),
+        (),
+        2 * 10**9,
+    )
     packed = shape((rows + rows // 2 + 4, LANES), BF16)
-    matrix = shape((2, BS // 2, BS), F32)
-    *chunks, gw1, gw2, gb1 = call(
+    scratch, sems = scratch_for(assignment)
+    both = shape((2, NB * rows, wide), BF16)
+    *chunks, points1, hidden1, grad_pre, grad_y = call(
         filter_kernel,
-        (packed,) * NB + (matrix, matrix, shape((2, BS // 2), F32)),
+        (packed,) * NB + (vectors, vectors, both, both),
         scratch
         + [
-            pltpu.VMEM((n_rows, rows, 2 * LANES), F32),
-            pltpu.VMEM((2, NB, rows, 2 * LANES), F32),
+            pltpu.VMEM((n_rows, rows, wide), F32),
+            by_pair,
+            pltpu.VMEM((NB * rows, wide), F32),
             sems,
         ],
-        (own, other, *mats),
-        far,
+        (*received, other, slope0, mat1, mat2, bias, lat, lat_t),
+        (assignment,),
     )
     backs = swap(chunks)
-    far = (mode_counts, assignment, field, forward)
-    scratch, sems = scratch_for(*far)
+    matrix = shape((2, BS // 2, BS), F32)
+    gw1, gw2, gb1 = call(
+        products_kernel,
+        (matrix, matrix, shape((2, BS // 2), F32)),
+        [],
+        (points0, hidden0, points1, hidden1, grad_pre, grad_y),
+        (),
+        2 * 10**9,
+    )
     total = call(
-        functools.partial(compose_kernel, q),
+        compose_kernel,
         shape((length, width), BF16),
-        scratch + [pltpu.VMEM((NB, rows, 2 * LANES), F32), sems],
-        backs,
-        far,
-    )
-    shifted = from_behind(total[None, None], "section", -1)
+        [by_pair],
+        (*backs, field, forward),
+        (),
+    )
+    shifted = from_next(total[None, None], "section")
     return shifted, gw1.swapaxes(1, 2)[None], gw2.swapaxes(1, 2)[None], gb1[None]
 
 

time: 35.9 us -> 36.2 us (level)
  the two profiles are of different devices: /device:TPU:0 before, /device:TPU:4 now
where the time goes in v7:
time: 36.2 us; the launch traced here: 36 us
  starting transfers between devices  13.6 us (38%)
  waiting for transfers between devices  13.3 us (37%)
  Pallas kernels  7.69 us (21%)
  between operations  0.72 us (2%)
  other arithmetic  0.68 us (2%)
    ppermute x6, starting transfers between devices, swap(): lax.ppermute(chunks[d], 'lat', pairs[d])  8.9 us
    ppermute x6, waiting for transfers between devices, swap(): lax.ppermute(chunks[d], 'lat', pairs[d])  8.71 us
    pallas_call x7, Pallas kernels, call(): pl.pallas_call(kernel, out_shape=outs, in_specs=[VMEM] * len(near) + [HBM...  7.69 us
    ppermute x1, waiting for transfers between devices, from_next(): even = lax.ppermute(value, axis, [(i, i - 1) for i in range(1, length, 2)])  4.38 us
    ppermute x1, starting transfers between devices, from_next(): odd = lax.ppermute(value, axis, [(i, i - 1) for i in range(2, length, 2)])  3.35 us
    ppermute x1, starting transfers between devices, from_next(): even = lax.ppermute(value, axis, [(i, i - 1) for i in range(1, length, 2)])  1.29 us
  transfers between devices with their start and end apart: 9, of which 6 were waited for; matrix products, arithmetic and copies ran while one was open for 0% of the time, Pallas kernels for 9%

profile of v7, /device:TPU:4, one launch (start us, length us, event | category | flops | bytes accessed | tf_op | source)
XLA Modules:
  0.0 36.0 jit_solution(4899189790740452646)
XLA Ops:
  0.6 1.7 %shard_map.138 = (bf16[72,384]{1,0:T(8,128)(2,1)S(1)}, bf16[72,384]{1,0:T(8,128)(2,1)S(1)}, bf16[72,384]{1,0:T(8,128)(2,1)S(1)}, bf16[72,384]{1,0:T(8,128)(2,1)S(1)}) custom-call(s32[8]{0:T(128)} %refs_0_.3, s32[8]{0:T(128)} %refs_11_.1, bf16[180,384]{1,0:T(8,128)(2,1)} %bitcast.17, bf16[144,180]{1,0:T(8,128)(2,1)} %constant.29.clone.refs_3_, ...), custom_call_target="tpu_custom_call" | custom-call | flops 100000000 | bytes 1000000 | tf_op jit(solution)/shard_map/pallas_call | solution.py:288
  2.3 1.6 %collective-permute-start = (bf16[72,384]{1,0:T(8,128)(2,1)S(1)}, bf16[72,384]{1,0:T(8,128)(2,1)S(1)}, u32[]{:S(2)}, u32[]{:S(2)}) collective-permute-start(bf16[72,384]{1,0:T(8,128)(2,1)S(1)} %get-tuple-element.30), channel_id=1, source_target_pairs={{0,2},{1,3},{2,0},{3,1},{4,6},{5,7},{6,4},{7,5},{8,10},{9,11},{10,... | collective-permute-start | bytes 165896 | tf_op jit(solution)/shard_map/ppermute | solution.py:330
  4.0 2.6 %collective-permute-start.1 = (bf16[72,384]{1,0:T(8,128)(2,1)S(1)}, bf16[72,384]{1,0:T(8,128)(2,1)S(1)}, u32[]{:S(2)}, u32[]{:S(2)}) collective-permute-start(bf16[72,384]{1,0:T(8,128)(2,1)S(1)} %get-tuple-element.31), channel_id=1, source_target_pairs={{0,4},{1,5},{2,6},{3,7},{4,0},{5,1},{6,2},{7,3},{8,12},{9,13},{10,... | collective-permute-start | bytes 165896 | tf_op jit(solution)/shard_map/ppermute | solution.py:330
  6.6 0.2 collective-permute-start.2
  6.8 3.3 %collective-permute-done.1.refs_2_ = bf16[72,384]{1,0:T(8,128)(2,1)S(1)} collective-permute-done((bf16[72,384]{1,0:T(8,128)(2,1)S(1)}, bf16[72,384]{1,0:T(8,128)(2,1)S(1)}, u32[]{:S(2)}, u32[]{:S(2)}) %collective-permute-start.1) | collective-permute-done | bytes 55328 | tf_op jit(solution)/shard_map/ppermute | solution.py:330
  10.1 2.4 %collective-permute-done.2.refs_3_ = bf16[72,384]{1,0:T(8,128)(2,1)S(1)} collective-permute-done((bf16[72,384]{1,0:T(8,128)(2,1)S(1)}, bf16[72,384]{1,0:T(8,128)(2,1)S(1)}, u32[]{:S(2)}, u32[]{:S(2)}) %collective-permute-start.2) | collective-permute-done | bytes 55328 | tf_op jit(solution)/shard_map/ppermute | solution.py:330
  12.5 0.1 collective-permute-start.3
  12.6 1.7 %shard_map.140 = (bf16[256,256]{1,0:T(8,128)(2,1)S(1)}, bf16[256,256]{1,0:T(8,128)(2,1)S(1)}, f32[1,256]{1,0:T(1,128)S(1)}, bf16[576,576]{1,0:T(8,128)(2,1)S(1)}...) custom-call(s32[8]{0:T(128)} %refs_0_.3, s32[8]{0:T(128)} %refs_11_.1, ...), custom_call_target="tpu_custom_call" | custom-call | flops 2000000000 | bytes 1000000 | tf_op jit(solution)/shard_map/pallas_call | solution.py:288
  14.3 0.4 shard_map.141
  14.6 0.0 collective-permute-done.3.refs_4_
  14.7 2.4 %shard_map.142 = (bf16[112,128]{1,0:T(8,128)(2,1)S(1)}, bf16[112,128]{1,0:T(8,128)(2,1)S(1)}, bf16[112,128]{1,0:T(8,128)(2,1)S(1)}, bf16[112,128]{1,0:T(8,128)(2...) custom-call(bf16[72,384]{1,0:T(8,128)(2,1)S(1)} %get-tuple-element.2, ...), custom_call_target="tpu_custom_call" | custom-call | flops 100000000 | bytes 1000000 | tf_op jit(solution)/shard_map/pallas_call | solution.py:288
  17.1 0.1 collective-permute-start.4
  17.2 1.7 %collective-permute-start.5 = (bf16[112,128]{1,0:T(8,128)(2,1)S(1)}, bf16[112,128]{1,0:T(8,128)(2,1)S(1)}, u32[]{:S(2)}, u32[]{:S(2)}) collective-permute-start(bf16[112,128]{1,0:T(8,128)(2,1)S(1)} %get-tuple-element.41), channel_id=1, source_target_pairs={{0,4},{1,5},{2,6},{3,7},{4,0},{5,1},{6,2},{7,3},{8,12},{9,13},{10,... | collective-permute-start | bytes 86024 | tf_op jit(solution)/shard_map/ppermute | solution.py:330
  18.8 2.7 %collective-permute-start.6 = (bf16[112,128]{1,0:T(8,128)(2,1)S(1)}, bf16[112,128]{1,0:T(8,128)(2,1)S(1)}, u32[]{:S(2)}, u32[]{:S(2)}) collective-permute-start(bf16[112,128]{1,0:T(8,128)(2,1)S(1)} %get-tuple-element.42), channel_id=1, source_target_pairs={{0,6},{1,7},{2,4},{3,5},{4,2},{5,3},{6,0},{7,1},{8,14},{9,15},{10,... | collective-permute-start | bytes 86024 | tf_op jit(solution)/shard_map/ppermute | solution.py:330
  21.5 0.0 collective-permute-done.4.refs_1_
  21.5 0.5 %collective-permute-done.5.refs_2_ = bf16[112,128]{1,0:T(8,128)(2,1)S(1)} collective-permute-done((bf16[112,128]{1,0:T(8,128)(2,1)S(1)}, bf16[112,128]{1,0:T(8,128)(2,1)S(1)}, u32[]{:S(2)}, u32[]{:S(2)}) %collective-permute-start.5) | collective-permute-done | bytes 28704 | tf_op jit(solution)/shard_map/ppermute | solution.py:330
  22.0 2.5 %collective-permute-done.6.refs_3_ = bf16[112,128]{1,0:T(8,128)(2,1)S(1)} collective-permute-done((bf16[112,128]{1,0:T(8,128)(2,1)S(1)}, bf16[112,128]{1,0:T(8,128)(2,1)S(1)}, u32[]{:S(2)}, u32[]{:S(2)}) %collective-permute-start.6) | collective-permute-done | bytes 28704 | tf_op jit(solution)/shard_map/ppermute | solution.py:330
  24.5 0.4 %shard_map.143 = bf16[180,384]{1,0:T(8,128)(2,1)S(1)} custom-call(bf16[112,128]{1,0:T(8,128)(2,1)S(1)} %get-tuple-element.39.refs_0_, bf16[112,128]{1,0:T(8,128)(2,1)S(1)} %collective-permute-done.4.refs_1_, bf16[112,128]{1,0:T(8,128)(2,1)S(1)} %collective-permute-done.5.refs_2_, bf16[112,128]{1,0:T(8,128)(2,1)S(1)} %collective-permute-done.6.refs_3_, ...), custom_call_target="tpu_custom_call" | custom-call | flops 100000000 | bytes 1000000 | tf_op jit(solution)/shard_map/pallas_call | solution.py:288
  25.0 3.3 %collective-permute-start.7 = (bf16[1,1,180,384]{3,2,1,0:T(8,128)(2,1)S(1)}, bf16[1,1,180,384]{3,2,1,0:T(8,128)(2,1)S(1)}, u32[]{:S(2)}, u32[]{:S(2)}) collective-permute-start(bf16[1,1,180,384]{3,2,1,0:T(8,128)(2,1)S(1)} %bitcast.13), channel_id=1, source_target_pairs={{16,8},{17,9},{18,10},{19,11},{20,12},{21,13},{22,14},{23,15}} | collective-permute-start | bytes 414728 | tf_op jit(solution)/shard_map/ppermute | solution.py:28
  28.3 1.3 %collective-permute-start.8 = (bf16[1,1,180,384]{3,2,1,0:T(8,128)(2,1)S(1)}, bf16[1,1,180,384]{3,2,1,0:T(8,128)(2,1)S(1)}, u32[]{:S(2)}, u32[]{:S(2)}) collective-permute-start(bf16[1,1,180,384]{3,2,1,0:T(8,128)(2,1)S(1)} %bitcast.14), channel_id=1, source_target_pairs={{8,0},{24,16},{9,1},{25,17},{10,2},{26,18},{11,3},{27,19},{12,4},{... | collective-permute-start | bytes 414728 | tf_op jit(solution)/shard_map/ppermute | solution.py:29
  29.6 1.1 %shard_map.144 = (f32[2,48,96]{2,1,0:T(8,128)}, f32[2,48,96]{2,1,0:T(8,128)}, f32[2,48]{1,0:T(2,128)}) custom-call(bf16[288,256]{1,0:T(8,128)(2,1)S(1)} %get-tuple-element.45.points0, bf16[288,256]{1,0:T(8,128)(2,1)S(1)} %get-tuple-element.46.hidden0, bf16[288,256]{1,0:T(8,128)(2,1)S(1)} %get-tuple-element.47.points1, ...), custom_call_target="tpu_custom_call" | custom-call | flops 2000000000 | bytes 1000000 | tf_op jit(solution)/shard_map/pallas_call | solution.py:288
  30.7 0.2 collective-permute-done.7
  30.9 4.4 %collective-permute-done.8 = bf16[1,1,180,384]{3,2,1,0:T(8,128)(2,1)S(1)} collective-permute-done((bf16[1,1,180,384]{3,2,1,0:T(8,128)(2,1)S(1)}, bf16[1,1,180,384]{3,2,1,0:T(8,128)(2,1)S(1)}, u32[]{:S(2)}, u32[]{:S(2)}) %collective-permute-start.8) | collective-permute-done | bytes 138272 | tf_op jit(solution)/shard_map/ppermute | solution.py:29
  35.3 0.7 %broadcast_select_fusion = bf16[1,1,180,384]{3,2,1,0:T(8,128)(2,1)} fusion(bf16[1,1,180,384]{3,2,1,0:T(8,128)(2,1)S(1)} %collective-permute-done.7, bf16[1,1,180,384]{3,2,1,0:T(8,128)(2,1)S(1)} %collective-permute-done.8, pred[]{:T(512)S(6)} %eq.5), kind=kLoop, calls=%fused_computation | loop fusion | flops 69120 | bytes 414721 | tf_op jit(solution)/shard_map/jit(_where)/select_n | solution.py:30
  (2 shorter events, 0.0 us)
Async XLA Ops:
  2.3 4.5 %collective-permute-start = (bf16[72,384]{1,0:T(8,128)(2,1)S(1)}, bf16[72,384]{1,0:T(8,128)(2,1)S(1)}, u32[]{:S(2)}, u32[]{:S(2)}) collective-permute-start(bf16[72,384]{1,0:T(8,128)(2,1)S(1)} %get-tuple-element.30), channel_id=1, source_target_pairs={{0,2},{1,3},{2,0},{3,1},{4,6},{5,7},{6,4},{7,5},{8,10},{9,11},{10,... | collective-permute-start | bytes 165896 | tf_op jit(solution)/shard_map/ppermute | solution.py:330
  4.0 6.1 %collective-permute-start.1 = (bf16[72,384]{1,0:T(8,128)(2,1)S(1)}, bf16[72,384]{1,0:T(8,128)(2,1)S(1)}, u32[]{:S(2)}, u32[]{:S(2)}) collective-permute-start(bf16[72,384]{1,0:T(8,128)(2,1)S(1)} %get-tuple-element.31), channel_id=1, source_target_pairs={{0,4},{1,5},{2,6},{3,7},{4,0},{5,1},{6,2},{7,3},{8,12},{9,13},{10,... | collective-permute-start | bytes 165896 | tf_op jit(solution)/shard_map/ppermute | solution.py:330
  6.6 6.0 %collective-permute-start.2 = (bf16[72,384]{1,0:T(8,128)(2,1)S(1)}, bf16[72,384]{1,0:T(8,128)(2,1)S(1)}, u32[]{:S(2)}, u32[]{:S(2)}) collective-permute-start(bf16[72,384]{1,0:T(8,128)(2,1)S(1)} %get-tuple-element.32), channel_id=1, source_target_pairs={{0,6},{1,7},{2,4},{3,5},{4,2},{5,3},{6,0},{7,1},{8,14},{9,15},{10,... | collective-permute-start | bytes 165896 | tf_op jit(solution)/shard_map/ppermute | solution.py:330
  12.5 2.1 %collective-permute-start.3 = (bf16[4,72,384]{2,1,0:T(8,128)(2,1)S(1)}, bf16[4,72,384]{2,1,0:T(8,128)(2,1)S(1)}, u32[]{:S(2)}, u32[]{:S(2)}) collective-permute-start(bf16[4,72,384]{2,1,0:T(8,128)(2,1)S(1)} %shard_map.139), channel_id=1, source_target_pairs={{0,1},{1,0},{2,3},{3,2},{4,5},{5,4},{6,7},{7,6},{8,9},{9,8},{10,11... | collective-permute-start | bytes 663560 | tf_op jit(solution)/shard_map/ppermute | solution.py:365
  17.1 4.5 %collective-permute-start.4 = (bf16[112,128]{1,0:T(8,128)(2,1)S(1)}, bf16[112,128]{1,0:T(8,128)(2,1)S(1)}, u32[]{:S(2)}, u32[]{:S(2)}) collective-permute-start(bf16[112,128]{1,0:T(8,128)(2,1)S(1)} %get-tuple-element.40), channel_id=1, source_target_pairs={{0,2},{1,3},{2,0},{3,1},{4,6},{5,7},{6,4},{7,5},{8,10},{9,11},{10,... | collective-permute-start | bytes 86024 | tf_op jit(solution)/shard_map/ppermute | solution.py:330
  17.2 4.9 %collective-permute-start.5 = (bf16[112,128]{1,0:T(8,128)(2,1)S(1)}, bf16[112,128]{1,0:T(8,128)(2,1)S(1)}, u32[]{:S(2)}, u32[]{:S(2)}) collective-permute-start(bf16[112,128]{1,0:T(8,128)(2,1)S(1)} %get-tuple-element.41), channel_id=1, source_target_pairs={{0,4},{1,5},{2,6},{3,7},{4,0},{5,1},{6,2},{7,3},{8,12},{9,13},{10,... | collective-permute-start | bytes 86024 | tf_op jit(solution)/shard_map/ppermute | solution.py:330
  18.8 5.7 %collective-permute-start.6 = (bf16[112,128]{1,0:T(8,128)(2,1)S(1)}, bf16[112,128]{1,0:T(8,128)(2,1)S(1)}, u32[]{:S(2)}, u32[]{:S(2)}) collective-permute-start(bf16[112,128]{1,0:T(8,128)(2,1)S(1)} %get-tuple-element.42), channel_id=1, source_target_pairs={{0,6},{1,7},{2,4},{3,5},{4,2},{5,3},{6,0},{7,1},{8,14},{9,15},{10,... | collective-permute-start | bytes 86024 | tf_op jit(solution)/shard_map/ppermute | solution.py:330
  25.0 5.9 %collective-permute-start.7 = (bf16[1,1,180,384]{3,2,1,0:T(8,128)(2,1)S(1)}, bf16[1,1,180,384]{3,2,1,0:T(8,128)(2,1)S(1)}, u32[]{:S(2)}, u32[]{:S(2)}) collective-permute-start(bf16[1,1,180,384]{3,2,1,0:T(8,128)(2,1)S(1)} %bitcast.13), channel_id=1, source_target_pairs={{16,8},{17,9},{18,10},{19,11},{20,12},{21,13},{22,14},{23,15}} | collective-permute-start | bytes 414728 | tf_op jit(solution)/shard_map/ppermute | solution.py:28
  28.3 7.0 %collective-permute-start.8 = (bf16[1,1,180,384]{3,2,1,0:T(8,128)(2,1)S(1)}, bf16[1,1,180,384]{3,2,1,0:T(8,128)(2,1)S(1)}, u32[]{:S(2)}, u32[]{:S(2)}) collective-permute-start(bf16[1,1,180,384]{3,2,1,0:T(8,128)(2,1)S(1)} %bitcast.14), channel_id=1, source_target_pairs={{8,0},{24,16},{9,1},{25,17},{10,2},{26,18},{11,3},{27,19},{12,4},{... | collective-permute-start | bytes 414728 | tf_op jit(solution)/shard_map/ppermute | solution.py:29

commit v8 on v7

--- a/solution.py
+++ b/solution.py
@@ -25,9 +25,8 @@
 
 def from_next(value, axis):
     length = lax.axis_size(axis)
-    odd = lax.ppermute(value, axis, [(i, i - 1) for i in range(2, length, 2)])
-    even = lax.ppermute(value, axis, [(i, i - 1) for i in range(1, length, 2)])
-    return jnp.where(lax.axis_index(axis) % 2 == 1, odd, even)
+    turned = lax.ppermute(value, axis, [(i, (i - 1) % length) for i in range(length)])
+    return jnp.where(lax.axis_index(axis) == length - 1, jnp.zeros_like(value), turned)
 
 
 def lon_tables(n_modes, length):
@@ -171,8 +170,8 @@
 
 
 def join_kernel(*refs):
-    out = refs[-1]
-    for d, ref in enumerate(refs[:-1]):
+    chunks, out = refs[:-2], refs[-1]
+    for d, ref in enumerate(chunks):
         out[d] = ref[...]
 
 
@@ -361,7 +360,7 @@
         far,
         2 * 10**9,
     )
-    own = call(join_kernel, shape((NB, rows, width), BF16), [], received, ())
+    own = call(join_kernel, shape((NB, rows, width), BF16), [], (*received, bias), ())
     other = lax.ppermute(own, "lat", [(i, i ^ 1) for i in range(2 * NB)])
     vectors = shape((NB * rows, wide), BF16)
     slopes = shape((NB * rows, wide), F32)

time: 36.2 us -> 31.8 us (0.88)
  the two profiles are of different devices: /device:TPU:4 before, /device:TPU:0 now
where the time goes in v8:
time: 31.8 us; the launch traced here: 31.6 us
  starting transfers between devices  12.7 us (40%)
  waiting for transfers between devices  9.88 us (31%)
  Pallas kernels  7.67 us (24%)
  between operations  0.7 us (2%)
  other arithmetic  0.68 us (2%)
    ppermute x6, starting transfers between devices, swap(): lax.ppermute(chunks[d], 'lat', pairs[d])  10.1 us
    pallas_call x7, Pallas kernels, call(): pl.pallas_call(kernel, out_shape=outs, in_specs=[VMEM] * len(near) + [HBM...  7.67 us
    ppermute x6, waiting for transfers between devices, swap(): lax.ppermute(chunks[d], 'lat', pairs[d])  7.27 us
    ppermute x1, starting transfers between devices, from_next(): lax.ppermute(value, axis, [(i, (i - 1) % length) for i in range(length)])  2.5 us
    ppermute x1, waiting for transfers between devices, from_next(): lax.ppermute(value, axis, [(i, (i - 1) % length) for i in range(length)])  1.52 us
    ppermute x1, waiting for transfers between devices, paired_blocks(): other = lax.ppermute(own, 'lat', [(i, i ^ 1) for i in range(2 * NB)])  1.1 us
    select_n x1, other arithmetic, from_next(): jnp.where(lax.axis_index(axis) == length - 1, jnp.zeros_like(value), turned)  0.68 us
  transfers between devices with their start and end apart: 8, of which 6 were waited for; matrix products, arithmetic and copies ran while one was open for 0% of the time, Pallas kernels for 10%

profile of v8, /device:TPU:0, one launch (start us, length us, event | category | flops | bytes accessed | tf_op | source)
XLA Modules:
  0.0 31.6 jit_solution(15160909385316039063)
XLA Ops:
  0.6 1.7 %shard_map.138 = (bf16[72,384]{1,0:T(8,128)(2,1)S(1)}, bf16[72,384]{1,0:T(8,128)(2,1)S(1)}, bf16[72,384]{1,0:T(8,128)(2,1)S(1)}, bf16[72,384]{1,0:T(8,128)(2,1)S(1)}) custom-call(s32[8]{0:T(128)} %refs_0_.3, s32[8]{0:T(128)} %refs_11_.1, bf16[180,384]{1,0:T(8,128)(2,1)} %bitcast.16, bf16[144,180]{1,0:T(8,128)(2,1)} %constant.19.clone.refs_3_, ...), custom_call_target="tpu_custom_call" | custom-call | flops 100000000 | bytes 1000000 | tf_op jit(solution)/shard_map/pallas_call | solution.py:287
  2.3 3.1 %collective-permute-start = (bf16[72,384]{1,0:T(8,128)(2,1)S(1)}, bf16[72,384]{1,0:T(8,128)(2,1)S(1)}, u32[]{:S(2)}, u32[]{:S(2)}) collective-permute-start(bf16[72,384]{1,0:T(8,128)(2,1)S(1)} %get-tuple-element.30), channel_id=1, source_target_pairs={{0,2},{1,3},{2,0},{3,1},{4,6},{5,7},{6,4},{7,5},{8,10},{9,11},{10,... | collective-permute-start | bytes 165896 | tf_op jit(solution)/shard_map/ppermute | solution.py:329
  5.4 2.6 %collective-permute-start.1 = (bf16[72,384]{1,0:T(8,128)(2,1)S(1)}, bf16[72,384]{1,0:T(8,128)(2,1)S(1)}, u32[]{:S(2)}, u32[]{:S(2)}) collective-permute-start(bf16[72,384]{1,0:T(8,128)(2,1)S(1)} %get-tuple-element.31), channel_id=1, source_target_pairs={{0,4},{1,5},{2,6},{3,7},{4,0},{5,1},{6,2},{7,3},{8,12},{9,13},{10,... | collective-permute-start | bytes 165896 | tf_op jit(solution)/shard_map/ppermute | solution.py:329
  8.0 0.0 collective-permute-start.2
  8.0 1.6 %shard_map.139 = (bf16[256,256]{1,0:T(8,128)(2,1)S(1)}, bf16[256,256]{1,0:T(8,128)(2,1)S(1)}, f32[1,256]{1,0:T(1,128)S(1)}, bf16[576,576]{1,0:T(8,128)(2,1)S(1)}...) custom-call(s32[8]{0:T(128)} %refs_0_.3, s32[8]{0:T(128)} %refs_11_.1, ...), custom_call_target="tpu_custom_call" | custom-call | flops 2000000000 | bytes 1000000 | tf_op jit(solution)/shard_map/pallas_call | solution.py:287
  9.7 0.0 collective-permute-done.refs_1_
  9.7 1.9 %collective-permute-done.1.refs_2_ = bf16[72,384]{1,0:T(8,128)(2,1)S(1)} collective-permute-done((bf16[72,384]{1,0:T(8,128)(2,1)S(1)}, bf16[72,384]{1,0:T(8,128)(2,1)S(1)}, u32[]{:S(2)}, u32[]{:S(2)}) %collective-permute-start.1) | collective-permute-done | bytes 55328 | tf_op jit(solution)/shard_map/ppermute | solution.py:329
  11.5 2.4 %collective-permute-done.2.refs_3_ = bf16[72,384]{1,0:T(8,128)(2,1)S(1)} collective-permute-done((bf16[72,384]{1,0:T(8,128)(2,1)S(1)}, bf16[72,384]{1,0:T(8,128)(2,1)S(1)}, u32[]{:S(2)}, u32[]{:S(2)}) %collective-permute-start.2) | collective-permute-done | bytes 55328 | tf_op jit(solution)/shard_map/ppermute | solution.py:329
  14.0 0.1 collective-permute-start.3
  14.1 0.4 %shard_map.141 = (bf16[288,256]{1,0:T(8,128)(2,1)S(1)}, bf16[288,256]{1,0:T(8,128)(2,1)S(1)}, f32[288,256]{1,0:T(8,128)S(1)}) custom-call(bf16[72,384]{1,0:T(8,128)(2,1)S(1)} %get-tuple-element.29.refs_0_, bf16[72,384]{1,0:T(8,128)(2,1)S(1)} %collective-permute-done.refs_1_, bf16[72,384]{1,0:T(8,128)(2,1)S(1)} %collective-permute-done.1.refs_2_, ...), custom_call_target="tpu_custom_call" | custom-call | flops 2000000000 | bytes 1000000 | tf_op jit(solution)/shard_map/pallas_call | solution.py:287
  14.4 1.1 %collective-permute-done.3.refs_4_ = bf16[4,72,384]{2,1,0:T(8,128)(2,1)S(1)} collective-permute-done((bf16[4,72,384]{2,1,0:T(8,128)(2,1)S(1)}, bf16[4,72,384]{2,1,0:T(8,128)(2,1)S(1)}, u32[]{:S(2)}, u32[]{:S(2)}) %collective-permute-start.3) | collective-permute-done | bytes 221216 | tf_op jit(solution)/shard_map/ppermute | solution.py:364
  15.5 2.4 %shard_map.142 = (bf16[112,128]{1,0:T(8,128)(2,1)S(1)}, bf16[112,128]{1,0:T(8,128)(2,1)S(1)}, bf16[112,128]{1,0:T(8,128)(2,1)S(1)}, bf16[112,128]{1,0:T(8,128)(2...) custom-call(bf16[72,384]{1,0:T(8,128)(2,1)S(1)} %get-tuple-element.2, ...), custom_call_target="tpu_custom_call" | custom-call | flops 100000000 | bytes 1000000 | tf_op jit(solution)/shard_map/pallas_call | solution.py:287
  18.0 0.1 collective-permute-start.4
  18.0 1.7 %collective-permute-start.5 = (bf16[112,128]{1,0:T(8,128)(2,1)S(1)}, bf16[112,128]{1,0:T(8,128)(2,1)S(1)}, u32[]{:S(2)}, u32[]{:S(2)}) collective-permute-start(bf16[112,128]{1,0:T(8,128)(2,1)S(1)} %get-tuple-element.41), channel_id=1, source_target_pairs={{0,4},{1,5},{2,6},{3,7},{4,0},{5,1},{6,2},{7,3},{8,12},{9,13},{10,... | collective-permute-start | bytes 86024 | tf_op jit(solution)/shard_map/ppermute | solution.py:329
  19.7 2.7 %collective-permute-start.6 = (bf16[112,128]{1,0:T(8,128)(2,1)S(1)}, bf16[112,128]{1,0:T(8,128)(2,1)S(1)}, u32[]{:S(2)}, u32[]{:S(2)}) collective-permute-start(bf16[112,128]{1,0:T(8,128)(2,1)S(1)} %get-tuple-element.42), channel_id=1, source_target_pairs={{0,6},{1,7},{2,4},{3,5},{4,2},{5,3},{6,0},{7,1},{8,14},{9,15},{10,... | collective-permute-start | bytes 86024 | tf_op jit(solution)/shard_map/ppermute | solution.py:329
  22.4 0.0 collective-permute-done.4.refs_1_
  22.4 1.0 %collective-permute-done.5.refs_2_ = bf16[112,128]{1,0:T(8,128)(2,1)S(1)} collective-permute-done((bf16[112,128]{1,0:T(8,128)(2,1)S(1)}, bf16[112,128]{1,0:T(8,128)(2,1)S(1)}, u32[]{:S(2)}, u32[]{:S(2)}) %collective-permute-start.5) | collective-permute-done | bytes 28704 | tf_op jit(solution)/shard_map/ppermute | solution.py:329
  23.4 2.0 %collective-permute-done.6.refs_3_ = bf16[112,128]{1,0:T(8,128)(2,1)S(1)} collective-permute-done((bf16[112,128]{1,0:T(8,128)(2,1)S(1)}, bf16[112,128]{1,0:T(8,128)(2,1)S(1)}, u32[]{:S(2)}, u32[]{:S(2)}) %collective-permute-start.6) | collective-permute-done | bytes 28704 | tf_op jit(solution)/shard_map/ppermute | solution.py:329
  25.4 0.4 %shard_map.143 = bf16[180,384]{1,0:T(8,128)(2,1)S(1)} custom-call(bf16[112,128]{1,0:T(8,128)(2,1)S(1)} %get-tuple-element.39.refs_0_, bf16[112,128]{1,0:T(8,128)(2,1)S(1)} %collective-permute-done.4.refs_1_, bf16[112,128]{1,0:T(8,128)(2,1)S(1)} %collective-permute-done.5.refs_2_, bf16[112,128]{1,0:T(8,128)(2,1)S(1)} %collective-permute-done.6.refs_3_, ...), custom_call_target="tpu_custom_call" | custom-call | flops 100000000 | bytes 1000000 | tf_op jit(solution)/shard_map/pallas_call | solution.py:287
  25.8 2.5 %collective-permute-start.7 = (bf16[1,1,180,384]{3,2,1,0:T(8,128)(2,1)S(1)}, bf16[1,1,180,384]{3,2,1,0:T(8,128)(2,1)S(1)}, u32[]{:S(2)}, u32[]{:S(2)}) collective-permute-start(bf16[1,1,180,384]{3,2,1,0:T(8,128)(2,1)S(1)} %bitcast.13), channel_id=1, source_target_pairs={{0,24},{8,0},{16,8},{24,16},{1,25},{9,1},{17,9},{25,17},{2,26},{10... | collective-permute-start | bytes 414728 | tf_op jit(solution)/shard_map/ppermute | solution.py:28
  28.3 1.1 %shard_map.144 = (f32[2,48,96]{2,1,0:T(8,128)}, f32[2,48,96]{2,1,0:T(8,128)}, f32[2,48]{1,0:T(2,128)}) custom-call(bf16[288,256]{1,0:T(8,128)(2,1)S(1)} %get-tuple-element.45.points0, bf16[288,256]{1,0:T(8,128)(2,1)S(1)} %get-tuple-element.46.hidden0, bf16[288,256]{1,0:T(8,128)(2,1)S(1)} %get-tuple-element.47.points1, ...), custom_call_target="tpu_custom_call" | custom-call | flops 2000000000 | bytes 1000000 | tf_op jit(solution)/shard_map/pallas_call | solution.py:287
  29.4 1.5 %collective-permute-done.7 = bf16[1,1,180,384]{3,2,1,0:T(8,128)(2,1)S(1)} collective-permute-done((bf16[1,1,180,384]{3,2,1,0:T(8,128)(2,1)S(1)}, bf16[1,1,180,384]{3,2,1,0:T(8,128)(2,1)S(1)}, u32[]{:S(2)}, u32[]{:S(2)}) %collective-permute-start.7) | collective-permute-done | bytes 138272 | tf_op jit(solution)/shard_map/ppermute | solution.py:28
  31.0 0.7 %broadcast_select_fusion = bf16[1,1,180,384]{3,2,1,0:T(8,128)(2,1)} fusion(bf16[1,1,180,384]{3,2,1,0:T(8,128)(2,1)S(1)} %collective-permute-done.7, pred[]{:T(512)S(6)} %eq.3), kind=kLoop, calls=%fused_computation | loop fusion | flops 69120 | bytes 276481 | tf_op jit(solution)/shard_map/jit(_where)/select_n | solution.py:29
  (1 shorter events, 0.0 us)
Async XLA Ops:
  2.3 7.3 %collective-permute-start = (bf16[72,384]{1,0:T(8,128)(2,1)S(1)}, bf16[72,384]{1,0:T(8,128)(2,1)S(1)}, u32[]{:S(2)}, u32[]{:S(2)}) collective-permute-start(bf16[72,384]{1,0:T(8,128)(2,1)S(1)} %get-tuple-element.30), channel_id=1, source_target_pairs={{0,2},{1,3},{2,0},{3,1},{4,6},{5,7},{6,4},{7,5},{8,10},{9,11},{10,... | collective-permute-start | bytes 165896 | tf_op jit(solution)/shard_map/ppermute | solution.py:329
  5.4 6.1 %collective-permute-start.1 = (bf16[72,384]{1,0:T(8,128)(2,1)S(1)}, bf16[72,384]{1,0:T(8,128)(2,1)S(1)}, u32[]{:S(2)}, u32[]{:S(2)}) collective-permute-start(bf16[72,384]{1,0:T(8,128)(2,1)S(1)} %get-tuple-element.31), channel_id=1, source_target_pairs={{0,4},{1,5},{2,6},{3,7},{4,0},{5,1},{6,2},{7,3},{8,12},{9,13},{10,... | collective-permute-start | bytes 165896 | tf_op jit(solution)/shard_map/ppermute | solution.py:329
  8.0 6.0 %collective-permute-start.2 = (bf16[72,384]{1,0:T(8,128)(2,1)S(1)}, bf16[72,384]{1,0:T(8,128)(2,1)S(1)}, u32[]{:S(2)}, u32[]{:S(2)}) collective-permute-start(bf16[72,384]{1,0:T(8,128)(2,1)S(1)} %get-tuple-element.32), channel_id=1, source_target_pairs={{0,6},{1,7},{2,4},{3,5},{4,2},{5,3},{6,0},{7,1},{8,14},{9,15},{10,... | collective-permute-start | bytes 165896 | tf_op jit(solution)/shard_map/ppermute | solution.py:329
  14.0 1.5 %collective-permute-start.3 = (bf16[4,72,384]{2,1,0:T(8,128)(2,1)S(1)}, bf16[4,72,384]{2,1,0:T(8,128)(2,1)S(1)}, u32[]{:S(2)}, u32[]{:S(2)}) collective-permute-start(bf16[4,72,384]{2,1,0:T(8,128)(2,1)S(1)} %shard_map.140), channel_id=1, source_target_pairs={{0,1},{1,0},{2,3},{3,2},{4,5},{5,4},{6,7},{7,6},{8,9},{9,8},{10,11... | collective-permute-start | bytes 663560 | tf_op jit(solution)/shard_map/ppermute | solution.py:364
  18.0 4.5 %collective-permute-start.4 = (bf16[112,128]{1,0:T(8,128)(2,1)S(1)}, bf16[112,128]{1,0:T(8,128)(2,1)S(1)}, u32[]{:S(2)}, u32[]{:S(2)}) collective-permute-start(bf16[112,128]{1,0:T(8,128)(2,1)S(1)} %get-tuple-element.40), channel_id=1, source_target_pairs={{0,2},{1,3},{2,0},{3,1},{4,6},{5,7},{6,4},{7,5},{8,10},{9,11},{10,... | collective-permute-start | bytes 86024 | tf_op jit(solution)/shard_map/ppermute | solution.py:329
  18.0 5.4 %collective-permute-start.5 = (bf16[112,128]{1,0:T(8,128)(2,1)S(1)}, bf16[112,128]{1,0:T(8,128)(2,1)S(1)}, u32[]{:S(2)}, u32[]{:S(2)}) collective-permute-start(bf16[112,128]{1,0:T(8,128)(2,1)S(1)} %get-tuple-element.41), channel_id=1, source_target_pairs={{0,4},{1,5},{2,6},{3,7},{4,0},{5,1},{6,2},{7,3},{8,12},{9,13},{10,... | collective-permute-start | bytes 86024 | tf_op jit(solution)/shard_map/ppermute | solution.py:329
  19.7 5.7 %collective-permute-start.6 = (bf16[112,128]{1,0:T(8,128)(2,1)S(1)}, bf16[112,128]{1,0:T(8,128)(2,1)S(1)}, u32[]{:S(2)}, u32[]{:S(2)}) collective-permute-start(bf16[112,128]{1,0:T(8,128)(2,1)S(1)} %get-tuple-element.42), channel_id=1, source_target_pairs={{0,6},{1,7},{2,4},{3,5},{4,2},{5,3},{6,0},{7,1},{8,14},{9,15},{10,... | collective-permute-start | bytes 86024 | tf_op jit(solution)/shard_map/ppermute | solution.py:329
  25.8 5.1 %collective-permute-start.7 = (bf16[1,1,180,384]{3,2,1,0:T(8,128)(2,1)S(1)}, bf16[1,1,180,384]{3,2,1,0:T(8,128)(2,1)S(1)}, u32[]{:S(2)}, u32[]{:S(2)}) collective-permute-start(bf16[1,1,180,384]{3,2,1,0:T(8,128)(2,1)S(1)} %bitcast.13), channel_id=1, source_target_pairs={{0,24},{8,0},{16,8},{24,16},{1,25},{9,1},{17,9},{25,17},{2,26},{10... | collective-permute-start | bytes 414728 | tf_op jit(solution)/shard_map/ppermute | solution.py:28

commit v9 on v7

--- a/solution.py
+++ b/solution.py
@@ -23,11 +23,9 @@
     return lax.ppermute(value, axis, pairs)
 
 
-def from_next(value, axis):
+def turn(value, axis):
     length = lax.axis_size(axis)
-    odd = lax.ppermute(value, axis, [(i, i - 1) for i in range(2, length, 2)])
-    even = lax.ppermute(value, axis, [(i, i - 1) for i in range(1, length, 2)])
-    return jnp.where(lax.axis_index(axis) % 2 == 1, odd, even)
+    return lax.ppermute(value, axis, [(i, (i - 1) % length) for i in range(length)])
 
 
 def lon_tables(n_modes, length):
@@ -170,9 +168,9 @@
     wait(copies[6:])
 
 
-def join_kernel(*refs):
+def join_kernel(count, *refs):
     out = refs[-1]
-    for d, ref in enumerate(refs[:-1]):
+    for d, ref in enumerate(refs[:count]):
         out[d] = ref[...]
 
 
@@ -265,17 +263,17 @@
         gb1[c : c + 1] = jnp.where(core == 0, line[:, :half], line[:, half:BS])
 
 
-def compose_kernel(*refs):
-    backs, (field, table, out, by_block) = refs[:4], refs[4:]
+def compose_kernel(last, three, one, field, table, out, by_block):
     rows = by_block.shape[1]
-    for d, back in enumerate(backs):
-        by_block[partner(d)] = jnp.concatenate(unpack(back[...].astype(F32), rows), axis=1)
+    for d, back in ((0, three[0]), (1, one[...]), (2, three[1]), (3, three[2])):
+        by_block[partner(d)] = jnp.concatenate(unpack(back.astype(F32), rows), axis=1)
     groups = [
         dense([by_block[n, :, g * LANES : (g + 1) * LANES] for n in range(NB)]) for g in range(2)
     ]
     groups = jnp.concatenate(groups, axis=0).astype(BF16)
     mixed = jnp.dot(table[...], groups, preferred_element_type=F32).astype(BF16)
-    out[...] = (field[...].astype(F32) + mixed.astype(F32)).astype(BF16)
+    whole = field[...].astype(F32) + mixed.astype(F32)
+    out[...] = jnp.where(lax.axis_index("section") == last, 0.0, whole).astype(BF16)
 
 
 VMEM = pl.BlockSpec(memory_space=pltpu.VMEM)
@@ -361,7 +359,14 @@
         far,
         2 * 10**9,
     )
-    own = call(join_kernel, shape((NB, rows, width), BF16), [], received, ())
+    next_field = turn(field, "section")
+    own = call(
+        functools.partial(join_kernel, NB),
+        shape((NB, rows, width), BF16),
+        [],
+        (*received, bias),
+        (),
+    )
     other = lax.ppermute(own, "lat", [(i, i ^ 1) for i in range(2 * NB)])
     vectors = shape((NB * rows, wide), BF16)
     slopes = shape((NB * rows, wide), F32)
@@ -400,14 +405,23 @@
         (),
         2 * 10**9,
     )
-    total = call(
-        compose_kernel,
+    three = call(
+        functools.partial(join_kernel, 3),
+        shape((3, *packed.shape), BF16),
+        [],
+        (backs[0], backs[2], backs[3]),
+        (),
+    )
+    three = turn(three, "section")
+    one = turn(backs[1], "section")
+    shifted = call(
+        functools.partial(compose_kernel, lax.axis_size("section") - 1),
         shape((length, width), BF16),
         [by_pair],
-        (*backs, field, forward),
-        (),
-    )
-    shifted = from_next(total[None, None], "section")
+        (three, one, next_field, forward),
+        (),
+    )
+    shifted = shifted[None, None]
     return shifted, gw1.swapaxes(1, 2)[None], gw2.swapaxes(1, 2)[None], gb1[None]
 
 

time: 36.2 us -> 32.2 us (0.89)
  the two profiles are of different devices: /device:TPU:4 before, /device:TPU:0 now
where the time goes in v9:
time: 32.2 us; the launch traced here: 32 us
  starting transfers between devices  14.8 us (46%)
  Pallas kernels  8.34 us (26%)
  waiting for transfers between devices  8.16 us (25%)
  between operations  0.69 us (2%)
    ppermute x6, starting transfers between devices, swap(): lax.ppermute(chunks[d], 'lat', pairs[d])  9.24 us
    pallas_call x8, Pallas kernels, call(): pl.pallas_call(kernel, out_shape=outs, in_specs=[VMEM] * len(near) + [HBM...  8.34 us
    ppermute x3, starting transfers between devices, turn(): lax.ppermute(value, axis, [(i, (i - 1) % length) for i in range(length)])  5.47 us
    ppermute x6, waiting for transfers between devices, swap(): lax.ppermute(chunks[d], 'lat', pairs[d])  4.85 us
    ppermute x3, waiting for transfers between devices, turn(): lax.ppermute(value, axis, [(i, (i - 1) % length) for i in range(length)])  2.22 us
    ppermute x1, waiting for transfers between devices, paired_blocks(): other = lax.ppermute(own, 'lat', [(i, i ^ 1) for i in range(2 * NB)])  1.1 us
  transfers between devices with their start and end apart: 10, of which 5 were waited for; matrix products, arithmetic and copies ran while one was open for 0% of the time, Pallas kernels for 10%

profile of v9, /device:TPU:0, one launch (start us, length us, event | category | flops | bytes accessed | tf_op | source)
XLA Modules:
  0.0 32.0 jit_solution(5648977830392548900)
XLA Ops:
  0.6 1.7 %shard_map.138 = (bf16[72,384]{1,0:T(8,128)(2,1)S(1)}, bf16[72,384]{1,0:T(8,128)(2,1)S(1)}, bf16[72,384]{1,0:T(8,128)(2,1)S(1)}, bf16[72,384]{1,0:T(8,128)(2,1)S(1)}) custom-call(s32[8]{0:T(128)} %refs_0_.3, s32[8]{0:T(128)} %refs_11_.1, bf16[180,384]{1,0:T(8,128)(2,1)} %bitcast.16, bf16[144,180]{1,0:T(8,128)(2,1)} %constant.10.clone.refs_3_, ...), custom_call_target="tpu_custom_call" | custom-call | flops 100000000 | bytes 1000000 | tf_op jit(solution)/shard_map/pallas_call | solution.py:286
  2.3 3.1 %collective-permute-start = (bf16[72,384]{1,0:T(8,128)(2,1)S(1)}, bf16[72,384]{1,0:T(8,128)(2,1)S(1)}, u32[]{:S(2)}, u32[]{:S(2)}) collective-permute-start(bf16[72,384]{1,0:T(8,128)(2,1)S(1)} %get-tuple-element.30), channel_id=1, source_target_pairs={{0,2},{1,3},{2,0},{3,1},{4,6},{5,7},{6,4},{7,5},{8,10},{9,11},{10,... | collective-permute-start | bytes 165896 | tf_op jit(solution)/shard_map/ppermute | solution.py:328
  5.4 2.6 %collective-permute-start.1 = (bf16[72,384]{1,0:T(8,128)(2,1)S(1)}, bf16[72,384]{1,0:T(8,128)(2,1)S(1)}, u32[]{:S(2)}, u32[]{:S(2)}) collective-permute-start(bf16[72,384]{1,0:T(8,128)(2,1)S(1)} %get-tuple-element.31), channel_id=1, source_target_pairs={{0,4},{1,5},{2,6},{3,7},{4,0},{5,1},{6,2},{7,3},{8,12},{9,13},{10,... | collective-permute-start | bytes 165896 | tf_op jit(solution)/shard_map/ppermute | solution.py:328
  8.0 0.0 collective-permute-start.2
  8.0 1.6 %shard_map.139 = (bf16[256,256]{1,0:T(8,128)(2,1)S(1)}, bf16[256,256]{1,0:T(8,128)(2,1)S(1)}, f32[1,256]{1,0:T(1,128)S(1)}, bf16[576,576]{1,0:T(8,128)(2,1)S(1)}...) custom-call(s32[8]{0:T(128)} %refs_0_.3, s32[8]{0:T(128)} %refs_11_.1, ...), custom_call_target="tpu_custom_call" | custom-call | flops 2000000000 | bytes 1000000 | tf_op jit(solution)/shard_map/pallas_call | solution.py:286
  9.7 0.0 collective-permute-done.refs_1_
  9.7 1.9 %collective-permute-done.1.refs_2_ = bf16[72,384]{1,0:T(8,128)(2,1)S(1)} collective-permute-done((bf16[72,384]{1,0:T(8,128)(2,1)S(1)}, bf16[72,384]{1,0:T(8,128)(2,1)S(1)}, u32[]{:S(2)}, u32[]{:S(2)}) %collective-permute-start.1) | collective-permute-done | bytes 55328 | tf_op jit(solution)/shard_map/ppermute | solution.py:328
  11.5 2.4 %collective-permute-done.2.refs_3_ = bf16[72,384]{1,0:T(8,128)(2,1)S(1)} collective-permute-done((bf16[72,384]{1,0:T(8,128)(2,1)S(1)}, bf16[72,384]{1,0:T(8,128)(2,1)S(1)}, u32[]{:S(2)}, u32[]{:S(2)}) %collective-permute-start.2) | collective-permute-done | bytes 55328 | tf_op jit(solution)/shard_map/ppermute | solution.py:328
  14.0 0.1 collective-permute-start.3
  14.1 0.4 %shard_map.141 = (bf16[288,256]{1,0:T(8,128)(2,1)S(1)}, bf16[288,256]{1,0:T(8,128)(2,1)S(1)}, f32[288,256]{1,0:T(8,128)S(1)}) custom-call(bf16[72,384]{1,0:T(8,128)(2,1)S(1)} %get-tuple-element.29.refs_0_, bf16[72,384]{1,0:T(8,128)(2,1)S(1)} %collective-permute-done.refs_1_, bf16[72,384]{1,0:T(8,128)(2,1)S(1)} %collective-permute-done.1.refs_2_, ...), custom_call_target="tpu_custom_call" | custom-call | flops 2000000000 | bytes 1000000 | tf_op jit(solution)/shard_map/pallas_call | solution.py:286
  14.4 1.1 %collective-permute-done.3.refs_4_ = bf16[4,72,384]{2,1,0:T(8,128)(2,1)S(1)} collective-permute-done((bf16[4,72,384]{2,1,0:T(8,128)(2,1)S(1)}, bf16[4,72,384]{2,1,0:T(8,128)(2,1)S(1)}, u32[]{:S(2)}, u32[]{:S(2)}) %collective-permute-start.3) | collective-permute-done | bytes 221216 | tf_op jit(solution)/shard_map/ppermute | solution.py:370
  15.5 2.4 %shard_map.142 = (bf16[112,128]{1,0:T(8,128)(2,1)S(1)}, bf16[112,128]{1,0:T(8,128)(2,1)S(1)}, bf16[112,128]{1,0:T(8,128)(2,1)S(1)}, bf16[112,128]{1,0:T(8,128)(2...) custom-call(bf16[72,384]{1,0:T(8,128)(2,1)S(1)} %get-tuple-element.2, ...), custom_call_target="tpu_custom_call" | custom-call | flops 100000000 | bytes 1000000 | tf_op jit(solution)/shard_map/pallas_call | solution.py:286
  18.0 0.9 %collective-permute-start.4 = (bf16[112,128]{1,0:T(8,128)(2,1)S(1)}, bf16[112,128]{1,0:T(8,128)(2,1)S(1)}, u32[]{:S(2)}, u32[]{:S(2)}) collective-permute-start(bf16[112,128]{1,0:T(8,128)(2,1)S(1)} %get-tuple-element.40), channel_id=1, source_target_pairs={{0,4},{1,5},{2,6},{3,7},{4,0},{5,1},{6,2},{7,3},{8,12},{9,13},{10,... | collective-permute-start | bytes 86024 | tf_op jit(solution)/shard_map/ppermute | solution.py:328
  18.8 0.9 %collective-permute-start.5 = (bf16[112,128]{1,0:T(8,128)(2,1)S(1)}, bf16[112,128]{1,0:T(8,128)(2,1)S(1)}, u32[]{:S(2)}, u32[]{:S(2)}) collective-permute-start(bf16[112,128]{1,0:T(8,128)(2,1)S(1)} %get-tuple-element.41), channel_id=1, source_target_pairs={{0,6},{1,7},{2,4},{3,5},{4,2},{5,3},{6,0},{7,1},{8,14},{9,15},{10,... | collective-permute-start | bytes 86024 | tf_op jit(solution)/shard_map/ppermute | solution.py:328
  19.7 1.8 %collective-permute-start.7 = (bf16[112,128]{1,0:T(8,128)(2,1)S(1)}, bf16[112,128]{1,0:T(8,128)(2,1)S(1)}, u32[]{:S(2)}, u32[]{:S(2)}) collective-permute-start(bf16[112,128]{1,0:T(8,128)(2,1)S(1)} %get-tuple-element.42), channel_id=1, source_target_pairs={{0,2},{1,3},{2,0},{3,1},{4,6},{5,7},{6,4},{7,5},{8,10},{9,11},{10,... | collective-permute-start | bytes 86024 | tf_op jit(solution)/shard_map/ppermute | solution.py:328
  21.5 2.4 %collective-permute-start.9 = (bf16[180,384]{1,0:T(8,128)(2,1)S(1)}, bf16[180,384]{1,0:T(8,128)(2,1)S(1)}, u32[]{:S(2)}, u32[]{:S(2)}) collective-permute-start(bf16[180,384]{1,0:T(8,128)(2,1)S(1)} %get-tuple-element.43), channel_id=1, source_target_pairs={{0,24},{8,0},{16,8},{24,16},{1,25},{9,1},{17,9},{25,17},{2,26},{10... | collective-permute-start | bytes 414728 | tf_op jit(solution)/shard_map/ppermute | solution.py:28
  24.0 0.5 %collective-permute-done.5.refs_2_ = bf16[112,128]{1,0:T(8,128)(2,1)S(1)} collective-permute-done((bf16[112,128]{1,0:T(8,128)(2,1)S(1)}, bf16[112,128]{1,0:T(8,128)(2,1)S(1)}, u32[]{:S(2)}, u32[]{:S(2)}) %collective-permute-start.5) | collective-permute-done | bytes 28704 | tf_op jit(solution)/shard_map/ppermute | solution.py:328
  24.5 2.5 %collective-permute-start.6 = (bf16[3,112,128]{2,1,0:T(8,128)(2,1)S(1)}, bf16[3,112,128]{2,1,0:T(8,128)(2,1)S(1)}, u32[]{:S(2)}, u32[]{:S(2)}) collective-permute-start(bf16[3,112,128]{2,1,0:T(8,128)(2,1)S(1)} %shard_map.143), channel_id=1, source_target_pairs={{0,24},{8,0},{16,8},{24,16},{1,25},{9,1},{17,9},{25,17},{2,26},{10... | collective-permute-start | bytes 258056 | tf_op jit(solution)/shard_map/ppermute | solution.py:28
  27.0 0.0 collective-permute-done.7
  27.0 0.5 %collective-permute-start.8 = (bf16[112,128]{1,0:T(8,128)(2,1)S(1)}, bf16[112,128]{1,0:T(8,128)(2,1)S(1)}, u32[]{:S(2)}, u32[]{:S(2)}) collective-permute-start(bf16[112,128]{1,0:T(8,128)(2,1)S(1)} %collective-permute-done.7), channel_id=1, source_target_pairs={{0,24},{8,0},{16,8},{24,16},{1,25},{9,1},{17,9},{25,17},{2,26},{10... | collective-permute-start | bytes 86024 | tf_op jit(solution)/shard_map/ppermute | solution.py:28
  27.5 1.1 %shard_map.145 = (f32[2,48,96]{2,1,0:T(8,128)}, f32[2,48,96]{2,1,0:T(8,128)}, f32[2,48]{1,0:T(2,128)}) custom-call(bf16[288,256]{1,0:T(8,128)(2,1)S(1)} %get-tuple-element.45.points0, bf16[288,256]{1,0:T(8,128)(2,1)S(1)} %get-tuple-element.46.hidden0, bf16[288,256]{1,0:T(8,128)(2,1)S(1)} %get-tuple-element.47.points1, ...), custom_call_target="tpu_custom_call" | custom-call | flops 2000000000 | bytes 1000000 | tf_op jit(solution)/shard_map/pallas_call | solution.py:286
  28.7 0.0 collective-permute-done.9.field
  28.7 2.2 %collective-permute-done.8.one = bf16[112,128]{1,0:T(8,128)(2,1)S(1)} collective-permute-done((bf16[112,128]{1,0:T(8,128)(2,1)S(1)}, bf16[112,128]{1,0:T(8,128)(2,1)S(1)}, u32[]{:S(2)}, u32[]{:S(2)}) %collective-permute-start.8) | collective-permute-done | bytes 28704 | tf_op jit(solution)/shard_map/ppermute | solution.py:28
  30.9 1.1 %shard_map.144 = bf16[180,384]{1,0:T(8,128)(2,1)} custom-call(bf16[3,112,128]{2,1,0:T(8,128)(2,1)S(1)} %collective-permute-done.6.three, bf16[112,128]{1,0:T(8,128)(2,1)S(1)} %collective-permute-done.8.one, bf16[180,384]{1,0:T(8,128)(2,1)S(1)} %collective-permute-done.9.field, bf16[180,144]{1,0:T(8,128)(2,1)S(1)} %get-tuple-element.44.table), custom_call_target="tpu_custom_call" | custom-call | flops 100000000 | bytes 1000000 | tf_op jit(solution)/shard_map/pallas_call | solution.py:286
  (4 shorter events, 0.0 us)
Async XLA Ops:
  2.3 7.3 %collective-permute-start = (bf16[72,384]{1,0:T(8,128)(2,1)S(1)}, bf16[72,384]{1,0:T(8,128)(2,1)S(1)}, u32[]{:S(2)}, u32[]{:S(2)}) collective-permute-start(bf16[72,384]{1,0:T(8,128)(2,1)S(1)} %get-tuple-element.30), channel_id=1, source_target_pairs={{0,2},{1,3},{2,0},{3,1},{4,6},{5,7},{6,4},{7,5},{8,10},{9,11},{10,... | collective-permute-start | bytes 165896 | tf_op jit(solution)/shard_map/ppermute | solution.py:328
  5.4 6.1 %collective-permute-start.1 = (bf16[72,384]{1,0:T(8,128)(2,1)S(1)}, bf16[72,384]{1,0:T(8,128)(2,1)S(1)}, u32[]{:S(2)}, u32[]{:S(2)}) collective-permute-start(bf16[72,384]{1,0:T(8,128)(2,1)S(1)} %get-tuple-element.31), channel_id=1, source_target_pairs={{0,4},{1,5},{2,6},{3,7},{4,0},{5,1},{6,2},{7,3},{8,12},{9,13},{10,... | collective-permute-start | bytes 165896 | tf_op jit(solution)/shard_map/ppermute | solution.py:328
  8.0 6.0 %collective-permute-start.2 = (bf16[72,384]{1,0:T(8,128)(2,1)S(1)}, bf16[72,384]{1,0:T(8,128)(2,1)S(1)}, u32[]{:S(2)}, u32[]{:S(2)}) collective-permute-start(bf16[72,384]{1,0:T(8,128)(2,1)S(1)} %get-tuple-element.32), channel_id=1, source_target_pairs={{0,6},{1,7},{2,4},{3,5},{4,2},{5,3},{6,0},{7,1},{8,14},{9,15},{10,... | collective-permute-start | bytes 165896 | tf_op jit(solution)/shard_map/ppermute | solution.py:328
  14.0 1.5 %collective-permute-start.3 = (bf16[4,72,384]{2,1,0:T(8,128)(2,1)S(1)}, bf16[4,72,384]{2,1,0:T(8,128)(2,1)S(1)}, u32[]{:S(2)}, u32[]{:S(2)}) collective-permute-start(bf16[4,72,384]{2,1,0:T(8,128)(2,1)S(1)} %shard_map.140), channel_id=1, source_target_pairs={{0,1},{1,0},{2,3},{3,2},{4,5},{5,4},{6,7},{7,6},{8,9},{9,8},{10,11... | collective-permute-start | bytes 663560 | tf_op jit(solution)/shard_map/ppermute | solution.py:370
  18.0 6.0 %collective-permute-start.4 = (bf16[112,128]{1,0:T(8,128)(2,1)S(1)}, bf16[112,128]{1,0:T(8,128)(2,1)S(1)}, u32[]{:S(2)}, u32[]{:S(2)}) collective-permute-start(bf16[112,128]{1,0:T(8,128)(2,1)S(1)} %get-tuple-element.40), channel_id=1, source_target_pairs={{0,4},{1,5},{2,6},{3,7},{4,0},{5,1},{6,2},{7,3},{8,12},{9,13},{10,... | collective-permute-start | bytes 86024 | tf_op jit(solution)/shard_map/ppermute | solution.py:328
  18.8 5.7 %collective-permute-start.5 = (bf16[112,128]{1,0:T(8,128)(2,1)S(1)}, bf16[112,128]{1,0:T(8,128)(2,1)S(1)}, u32[]{:S(2)}, u32[]{:S(2)}) collective-permute-start(bf16[112,128]{1,0:T(8,128)(2,1)S(1)} %get-tuple-element.41), channel_id=1, source_target_pairs={{0,6},{1,7},{2,4},{3,5},{4,2},{5,3},{6,0},{7,1},{8,14},{9,15},{10,... | collective-permute-start | bytes 86024 | tf_op jit(solution)/shard_map/ppermute | solution.py:328
  19.7 7.3 %collective-permute-start.7 = (bf16[112,128]{1,0:T(8,128)(2,1)S(1)}, bf16[112,128]{1,0:T(8,128)(2,1)S(1)}, u32[]{:S(2)}, u32[]{:S(2)}) collective-permute-start(bf16[112,128]{1,0:T(8,128)(2,1)S(1)} %get-tuple-element.42), channel_id=1, source_target_pairs={{0,2},{1,3},{2,0},{3,1},{4,6},{5,7},{6,4},{7,5},{8,10},{9,11},{10,... | collective-permute-start | bytes 86024 | tf_op jit(solution)/shard_map/ppermute | solution.py:328
  21.5 7.2 %collective-permute-start.9 = (bf16[180,384]{1,0:T(8,128)(2,1)S(1)}, bf16[180,384]{1,0:T(8,128)(2,1)S(1)}, u32[]{:S(2)}, u32[]{:S(2)}) collective-permute-start(bf16[180,384]{1,0:T(8,128)(2,1)S(1)} %get-tuple-element.43), channel_id=1, source_target_pairs={{0,24},{8,0},{16,8},{24,16},{1,25},{9,1},{17,9},{25,17},{2,26},{10... | collective-permute-start | bytes 414728 | tf_op jit(solution)/shard_map/ppermute | solution.py:28
  24.5 6.4 %collective-permute-start.6 = (bf16[3,112,128]{2,1,0:T(8,128)(2,1)S(1)}, bf16[3,112,128]{2,1,0:T(8,128)(2,1)S(1)}, u32[]{:S(2)}, u32[]{:S(2)}) collective-permute-start(bf16[3,112,128]{2,1,0:T(8,128)(2,1)S(1)} %shard_map.143), channel_id=1, source_target_pairs={{0,24},{8,0},{16,8},{24,16},{1,25},{9,1},{17,9},{25,17},{2,26},{10... | collective-permute-start | bytes 258056 | tf_op jit(solution)/shard_map/ppermute | solution.py:28
  27.0 3.9 %collective-permute-start.8 = (bf16[112,128]{1,0:T(8,128)(2,1)S(1)}, bf16[112,128]{1,0:T(8,128)(2,1)S(1)}, u32[]{:S(2)}, u32[]{:S(2)}) collective-permute-start(bf16[112,128]{1,0:T(8,128)(2,1)S(1)} %collective-permute-done.7), channel_id=1, source_target_pairs={{0,24},{8,0},{16,8},{24,16},{1,25},{9,1},{17,9},{25,17},{2,26},{10... | collective-permute-start | bytes 86024 | tf_op jit(solution)/shard_map/ppermute | solution.py:28

commit v10 on v9

--- a/solution.py
+++ b/solution.py
@@ -248,7 +248,7 @@
         out[...] = pack(band).astype(BF16)
 
 
-def products_kernel(points0, hidden0, points1, hidden1, grad_pre, grad_y, gw1, gw2, gb1):
+def products_kernel(points0, hidden0, points1, hidden1, grad_pre, grad_y, _, gw1, gw2, gb1):
     core = lax.rem(lax.axis_index("lat"), 2)
     half = BS // 2
     for ref, grads, values in ((gw1, grad_pre, (points0, points1)), (gw2, grad_y, (hidden0, hidden1))):
@@ -401,7 +401,7 @@
         products_kernel,
         (matrix, matrix, shape((2, BS // 2), F32)),
         [],
-        (points0, hidden0, points1, hidden1, grad_pre, grad_y),
+        (points0, hidden0, points1, hidden1, grad_pre, grad_y, next_field),
         (),
         2 * 10**9,
     )
@@ -409,7 +409,7 @@
         functools.partial(join_kernel, 3),
         shape((3, *packed.shape), BF16),
         [],
-        (backs[0], backs[2], backs[3]),
+        (backs[0], backs[2], backs[3], gb1),
         (),
     )
     three = turn(three, "section")

time: 32.2 us -> 36.7 us (1.14)
  waiting for transfers between devices: 8.16 us -> 14.8 us
  starting transfers between devices: 14.8 us -> 12 us
  local copies, waits for them, and re-layouts: 0 us -> 0.68 us
    ppermute x6, waiting for transfers between devices: 4.85 us -> 11.8 us  [swap(): lax.ppermute(chunks[d], 'lat', pairs[d])]
    ppermute x6, starting transfers between devices: 9.24 us -> 7.44 us  [swap(): lax.ppermute(chunks[d], 'lat', pairs[d])]
    ppermute x1, waiting for transfers between devices: 1.1 us -> 0.01 us  [paired_blocks(): other = lax.ppermute(own, 'lat', [(i, i ^ 1) for i in range(2 * NB)])]
    ppermute x3, starting transfers between devices: 5.47 us -> 4.47 us  [turn(): lax.ppermute(value, axis, [(i, (i - 1) % length) for i in range(length)])]
    ppermute x3, waiting for transfers between devices: 2.22 us -> 2.93 us  [turn(): lax.ppermute(value, axis, [(i, (i - 1) % length) for i in range(length)])]
    unnamed x0 -> x2, local copies, waits for them, and re-layouts: none -> 0.68 us
  transfers between devices with their start and end apart: 10 -> 10, of which waited for: 5 -> 6; matrix products, arithmetic and copies ran while one was open for 0% -> 0% of each run, Pallas kernels for 10% -> 15%
where the time goes in v10:
time: 36.7 us; the launch traced here: 36.5 us
  waiting for transfers between devices  14.8 us (40%)
  starting transfers between devices  12 us (33%)
  Pallas kernels  8.35 us (23%)
  between operations  0.7 us (2%)
  local copies, waits for them, and re-layouts  0.68 us (2%)
    ppermute x6, waiting for transfers between devices, swap(): lax.ppermute(chunks[d], 'lat', pairs[d])  11.8 us
    pallas_call x8, Pallas kernels, call(): pl.pallas_call(kernel, out_shape=outs, in_specs=[VMEM] * len(near) + [HBM...  8.35 us
    ppermute x6, starting transfers between devices, swap(): lax.ppermute(chunks[d], 'lat', pairs[d])  7.44 us
    ppermute x3, starting transfers between devices, turn(): lax.ppermute(value, axis, [(i, (i - 1) % length) for i in range(length)])  4.47 us
    ppermute x3, waiting for transfers between devices, turn(): lax.ppermute(value, axis, [(i, (i - 1) % length) for i in range(length)])  2.93 us
  transfers between devices with their start and end apart: 10, of which 6 were waited for; matrix products, arithmetic and copies ran while one was open for 0% of the time, Pallas kernels for 15%

profile of v10, /device:TPU:0, one launch (start us, length us, event | category | flops | bytes accessed | tf_op | source)
XLA Modules:
  0.0 36.5 jit_solution(8147821032093283784)
XLA Ops:
  0.6 1.7 %shard_map.138 = (bf16[72,384]{1,0:T(8,128)(2,1)S(1)}, bf16[72,384]{1,0:T(8,128)(2,1)S(1)}, bf16[72,384]{1,0:T(8,128)(2,1)S(1)}, bf16[72,384]{1,0:T(8,128)(2,1)S(1)}) custom-call(s32[8]{0:T(128)} %refs_0_.3, s32[8]{0:T(128)} %refs_11_.1, bf16[180,384]{1,0:T(8,128)(2,1)} %bitcast.17, bf16[144,180]{1,0:T(8,128)(2,1)} %constant.10.clone.refs_3_, ...), custom_call_target="tpu_custom_call" | custom-call | flops 100000000 | bytes 1000000 | tf_op jit(solution)/shard_map/pallas_call | solution.py:286
  2.3 3.1 %collective-permute-start = (bf16[72,384]{1,0:T(8,128)(2,1)S(1)}, bf16[72,384]{1,0:T(8,128)(2,1)S(1)}, u32[]{:S(2)}, u32[]{:S(2)}) collective-permute-start(bf16[72,384]{1,0:T(8,128)(2,1)S(1)} %get-tuple-element.30), channel_id=1, source_target_pairs={{0,2},{1,3},{2,0},{3,1},{4,6},{5,7},{6,4},{7,5},{8,10},{9,11},{10,... | collective-permute-start | bytes 165896 | tf_op jit(solution)/shard_map/ppermute | solution.py:328
  5.4 2.6 %collective-permute-start.1 = (bf16[72,384]{1,0:T(8,128)(2,1)S(1)}, bf16[72,384]{1,0:T(8,128)(2,1)S(1)}, u32[]{:S(2)}, u32[]{:S(2)}) collective-permute-start(bf16[72,384]{1,0:T(8,128)(2,1)S(1)} %get-tuple-element.31), channel_id=1, source_target_pairs={{0,4},{1,5},{2,6},{3,7},{4,0},{5,1},{6,2},{7,3},{8,12},{9,13},{10,... | collective-permute-start | bytes 165896 | tf_op jit(solution)/shard_map/ppermute | solution.py:328
  8.0 0.0 collective-permute-start.2
  8.0 1.6 %shard_map.139 = (bf16[256,256]{1,0:T(8,128)(2,1)S(1)}, bf16[256,256]{1,0:T(8,128)(2,1)S(1)}, f32[1,256]{1,0:T(1,128)S(1)}, bf16[576,576]{1,0:T(8,128)(2,1)S(1)}...) custom-call(s32[8]{0:T(128)} %refs_0_.3, s32[8]{0:T(128)} %refs_11_.1, ...), custom_call_target="tpu_custom_call" | custom-call | flops 2000000000 | bytes 1000000 | tf_op jit(solution)/shard_map/pallas_call | solution.py:286
  9.7 0.0 collective-permute-done.refs_1_
  9.7 1.9 %collective-permute-done.1.refs_2_ = bf16[72,384]{1,0:T(8,128)(2,1)S(1)} collective-permute-done((bf16[72,384]{1,0:T(8,128)(2,1)S(1)}, bf16[72,384]{1,0:T(8,128)(2,1)S(1)}, u32[]{:S(2)}, u32[]{:S(2)}) %collective-permute-start.1) | collective-permute-done | bytes 55328 | tf_op jit(solution)/shard_map/ppermute | solution.py:328
  11.5 2.4 %collective-permute-done.2.refs_3_ = bf16[72,384]{1,0:T(8,128)(2,1)S(1)} collective-permute-done((bf16[72,384]{1,0:T(8,128)(2,1)S(1)}, bf16[72,384]{1,0:T(8,128)(2,1)S(1)}, u32[]{:S(2)}, u32[]{:S(2)}) %collective-permute-start.2) | collective-permute-done | bytes 55328 | tf_op jit(solution)/shard_map/ppermute | solution.py:328
  14.0 0.1 collective-permute-start.3
  14.1 2.5 %collective-permute-start.6 = (bf16[180,384]{1,0:T(8,128)(2,1)S(1)}, bf16[180,384]{1,0:T(8,128)(2,1)S(1)}, u32[]{:S(2)}, u32[]{:S(2)}) collective-permute-start(bf16[180,384]{1,0:T(8,128)(2,1)S(1)} %get-tuple-element.48), channel_id=1, source_target_pairs={{0,24},{8,0},{16,8},{24,16},{1,25},{9,1},{17,9},{25,17},{2,26},{10... | collective-permute-start | bytes 414728 | tf_op jit(solution)/shard_map/ppermute | solution.py:28
  16.6 0.4 shard_map.141
  16.9 2.4 %shard_map.142 = (bf16[112,128]{1,0:T(8,128)(2,1)S(1)}, bf16[112,128]{1,0:T(8,128)(2,1)S(1)}, bf16[112,128]{1,0:T(8,128)(2,1)S(1)}, bf16[112,128]{1,0:T(8,128)(2...) custom-call(bf16[72,384]{1,0:T(8,128)(2,1)S(1)} %get-tuple-element.2, ...), custom_call_target="tpu_custom_call" | custom-call | flops 100000000 | bytes 1000000 | tf_op jit(solution)/shard_map/pallas_call | solution.py:286
  19.4 0.9 %collective-permute-start.4 = (bf16[112,128]{1,0:T(8,128)(2,1)S(1)}, bf16[112,128]{1,0:T(8,128)(2,1)S(1)}, u32[]{:S(2)}, u32[]{:S(2)}) collective-permute-start(bf16[112,128]{1,0:T(8,128)(2,1)S(1)} %get-tuple-element.40), channel_id=1, source_target_pairs={{0,4},{1,5},{2,6},{3,7},{4,0},{5,1},{6,2},{7,3},{8,12},{9,13},{10,... | collective-permute-start | bytes 86024 | tf_op jit(solution)/shard_map/ppermute | solution.py:328
  20.2 0.9 %collective-permute-start.5 = (bf16[112,128]{1,0:T(8,128)(2,1)S(1)}, bf16[112,128]{1,0:T(8,128)(2,1)S(1)}, u32[]{:S(2)}, u32[]{:S(2)}) collective-permute-start(bf16[112,128]{1,0:T(8,128)(2,1)S(1)} %get-tuple-element.41), channel_id=1, source_target_pairs={{0,6},{1,7},{2,4},{3,5},{4,2},{5,3},{6,0},{7,1},{8,14},{9,15},{10,... | collective-permute-start | bytes 86024 | tf_op jit(solution)/shard_map/ppermute | solution.py:328
  21.1 1.1 %shard_map.143 = (f32[2,48,96]{2,1,0:T(8,128)}, f32[2,48,96]{2,1,0:T(8,128)}, f32[2,48]{1,0:T(2,128)}) custom-call(bf16[288,256]{1,0:T(8,128)(2,1)S(1)} %get-tuple-element.42.points0, bf16[288,256]{1,0:T(8,128)(2,1)S(1)} %get-tuple-element.43.hidden0, bf16[288,256]{1,0:T(8,128)(2,1)S(1)} %get-tuple-element.44.points1, ...), custom_call_target="tpu_custom_call" | custom-call | flops 2000000000 | bytes 1000000 | tf_op jit(solution)/shard_map/pallas_call | solution.py:286
  22.2 2.0 %collective-permute-done.4.refs_1_ = bf16[112,128]{1,0:T(8,128)(2,1)S(1)} collective-permute-done((bf16[112,128]{1,0:T(8,128)(2,1)S(1)}, bf16[112,128]{1,0:T(8,128)(2,1)S(1)}, u32[]{:S(2)}, u32[]{:S(2)}) %collective-permute-start.4) | collective-permute-done | bytes 28704 | tf_op jit(solution)/shard_map/ppermute | solution.py:328
  24.2 1.7 %collective-permute-done.5.refs_2_ = bf16[112,128]{1,0:T(8,128)(2,1)S(1)} collective-permute-done((bf16[112,128]{1,0:T(8,128)(2,1)S(1)}, bf16[112,128]{1,0:T(8,128)(2,1)S(1)}, u32[]{:S(2)}, u32[]{:S(2)}) %collective-permute-start.5) | collective-permute-done | bytes 28704 | tf_op jit(solution)/shard_map/ppermute | solution.py:328
  25.9 0.7 %copy-done = f32[2,48]{1,0:T(2,128)S(1)} copy-done((f32[2,48]{1,0:T(2,128)S(1)}, f32[2,48]{1,0:T(2,128)}, u32[]{:S(2)}) %copy-start) | copy-done | bytes 408
  26.6 1.0 %collective-permute-start.7 = (bf16[3,112,128]{2,1,0:T(8,128)(2,1)S(1)}, bf16[3,112,128]{2,1,0:T(8,128)(2,1)S(1)}, u32[]{:S(2)}, u32[]{:S(2)}) collective-permute-start(bf16[3,112,128]{2,1,0:T(8,128)(2,1)S(1)} %shard_map.144), channel_id=1, source_target_pairs={{0,24},{8,0},{16,8},{24,16},{1,25},{9,1},{17,9},{25,17},{2,26},{10... | collective-permute-start | bytes 258056 | tf_op jit(solution)/shard_map/ppermute | solution.py:28
  27.6 0.0 collective-permute-start.8
  27.6 3.9 %collective-permute-done.8 = bf16[112,128]{1,0:T(8,128)(2,1)S(1)} collective-permute-done((bf16[112,128]{1,0:T(8,128)(2,1)S(1)}, bf16[112,128]{1,0:T(8,128)(2,1)S(1)}, u32[]{:S(2)}, u32[]{:S(2)}) %collective-permute-start.8) | collective-permute-done | bytes 28704 | tf_op jit(solution)/shard_map/ppermute | solution.py:328
  31.5 0.9 %collective-permute-start.9 = (bf16[112,128]{1,0:T(8,128)(2,1)S(1)}, bf16[112,128]{1,0:T(8,128)(2,1)S(1)}, u32[]{:S(2)}, u32[]{:S(2)}) collective-permute-start(bf16[112,128]{1,0:T(8,128)(2,1)S(1)} %collective-permute-done.8), channel_id=1, source_target_pairs={{0,24},{8,0},{16,8},{24,16},{1,25},{9,1},{17,9},{25,17},{2,26},{10... | collective-permute-start | bytes 86024 | tf_op jit(solution)/shard_map/ppermute | solution.py:28
  32.4 2.9 %collective-permute-done.9.one = bf16[112,128]{1,0:T(8,128)(2,1)S(1)} collective-permute-done((bf16[112,128]{1,0:T(8,128)(2,1)S(1)}, bf16[112,128]{1,0:T(8,128)(2,1)S(1)}, u32[]{:S(2)}, u32[]{:S(2)}) %collective-permute-start.9) | collective-permute-done | bytes 28704 | tf_op jit(solution)/shard_map/ppermute | solution.py:28
  35.4 1.1 %shard_map.145 = bf16[180,384]{1,0:T(8,128)(2,1)} custom-call(bf16[3,112,128]{2,1,0:T(8,128)(2,1)S(1)} %collective-permute-done.7.three, bf16[112,128]{1,0:T(8,128)(2,1)S(1)} %collective-permute-done.9.one, bf16[180,384]{1,0:T(8,128)(2,1)S(1)} %collective-permute-done.6._.field, bf16[180,144]{1,0:T(8,128)(2,1)S(1)} %get-tuple-element.51.table), custom_call_target="tpu_custom_call" | custom-call | flops 100000000 | bytes 1000000 | tf_op jit(solution)/shard_map/pallas_call | solution.py:286
  (6 shorter events, 0.0 us)
Async XLA Ops:
  2.3 7.3 %collective-permute-start = (bf16[72,384]{1,0:T(8,128)(2,1)S(1)}, bf16[72,384]{1,0:T(8,128)(2,1)S(1)}, u32[]{:S(2)}, u32[]{:S(2)}) collective-permute-start(bf16[72,384]{1,0:T(8,128)(2,1)S(1)} %get-tuple-element.30), channel_id=1, source_target_pairs={{0,2},{1,3},{2,0},{3,1},{4,6},{5,7},{6,4},{7,5},{8,10},{9,11},{10,... | collective-permute-start | bytes 165896 | tf_op jit(solution)/shard_map/ppermute | solution.py:328
  5.4 6.1 %collective-permute-start.1 = (bf16[72,384]{1,0:T(8,128)(2,1)S(1)}, bf16[72,384]{1,0:T(8,128)(2,1)S(1)}, u32[]{:S(2)}, u32[]{:S(2)}) collective-permute-start(bf16[72,384]{1,0:T(8,128)(2,1)S(1)} %get-tuple-element.31), channel_id=1, source_target_pairs={{0,4},{1,5},{2,6},{3,7},{4,0},{5,1},{6,2},{7,3},{8,12},{9,13},{10,... | collective-permute-start | bytes 165896 | tf_op jit(solution)/shard_map/ppermute | solution.py:328
  8.0 6.0 %collective-permute-start.2 = (bf16[72,384]{1,0:T(8,128)(2,1)S(1)}, bf16[72,384]{1,0:T(8,128)(2,1)S(1)}, u32[]{:S(2)}, u32[]{:S(2)}) collective-permute-start(bf16[72,384]{1,0:T(8,128)(2,1)S(1)} %get-tuple-element.32), channel_id=1, source_target_pairs={{0,6},{1,7},{2,4},{3,5},{4,2},{5,3},{6,0},{7,1},{8,14},{9,15},{10,... | collective-permute-start | bytes 165896 | tf_op jit(solution)/shard_map/ppermute | solution.py:328
  14.0 2.9 %collective-permute-start.3 = (bf16[4,72,384]{2,1,0:T(8,128)(2,1)S(1)}, bf16[4,72,384]{2,1,0:T(8,128)(2,1)S(1)}, u32[]{:S(2)}, u32[]{:S(2)}) collective-permute-start(bf16[4,72,384]{2,1,0:T(8,128)(2,1)S(1)} %shard_map.140), channel_id=1, source_target_pairs={{0,1},{1,0},{2,3},{3,2},{4,5},{5,4},{6,7},{7,6},{8,9},{9,8},{10,11... | collective-permute-start | bytes 663560 | tf_op jit(solution)/shard_map/ppermute | solution.py:370
  14.1 7.0 %collective-permute-start.6 = (bf16[180,384]{1,0:T(8,128)(2,1)S(1)}, bf16[180,384]{1,0:T(8,128)(2,1)S(1)}, u32[]{:S(2)}, u32[]{:S(2)}) collective-permute-start(bf16[180,384]{1,0:T(8,128)(2,1)S(1)} %get-tuple-element.48), channel_id=1, source_target_pairs={{0,24},{8,0},{16,8},{24,16},{1,25},{9,1},{17,9},{25,17},{2,26},{10... | collective-permute-start | bytes 414728 | tf_op jit(solution)/shard_map/ppermute | solution.py:28
  19.4 4.8 %collective-permute-start.4 = (bf16[112,128]{1,0:T(8,128)(2,1)S(1)}, bf16[112,128]{1,0:T(8,128)(2,1)S(1)}, u32[]{:S(2)}, u32[]{:S(2)}) collective-permute-start(bf16[112,128]{1,0:T(8,128)(2,1)S(1)} %get-tuple-element.40), channel_id=1, source_target_pairs={{0,4},{1,5},{2,6},{3,7},{4,0},{5,1},{6,2},{7,3},{8,12},{9,13},{10,... | collective-permute-start | bytes 86024 | tf_op jit(solution)/shard_map/ppermute | solution.py:328
  20.2 5.7 %collective-permute-start.5 = (bf16[112,128]{1,0:T(8,128)(2,1)S(1)}, bf16[112,128]{1,0:T(8,128)(2,1)S(1)}, u32[]{:S(2)}, u32[]{:S(2)}) collective-permute-start(bf16[112,128]{1,0:T(8,128)(2,1)S(1)} %get-tuple-element.41), channel_id=1, source_target_pairs={{0,6},{1,7},{2,4},{3,5},{4,2},{5,3},{6,0},{7,1},{8,14},{9,15},{10,... | collective-permute-start | bytes 86024 | tf_op jit(solution)/shard_map/ppermute | solution.py:328
  25.9 0.7 %copy-start = (f32[2,48]{1,0:T(2,128)S(1)}, f32[2,48]{1,0:T(2,128)}, u32[]{:S(2)}) copy-start(f32[2,48]{1,0:T(2,128)} %get-tuple-element.49.refs_3_) | copy-start | bytes 1156
  26.6 8.8 %collective-permute-start.7 = (bf16[3,112,128]{2,1,0:T(8,128)(2,1)S(1)}, bf16[3,112,128]{2,1,0:T(8,128)(2,1)S(1)}, u32[]{:S(2)}, u32[]{:S(2)}) collective-permute-start(bf16[3,112,128]{2,1,0:T(8,128)(2,1)S(1)} %shard_map.144), channel_id=1, source_target_pairs={{0,24},{8,0},{16,8},{24,16},{1,25},{9,1},{17,9},{25,17},{2,26},{10... | collective-permute-start | bytes 258056 | tf_op jit(solution)/shard_map/ppermute | solution.py:28
  27.6 3.9 %collective-permute-start.8 = (bf16[112,128]{1,0:T(8,128)(2,1)S(1)}, bf16[112,128]{1,0:T(8,128)(2,1)S(1)}, u32[]{:S(2)}, u32[]{:S(2)}) collective-permute-start(bf16[112,128]{1,0:T(8,128)(2,1)S(1)} %get-tuple-element.50), channel_id=1, source_target_pairs={{0,2},{1,3},{2,0},{3,1},{4,6},{5,7},{6,4},{7,5},{8,10},{9,11},{10,... | collective-permute-start | bytes 86024 | tf_op jit(solution)/shard_map/ppermute | solution.py:328
  31.5 3.9 %collective-permute-start.9 = (bf16[112,128]{1,0:T(8,128)(2,1)S(1)}, bf16[112,128]{1,0:T(8,128)(2,1)S(1)}, u32[]{:S(2)}, u32[]{:S(2)}) collective-permute-start(bf16[112,128]{1,0:T(8,128)(2,1)S(1)} %collective-permute-done.8), channel_id=1, source_target_pairs={{0,24},{8,0},{16,8},{24,16},{1,25},{9,1},{17,9},{25,17},{2,26},{10... | collective-permute-start | bytes 86024 | tf_op jit(solution)/shard_map/ppermute | solution.py:28

commit v11 on v9

--- a/solution.py
+++ b/solution.py
@@ -168,10 +168,12 @@
     wait(copies[6:])
 
 
-def join_kernel(count, *refs):
-    out = refs[-1]
-    for d, ref in enumerate(refs[:count]):
-        out[d] = ref[...]
+ORDER = (0, 3, 2, 1)
+
+
+def join_kernel(*refs):
+    for d, ref in zip(ORDER, refs):
+        refs[-1][d] = ref[...]
 
 
 def pack(band):
@@ -207,8 +209,9 @@
 
 
 def own_kernel(*refs):
-    chunks, (mat1, bias), (points, hidden, slope), by_pair = refs[:4], refs[4:6], refs[6:9], refs[9]
-    silu_points([chunk[...].astype(F32) for chunk in chunks], mat1, bias, by_pair, points, hidden, slope)
+    mat1, bias, points, hidden, slope, by_pair = refs[NB:]
+    chunks = [refs[i][...].astype(F32) for i in ORDER]
+    silu_points(chunks, mat1, bias, by_pair, points, hidden, slope)
 
 
 def filter_kernel(*refs):
@@ -217,7 +220,7 @@
     assign, by_lat, by_pair, slope, sems = refs[20:]
     copies = fetch(sems, (assign_hbm,), (assign,))
     core = lax.rem(lax.axis_index("lat"), 2)
-    sides = [[own[...].astype(F32) for own in owns], [other[d].astype(F32) for d in range(NB)]]
+    sides = [[owns[i][...].astype(F32) for i in ORDER], [other[d].astype(F32) for d in range(NB)]]
     silu_points(sides[1], mat1, bias, by_pair, points, hidden, slope)
     wait(copies)
     for side, chunks in zip((core, 1 - core), sides):
@@ -263,10 +266,10 @@
         gb1[c : c + 1] = jnp.where(core == 0, line[:, :half], line[:, half:BS])
 
 
-def compose_kernel(last, three, one, field, table, out, by_block):
+def compose_kernel(last, four, field, table, out, by_block):
     rows = by_block.shape[1]
-    for d, back in ((0, three[0]), (1, one[...]), (2, three[1]), (3, three[2])):
-        by_block[partner(d)] = jnp.concatenate(unpack(back.astype(F32), rows), axis=1)
+    for d in range(NB):
+        by_block[partner(d)] = jnp.concatenate(unpack(four[d].astype(F32), rows), axis=1)
     groups = [
         dense([by_block[n, :, g * LANES : (g + 1) * LANES] for n in range(NB)]) for g in range(2)
     ]
@@ -325,7 +328,7 @@
 
     def swap(chunks):
         pairs = [[(i, i ^ (2 * d)) for i in range(2 * NB)] for d in range(NB)]
-        return [chunks[0]] + [lax.ppermute(chunks[d], "lat", pairs[d]) for d in (3, 2, 1)][::-1]
+        return [lax.ppermute(chunks[d], "lat", pairs[d]) if d else chunks[0] for d in ORDER]
 
     field = grad_out.reshape(length, width)
     shape = jax.ShapeDtypeStruct
@@ -361,7 +364,7 @@
     )
     next_field = turn(field, "section")
     own = call(
-        functools.partial(join_kernel, NB),
+        join_kernel,
         shape((NB, rows, width), BF16),
         [],
         (*received, bias),
@@ -405,20 +408,12 @@
         (),
         2 * 10**9,
     )
-    three = call(
-        functools.partial(join_kernel, 3),
-        shape((3, *packed.shape), BF16),
-        [],
-        (backs[0], backs[2], backs[3]),
-        (),
-    )
-    three = turn(three, "section")
-    one = turn(backs[1], "section")
+    four = turn(call(join_kernel, shape((NB, *packed.shape), BF16), [], backs, ()), "section")
     shifted = call(
         functools.partial(compose_kernel, lax.axis_size("section") - 1),
         shape((length, width), BF16),
         [by_pair],
-        (three, one, next_field, forward),
+        (four, next_field, forward),
         (),
     )
     shifted = shifted[None, None]

time: 32.2 us -> 30 us (0.932)
  waiting for transfers between devices: 8.16 us -> 5.55 us
  starting transfers between devices: 14.8 us -> 15.2 us
    ppermute x6, waiting for transfers between devices: 4.85 us -> 3.2 us  [swap(): lax.ppermute(chunks[d], 'lat', pairs[d])]
    ppermute x6, starting transfers between devices: 9.24 us -> 10.2 us  [swap(): lax.ppermute(chunks[d], 'lat', pairs[d])]
    ppermute x3 -> x2, waiting for transfers between devices: 2.22 us -> 1.25 us  [turn(): lax.ppermute(value, axis, [(i, (i - 1) % length) for i in range(length)])]
    ppermute x3 -> x2, starting transfers between devices: 5.47 us -> 4.94 us  [turn(): lax.ppermute(value, axis, [(i, (i - 1) % length) for i in range(length)])]
  transfers between devices with their start and end apart: 10 -> 9, of which waited for: 5 -> 5; matrix products, arithmetic and copies ran while one was open for 0% -> 0% of each run, Pallas kernels for 10% -> 10%
where the time goes in v11:
time: 30 us; the launch traced here: 29.8 us
  starting transfers between devices  15.2 us (51%)
  Pallas kernels  8.34 us (28%)
  waiting for transfers between devices  5.55 us (18%)
  between operations  0.69 us (2%)
    ppermute x6, starting transfers between devices, swap(): lax.ppermute(chunks[d], 'lat', pairs[d])  10.2 us
    pallas_call x8, Pallas kernels, call(): pl.pallas_call(kernel, out_shape=outs, in_specs=[VMEM] * len(near) + [HBM...  8.34 us
    ppermute x2, starting transfers between devices, turn(): lax.ppermute(value, axis, [(i, (i - 1) % length) for i in range(length)])  4.94 us
    ppermute x6, waiting for transfers between devices, swap(): lax.ppermute(chunks[d], 'lat', pairs[d])  3.2 us
    ppermute x2, waiting for transfers between devices, turn(): lax.ppermute(value, axis, [(i, (i - 1) % length) for i in range(length)])  1.25 us
    ppermute x1, waiting for transfers between devices, paired_blocks(): other = lax.ppermute(own, 'lat', [(i, i ^ 1) for i in range(2 * NB)])  1.1 us
  transfers between devices with their start and end apart: 9, of which 5 were waited for; matrix products, arithmetic and copies ran while one was open for 0% of the time, Pallas kernels for 10%

profile of v11, /device:TPU:0, one launch (start us, length us, event | category | flops | bytes accessed | tf_op | source)
XLA Modules:
  0.0 29.8 jit_solution(5094295994665322840)
XLA Ops:
  0.6 1.7 %shard_map.138 = (bf16[72,384]{1,0:T(8,128)(2,1)S(1)}, bf16[72,384]{1,0:T(8,128)(2,1)S(1)}, bf16[72,384]{1,0:T(8,128)(2,1)S(1)}, bf16[72,384]{1,0:T(8,128)(2,1)S(1)}) custom-call(s32[8]{0:T(128)} %refs_0_.3, s32[8]{0:T(128)} %refs_11_.1, bf16[180,384]{1,0:T(8,128)(2,1)} %bitcast.16, bf16[144,180]{1,0:T(8,128)(2,1)} %constant.10.clone.refs_3_, ...), custom_call_target="tpu_custom_call" | custom-call | flops 100000000 | bytes 1000000 | tf_op jit(solution)/shard_map/pallas_call | solution.py:289
  2.3 5.1 %collective-permute-start = (bf16[72,384]{1,0:T(8,128)(2,1)S(1)}, bf16[72,384]{1,0:T(8,128)(2,1)S(1)}, u32[]{:S(2)}, u32[]{:S(2)}) collective-permute-start(bf16[72,384]{1,0:T(8,128)(2,1)S(1)} %get-tuple-element.30), channel_id=1, source_target_pairs={{0,6},{1,7},{2,4},{3,5},{4,2},{5,3},{6,0},{7,1},{8,14},{9,15},{10,... | collective-permute-start | bytes 165896 | tf_op jit(solution)/shard_map/ppermute | solution.py:331
  7.5 0.0 collective-permute-start.1
  7.5 0.6 %collective-permute-start.2 = (bf16[72,384]{1,0:T(8,128)(2,1)S(1)}, bf16[72,384]{1,0:T(8,128)(2,1)S(1)}, u32[]{:S(2)}, u32[]{:S(2)}) collective-permute-start(bf16[72,384]{1,0:T(8,128)(2,1)S(1)} %get-tuple-element.32), channel_id=1, source_target_pairs={{0,2},{1,3},{2,0},{3,1},{4,6},{5,7},{6,4},{7,5},{8,10},{9,11},{10,... | collective-permute-start | bytes 165896 | tf_op jit(solution)/shard_map/ppermute | solution.py:331
  8.1 1.6 %shard_map.139 = (bf16[256,256]{1,0:T(8,128)(2,1)S(1)}, bf16[256,256]{1,0:T(8,128)(2,1)S(1)}, f32[1,256]{1,0:T(1,128)S(1)}, bf16[576,576]{1,0:T(8,128)(2,1)S(1)}...) custom-call(s32[8]{0:T(128)} %refs_0_.3, s32[8]{0:T(128)} %refs_11_.1, ...), custom_call_target="tpu_custom_call" | custom-call | flops 2000000000 | bytes 1000000 | tf_op jit(solution)/shard_map/pallas_call | solution.py:289
  9.7 0.1 collective-permute-done.refs_1_
  9.8 2.7 %collective-permute-done.1.refs_2_ = bf16[72,384]{1,0:T(8,128)(2,1)S(1)} collective-permute-done((bf16[72,384]{1,0:T(8,128)(2,1)S(1)}, bf16[72,384]{1,0:T(8,128)(2,1)S(1)}, u32[]{:S(2)}, u32[]{:S(2)}) %collective-permute-start.1) | collective-permute-done | bytes 55328 | tf_op jit(solution)/shard_map/ppermute | solution.py:331
  12.5 0.0 collective-permute-done.2.refs_3_
  12.5 0.1 collective-permute-start.3
  12.6 0.4 %shard_map.141 = (bf16[288,256]{1,0:T(8,128)(2,1)S(1)}, bf16[288,256]{1,0:T(8,128)(2,1)S(1)}, f32[288,256]{1,0:T(8,128)S(1)}) custom-call(bf16[72,384]{1,0:T(8,128)(2,1)S(1)} %get-tuple-element.29.refs_0_, bf16[72,384]{1,0:T(8,128)(2,1)S(1)} %collective-permute-done.refs_1_, bf16[72,384]{1,0:T(8,128)(2,1)S(1)} %collective-permute-done.1.refs_2_, ...), custom_call_target="tpu_custom_call" | custom-call | flops 2000000000 | bytes 1000000 | tf_op jit(solution)/shard_map/pallas_call | solution.py:289
  13.0 1.1 %collective-permute-done.3.refs_4_ = bf16[4,72,384]{2,1,0:T(8,128)(2,1)S(1)} collective-permute-done((bf16[4,72,384]{2,1,0:T(8,128)(2,1)S(1)}, bf16[4,72,384]{2,1,0:T(8,128)(2,1)S(1)}, u32[]{:S(2)}, u32[]{:S(2)}) %collective-permute-start.3) | collective-permute-done | bytes 221216 | tf_op jit(solution)/shard_map/ppermute | solution.py:373
  14.1 2.4 %shard_map.142 = (bf16[112,128]{1,0:T(8,128)(2,1)S(1)}, bf16[112,128]{1,0:T(8,128)(2,1)S(1)}, bf16[112,128]{1,0:T(8,128)(2,1)S(1)}, bf16[112,128]{1,0:T(8,128)(2...) custom-call(bf16[72,384]{1,0:T(8,128)(2,1)S(1)} %get-tuple-element.2, ...), custom_call_target="tpu_custom_call" | custom-call | flops 100000000 | bytes 1000000 | tf_op jit(solution)/shard_map/pallas_call | solution.py:289
  16.5 2.6 %collective-permute-start.4 = (bf16[112,128]{1,0:T(8,128)(2,1)S(1)}, bf16[112,128]{1,0:T(8,128)(2,1)S(1)}, u32[]{:S(2)}, u32[]{:S(2)}) collective-permute-start(bf16[112,128]{1,0:T(8,128)(2,1)S(1)} %get-tuple-element.40), channel_id=1, source_target_pairs={{0,6},{1,7},{2,4},{3,5},{4,2},{5,3},{6,0},{7,1},{8,14},{9,15},{10,... | collective-permute-start | bytes 86024 | tf_op jit(solution)/shard_map/ppermute | solution.py:331
  19.1 0.0 collective-permute-start.5
  19.1 1.9 %collective-permute-start.6 = (bf16[112,128]{1,0:T(8,128)(2,1)S(1)}, bf16[112,128]{1,0:T(8,128)(2,1)S(1)}, u32[]{:S(2)}, u32[]{:S(2)}) collective-permute-start(bf16[112,128]{1,0:T(8,128)(2,1)S(1)} %get-tuple-element.42), channel_id=1, source_target_pairs={{0,2},{1,3},{2,0},{3,1},{4,6},{5,7},{6,4},{7,5},{8,10},{9,11},{10,... | collective-permute-start | bytes 86024 | tf_op jit(solution)/shard_map/ppermute | solution.py:331
  20.9 2.4 %collective-permute-start.8 = (bf16[180,384]{1,0:T(8,128)(2,1)S(1)}, bf16[180,384]{1,0:T(8,128)(2,1)S(1)}, u32[]{:S(2)}, u32[]{:S(2)}) collective-permute-start(bf16[180,384]{1,0:T(8,128)(2,1)S(1)} %get-tuple-element.43), channel_id=1, source_target_pairs={{0,24},{8,0},{16,8},{24,16},{1,25},{9,1},{17,9},{25,17},{2,26},{10... | collective-permute-start | bytes 414728 | tf_op jit(solution)/shard_map/ppermute | solution.py:28
  23.4 0.0 collective-permute-done.4.refs_1_
  23.4 0.4 %collective-permute-done.5.refs_2_ = bf16[112,128]{1,0:T(8,128)(2,1)S(1)} collective-permute-done((bf16[112,128]{1,0:T(8,128)(2,1)S(1)}, bf16[112,128]{1,0:T(8,128)(2,1)S(1)}, u32[]{:S(2)}, u32[]{:S(2)}) %collective-permute-start.5) | collective-permute-done | bytes 28704 | tf_op jit(solution)/shard_map/ppermute | solution.py:331
  23.8 0.0 collective-permute-done.6.refs_3_
  23.8 2.5 %collective-permute-start.7 = (bf16[4,112,128]{2,1,0:T(8,128)(2,1)S(1)}, bf16[4,112,128]{2,1,0:T(8,128)(2,1)S(1)}, u32[]{:S(2)}, u32[]{:S(2)}) collective-permute-start(bf16[4,112,128]{2,1,0:T(8,128)(2,1)S(1)} %shard_map.143), channel_id=1, source_target_pairs={{0,24},{8,0},{16,8},{24,16},{1,25},{9,1},{17,9},{25,17},{2,26},{10... | collective-permute-start | bytes 344072 | tf_op jit(solution)/shard_map/ppermute | solution.py:28
  26.3 1.1 %shard_map.145 = (f32[2,48,96]{2,1,0:T(8,128)}, f32[2,48,96]{2,1,0:T(8,128)}, f32[2,48]{1,0:T(2,128)}) custom-call(bf16[288,256]{1,0:T(8,128)(2,1)S(1)} %get-tuple-element.45.points0, bf16[288,256]{1,0:T(8,128)(2,1)S(1)} %get-tuple-element.46.hidden0, bf16[288,256]{1,0:T(8,128)(2,1)S(1)} %get-tuple-element.47.points1, ...), custom_call_target="tpu_custom_call" | custom-call | flops 2000000000 | bytes 1000000 | tf_op jit(solution)/shard_map/pallas_call | solution.py:289
  27.5 0.0 collective-permute-done.8.field
  27.5 1.2 %collective-permute-done.7.four = bf16[4,112,128]{2,1,0:T(8,128)(2,1)S(1)} collective-permute-done((bf16[4,112,128]{2,1,0:T(8,128)(2,1)S(1)}, bf16[4,112,128]{2,1,0:T(8,128)(2,1)S(1)}, u32[]{:S(2)}, u32[]{:S(2)}) %collective-permute-start.7) | collective-permute-done | bytes 114720 | tf_op jit(solution)/shard_map/ppermute | solution.py:28
  28.7 1.1 %shard_map.144 = bf16[180,384]{1,0:T(8,128)(2,1)} custom-call(bf16[4,112,128]{2,1,0:T(8,128)(2,1)S(1)} %collective-permute-done.7.four, bf16[180,384]{1,0:T(8,128)(2,1)S(1)} %collective-permute-done.8.field, bf16[180,144]{1,0:T(8,128)(2,1)S(1)} %get-tuple-element.44.table), custom_call_target="tpu_custom_call" | custom-call | flops 100000000 | bytes 1000000 | tf_op jit(solution)/shard_map/pallas_call | solution.py:289
  (2 shorter events, 0.0 us)
Async XLA Ops:
  2.3 7.5 %collective-permute-start = (bf16[72,384]{1,0:T(8,128)(2,1)S(1)}, bf16[72,384]{1,0:T(8,128)(2,1)S(1)}, u32[]{:S(2)}, u32[]{:S(2)}) collective-permute-start(bf16[72,384]{1,0:T(8,128)(2,1)S(1)} %get-tuple-element.30), channel_id=1, source_target_pairs={{0,6},{1,7},{2,4},{3,5},{4,2},{5,3},{6,0},{7,1},{8,14},{9,15},{10,... | collective-permute-start | bytes 165896 | tf_op jit(solution)/shard_map/ppermute | solution.py:331
  7.5 5.1 %collective-permute-start.1 = (bf16[72,384]{1,0:T(8,128)(2,1)S(1)}, bf16[72,384]{1,0:T(8,128)(2,1)S(1)}, u32[]{:S(2)}, u32[]{:S(2)}) collective-permute-start(bf16[72,384]{1,0:T(8,128)(2,1)S(1)} %get-tuple-element.31), channel_id=1, source_target_pairs={{0,4},{1,5},{2,6},{3,7},{4,0},{5,1},{6,2},{7,3},{8,12},{9,13},{10,... | collective-permute-start | bytes 165896 | tf_op jit(solution)/shard_map/ppermute | solution.py:331
  7.5 5.1 %collective-permute-start.2 = (bf16[72,384]{1,0:T(8,128)(2,1)S(1)}, bf16[72,384]{1,0:T(8,128)(2,1)S(1)}, u32[]{:S(2)}, u32[]{:S(2)}) collective-permute-start(bf16[72,384]{1,0:T(8,128)(2,1)S(1)} %get-tuple-element.32), channel_id=1, source_target_pairs={{0,2},{1,3},{2,0},{3,1},{4,6},{5,7},{6,4},{7,5},{8,10},{9,11},{10,... | collective-permute-start | bytes 165896 | tf_op jit(solution)/shard_map/ppermute | solution.py:331
  12.5 1.5 %collective-permute-start.3 = (bf16[4,72,384]{2,1,0:T(8,128)(2,1)S(1)}, bf16[4,72,384]{2,1,0:T(8,128)(2,1)S(1)}, u32[]{:S(2)}, u32[]{:S(2)}) collective-permute-start(bf16[4,72,384]{2,1,0:T(8,128)(2,1)S(1)} %shard_map.140), channel_id=1, source_target_pairs={{0,1},{1,0},{2,3},{3,2},{4,5},{5,4},{6,7},{7,6},{8,9},{9,8},{10,11... | collective-permute-start | bytes 663560 | tf_op jit(solution)/shard_map/ppermute | solution.py:373
  16.5 6.9 %collective-permute-start.4 = (bf16[112,128]{1,0:T(8,128)(2,1)S(1)}, bf16[112,128]{1,0:T(8,128)(2,1)S(1)}, u32[]{:S(2)}, u32[]{:S(2)}) collective-permute-start(bf16[112,128]{1,0:T(8,128)(2,1)S(1)} %get-tuple-element.40), channel_id=1, source_target_pairs={{0,6},{1,7},{2,4},{3,5},{4,2},{5,3},{6,0},{7,1},{8,14},{9,15},{10,... | collective-permute-start | bytes 86024 | tf_op jit(solution)/shard_map/ppermute | solution.py:331
  19.1 4.8 %collective-permute-start.5 = (bf16[112,128]{1,0:T(8,128)(2,1)S(1)}, bf16[112,128]{1,0:T(8,128)(2,1)S(1)}, u32[]{:S(2)}, u32[]{:S(2)}) collective-permute-start(bf16[112,128]{1,0:T(8,128)(2,1)S(1)} %get-tuple-element.41), channel_id=1, source_target_pairs={{0,4},{1,5},{2,6},{3,7},{4,0},{5,1},{6,2},{7,3},{8,12},{9,13},{10,... | collective-permute-start | bytes 86024 | tf_op jit(solution)/shard_map/ppermute | solution.py:331
  19.1 4.8 %collective-permute-start.6 = (bf16[112,128]{1,0:T(8,128)(2,1)S(1)}, bf16[112,128]{1,0:T(8,128)(2,1)S(1)}, u32[]{:S(2)}, u32[]{:S(2)}) collective-permute-start(bf16[112,128]{1,0:T(8,128)(2,1)S(1)} %get-tuple-element.42), channel_id=1, source_target_pairs={{0,2},{1,3},{2,0},{3,1},{4,6},{5,7},{6,4},{7,5},{8,10},{9,11},{10,... | collective-permute-start | bytes 86024 | tf_op jit(solution)/shard_map/ppermute | solution.py:331
  20.9 6.5 %collective-permute-start.8 = (bf16[180,384]{1,0:T(8,128)(2,1)S(1)}, bf16[180,384]{1,0:T(8,128)(2,1)S(1)}, u32[]{:S(2)}, u32[]{:S(2)}) collective-permute-start(bf16[180,384]{1,0:T(8,128)(2,1)S(1)} %get-tuple-element.43), channel_id=1, source_target_pairs={{0,24},{8,0},{16,8},{24,16},{1,25},{9,1},{17,9},{25,17},{2,26},{10... | collective-permute-start | bytes 414728 | tf_op jit(solution)/shard_map/ppermute | solution.py:28
  23.8 4.9 %collective-permute-start.7 = (bf16[4,112,128]{2,1,0:T(8,128)(2,1)S(1)}, bf16[4,112,128]{2,1,0:T(8,128)(2,1)S(1)}, u32[]{:S(2)}, u32[]{:S(2)}) collective-permute-start(bf16[4,112,128]{2,1,0:T(8,128)(2,1)S(1)} %shard_map.143), channel_id=1, source_target_pairs={{0,24},{8,0},{16,8},{24,16},{1,25},{9,1},{17,9},{25,17},{2,26},{10... | collective-permute-start | bytes 344072 | tf_op jit(solution)/shard_map/ppermute | solution.py:28

commit v12 on v11

--- a/solution.py
+++ b/solution.py
@@ -251,7 +251,7 @@
         out[...] = pack(band).astype(BF16)
 
 
-def products_kernel(points0, hidden0, points1, hidden1, grad_pre, grad_y, gw1, gw2, gb1):
+def products_kernel(points0, hidden0, points1, hidden1, grad_pre, grad_y, _, gw1, gw2, gb1):
     core = lax.rem(lax.axis_index("lat"), 2)
     half = BS // 2
     for ref, grads, values in ((gw1, grad_pre, (points0, points1)), (gw2, grad_y, (hidden0, hidden1))):
@@ -404,11 +404,12 @@
         products_kernel,
         (matrix, matrix, shape((2, BS // 2), F32)),
         [],
-        (points0, hidden0, points1, hidden1, grad_pre, grad_y),
+        (points0, hidden0, points1, hidden1, grad_pre, grad_y, next_field),
         (),
         2 * 10**9,
     )
-    four = turn(call(join_kernel, shape((NB, *packed.shape), BF16), [], backs, ()), "section")
+    four = call(join_kernel, shape((NB, *packed.shape), BF16), [], (*backs, gb1), ())
+    four = turn(four, "section")
     shifted = call(
         functools.partial(compose_kernel, lax.axis_size("section") - 1),
         shape((length, width), BF16),

time: 30 us -> 32.1 us (1.070)
  waiting for transfers between devices: 5.55 us -> 8.3 us
  starting transfers between devices: 15.2 us -> 13.9 us
  local copies, waits for them, and re-layouts: 0 us -> 0.68 us
    ppermute x2, waiting for transfers between devices: 1.25 us -> 3.77 us  [turn(): lax.ppermute(value, axis, [(i, (i - 1) % length) for i in range(length)])]
    ppermute x2, starting transfers between devices: 4.94 us -> 3.58 us  [turn(): lax.ppermute(value, axis, [(i, (i - 1) % length) for i in range(length)])]
    ppermute x6, waiting for transfers between devices: 3.2 us -> 4.54 us  [swap(): lax.ppermute(chunks[d], 'lat', pairs[d])]
    ppermute x1, waiting for transfers between devices: 1.1 us -> 0.01 us  [paired_blocks(): other = lax.ppermute(own, 'lat', [(i, i ^ 1) for i in range(2 * NB)])]
    unnamed x0 -> x2, local copies, waits for them, and re-layouts: none -> 0.68 us
  transfers between devices with their start and end apart: 9 -> 9, of which waited for: 5 -> 5; matrix products, arithmetic and copies ran while one was open for 0% -> 0% of each run, Pallas kernels for 10% -> 17%
where the time goes in v12:
time: 32.1 us; the launch traced here: 31.9 us
  starting transfers between devices  13.9 us (43%)
  Pallas kernels  8.34 us (26%)
  waiting for transfers between devices  8.3 us (26%)
  between operations  0.7 us (2%)
  local copies, waits for them, and re-layouts  0.68 us (2%)
    ppermute x6, starting transfers between devices, swap(): lax.ppermute(chunks[d], 'lat', pairs[d])  10.2 us
    pallas_call x8, Pallas kernels, call(): pl.pallas_call(kernel, out_shape=outs, in_specs=[VMEM] * len(near) + [HBM...  8.34 us
    ppermute x6, waiting for transfers between devices, swap(): lax.ppermute(chunks[d], 'lat', pairs[d])  4.54 us
    ppermute x2, waiting for transfers between devices, turn(): lax.ppermute(value, axis, [(i, (i - 1) % length) for i in range(length)])  3.77 us
    ppermute x2, starting transfers between devices, turn(): lax.ppermute(value, axis, [(i, (i - 1) % length) for i in range(length)])  3.58 us
    unnamed x2, local copies, waits for them, and re-layouts  0.68 us
  transfers between devices with their start and end apart: 9, of which 5 were waited for; matrix products, arithmetic and copies ran while one was open for 0% of the time, Pallas kernels for 17%

profile of v12, /device:TPU:0, one launch (start us, length us, event | category | flops | bytes accessed | tf_op | source)
XLA Modules:
  0.0 31.9 jit_solution(1945094498320165361)
XLA Ops:
  0.6 1.7 %shard_map.138 = (bf16[72,384]{1,0:T(8,128)(2,1)S(1)}, bf16[72,384]{1,0:T(8,128)(2,1)S(1)}, bf16[72,384]{1,0:T(8,128)(2,1)S(1)}, bf16[72,384]{1,0:T(8,128)(2,1)S(1)}) custom-call(s32[8]{0:T(128)} %refs_0_.3, s32[8]{0:T(128)} %refs_11_.1, bf16[180,384]{1,0:T(8,128)(2,1)} %bitcast.17, bf16[144,180]{1,0:T(8,128)(2,1)} %constant.10.clone.refs_3_, ...), custom_call_target="tpu_custom_call" | custom-call | flops 100000000 | bytes 1000000 | tf_op jit(solution)/shard_map/pallas_call | solution.py:289
  2.3 5.1 %collective-permute-start = (bf16[72,384]{1,0:T(8,128)(2,1)S(1)}, bf16[72,384]{1,0:T(8,128)(2,1)S(1)}, u32[]{:S(2)}, u32[]{:S(2)}) collective-permute-start(bf16[72,384]{1,0:T(8,128)(2,1)S(1)} %get-tuple-element.30), channel_id=1, source_target_pairs={{0,6},{1,7},{2,4},{3,5},{4,2},{5,3},{6,0},{7,1},{8,14},{9,15},{10,... | collective-permute-start | bytes 165896 | tf_op jit(solution)/shard_map/ppermute | solution.py:331
  7.5 0.0 collective-permute-start.1
  7.5 0.6 %collective-permute-start.2 = (bf16[72,384]{1,0:T(8,128)(2,1)S(1)}, bf16[72,384]{1,0:T(8,128)(2,1)S(1)}, u32[]{:S(2)}, u32[]{:S(2)}) collective-permute-start(bf16[72,384]{1,0:T(8,128)(2,1)S(1)} %get-tuple-element.32), channel_id=1, source_target_pairs={{0,2},{1,3},{2,0},{3,1},{4,6},{5,7},{6,4},{7,5},{8,10},{9,11},{10,... | collective-permute-start | bytes 165896 | tf_op jit(solution)/shard_map/ppermute | solution.py:331
  8.1 1.6 %shard_map.139 = (bf16[256,256]{1,0:T(8,128)(2,1)S(1)}, bf16[256,256]{1,0:T(8,128)(2,1)S(1)}, f32[1,256]{1,0:T(1,128)S(1)}, bf16[576,576]{1,0:T(8,128)(2,1)S(1)}...) custom-call(s32[8]{0:T(128)} %refs_0_.3, s32[8]{0:T(128)} %refs_11_.1, ...), custom_call_target="tpu_custom_call" | custom-call | flops 2000000000 | bytes 1000000 | tf_op jit(solution)/shard_map/pallas_call | solution.py:289
  9.7 0.1 collective-permute-done.refs_1_
  9.8 2.7 %collective-permute-done.1.refs_2_ = bf16[72,384]{1,0:T(8,128)(2,1)S(1)} collective-permute-done((bf16[72,384]{1,0:T(8,128)(2,1)S(1)}, bf16[72,384]{1,0:T(8,128)(2,1)S(1)}, u32[]{:S(2)}, u32[]{:S(2)}) %collective-permute-start.1) | collective-permute-done | bytes 55328 | tf_op jit(solution)/shard_map/ppermute | solution.py:331
  12.5 0.0 collective-permute-done.2.refs_3_
  12.5 0.1 collective-permute-start.3
  12.6 2.5 %collective-permute-start.7 = (bf16[180,384]{1,0:T(8,128)(2,1)S(1)}, bf16[180,384]{1,0:T(8,128)(2,1)S(1)}, u32[]{:S(2)}, u32[]{:S(2)}) collective-permute-start(bf16[180,384]{1,0:T(8,128)(2,1)S(1)} %get-tuple-element.49), channel_id=1, source_target_pairs={{0,24},{8,0},{16,8},{24,16},{1,25},{9,1},{17,9},{25,17},{2,26},{10... | collective-permute-start | bytes 414728 | tf_op jit(solution)/shard_map/ppermute | solution.py:28
  15.1 0.4 %shard_map.141 = (bf16[288,256]{1,0:T(8,128)(2,1)S(1)}, bf16[288,256]{1,0:T(8,128)(2,1)S(1)}, f32[288,256]{1,0:T(8,128)S(1)}) custom-call(bf16[72,384]{1,0:T(8,128)(2,1)S(1)} %get-tuple-element.29.refs_0_, bf16[72,384]{1,0:T(8,128)(2,1)S(1)} %collective-permute-done.refs_1_, bf16[72,384]{1,0:T(8,128)(2,1)S(1)} %collective-permute-done.1.refs_2_, ...), custom_call_target="tpu_custom_call" | custom-call | flops 2000000000 | bytes 1000000 | tf_op jit(solution)/shard_map/pallas_call | solution.py:289
  15.5 2.4 %shard_map.142 = (bf16[112,128]{1,0:T(8,128)(2,1)S(1)}, bf16[112,128]{1,0:T(8,128)(2,1)S(1)}, bf16[112,128]{1,0:T(8,128)(2,1)S(1)}, bf16[112,128]{1,0:T(8,128)(2...) custom-call(bf16[72,384]{1,0:T(8,128)(2,1)S(1)} %get-tuple-element.2, ...), custom_call_target="tpu_custom_call" | custom-call | flops 100000000 | bytes 1000000 | tf_op jit(solution)/shard_map/pallas_call | solution.py:289
  17.9 2.6 %collective-permute-start.4 = (bf16[112,128]{1,0:T(8,128)(2,1)S(1)}, bf16[112,128]{1,0:T(8,128)(2,1)S(1)}, u32[]{:S(2)}, u32[]{:S(2)}) collective-permute-start(bf16[112,128]{1,0:T(8,128)(2,1)S(1)} %get-tuple-element.40), channel_id=1, source_target_pairs={{0,6},{1,7},{2,4},{3,5},{4,2},{5,3},{6,0},{7,1},{8,14},{9,15},{10,... | collective-permute-start | bytes 86024 | tf_op jit(solution)/shard_map/ppermute | solution.py:331
  20.5 0.0 collective-permute-start.5
  20.5 1.9 %collective-permute-start.6 = (bf16[112,128]{1,0:T(8,128)(2,1)S(1)}, bf16[112,128]{1,0:T(8,128)(2,1)S(1)}, u32[]{:S(2)}, u32[]{:S(2)}) collective-permute-start(bf16[112,128]{1,0:T(8,128)(2,1)S(1)} %get-tuple-element.42), channel_id=1, source_target_pairs={{0,2},{1,3},{2,0},{3,1},{4,6},{5,7},{6,4},{7,5},{8,10},{9,11},{10,... | collective-permute-start | bytes 86024 | tf_op jit(solution)/shard_map/ppermute | solution.py:331
  22.4 0.0 collective-permute-done.7._.field
  22.4 1.1 %shard_map.143 = (f32[2,48,96]{2,1,0:T(8,128)}, f32[2,48,96]{2,1,0:T(8,128)}, f32[2,48]{1,0:T(2,128)}) custom-call(bf16[288,256]{1,0:T(8,128)(2,1)S(1)} %get-tuple-element.43.points0, bf16[288,256]{1,0:T(8,128)(2,1)S(1)} %get-tuple-element.44.hidden0, bf16[288,256]{1,0:T(8,128)(2,1)S(1)} %get-tuple-element.45.points1, ...), custom_call_target="tpu_custom_call" | custom-call | flops 2000000000 | bytes 1000000 | tf_op jit(solution)/shard_map/pallas_call | solution.py:289
  23.5 0.4 %collective-permute-done.4.refs_1_ = bf16[112,128]{1,0:T(8,128)(2,1)S(1)} collective-permute-done((bf16[112,128]{1,0:T(8,128)(2,1)S(1)}, bf16[112,128]{1,0:T(8,128)(2,1)S(1)}, u32[]{:S(2)}, u32[]{:S(2)}) %collective-permute-start.4) | collective-permute-done | bytes 28704 | tf_op jit(solution)/shard_map/ppermute | solution.py:331
  23.9 1.3 %collective-permute-done.5.refs_2_ = bf16[112,128]{1,0:T(8,128)(2,1)S(1)} collective-permute-done((bf16[112,128]{1,0:T(8,128)(2,1)S(1)}, bf16[112,128]{1,0:T(8,128)(2,1)S(1)}, u32[]{:S(2)}, u32[]{:S(2)}) %collective-permute-start.5) | collective-permute-done | bytes 28704 | tf_op jit(solution)/shard_map/ppermute | solution.py:331
  25.2 0.0 collective-permute-done.6.refs_3_
  25.2 0.7 %copy-done = f32[2,48]{1,0:T(2,128)S(1)} copy-done((f32[2,48]{1,0:T(2,128)S(1)}, f32[2,48]{1,0:T(2,128)}, u32[]{:S(2)}) %copy-start) | copy-done | bytes 408
  25.9 1.1 %collective-permute-start.8 = (bf16[4,112,128]{2,1,0:T(8,128)(2,1)S(1)}, bf16[4,112,128]{2,1,0:T(8,128)(2,1)S(1)}, u32[]{:S(2)}, u32[]{:S(2)}) collective-permute-start(bf16[4,112,128]{2,1,0:T(8,128)(2,1)S(1)} %shard_map.144), channel_id=1, source_target_pairs={{0,24},{8,0},{16,8},{24,16},{1,25},{9,1},{17,9},{25,17},{2,26},{10... | collective-permute-start | bytes 344072 | tf_op jit(solution)/shard_map/ppermute | solution.py:28
  27.0 3.8 %collective-permute-done.8.four = bf16[4,112,128]{2,1,0:T(8,128)(2,1)S(1)} collective-permute-done((bf16[4,112,128]{2,1,0:T(8,128)(2,1)S(1)}, bf16[4,112,128]{2,1,0:T(8,128)(2,1)S(1)}, u32[]{:S(2)}, u32[]{:S(2)}) %collective-permute-start.8) | collective-permute-done | bytes 114720 | tf_op jit(solution)/shard_map/ppermute | solution.py:28
  30.8 1.1 %shard_map.145 = bf16[180,384]{1,0:T(8,128)(2,1)} custom-call(bf16[4,112,128]{2,1,0:T(8,128)(2,1)S(1)} %collective-permute-done.8.four, bf16[180,384]{1,0:T(8,128)(2,1)S(1)} %collective-permute-done.7._.field, bf16[180,144]{1,0:T(8,128)(2,1)S(1)} %get-tuple-element.51.table), custom_call_target="tpu_custom_call" | custom-call | flops 100000000 | bytes 1000000 | tf_op jit(solution)/shard_map/pallas_call | solution.py:289
  (4 shorter events, 0.0 us)
Async XLA Ops:
  2.3 7.5 %collective-permute-start = (bf16[72,384]{1,0:T(8,128)(2,1)S(1)}, bf16[72,384]{1,0:T(8,128)(2,1)S(1)}, u32[]{:S(2)}, u32[]{:S(2)}) collective-permute-start(bf16[72,384]{1,0:T(8,128)(2,1)S(1)} %get-tuple-element.30), channel_id=1, source_target_pairs={{0,6},{1,7},{2,4},{3,5},{4,2},{5,3},{6,0},{7,1},{8,14},{9,15},{10,... | collective-permute-start | bytes 165896 | tf_op jit(solution)/shard_map/ppermute | solution.py:331
  7.5 5.1 %collective-permute-start.1 = (bf16[72,384]{1,0:T(8,128)(2,1)S(1)}, bf16[72,384]{1,0:T(8,128)(2,1)S(1)}, u32[]{:S(2)}, u32[]{:S(2)}) collective-permute-start(bf16[72,384]{1,0:T(8,128)(2,1)S(1)} %get-tuple-element.31), channel_id=1, source_target_pairs={{0,4},{1,5},{2,6},{3,7},{4,0},{5,1},{6,2},{7,3},{8,12},{9,13},{10,... | collective-permute-start | bytes 165896 | tf_op jit(solution)/shard_map/ppermute | solution.py:331
  7.5 5.1 %collective-permute-start.2 = (bf16[72,384]{1,0:T(8,128)(2,1)S(1)}, bf16[72,384]{1,0:T(8,128)(2,1)S(1)}, u32[]{:S(2)}, u32[]{:S(2)}) collective-permute-start(bf16[72,384]{1,0:T(8,128)(2,1)S(1)} %get-tuple-element.32), channel_id=1, source_target_pairs={{0,2},{1,3},{2,0},{3,1},{4,6},{5,7},{6,4},{7,5},{8,10},{9,11},{10,... | collective-permute-start | bytes 165896 | tf_op jit(solution)/shard_map/ppermute | solution.py:331
  12.5 2.9 %collective-permute-start.3 = (bf16[4,72,384]{2,1,0:T(8,128)(2,1)S(1)}, bf16[4,72,384]{2,1,0:T(8,128)(2,1)S(1)}, u32[]{:S(2)}, u32[]{:S(2)}) collective-permute-start(bf16[4,72,384]{2,1,0:T(8,128)(2,1)S(1)} %shard_map.140), channel_id=1, source_target_pairs={{0,1},{1,0},{2,3},{3,2},{4,5},{5,4},{6,7},{7,6},{8,9},{9,8},{10,11... | collective-permute-start | bytes 663560 | tf_op jit(solution)/shard_map/ppermute | solution.py:373
  12.6 9.7 %collective-permute-start.7 = (bf16[180,384]{1,0:T(8,128)(2,1)S(1)}, bf16[180,384]{1,0:T(8,128)(2,1)S(1)}, u32[]{:S(2)}, u32[]{:S(2)}) collective-permute-start(bf16[180,384]{1,0:T(8,128)(2,1)S(1)} %get-tuple-element.49), channel_id=1, source_target_pairs={{0,24},{8,0},{16,8},{24,16},{1,25},{9,1},{17,9},{25,17},{2,26},{10... | collective-permute-start | bytes 414728 | tf_op jit(solution)/shard_map/ppermute | solution.py:28
  17.9 6.0 %collective-permute-start.4 = (bf16[112,128]{1,0:T(8,128)(2,1)S(1)}, bf16[112,128]{1,0:T(8,128)(2,1)S(1)}, u32[]{:S(2)}, u32[]{:S(2)}) collective-permute-start(bf16[112,128]{1,0:T(8,128)(2,1)S(1)} %get-tuple-element.40), channel_id=1, source_target_pairs={{0,6},{1,7},{2,4},{3,5},{4,2},{5,3},{6,0},{7,1},{8,14},{9,15},{10,... | collective-permute-start | bytes 86024 | tf_op jit(solution)/shard_map/ppermute | solution.py:331
  20.5 4.8 %collective-permute-start.5 = (bf16[112,128]{1,0:T(8,128)(2,1)S(1)}, bf16[112,128]{1,0:T(8,128)(2,1)S(1)}, u32[]{:S(2)}, u32[]{:S(2)}) collective-permute-start(bf16[112,128]{1,0:T(8,128)(2,1)S(1)} %get-tuple-element.41), channel_id=1, source_target_pairs={{0,4},{1,5},{2,6},{3,7},{4,0},{5,1},{6,2},{7,3},{8,12},{9,13},{10,... | collective-permute-start | bytes 86024 | tf_op jit(solution)/shard_map/ppermute | solution.py:331
  20.5 4.8 %collective-permute-start.6 = (bf16[112,128]{1,0:T(8,128)(2,1)S(1)}, bf16[112,128]{1,0:T(8,128)(2,1)S(1)}, u32[]{:S(2)}, u32[]{:S(2)}) collective-permute-start(bf16[112,128]{1,0:T(8,128)(2,1)S(1)} %get-tuple-element.42), channel_id=1, source_target_pairs={{0,2},{1,3},{2,0},{3,1},{4,6},{5,7},{6,4},{7,5},{8,10},{9,11},{10,... | collective-permute-start | bytes 86024 | tf_op jit(solution)/shard_map/ppermute | solution.py:331
  25.2 0.7 %copy-start = (f32[2,48]{1,0:T(2,128)S(1)}, f32[2,48]{1,0:T(2,128)}, u32[]{:S(2)}) copy-start(f32[2,48]{1,0:T(2,128)} %get-tuple-element.50.refs_4_) | copy-start | bytes 1156
  25.9 4.8 %collective-permute-start.8 = (bf16[4,112,128]{2,1,0:T(8,128)(2,1)S(1)}, bf16[4,112,128]{2,1,0:T(8,128)(2,1)S(1)}, u32[]{:S(2)}, u32[]{:S(2)}) collective-permute-start(bf16[4,112,128]{2,1,0:T(8,128)(2,1)S(1)} %shard_map.144), channel_id=1, source_target_pairs={{0,24},{8,0},{16,8},{24,16},{1,25},{9,1},{17,9},{25,17},{2,26},{10... | collective-permute-start | bytes 344072 | tf_op jit(solution)/shard_map/ppermute | solution.py:28

commit v13 on v11

--- a/solution.py
+++ b/solution.py
@@ -169,11 +169,13 @@
 
 
 ORDER = (0, 3, 2, 1)
+FIELD_ROWS = 192
 
 
 def join_kernel(*refs):
-    for d, ref in zip(ORDER, refs):
-        refs[-1][d] = ref[...]
+    out = refs[-1]
+    for i in range(out.shape[0]):
+        out[i] = refs[i][...]
 
 
 def pack(band):
@@ -215,12 +217,12 @@
 
 
 def filter_kernel(*refs):
-    owns, (other, slope_own, mat1, mat2, bias, lat, lat_t, assign_hbm) = refs[:4], refs[4:12]
-    outs, (points, hidden, grad_pre, grad_y) = refs[12:16], refs[16:20]
-    assign, by_lat, by_pair, slope, sems = refs[20:]
+    owns, (other, slope_own, mat1, mat2, bias, lat, lat_t, own_field, assign_hbm) = refs[:4], refs[4:13]
+    outs, (bundle, points, hidden, grad_pre, grad_y) = refs[13:16], refs[16:21]
+    assign, by_lat, by_pair, slope, sems = refs[21:]
     copies = fetch(sems, (assign_hbm,), (assign,))
     core = lax.rem(lax.axis_index("lat"), 2)
-    sides = [[owns[i][...].astype(F32) for i in ORDER], [other[d].astype(F32) for d in range(NB)]]
+    sides = [[owns[i][...].astype(F32) for i in ORDER], [other[i].astype(F32) for i in ORDER]]
     silu_points(sides[1], mat1, bias, by_pair, points, hidden, slope)
     wait(copies)
     for side, chunks in zip((core, 1 - core), sides):
@@ -246,9 +248,17 @@
     left = jnp.where(core == 0, inner[0], inner[1])
     right = jnp.where(core == 0, inner[1], inner[0])
     inner = jnp.concatenate([left, right], axis=1).astype(BF16)
-    for d, out in enumerate(outs):
-        band = dot(lat_t[assign[2 * partner(d) + core]], inner, (1, 0))
-        out[...] = pack(band).astype(BF16)
+    length = own_field.shape[0]
+    bundle[0:length] = own_field[...]
+    for i, d in enumerate(ORDER):
+        band = pack(dot(lat_t[assign[2 * partner(d) + core]], inner, (1, 0)))
+        if d:
+            outs[i - 1][...] = band.astype(BF16)
+        else:
+            rows = bundle.shape[0] - FIELD_ROWS
+            band = jnp.concatenate([band, jnp.zeros((3 * rows - band.shape[0], LANES), F32)], axis=0)
+            band = [band[i * rows : (i + 1) * rows] for i in range(3)]
+            bundle[FIELD_ROWS:] = jnp.concatenate(band, axis=1).astype(BF16)
 
 
 def products_kernel(points0, hidden0, points1, hidden1, grad_pre, grad_y, gw1, gw2, gb1):
@@ -266,16 +276,19 @@
         gb1[c : c + 1] = jnp.where(core == 0, line[:, :half], line[:, half:BS])
 
 
-def compose_kernel(last, four, field, table, out, by_block):
+def compose_kernel(last, three, bundle, table, out, by_block):
     rows = by_block.shape[1]
-    for d in range(NB):
-        by_block[partner(d)] = jnp.concatenate(unpack(four[d].astype(F32), rows), axis=1)
+    own = bundle[FIELD_ROWS:].astype(F32)
+    own = jnp.concatenate([own[:, i * LANES : (i + 1) * LANES] for i in range(3)], axis=0)
+    chunks = [own[: three.shape[1]]] + [three[i].astype(F32) for i in range(3)]
+    for d, chunk in zip(ORDER, chunks):
+        by_block[partner(d)] = jnp.concatenate(unpack(chunk, rows), axis=1)
     groups = [
         dense([by_block[n, :, g * LANES : (g + 1) * LANES] for n in range(NB)]) for g in range(2)
     ]
     groups = jnp.concatenate(groups, axis=0).astype(BF16)
     mixed = jnp.dot(table[...], groups, preferred_element_type=F32).astype(BF16)
-    whole = field[...].astype(F32) + mixed.astype(F32)
+    whole = bundle[0 : out.shape[0]].astype(F32) + mixed.astype(F32)
     out[...] = jnp.where(lax.axis_index("section") == last, 0.0, whole).astype(BF16)
 
 
@@ -327,8 +340,8 @@
     forward = jnp.asarray(by_group(forward).T)
 
     def swap(chunks):
-        pairs = [[(i, i ^ (2 * d)) for i in range(2 * NB)] for d in range(NB)]
-        return [lax.ppermute(chunks[d], "lat", pairs[d]) if d else chunks[0] for d in ORDER]
+        pairs = [[(i, i ^ (2 * d)) for i in range(2 * NB)] for d in ORDER[1:]]
+        return [lax.ppermute(chunk, "lat", p) for chunk, p in zip(chunks, pairs)]
 
     field = grad_out.reshape(length, width)
     shape = jax.ShapeDtypeStruct
@@ -341,7 +354,7 @@
         (),
         far,
     )
-    received = swap(sent)
+    received = [sent[0], *swap([sent[d] for d in ORDER[1:]])]
     far = (mode_counts, assignment, w1[0], w2[0], b1[0], forward)
     scratch, _ = scratch_for(*far)
     far = (*far, lat, lat_t, field)
@@ -362,7 +375,6 @@
         far,
         2 * 10**9,
     )
-    next_field = turn(field, "section")
     own = call(
         join_kernel,
         shape((NB, rows, width), BF16),
@@ -385,9 +397,11 @@
     packed = shape((rows + rows // 2 + 4, LANES), BF16)
     scratch, sems = scratch_for(assignment)
     both = shape((2, NB * rows, wide), BF16)
-    *chunks, points1, hidden1, grad_pre, grad_y = call(
+    tail = -(-packed.shape[0] // 48) * 16
+    bundle = shape((FIELD_ROWS + tail, width), BF16)
+    *chunks, bundle, points1, hidden1, grad_pre, grad_y = call(
         filter_kernel,
-        (packed,) * NB + (vectors, vectors, both, both),
+        (packed,) * (NB - 1) + (bundle, vectors, vectors, both, both),
         scratch
         + [
             pltpu.VMEM((n_rows, rows, wide), F32),
@@ -395,7 +409,7 @@
             pltpu.VMEM((NB * rows, wide), F32),
             sems,
         ],
-        (*received, other, slope0, mat1, mat2, bias, lat, lat_t),
+        (*received, other, slope0, mat1, mat2, bias, lat, lat_t, field),
         (assignment,),
     )
     backs = swap(chunks)
@@ -408,12 +422,14 @@
         (),
         2 * 10**9,
     )
-    four = turn(call(join_kernel, shape((NB, *packed.shape), BF16), [], backs, ()), "section")
+    three = call(join_kernel, shape((NB - 1, *packed.shape), BF16), [], backs, ())
+    three = turn(three, "section")
+    bundle = turn(bundle, "section")
     shifted = call(
         functools.partial(compose_kernel, lax.axis_size("section") - 1),
         shape((length, width), BF16),
         [by_pair],
-        (four, next_field, forward),
+        (three, bundle, forward),
         (),
     )
     shifted = shifted[None, None]

time: 30 us -> 30 us (level)
  no operation moved by 1% of the time
where the time goes in v13:
time: 30 us; the launch traced here: 29.8 us
  starting transfers between devices  15.2 us (51%)
  Pallas kernels  8.41 us (28%)
  waiting for transfers between devices  5.48 us (18%)
  between operations  0.69 us (2%)
    ppermute x6, starting transfers between devices, swap(): return [lax.ppermute(chunk, 'lat', p) for chunk, p in zip(chunks, pairs)]  10.2 us
    pallas_call x8, Pallas kernels, call(): pl.pallas_call(kernel, out_shape=outs, in_specs=[VMEM] * len(near) + [HBM...  8.41 us
    ppermute x2, starting transfers between devices, turn(): lax.ppermute(value, axis, [(i, (i - 1) % length) for i in range(length)])  4.94 us
    ppermute x6, waiting for transfers between devices, swap(): return [lax.ppermute(chunk, 'lat', p) for chunk, p in zip(chunks, pairs)]  3.2 us
    ppermute x2, waiting for transfers between devices, turn(): lax.ppermute(value, axis, [(i, (i - 1) % length) for i in range(length)])  1.18 us
    ppermute x1, waiting for transfers between devices, paired_blocks(): other = lax.ppermute(own, 'lat', [(i, i ^ 1) for i in range(2 * NB)])  1.1 us
  transfers between devices with their start and end apart: 9, of which 5 were waited for; matrix products, arithmetic and copies ran while one was open for 0% of the time, Pallas kernels for 10%

profile of v13, /device:TPU:0, one launch (start us, length us, event | category | flops | bytes accessed | tf_op | source)
XLA Modules:
  0.0 29.8 jit_solution(16418462332073084293)
XLA Ops:
  0.6 1.7 %shard_map.138 = (bf16[72,384]{1,0:T(8,128)(2,1)S(1)}, bf16[72,384]{1,0:T(8,128)(2,1)S(1)}, bf16[72,384]{1,0:T(8,128)(2,1)S(1)}, bf16[72,384]{1,0:T(8,128)(2,1)S(1)}) custom-call(s32[8]{0:T(128)} %refs_0_.3, s32[8]{0:T(128)} %refs_12_.1, bf16[180,384]{1,0:T(8,128)(2,1)} %bitcast.16, bf16[144,180]{1,0:T(8,128)(2,1)} %constant.10.clone.refs_3_, ...), custom_call_target="tpu_custom_call" | custom-call | flops 100000000 | bytes 1000000 | tf_op jit(solution)/shard_map/pallas_call | solution.py:302
  2.3 5.1 %collective-permute-start = (bf16[72,384]{1,0:T(8,128)(2,1)S(1)}, bf16[72,384]{1,0:T(8,128)(2,1)S(1)}, u32[]{:S(2)}, u32[]{:S(2)}) collective-permute-start(bf16[72,384]{1,0:T(8,128)(2,1)S(1)} %get-tuple-element.30), channel_id=1, source_target_pairs={{0,6},{1,7},{2,4},{3,5},{4,2},{5,3},{6,0},{7,1},{8,14},{9,15},{10,... | collective-permute-start | bytes 165896 | tf_op jit(solution)/shard_map/ppermute | solution.py:344
  7.5 0.0 collective-permute-start.1
  7.5 0.6 %collective-permute-start.2 = (bf16[72,384]{1,0:T(8,128)(2,1)S(1)}, bf16[72,384]{1,0:T(8,128)(2,1)S(1)}, u32[]{:S(2)}, u32[]{:S(2)}) collective-permute-start(bf16[72,384]{1,0:T(8,128)(2,1)S(1)} %get-tuple-element.32), channel_id=1, source_target_pairs={{0,2},{1,3},{2,0},{3,1},{4,6},{5,7},{6,4},{7,5},{8,10},{9,11},{10,... | collective-permute-start | bytes 165896 | tf_op jit(solution)/shard_map/ppermute | solution.py:344
  8.1 1.6 %shard_map.139 = (bf16[256,256]{1,0:T(8,128)(2,1)S(1)}, bf16[256,256]{1,0:T(8,128)(2,1)S(1)}, f32[1,256]{1,0:T(1,128)S(1)}, bf16[576,576]{1,0:T(8,128)(2,1)S(1)}...) custom-call(s32[8]{0:T(128)} %refs_0_.3, s32[8]{0:T(128)} %refs_12_.1, ...), custom_call_target="tpu_custom_call" | custom-call | flops 2000000000 | bytes 1000000 | tf_op jit(solution)/shard_map/pallas_call | solution.py:302
  9.7 0.1 collective-permute-done.refs_1_
  9.8 2.7 %collective-permute-done.1.refs_2_ = bf16[72,384]{1,0:T(8,128)(2,1)S(1)} collective-permute-done((bf16[72,384]{1,0:T(8,128)(2,1)S(1)}, bf16[72,384]{1,0:T(8,128)(2,1)S(1)}, u32[]{:S(2)}, u32[]{:S(2)}) %collective-permute-start.1) | collective-permute-done | bytes 55328 | tf_op jit(solution)/shard_map/ppermute | solution.py:344
  12.5 0.0 collective-permute-done.2.refs_3_
  12.5 0.1 collective-permute-start.3
  12.6 0.4 %shard_map.141 = (bf16[288,256]{1,0:T(8,128)(2,1)S(1)}, bf16[288,256]{1,0:T(8,128)(2,1)S(1)}, f32[288,256]{1,0:T(8,128)S(1)}) custom-call(bf16[72,384]{1,0:T(8,128)(2,1)S(1)} %get-tuple-element.29.refs_0_, bf16[72,384]{1,0:T(8,128)(2,1)S(1)} %collective-permute-done.refs_1_, bf16[72,384]{1,0:T(8,128)(2,1)S(1)} %collective-permute-done.1.refs_2_, ...), custom_call_target="tpu_custom_call" | custom-call | flops 2000000000 | bytes 1000000 | tf_op jit(solution)/shard_map/pallas_call | solution.py:302
  13.0 1.1 %collective-permute-done.3.refs_4_ = bf16[4,72,384]{2,1,0:T(8,128)(2,1)S(1)} collective-permute-done((bf16[4,72,384]{2,1,0:T(8,128)(2,1)S(1)}, bf16[4,72,384]{2,1,0:T(8,128)(2,1)S(1)}, u32[]{:S(2)}, u32[]{:S(2)}) %collective-permute-start.3) | collective-permute-done | bytes 221216 | tf_op jit(solution)/shard_map/ppermute | solution.py:385
  14.1 2.5 %shard_map.142 = (bf16[112,128]{1,0:T(8,128)(2,1)S(1)}, bf16[112,128]{1,0:T(8,128)(2,1)S(1)}, bf16[112,128]{1,0:T(8,128)(2,1)S(1)}, bf16[240,384]{1,0:T(8,128)(2...) custom-call(bf16[72,384]{1,0:T(8,128)(2,1)S(1)} %get-tuple-element.2, ...), custom_call_target="tpu_custom_call" | custom-call | flops 100000000 | bytes 1000000 | tf_op jit(solution)/shard_map/pallas_call | solution.py:302
  16.6 2.6 %collective-permute-start.4 = (bf16[112,128]{1,0:T(8,128)(2,1)S(1)}, bf16[112,128]{1,0:T(8,128)(2,1)S(1)}, u32[]{:S(2)}, u32[]{:S(2)}) collective-permute-start(bf16[112,128]{1,0:T(8,128)(2,1)S(1)} %get-tuple-element.40), channel_id=1, source_target_pairs={{0,6},{1,7},{2,4},{3,5},{4,2},{5,3},{6,0},{7,1},{8,14},{9,15},{10,... | collective-permute-start | bytes 86024 | tf_op jit(solution)/shard_map/ppermute | solution.py:344
  19.1 0.0 collective-permute-start.5
  19.1 1.9 %collective-permute-start.6 = (bf16[112,128]{1,0:T(8,128)(2,1)S(1)}, bf16[112,128]{1,0:T(8,128)(2,1)S(1)}, u32[]{:S(2)}, u32[]{:S(2)}) collective-permute-start(bf16[112,128]{1,0:T(8,128)(2,1)S(1)} %get-tuple-element.42), channel_id=1, source_target_pairs={{0,2},{1,3},{2,0},{3,1},{4,6},{5,7},{6,4},{7,5},{8,10},{9,11},{10,... | collective-permute-start | bytes 86024 | tf_op jit(solution)/shard_map/ppermute | solution.py:344
  21.0 2.4 %collective-permute-start.8 = (bf16[240,384]{1,0:T(8,128)(2,1)S(1)}, bf16[240,384]{1,0:T(8,128)(2,1)S(1)}, u32[]{:S(2)}, u32[]{:S(2)}) collective-permute-start(bf16[240,384]{1,0:T(8,128)(2,1)S(1)} %get-tuple-element.43), channel_id=1, source_target_pairs={{0,24},{8,0},{16,8},{24,16},{1,25},{9,1},{17,9},{25,17},{2,26},{10... | collective-permute-start | bytes 552968 | tf_op jit(solution)/shard_map/ppermute | solution.py:28
  23.5 0.0 collective-permute-done.4.refs_0_
  23.5 0.4 %collective-permute-done.5.refs_1_ = bf16[112,128]{1,0:T(8,128)(2,1)S(1)} collective-permute-done((bf16[112,128]{1,0:T(8,128)(2,1)S(1)}, bf16[112,128]{1,0:T(8,128)(2,1)S(1)}, u32[]{:S(2)}, u32[]{:S(2)}) %collective-permute-start.5) | collective-permute-done | bytes 28704 | tf_op jit(solution)/shard_map/ppermute | solution.py:344
  23.9 0.0 collective-permute-done.6.refs_2_
  23.9 2.5 %collective-permute-start.7 = (bf16[3,112,128]{2,1,0:T(8,128)(2,1)S(1)}, bf16[3,112,128]{2,1,0:T(8,128)(2,1)S(1)}, u32[]{:S(2)}, u32[]{:S(2)}) collective-permute-start(bf16[3,112,128]{2,1,0:T(8,128)(2,1)S(1)} %shard_map.143), channel_id=1, source_target_pairs={{0,24},{8,0},{16,8},{24,16},{1,25},{9,1},{17,9},{25,17},{2,26},{10... | collective-permute-start | bytes 258056 | tf_op jit(solution)/shard_map/ppermute | solution.py:28
  26.4 1.1 %shard_map.145 = (f32[2,48,96]{2,1,0:T(8,128)}, f32[2,48,96]{2,1,0:T(8,128)}, f32[2,48]{1,0:T(2,128)}) custom-call(bf16[288,256]{1,0:T(8,128)(2,1)S(1)} %get-tuple-element.45.points0, bf16[288,256]{1,0:T(8,128)(2,1)S(1)} %get-tuple-element.46.hidden0, bf16[288,256]{1,0:T(8,128)(2,1)S(1)} %get-tuple-element.47.points1, ...), custom_call_target="tpu_custom_call" | custom-call | flops 2000000000 | bytes 1000000 | tf_op jit(solution)/shard_map/pallas_call | solution.py:302
  27.5 1.2 %collective-permute-done.7.three = bf16[3,112,128]{2,1,0:T(8,128)(2,1)S(1)} collective-permute-done((bf16[3,112,128]{2,1,0:T(8,128)(2,1)S(1)}, bf16[3,112,128]{2,1,0:T(8,128)(2,1)S(1)}, u32[]{:S(2)}, u32[]{:S(2)}) %collective-permute-start.7) | collective-permute-done | bytes 86048 | tf_op jit(solution)/shard_map/ppermute | solution.py:28
  28.7 0.0 collective-permute-done.8.bundle
  28.7 1.1 %shard_map.144 = bf16[180,384]{1,0:T(8,128)(2,1)} custom-call(bf16[3,112,128]{2,1,0:T(8,128)(2,1)S(1)} %collective-permute-done.7.three, bf16[240,384]{1,0:T(8,128)(2,1)S(1)} %collective-permute-done.8.bundle, bf16[180,144]{1,0:T(8,128)(2,1)S(1)} %get-tuple-element.44.table), custom_call_target="tpu_custom_call" | custom-call | flops 100000000 | bytes 1000000 | tf_op jit(solution)/shard_map/pallas_call | solution.py:302
  (2 shorter events, 0.0 us)
Async XLA Ops:
  2.3 7.5 %collective-permute-start = (bf16[72,384]{1,0:T(8,128)(2,1)S(1)}, bf16[72,384]{1,0:T(8,128)(2,1)S(1)}, u32[]{:S(2)}, u32[]{:S(2)}) collective-permute-start(bf16[72,384]{1,0:T(8,128)(2,1)S(1)} %get-tuple-element.30), channel_id=1, source_target_pairs={{0,6},{1,7},{2,4},{3,5},{4,2},{5,3},{6,0},{7,1},{8,14},{9,15},{10,... | collective-permute-start | bytes 165896 | tf_op jit(solution)/shard_map/ppermute | solution.py:344
  7.5 5.1 %collective-permute-start.1 = (bf16[72,384]{1,0:T(8,128)(2,1)S(1)}, bf16[72,384]{1,0:T(8,128)(2,1)S(1)}, u32[]{:S(2)}, u32[]{:S(2)}) collective-permute-start(bf16[72,384]{1,0:T(8,128)(2,1)S(1)} %get-tuple-element.31), channel_id=1, source_target_pairs={{0,4},{1,5},{2,6},{3,7},{4,0},{5,1},{6,2},{7,3},{8,12},{9,13},{10,... | collective-permute-start | bytes 165896 | tf_op jit(solution)/shard_map/ppermute | solution.py:344
  7.5 5.1 %collective-permute-start.2 = (bf16[72,384]{1,0:T(8,128)(2,1)S(1)}, bf16[72,384]{1,0:T(8,128)(2,1)S(1)}, u32[]{:S(2)}, u32[]{:S(2)}) collective-permute-start(bf16[72,384]{1,0:T(8,128)(2,1)S(1)} %get-tuple-element.32), channel_id=1, source_target_pairs={{0,2},{1,3},{2,0},{3,1},{4,6},{5,7},{6,4},{7,5},{8,10},{9,11},{10,... | collective-permute-start | bytes 165896 | tf_op jit(solution)/shard_map/ppermute | solution.py:344
  12.5 1.5 %collective-permute-start.3 = (bf16[4,72,384]{2,1,0:T(8,128)(2,1)S(1)}, bf16[4,72,384]{2,1,0:T(8,128)(2,1)S(1)}, u32[]{:S(2)}, u32[]{:S(2)}) collective-permute-start(bf16[4,72,384]{2,1,0:T(8,128)(2,1)S(1)} %shard_map.140), channel_id=1, source_target_pairs={{0,1},{1,0},{2,3},{3,2},{4,5},{5,4},{6,7},{7,6},{8,9},{9,8},{10,11... | collective-permute-start | bytes 663560 | tf_op jit(solution)/shard_map/ppermute | solution.py:385
  16.6 6.9 %collective-permute-start.4 = (bf16[112,128]{1,0:T(8,128)(2,1)S(1)}, bf16[112,128]{1,0:T(8,128)(2,1)S(1)}, u32[]{:S(2)}, u32[]{:S(2)}) collective-permute-start(bf16[112,128]{1,0:T(8,128)(2,1)S(1)} %get-tuple-element.40), channel_id=1, source_target_pairs={{0,6},{1,7},{2,4},{3,5},{4,2},{5,3},{6,0},{7,1},{8,14},{9,15},{10,... | collective-permute-start | bytes 86024 | tf_op jit(solution)/shard_map/ppermute | solution.py:344
  19.1 4.8 %collective-permute-start.5 = (bf16[112,128]{1,0:T(8,128)(2,1)S(1)}, bf16[112,128]{1,0:T(8,128)(2,1)S(1)}, u32[]{:S(2)}, u32[]{:S(2)}) collective-permute-start(bf16[112,128]{1,0:T(8,128)(2,1)S(1)} %get-tuple-element.41), channel_id=1, source_target_pairs={{0,4},{1,5},{2,6},{3,7},{4,0},{5,1},{6,2},{7,3},{8,12},{9,13},{10,... | collective-permute-start | bytes 86024 | tf_op jit(solution)/shard_map/ppermute | solution.py:344
  19.1 4.8 %collective-permute-start.6 = (bf16[112,128]{1,0:T(8,128)(2,1)S(1)}, bf16[112,128]{1,0:T(8,128)(2,1)S(1)}, u32[]{:S(2)}, u32[]{:S(2)}) collective-permute-start(bf16[112,128]{1,0:T(8,128)(2,1)S(1)} %get-tuple-element.42), channel_id=1, source_target_pairs={{0,2},{1,3},{2,0},{3,1},{4,6},{5,7},{6,4},{7,5},{8,10},{9,11},{10,... | collective-permute-start | bytes 86024 | tf_op jit(solution)/shard_map/ppermute | solution.py:344
  21.0 7.7 %collective-permute-start.8 = (bf16[240,384]{1,0:T(8,128)(2,1)S(1)}, bf16[240,384]{1,0:T(8,128)(2,1)S(1)}, u32[]{:S(2)}, u32[]{:S(2)}) collective-permute-start(bf16[240,384]{1,0:T(8,128)(2,1)S(1)} %get-tuple-element.43), channel_id=1, source_target_pairs={{0,24},{8,0},{16,8},{24,16},{1,25},{9,1},{17,9},{25,17},{2,26},{10... | collective-permute-start | bytes 552968 | tf_op jit(solution)/shard_map/ppermute | solution.py:28
  23.9 4.8 %collective-permute-start.7 = (bf16[3,112,128]{2,1,0:T(8,128)(2,1)S(1)}, bf16[3,112,128]{2,1,0:T(8,128)(2,1)S(1)}, u32[]{:S(2)}, u32[]{:S(2)}) collective-permute-start(bf16[3,112,128]{2,1,0:T(8,128)(2,1)S(1)} %shard_map.143), channel_id=1, source_target_pairs={{0,24},{8,0},{16,8},{24,16},{1,25},{9,1},{17,9},{25,17},{2,26},{10... | collective-permute-start | bytes 258056 | tf_op jit(solution)/shard_map/ppermute | solution.py:28

commit v14 on v13

--- a/solution.py
+++ b/solution.py
@@ -119,9 +119,10 @@
         ]
         for n in range(NB)
     ]
-    wait(copies[:4])
+    wait(copies[2:4])
     rows = by_block.shape[1]
     spectral = jnp.dot(table[...], field[...], preferred_element_type=F32)
+    wait(copies[:2])
     active = counts[assign[lax.axis_index("lat")]]
     mode = mode_numbers((rows, spectral.shape[1]), 0, q)
     groups = [
@@ -210,25 +211,33 @@
     slope[...] = sig * (1.0 + pre * (1.0 - sig))
 
 
+def row_groups(chunk):
+    return jnp.concatenate([window(chunk, j * BS) for j in range(2)], axis=1)
+
+
 def own_kernel(*refs):
-    mat1, bias, points, hidden, slope, by_pair = refs[NB:]
+    early, mat1, bias, points, hidden, slope, fields, by_pair = refs[NB:]
     chunks = [refs[i][...].astype(F32) for i in ORDER]
     silu_points(chunks, mat1, bias, by_pair, points, hidden, slope)
+    for i in range(NB):
+        fields[i] = row_groups(refs[i][...].astype(F32))
+    for i in range(2):
+        fields[NB + i] = row_groups(early[i].astype(F32))
 
 
 def filter_kernel(*refs):
-    owns, (other, slope_own, mat1, mat2, bias, lat, lat_t, own_field, assign_hbm) = refs[:4], refs[4:13]
-    outs, (bundle, points, hidden, grad_pre, grad_y) = refs[13:16], refs[16:21]
-    assign, by_lat, by_pair, slope, sems = refs[21:]
+    early, late, fields, slope_own, mat1, mat2, bias, lat, lat_t, own_field, assign_hbm = refs[:11]
+    outs, (bundle, points, hidden, grad_pre, grad_y) = refs[11:14], refs[14:19]
+    assign, by_lat, by_pair, slope, sems = refs[19:]
     copies = fetch(sems, (assign_hbm,), (assign,))
     core = lax.rem(lax.axis_index("lat"), 2)
-    sides = [[owns[i][...].astype(F32) for i in ORDER], [other[i].astype(F32) for i in ORDER]]
-    silu_points(sides[1], mat1, bias, by_pair, points, hidden, slope)
+    others = [half[i].astype(F32) for half in (early, late) for i in range(2)]
+    silu_points([others[i] for i in ORDER], mat1, bias, by_pair, points, hidden, slope)
     wait(copies)
-    for side, chunks in zip((core, 1 - core), sides):
-        for d, chunk in enumerate(chunks):
-            groups = [window(chunk, j * BS) for j in range(2)]
-            by_lat[assign[2 * partner(d) + side]] = jnp.concatenate(groups, axis=1)
+    for i, d in enumerate(ORDER):
+        by_lat[assign[2 * partner(d) + core]] = fields[i]
+        spectrum = fields[NB + i] if i < 2 else row_groups(others[i])
+        by_lat[assign[2 * partner(d) + 1 - core]] = spectrum
     field = by_lat[...].reshape(lat.shape[1], 2 * LANES).astype(BF16)
     waves = dot(lat[...], field, (1, 0)).astype(BF16)
     rows = waves.shape[0] // 2
@@ -343,6 +352,9 @@
         pairs = [[(i, i ^ (2 * d)) for i in range(2 * NB)] for d in ORDER[1:]]
         return [lax.ppermute(chunk, "lat", p) for chunk, p in zip(chunks, pairs)]
 
+    def twin(value):
+        return lax.ppermute(value, "lat", [(i, i ^ 1) for i in range(2 * NB)])
+
     field = grad_out.reshape(length, width)
     shape = jax.ShapeDtypeStruct
     far = (mode_counts, assignment, field, inverse, spec_saved[0])
@@ -375,22 +387,17 @@
         far,
         2 * 10**9,
     )
-    own = call(
-        join_kernel,
-        shape((NB, rows, width), BF16),
-        [],
-        (*received, bias),
-        (),
-    )
-    other = lax.ppermute(own, "lat", [(i, i ^ 1) for i in range(2 * NB)])
+    pair = shape((2, rows, width), BF16)
+    early = twin(call(join_kernel, pair, [], received[:2], ()))
+    late = twin(call(join_kernel, pair, [], (*received[2:], bias), ()))
     vectors = shape((NB * rows, wide), BF16)
     slopes = shape((NB * rows, wide), F32)
     by_pair = pltpu.VMEM((NB, rows, wide), F32)
-    points0, hidden0, slope0 = call(
+    points0, hidden0, slope0, fields = call(
         own_kernel,
-        (vectors, vectors, slopes),
+        (vectors, vectors, slopes, shape((NB + 2, rows, wide), F32)),
         [by_pair],
-        (*received, mat1, bias),
+        (*received, early, mat1, bias),
         (),
         2 * 10**9,
     )
@@ -409,7 +416,7 @@
             pltpu.VMEM((NB * rows, wide), F32),
             sems,
         ],
-        (*received, other, slope0, mat1, mat2, bias, lat, lat_t, field),
+        (early, late, fields, slope0, mat1, mat2, bias, lat, lat_t, field),
         (assignment,),
     )
     backs = swap(chunks)

time: 30 us -> 30.5 us (1.017)
  waiting for transfers between devices: 5.48 us -> 5.98 us
    ppermute x6, waiting for transfers between devices: 3.2 us -> 4.07 us  [swap(): return [lax.ppermute(chunk, 'lat', p) for chunk, p in zip(chunks, pairs)]]
    ppermute x1 -> x2, waiting for transfers between devices: 1.1 us -> 0.92 us  [twin(): return lax.ppermute(value, 'lat', [(i, i ^ 1) for i in range(2 * NB)])]
    pallas_call x8 -> x9, Pallas kernels: 8.41 us -> 8.37 us  [call(): pl.pallas_call(kernel, out_shape=outs, in_specs=[VMEM] * len(near) + [HBM...]
  transfers between devices with their start and end apart: 9 -> 10, of which waited for: 5 -> 5; matrix products, arithmetic and copies ran while one was open for 0% -> 0% of each run, Pallas kernels for 10% -> 10%
where the time goes in v14:
time: 30.5 us; the launch traced here: 30.4 us
  starting transfers between devices  15.3 us (50%)
  Pallas kernels  8.37 us (27%)
  waiting for transfers between devices  5.98 us (20%)
  between operations  0.71 us (2%)
    ppermute x6, starting transfers between devices, swap(): return [lax.ppermute(chunk, 'lat', p) for chunk, p in zip(chunks, pairs)]  10.2 us
    pallas_call x9, Pallas kernels, call(): pl.pallas_call(kernel, out_shape=outs, in_specs=[VMEM] * len(near) + [HBM...  8.37 us
    ppermute x2, starting transfers between devices, turn(): lax.ppermute(value, axis, [(i, (i - 1) % length) for i in range(length)])  4.96 us
    ppermute x6, waiting for transfers between devices, swap(): return [lax.ppermute(chunk, 'lat', p) for chunk, p in zip(chunks, pairs)]  4.07 us
    ppermute x2, waiting for transfers between devices, turn(): lax.ppermute(value, axis, [(i, (i - 1) % length) for i in range(length)])  0.99 us
    ppermute x2, waiting for transfers between devices, twin(): return lax.ppermute(value, 'lat', [(i, i ^ 1) for i in range(2 * NB)])  0.92 us
  transfers between devices with their start and end apart: 10, of which 5 were waited for; matrix products, arithmetic and copies ran while one was open for 0% of the time, Pallas kernels for 10%

profile of v14, /device:TPU:0, one launch (start us, length us, event | category | flops | bytes accessed | tf_op | source)
XLA Modules:
  0.0 30.4 jit_solution(15868310388948373374)
XLA Ops:
  0.6 1.8 %shard_map.138 = (bf16[72,384]{1,0:T(8,128)(2,1)S(1)}, bf16[72,384]{1,0:T(8,128)(2,1)S(1)}, bf16[72,384]{1,0:T(8,128)(2,1)S(1)}, bf16[72,384]{1,0:T(8,128)(2,1)S(1)}) custom-call(s32[8]{0:T(128)} %refs_0_.3, s32[8]{0:T(128)} %refs_10_.1, bf16[180,384]{1,0:T(8,128)(2,1)} %bitcast.16, bf16[144,180]{1,0:T(8,128)(2,1)} %constant.10.clone.refs_3_, ...), custom_call_target="tpu_custom_call" | custom-call | flops 100000000 | bytes 1000000 | tf_op jit(solution)/shard_map/pallas_call | solution.py:311
  2.4 5.1 %collective-permute-start = (bf16[72,384]{1,0:T(8,128)(2,1)S(1)}, bf16[72,384]{1,0:T(8,128)(2,1)S(1)}, u32[]{:S(2)}, u32[]{:S(2)}) collective-permute-start(bf16[72,384]{1,0:T(8,128)(2,1)S(1)} %get-tuple-element.31), channel_id=1, source_target_pairs={{0,6},{1,7},{2,4},{3,5},{4,2},{5,3},{6,0},{7,1},{8,14},{9,15},{10,... | collective-permute-start | bytes 165896 | tf_op jit(solution)/shard_map/ppermute | solution.py:353
  7.5 0.0 collective-permute-start.2
  7.5 0.6 %collective-permute-start.3 = (bf16[72,384]{1,0:T(8,128)(2,1)S(1)}, bf16[72,384]{1,0:T(8,128)(2,1)S(1)}, u32[]{:S(2)}, u32[]{:S(2)}) collective-permute-start(bf16[72,384]{1,0:T(8,128)(2,1)S(1)} %get-tuple-element.33), channel_id=1, source_target_pairs={{0,2},{1,3},{2,0},{3,1},{4,6},{5,7},{6,4},{7,5},{8,10},{9,11},{10,... | collective-permute-start | bytes 165896 | tf_op jit(solution)/shard_map/ppermute | solution.py:353
  8.1 1.7 %collective-permute-done.refs_1_ = bf16[72,384]{1,0:T(8,128)(2,1)S(1)} collective-permute-done((bf16[72,384]{1,0:T(8,128)(2,1)S(1)}, bf16[72,384]{1,0:T(8,128)(2,1)S(1)}, u32[]{:S(2)}, u32[]{:S(2)}) %collective-permute-start) | collective-permute-done | bytes 55328 | tf_op jit(solution)/shard_map/ppermute | solution.py:353
  9.9 0.1 collective-permute-start.1
  10.0 1.7 %shard_map.140 = (bf16[256,256]{1,0:T(8,128)(2,1)S(1)}, bf16[256,256]{1,0:T(8,128)(2,1)S(1)}, f32[1,256]{1,0:T(1,128)S(1)}, bf16[576,576]{1,0:T(8,128)(2,1)S(1)}...) custom-call(s32[8]{0:T(128)} %refs_0_.3, s32[8]{0:T(128)} %refs_10_.1, ...), custom_call_target="tpu_custom_call" | custom-call | flops 2000000000 | bytes 1000000 | tf_op jit(solution)/shard_map/pallas_call | solution.py:311
  11.6 0.9 %collective-permute-done.2.refs_0_.refs_2_ = bf16[72,384]{1,0:T(8,128)(2,1)S(1)} collective-permute-done((bf16[72,384]{1,0:T(8,128)(2,1)S(1)}, bf16[72,384]{1,0:T(8,128)(2,1)S(1)}, u32[]{:S(2)}, u32[]{:S(2)}) %collective-permute-start.2) | collective-permute-done | bytes 55328 | tf_op jit(solution)/shard_map/ppermute | solution.py:353
  12.6 0.0 collective-permute-done.3.refs_1_.refs_3_
  12.6 0.1 collective-permute-start.4
  12.7 0.0 collective-permute-done.1.refs_4_.refs_0_
  12.7 0.4 %shard_map.142 = (bf16[288,256]{1,0:T(8,128)(2,1)S(1)}, bf16[288,256]{1,0:T(8,128)(2,1)S(1)}, f32[288,256]{1,0:T(8,128)S(1)}, f32[6,72,256]{2,1,0:T(8,128)S(1)}) custom-call(bf16[72,384]{1,0:T(8,128)(2,1)S(1)} %get-tuple-element.30.refs_0_, bf16[72,384]{1,0:T(8,128)(2,1)S(1)} %collective-permute-done.refs_1_, ...), custom_call_target="tpu_custom_call" | custom-call | flops 2000000000 | bytes 1000000 | tf_op jit(solution)/shard_map/pallas_call | solution.py:311
  13.0 0.9 %collective-permute-done.4.refs_1_ = bf16[2,72,384]{2,1,0:T(8,128)(2,1)S(1)} collective-permute-done((bf16[2,72,384]{2,1,0:T(8,128)(2,1)S(1)}, bf16[2,72,384]{2,1,0:T(8,128)(2,1)S(1)}, u32[]{:S(2)}, u32[]{:S(2)}) %collective-permute-start.4) | collective-permute-done | bytes 110624 | tf_op jit(solution)/shard_map/ppermute | solution.py:356
  14.0 2.4 %shard_map.143 = (bf16[112,128]{1,0:T(8,128)(2,1)S(1)}, bf16[112,128]{1,0:T(8,128)(2,1)S(1)}, bf16[112,128]{1,0:T(8,128)(2,1)S(1)}, bf16[240,384]{1,0:T(8,128)(2...) custom-call(bf16[2,72,384]{2,1,0:T(8,128)(2,1)S(1)} %collective-perm, ...), custom_call_target="tpu_custom_call" | custom-call | flops 100000000 | bytes 1000000 | tf_op jit(solution)/shard_map/pallas_call | solution.py:311
  16.3 3.5 %collective-permute-start.5 = (bf16[112,128]{1,0:T(8,128)(2,1)S(1)}, bf16[112,128]{1,0:T(8,128)(2,1)S(1)}, u32[]{:S(2)}, u32[]{:S(2)}) collective-permute-start(bf16[112,128]{1,0:T(8,128)(2,1)S(1)} %get-tuple-element.42), channel_id=1, source_target_pairs={{0,6},{1,7},{2,4},{3,5},{4,2},{5,3},{6,0},{7,1},{8,14},{9,15},{10,... | collective-permute-start | bytes 86024 | tf_op jit(solution)/shard_map/ppermute | solution.py:353
  19.9 0.0 collective-permute-start.6
  19.9 0.9 %collective-permute-start.7 = (bf16[112,128]{1,0:T(8,128)(2,1)S(1)}, bf16[112,128]{1,0:T(8,128)(2,1)S(1)}, u32[]{:S(2)}, u32[]{:S(2)}) collective-permute-start(bf16[112,128]{1,0:T(8,128)(2,1)S(1)} %get-tuple-element.44), channel_id=1, source_target_pairs={{0,2},{1,3},{2,0},{3,1},{4,6},{5,7},{6,4},{7,5},{8,10},{9,11},{10,... | collective-permute-start | bytes 86024 | tf_op jit(solution)/shard_map/ppermute | solution.py:353
  20.8 2.5 %collective-permute-start.9 = (bf16[240,384]{1,0:T(8,128)(2,1)S(1)}, bf16[240,384]{1,0:T(8,128)(2,1)S(1)}, u32[]{:S(2)}, u32[]{:S(2)}) collective-permute-start(bf16[240,384]{1,0:T(8,128)(2,1)S(1)} %get-tuple-element.45), channel_id=1, source_target_pairs={{0,24},{8,0},{16,8},{24,16},{1,25},{9,1},{17,9},{25,17},{2,26},{10... | collective-permute-start | bytes 552968 | tf_op jit(solution)/shard_map/ppermute | solution.py:28
  23.2 1.4 %collective-permute-done.6.refs_1_ = bf16[112,128]{1,0:T(8,128)(2,1)S(1)} collective-permute-done((bf16[112,128]{1,0:T(8,128)(2,1)S(1)}, bf16[112,128]{1,0:T(8,128)(2,1)S(1)}, u32[]{:S(2)}, u32[]{:S(2)}) %collective-permute-start.6) | collective-permute-done | bytes 28704 | tf_op jit(solution)/shard_map/ppermute | solution.py:353
  24.7 2.5 %collective-permute-start.8 = (bf16[3,112,128]{2,1,0:T(8,128)(2,1)S(1)}, bf16[3,112,128]{2,1,0:T(8,128)(2,1)S(1)}, u32[]{:S(2)}, u32[]{:S(2)}) collective-permute-start(bf16[3,112,128]{2,1,0:T(8,128)(2,1)S(1)} %shard_map.144), channel_id=1, source_target_pairs={{0,24},{8,0},{16,8},{24,16},{1,25},{9,1},{17,9},{25,17},{2,26},{10... | collective-permute-start | bytes 258056 | tf_op jit(solution)/shard_map/ppermute | solution.py:28
  27.2 1.1 %shard_map.146 = (f32[2,48,96]{2,1,0:T(8,128)}, f32[2,48,96]{2,1,0:T(8,128)}, f32[2,48]{1,0:T(2,128)}) custom-call(bf16[288,256]{1,0:T(8,128)(2,1)S(1)} %get-tuple-element.47.points0, bf16[288,256]{1,0:T(8,128)(2,1)S(1)} %get-tuple-element.48.hidden0, bf16[288,256]{1,0:T(8,128)(2,1)S(1)} %get-tuple-element.49.points1, ...), custom_call_target="tpu_custom_call" | custom-call | flops 2000000000 | bytes 1000000 | tf_op jit(solution)/shard_map/pallas_call | solution.py:311
  28.3 1.0 %collective-permute-done.8.three = bf16[3,112,128]{2,1,0:T(8,128)(2,1)S(1)} collective-permute-done((bf16[3,112,128]{2,1,0:T(8,128)(2,1)S(1)}, bf16[3,112,128]{2,1,0:T(8,128)(2,1)S(1)}, u32[]{:S(2)}, u32[]{:S(2)}) %collective-permute-start.8) | collective-permute-done | bytes 86048 | tf_op jit(solution)/shard_map/ppermute | solution.py:28
  29.3 0.0 collective-permute-done.9.bundle
  29.3 1.1 %shard_map.145 = bf16[180,384]{1,0:T(8,128)(2,1)} custom-call(bf16[3,112,128]{2,1,0:T(8,128)(2,1)S(1)} %collective-permute-done.8.three, bf16[240,384]{1,0:T(8,128)(2,1)S(1)} %collective-permute-done.9.bundle, bf16[180,144]{1,0:T(8,128)(2,1)S(1)} %get-tuple-element.46.table), custom_call_target="tpu_custom_call" | custom-call | flops 100000000 | bytes 1000000 | tf_op jit(solution)/shard_map/pallas_call | solution.py:311
  (5 shorter events, 0.0 us)
Async XLA Ops:
  2.4 7.5 %collective-permute-start = (bf16[72,384]{1,0:T(8,128)(2,1)S(1)}, bf16[72,384]{1,0:T(8,128)(2,1)S(1)}, u32[]{:S(2)}, u32[]{:S(2)}) collective-permute-start(bf16[72,384]{1,0:T(8,128)(2,1)S(1)} %get-tuple-element.31), channel_id=1, source_target_pairs={{0,6},{1,7},{2,4},{3,5},{4,2},{5,3},{6,0},{7,1},{8,14},{9,15},{10,... | collective-permute-start | bytes 165896 | tf_op jit(solution)/shard_map/ppermute | solution.py:353
  7.5 5.1 %collective-permute-start.2 = (bf16[72,384]{1,0:T(8,128)(2,1)S(1)}, bf16[72,384]{1,0:T(8,128)(2,1)S(1)}, u32[]{:S(2)}, u32[]{:S(2)}) collective-permute-start(bf16[72,384]{1,0:T(8,128)(2,1)S(1)} %get-tuple-element.32), channel_id=1, source_target_pairs={{0,4},{1,5},{2,6},{3,7},{4,0},{5,1},{6,2},{7,3},{8,12},{9,13},{10,... | collective-permute-start | bytes 165896 | tf_op jit(solution)/shard_map/ppermute | solution.py:353
  7.5 5.1 %collective-permute-start.3 = (bf16[72,384]{1,0:T(8,128)(2,1)S(1)}, bf16[72,384]{1,0:T(8,128)(2,1)S(1)}, u32[]{:S(2)}, u32[]{:S(2)}) collective-permute-start(bf16[72,384]{1,0:T(8,128)(2,1)S(1)} %get-tuple-element.33), channel_id=1, source_target_pairs={{0,2},{1,3},{2,0},{3,1},{4,6},{5,7},{6,4},{7,5},{8,10},{9,11},{10,... | collective-permute-start | bytes 165896 | tf_op jit(solution)/shard_map/ppermute | solution.py:353
  9.9 2.8 %collective-permute-start.1 = (bf16[2,72,384]{2,1,0:T(8,128)(2,1)S(1)}, bf16[2,72,384]{2,1,0:T(8,128)(2,1)S(1)}, u32[]{:S(2)}, u32[]{:S(2)}) collective-permute-start(bf16[2,72,384]{2,1,0:T(8,128)(2,1)S(1)} %shard_map.139), channel_id=1, source_target_pairs={{0,1},{1,0},{2,3},{3,2},{4,5},{5,4},{6,7},{7,6},{8,9},{9,8},{10,11... | collective-permute-start | bytes 331784 | tf_op jit(solution)/shard_map/ppermute | solution.py:356
  12.6 1.4 %collective-permute-start.4 = (bf16[2,72,384]{2,1,0:T(8,128)(2,1)S(1)}, bf16[2,72,384]{2,1,0:T(8,128)(2,1)S(1)}, u32[]{:S(2)}, u32[]{:S(2)}) collective-permute-start(bf16[2,72,384]{2,1,0:T(8,128)(2,1)S(1)} %shard_map.141), channel_id=1, source_target_pairs={{0,1},{1,0},{2,3},{3,2},{4,5},{5,4},{6,7},{7,6},{8,9},{9,8},{10,11... | collective-permute-start | bytes 331784 | tf_op jit(solution)/shard_map/ppermute | solution.py:356
  16.3 6.9 %collective-permute-start.5 = (bf16[112,128]{1,0:T(8,128)(2,1)S(1)}, bf16[112,128]{1,0:T(8,128)(2,1)S(1)}, u32[]{:S(2)}, u32[]{:S(2)}) collective-permute-start(bf16[112,128]{1,0:T(8,128)(2,1)S(1)} %get-tuple-element.42), channel_id=1, source_target_pairs={{0,6},{1,7},{2,4},{3,5},{4,2},{5,3},{6,0},{7,1},{8,14},{9,15},{10,... | collective-permute-start | bytes 86024 | tf_op jit(solution)/shard_map/ppermute | solution.py:353
  19.9 4.8 %collective-permute-start.6 = (bf16[112,128]{1,0:T(8,128)(2,1)S(1)}, bf16[112,128]{1,0:T(8,128)(2,1)S(1)}, u32[]{:S(2)}, u32[]{:S(2)}) collective-permute-start(bf16[112,128]{1,0:T(8,128)(2,1)S(1)} %get-tuple-element.43), channel_id=1, source_target_pairs={{0,4},{1,5},{2,6},{3,7},{4,0},{5,1},{6,2},{7,3},{8,12},{9,13},{10,... | collective-permute-start | bytes 86024 | tf_op jit(solution)/shard_map/ppermute | solution.py:353
  19.9 4.8 %collective-permute-start.7 = (bf16[112,128]{1,0:T(8,128)(2,1)S(1)}, bf16[112,128]{1,0:T(8,128)(2,1)S(1)}, u32[]{:S(2)}, u32[]{:S(2)}) collective-permute-start(bf16[112,128]{1,0:T(8,128)(2,1)S(1)} %get-tuple-element.44), channel_id=1, source_target_pairs={{0,2},{1,3},{2,0},{3,1},{4,6},{5,7},{6,4},{7,5},{8,10},{9,11},{10,... | collective-permute-start | bytes 86024 | tf_op jit(solution)/shard_map/ppermute | solution.py:353
  20.8 8.5 %collective-permute-start.9 = (bf16[240,384]{1,0:T(8,128)(2,1)S(1)}, bf16[240,384]{1,0:T(8,128)(2,1)S(1)}, u32[]{:S(2)}, u32[]{:S(2)}) collective-permute-start(bf16[240,384]{1,0:T(8,128)(2,1)S(1)} %get-tuple-element.45), channel_id=1, source_target_pairs={{0,24},{8,0},{16,8},{24,16},{1,25},{9,1},{17,9},{25,17},{2,26},{10... | collective-permute-start | bytes 552968 | tf_op jit(solution)/shard_map/ppermute | solution.py:28
  24.7 4.6 %collective-permute-start.8 = (bf16[3,112,128]{2,1,0:T(8,128)(2,1)S(1)}, bf16[3,112,128]{2,1,0:T(8,128)(2,1)S(1)}, u32[]{:S(2)}, u32[]{:S(2)}) collective-permute-start(bf16[3,112,128]{2,1,0:T(8,128)(2,1)S(1)} %shard_map.144), channel_id=1, source_target_pairs={{0,24},{8,0},{16,8},{24,16},{1,25},{9,1},{17,9},{25,17},{2,26},{10... | collective-permute-start | bytes 258056 | tf_op jit(solution)/shard_map/ppermute | solution.py:28

commit v15 on v13

--- a/solution.py
+++ b/solution.py
@@ -80,11 +80,43 @@
 
 def mode_numbers(shape, axis, q):
     number = lax.broadcasted_iota(jnp.int32, shape, axis)
-    number = jnp.where(number >= NB * q, number - NB * q, number)
+    second = number >= NB * q
+    number = jnp.where(second, number - NB * q, number)
     mode = number
     for z in range(1, NB):
         mode = jnp.where(number >= z * q, number + z * q, mode)
-    return mode
+    return jnp.where(second, mode + q, mode)
+
+
+def eight_points(x, sign):
+    root = float(np.float32(1.0 / math.sqrt(8.0)).astype(BF16))
+
+    def add(a, b):
+        return a[0] + b[0], a[1] + b[1]
+
+    def sub(a, b):
+        return a[0] - b[0], a[1] - b[1]
+
+    def times_i(a, by):
+        return (-a[1], a[0]) if by > 0 else (a[1], -a[0])
+
+    def scale(a, by):
+        return a[0] * by, a[1] * by
+
+    def four(a, b, c, d):
+        total, far, other, near = add(a, c), sub(a, c), add(b, d), sub(b, d)
+        near = times_i(near, sign)
+        return add(total, other), add(far, near), sub(total, other), sub(far, near)
+
+    even = [scale(a, root) for a in four(*x[0::2])]
+    odd = four(*x[1::2])
+    turned = [
+        scale(odd[0], root),
+        scale(add(odd[1], times_i(odd[1], sign)), 0.25),
+        scale(times_i(odd[2], sign), root),
+        scale(sub(times_i(odd[3], sign), odd[3]), 0.25),
+    ]
+    return [add(a, b) for a, b in zip(even, turned)] + [sub(a, b) for a, b in zip(even, turned)]
 
 
 def fetch(sems, sources, targets):
@@ -123,30 +155,26 @@
     rows = by_block.shape[1]
     spectral = jnp.dot(table[...], field[...], preferred_element_type=F32)
     active = counts[assign[lax.axis_index("lat")]]
-    mode = mode_numbers((rows, spectral.shape[1]), 0, q)
-    groups = [
-        jnp.where(mode < active - g * q, spectral[g * rows : (g + 1) * rows], 0.0)
-        for g in range(2)
-    ]
+    held_modes = mode_numbers((rows, spectral.shape[1]), 0, q) < active
+    spectra = [jnp.where(held_modes, spectral[c * rows : (c + 1) * rows], 0.0) for c in range(2)]
     for n in range(NB):
-        pieces = [window(group, n * BS) for group in groups]
+        pieces = [window(spectrum, n * BS) for spectrum in spectra]
         by_block[n] = dense(pieces + points[n]).astype(BF16)
     for d, out in enumerate(outs):
         out[...] = by_block[partner(d)]
 
 
 def ready_kernel(q, *refs):
-    hbm, (mat1, mat2, bias, lat, lat_t, own_field, own_table) = refs[:9], refs[9:16]
-    counts, assign, w1, w2, b1, table, sems = refs[16:]
-    copies = fetch(sems, hbm, (counts, assign, w1, w2, b1, table, lat, lat_t, own_field))
+    hbm, (mat1, mat2, bias, own_field, own_table) = refs[:7], refs[7:12]
+    counts, assign, w1, w2, b1, table, sems = refs[12:]
+    copies = fetch(sems, hbm, (counts, assign, w1, w2, b1, table, own_field))
     wait(copies[:6])
     active = counts[assign[lax.axis_index("lat")]]
     rows = table.shape[1] // 2
-    mode = mode_numbers((table.shape[0], rows), 1, q)
-    for g in range(2):
-        part = table[:, g * rows : (g + 1) * rows].astype(F32)
-        part = jnp.where(mode < active - g * q, part, 0.0)
-        own_table[:, g * rows : (g + 1) * rows] = part.astype(BF16)
+    held_modes = mode_numbers((table.shape[0], rows), 1, q) < active
+    for c in range(2):
+        part = table[:, c * rows : (c + 1) * rows].astype(F32)
+        own_table[:, c * rows : (c + 1) * rows] = jnp.where(held_modes, part, 0.0).astype(BF16)
     block = lax.axis_index("lat") // 2
 
     def pick(x):
@@ -217,9 +245,9 @@
 
 
 def filter_kernel(*refs):
-    owns, (other, slope_own, mat1, mat2, bias, lat, lat_t, own_field, assign_hbm) = refs[:4], refs[4:13]
-    outs, (bundle, points, hidden, grad_pre, grad_y) = refs[13:16], refs[16:21]
-    assign, by_lat, by_pair, slope, sems = refs[21:]
+    owns, (other, slope_own, mat1, mat2, bias, own_field, assign_hbm) = refs[:4], refs[4:11]
+    outs, (bundle, points, hidden, grad_pre, grad_y) = refs[11:14], refs[14:19]
+    assign, by_lat, by_pair, slope, real, imag, sems = refs[19:]
     copies = fetch(sems, (assign_hbm,), (assign,))
     core = lax.rem(lax.axis_index("lat"), 2)
     sides = [[owns[i][...].astype(F32) for i in ORDER], [other[i].astype(F32) for i in ORDER]]
@@ -227,37 +255,44 @@
     wait(copies)
     for side, chunks in zip((core, 1 - core), sides):
         for d, chunk in enumerate(chunks):
-            groups = [window(chunk, j * BS) for j in range(2)]
-            by_lat[assign[2 * partner(d) + side]] = jnp.concatenate(groups, axis=1)
-    field = by_lat[...].reshape(lat.shape[1], 2 * LANES).astype(BF16)
-    waves = dot(lat[...], field, (1, 0)).astype(BF16)
-    rows = waves.shape[0] // 2
-    inner = []
-    for side, slopes in enumerate((slope_own, slope)):
-        dy = []
-        for c in range(2):
-            part = waves[c * rows : (c + 1) * rows]
-            flip = core == 0 if side == 0 else core == 1
-            dy.append(jnp.where(flip, part[:, :LANES], part[:, LANES:]))
-        dy = jnp.concatenate(dy, axis=1)
-        dp = (dot(dy, mat2[...], (1, 1)) * slopes[...]).astype(BF16)
-        dv = dot(dp, mat1[...], (1, 1))
-        grad_y[side] = dy
-        grad_pre[side] = dp
-        inner.append(jnp.concatenate([dv[:, :LANES], dv[:, LANES:]], axis=0))
-    left = jnp.where(core == 0, inner[0], inner[1])
-    right = jnp.where(core == 0, inner[1], inner[0])
-    inner = jnp.concatenate([left, right], axis=1).astype(BF16)
+            parts = [window(chunk, j * BS) for j in range(2)]
+            by_lat[assign[2 * partner(d) + side]] = jnp.concatenate(parts, axis=1)
+    n_rows, rows, _ = by_lat.shape
+    half = rows * n_rows // 2
+    waves = eight_points([(by_lat[r][:, :LANES], by_lat[r][:, LANES:]) for r in range(n_rows)], -1)
+    for k, wave in enumerate(waves):
+        real[k * rows : (k + 1) * rows] = wave[0]
+        imag[k * rows : (k + 1) * rows] = wave[1]
+    dy = [
+        jnp.concatenate([ref[pl.ds(m, n_rows, stride=rows), :] for m in range(rows)], axis=0)
+        for ref in (real, imag)
+    ]
+    dy = jnp.concatenate(dy, axis=1).astype(BF16)
+    dy = [jnp.where(core == side, dy[:half], dy[half:]) for side in range(2)]
+    dh = dot(jnp.concatenate(dy, axis=0), mat2[...], (1, 1))
+    dp = [(dh[:half] * slope_own[...]).astype(BF16), (dh[half:] * slope[...]).astype(BF16)]
+    dv = dot(jnp.concatenate(dp, axis=0), mat1[...], (1, 1)).astype(BF16).astype(F32)
+    for side in range(2):
+        grad_y[side] = dy[side]
+        grad_pre[side] = dp[side]
+        place = pl.ds(pl.multiple_of((core if side == 0 else 1 - core) * half, 8), half)
+        real[place] = dv[side * half : (side + 1) * half, :LANES]
+        imag[place] = dv[side * half : (side + 1) * half, LANES:]
+    inner = [
+        tuple(ref[pl.ds(k, rows, stride=n_rows), :] for ref in (real, imag)) for k in range(n_rows)
+    ]
+    for r, band in enumerate(eight_points(inner, 1)):
+        by_lat[r] = jnp.concatenate(band, axis=1)
     length = own_field.shape[0]
     bundle[0:length] = own_field[...]
     for i, d in enumerate(ORDER):
-        band = pack(dot(lat_t[assign[2 * partner(d) + core]], inner, (1, 0)))
+        band = pack(by_lat[assign[2 * partner(d) + core]])
         if d:
             outs[i - 1][...] = band.astype(BF16)
         else:
-            rows = bundle.shape[0] - FIELD_ROWS
-            band = jnp.concatenate([band, jnp.zeros((3 * rows - band.shape[0], LANES), F32)], axis=0)
-            band = [band[i * rows : (i + 1) * rows] for i in range(3)]
+            tail = bundle.shape[0] - FIELD_ROWS
+            band = jnp.concatenate([band, jnp.zeros((3 * tail - band.shape[0], LANES), F32)], axis=0)
+            band = [band[i * tail : (i + 1) * tail] for i in range(3)]
             bundle[FIELD_ROWS:] = jnp.concatenate(band, axis=1).astype(BF16)
 
 
@@ -325,19 +360,12 @@
     rows = 2 * NB * q
     forward, inverse = lon_tables(KM, length)
 
-    def by_group(table):
-        table = table.reshape(2, NB, 2, q, length).transpose(2, 0, 1, 3, 4)
+    def by_part(table):
+        table = table.reshape(2, NB, 2, q, length).transpose(0, 2, 1, 3, 4)
         return table.reshape(2 * rows, length).astype(BF16)
 
-    cosine, sine = lat_waves(n_rows)
-    waves = np.array([[cosine, sine], [-sine, cosine]])
-    lat = np.einsum("eckr,uv->eukrcv", waves, np.eye(NB * q))
-    lat = lat.reshape(2 * NB * q * n_rows, n_rows * rows).astype(BF16)
-    lat_t = np.ascontiguousarray(lat.T).reshape(n_rows, rows, -1)
-
-    lat, lat_t = jnp.asarray(lat), jnp.asarray(lat_t)
-    inverse = jnp.asarray(by_group(inverse))
-    forward = jnp.asarray(by_group(forward).T)
+    inverse = jnp.asarray(by_part(inverse))
+    forward = jnp.asarray(by_part(forward).T)
 
     def swap(chunks):
         pairs = [[(i, i ^ (2 * d)) for i in range(2 * NB)] for d in ORDER[1:]]
@@ -357,16 +385,14 @@
     received = [sent[0], *swap([sent[d] for d in ORDER[1:]])]
     far = (mode_counts, assignment, w1[0], w2[0], b1[0], forward)
     scratch, _ = scratch_for(*far)
-    far = (*far, lat, lat_t, field)
+    far = (*far, field)
     wide = 2 * LANES
-    mat1, mat2, bias, lat, lat_t, field, forward = call(
+    mat1, mat2, bias, field, forward = call(
         functools.partial(ready_kernel, q),
         (
             shape((wide, wide), BF16),
             shape((wide, wide), BF16),
             shape((1, wide), F32),
-            shape(lat.shape, BF16),
-            shape(lat_t.shape, BF16),
             shape(field.shape, BF16),
             shape(forward.shape, BF16),
         ),
@@ -407,9 +433,11 @@
             pltpu.VMEM((n_rows, rows, wide), F32),
             by_pair,
             pltpu.VMEM((NB * rows, wide), F32),
+            pltpu.VMEM((n_rows * rows, LANES), F32),
+            pltpu.VMEM((n_rows * rows, LANES), F32),
             sems,
         ],
-        (*received, other, slope0, mat1, mat2, bias, lat, lat_t, field),
+        (*received, other, slope0, mat1, mat2, bias, field),
         (assignment,),
     )
     backs = swap(chunks)

time: 30 us -> 29.1 us (0.970)
  Pallas kernels: 8.41 us -> 7.33 us
    pallas_call x8, Pallas kernels: 8.41 us -> 7.33 us  [call(): pl.pallas_call(kernel, out_shape=outs, in_specs=[VMEM] * len(near) + [HBM...]
where the time goes in v15:
time: 29.1 us; the launch traced here: 29 us
  starting transfers between devices  15.2 us (52%)
  Pallas kernels  7.33 us (25%)
  waiting for transfers between devices  5.72 us (20%)
  between operations  0.69 us (2%)
    ppermute x6, starting transfers between devices, swap(): return [lax.ppermute(chunk, 'lat', p) for chunk, p in zip(chunks, pairs)]  10.2 us
    pallas_call x8, Pallas kernels, call(): pl.pallas_call(kernel, out_shape=outs, in_specs=[VMEM] * len(near) + [HBM...  7.33 us
    ppermute x2, starting transfers between devices, turn(): lax.ppermute(value, axis, [(i, (i - 1) % length) for i in range(length)])  4.94 us
    ppermute x6, waiting for transfers between devices, swap(): return [lax.ppermute(chunk, 'lat', p) for chunk, p in zip(chunks, pairs)]  3.45 us
    ppermute x2, waiting for transfers between devices, turn(): lax.ppermute(value, axis, [(i, (i - 1) % length) for i in range(length)])  1.18 us
    ppermute x1, waiting for transfers between devices, paired_blocks(): other = lax.ppermute(own, 'lat', [(i, i ^ 1) for i in range(2 * NB)])  1.1 us
  transfers between devices with their start and end apart: 9, of which 5 were waited for; matrix products, arithmetic and copies ran while one was open for 0% of the time, Pallas kernels for 10%

profile of v15, /device:TPU:0, one launch (start us, length us, event | category | flops | bytes accessed | tf_op | source)
XLA Modules:
  0.0 29.0 jit_solution(7373600609077744542)
XLA Ops:
  0.6 1.7 %shard_map.120 = (bf16[72,384]{1,0:T(8,128)(2,1)S(1)}, bf16[72,384]{1,0:T(8,128)(2,1)S(1)}, bf16[72,384]{1,0:T(8,128)(2,1)S(1)}, bf16[72,384]{1,0:T(8,128)(2,1)S(1)}) custom-call(s32[8]{0:T(128)} %refs_0_.3, s32[8]{0:T(128)} %refs_10_.1, bf16[180,384]{1,0:T(8,128)(2,1)} %bitcast.16, bf16[144,180]{1,0:T(8,128)(2,1)} %constant.4.clone.refs_3_, ...), custom_call_target="tpu_custom_call" | custom-call | flops 100000000 | bytes 1000000 | tf_op jit(solution)/shard_map/pallas_call | solution.py:337
  2.3 5.1 %collective-permute-start = (bf16[72,384]{1,0:T(8,128)(2,1)S(1)}, bf16[72,384]{1,0:T(8,128)(2,1)S(1)}, u32[]{:S(2)}, u32[]{:S(2)}) collective-permute-start(bf16[72,384]{1,0:T(8,128)(2,1)S(1)} %get-tuple-element.28), channel_id=1, source_target_pairs={{0,6},{1,7},{2,4},{3,5},{4,2},{5,3},{6,0},{7,1},{8,14},{9,15},{10,... | collective-permute-start | bytes 165896 | tf_op jit(solution)/shard_map/ppermute | solution.py:372
  7.5 0.0 collective-permute-start.1
  7.5 0.6 %collective-permute-start.2 = (bf16[72,384]{1,0:T(8,128)(2,1)S(1)}, bf16[72,384]{1,0:T(8,128)(2,1)S(1)}, u32[]{:S(2)}, u32[]{:S(2)}) collective-permute-start(bf16[72,384]{1,0:T(8,128)(2,1)S(1)} %get-tuple-element.30), channel_id=1, source_target_pairs={{0,2},{1,3},{2,0},{3,1},{4,6},{5,7},{6,4},{7,5},{8,10},{9,11},{10,... | collective-permute-start | bytes 165896 | tf_op jit(solution)/shard_map/ppermute | solution.py:372
  8.1 1.4 %shard_map.121 = (bf16[256,256]{1,0:T(8,128)(2,1)S(1)}, bf16[256,256]{1,0:T(8,128)(2,1)S(1)}, f32[1,256]{1,0:T(1,128)S(1)}, bf16[180,384]{1,0:T(8,128)(2,1)S(1)}, bf16[180,144]{1,0:T(8,128)(2,1)S(1)}) custom-call(s32[8]{0:T(128)} %refs_0_.3, s32[8]{0:T(128)} %refs_10_.1, bf16[2,96,384]{2,1,0:T(8,128)(2,1)} %bitcast.14, bf16[2,96,384]{2,1,0:T(8,128)(2,1)} %bitcast.15, ...), custom_call_target="tpu_custom_call" | custom-call | flops 2000000000 | bytes 1000000 | tf_op jit(solution)/shard_map/pallas_call | solution.py:337
  9.5 0.3 %collective-permute-done.refs_1_ = bf16[72,384]{1,0:T(8,128)(2,1)S(1)} collective-permute-done((bf16[72,384]{1,0:T(8,128)(2,1)S(1)}, bf16[72,384]{1,0:T(8,128)(2,1)S(1)}, u32[]{:S(2)}, u32[]{:S(2)}) %collective-permute-start) | collective-permute-done | bytes 55328 | tf_op jit(solution)/shard_map/ppermute | solution.py:372
  9.8 2.7 %collective-permute-done.1.refs_2_ = bf16[72,384]{1,0:T(8,128)(2,1)S(1)} collective-permute-done((bf16[72,384]{1,0:T(8,128)(2,1)S(1)}, bf16[72,384]{1,0:T(8,128)(2,1)S(1)}, u32[]{:S(2)}, u32[]{:S(2)}) %collective-permute-start.1) | collective-permute-done | bytes 55328 | tf_op jit(solution)/shard_map/ppermute | solution.py:372
  12.5 0.0 collective-permute-done.2.refs_3_
  12.5 0.1 collective-permute-start.3
  12.6 0.4 %shard_map.123 = (bf16[288,256]{1,0:T(8,128)(2,1)S(1)}, bf16[288,256]{1,0:T(8,128)(2,1)S(1)}, f32[288,256]{1,0:T(8,128)S(1)}) custom-call(bf16[72,384]{1,0:T(8,128)(2,1)S(1)} %get-tuple-element.27.refs_0_, bf16[72,384]{1,0:T(8,128)(2,1)S(1)} %collective-permute-done.refs_1_, bf16[72,384]{1,0:T(8,128)(2,1)S(1)} %collective-permute-done.1.refs_2_, ...), custom_call_target="tpu_custom_call" | custom-call | flops 2000000000 | bytes 1000000 | tf_op jit(solution)/shard_map/pallas_call | solution.py:337
  13.0 1.1 %collective-permute-done.3.refs_4_ = bf16[4,72,384]{2,1,0:T(8,128)(2,1)S(1)} collective-permute-done((bf16[4,72,384]{2,1,0:T(8,128)(2,1)S(1)}, bf16[4,72,384]{2,1,0:T(8,128)(2,1)S(1)}, u32[]{:S(2)}, u32[]{:S(2)}) %collective-permute-start.3) | collective-permute-done | bytes 221216 | tf_op jit(solution)/shard_map/ppermute | solution.py:411
  14.1 1.6 %shard_map.124 = (bf16[112,128]{1,0:T(8,128)(2,1)S(1)}, bf16[112,128]{1,0:T(8,128)(2,1)S(1)}, bf16[112,128]{1,0:T(8,128)(2,1)S(1)}, bf16[240,384]{1,0:T(8,128)(2...) custom-call(bf16[72,384]{1,0:T(8,128)(2,1)S(1)} %get-tuple-element.2, ...), custom_call_target="tpu_custom_call" | custom-call | flops 100000000 | bytes 1000000 | tf_op jit(solution)/shard_map/pallas_call | solution.py:337
  15.7 2.6 %collective-permute-start.4 = (bf16[112,128]{1,0:T(8,128)(2,1)S(1)}, bf16[112,128]{1,0:T(8,128)(2,1)S(1)}, u32[]{:S(2)}, u32[]{:S(2)}) collective-permute-start(bf16[112,128]{1,0:T(8,128)(2,1)S(1)} %get-tuple-element.36), channel_id=1, source_target_pairs={{0,6},{1,7},{2,4},{3,5},{4,2},{5,3},{6,0},{7,1},{8,14},{9,15},{10,... | collective-permute-start | bytes 86024 | tf_op jit(solution)/shard_map/ppermute | solution.py:372
  18.3 0.0 collective-permute-start.5
  18.3 1.9 %collective-permute-start.6 = (bf16[112,128]{1,0:T(8,128)(2,1)S(1)}, bf16[112,128]{1,0:T(8,128)(2,1)S(1)}, u32[]{:S(2)}, u32[]{:S(2)}) collective-permute-start(bf16[112,128]{1,0:T(8,128)(2,1)S(1)} %get-tuple-element.38), channel_id=1, source_target_pairs={{0,2},{1,3},{2,0},{3,1},{4,6},{5,7},{6,4},{7,5},{8,10},{9,11},{10,... | collective-permute-start | bytes 86024 | tf_op jit(solution)/shard_map/ppermute | solution.py:372
  20.2 2.4 %collective-permute-start.8 = (bf16[240,384]{1,0:T(8,128)(2,1)S(1)}, bf16[240,384]{1,0:T(8,128)(2,1)S(1)}, u32[]{:S(2)}, u32[]{:S(2)}) collective-permute-start(bf16[240,384]{1,0:T(8,128)(2,1)S(1)} %get-tuple-element.39), channel_id=1, source_target_pairs={{0,24},{8,0},{16,8},{24,16},{1,25},{9,1},{17,9},{25,17},{2,26},{10... | collective-permute-start | bytes 552968 | tf_op jit(solution)/shard_map/ppermute | solution.py:28
  22.6 0.0 collective-permute-done.4.refs_0_
  22.6 0.4 %collective-permute-done.5.refs_1_ = bf16[112,128]{1,0:T(8,128)(2,1)S(1)} collective-permute-done((bf16[112,128]{1,0:T(8,128)(2,1)S(1)}, bf16[112,128]{1,0:T(8,128)(2,1)S(1)}, u32[]{:S(2)}, u32[]{:S(2)}) %collective-permute-start.5) | collective-permute-done | bytes 28704 | tf_op jit(solution)/shard_map/ppermute | solution.py:372
  23.1 0.0 collective-permute-done.6.refs_2_
  23.1 2.5 %collective-permute-start.7 = (bf16[3,112,128]{2,1,0:T(8,128)(2,1)S(1)}, bf16[3,112,128]{2,1,0:T(8,128)(2,1)S(1)}, u32[]{:S(2)}, u32[]{:S(2)}) collective-permute-start(bf16[3,112,128]{2,1,0:T(8,128)(2,1)S(1)} %shard_map.125), channel_id=1, source_target_pairs={{0,24},{8,0},{16,8},{24,16},{1,25},{9,1},{17,9},{25,17},{2,26},{10... | collective-permute-start | bytes 258056 | tf_op jit(solution)/shard_map/ppermute | solution.py:28
  25.6 1.1 %shard_map.127 = (f32[2,48,96]{2,1,0:T(8,128)}, f32[2,48,96]{2,1,0:T(8,128)}, f32[2,48]{1,0:T(2,128)}) custom-call(bf16[288,256]{1,0:T(8,128)(2,1)S(1)} %get-tuple-element.41.points0, bf16[288,256]{1,0:T(8,128)(2,1)S(1)} %get-tuple-element.42.hidden0, bf16[288,256]{1,0:T(8,128)(2,1)S(1)} %get-tuple-element.43.points1, ...), custom_call_target="tpu_custom_call" | custom-call | flops 2000000000 | bytes 1000000 | tf_op jit(solution)/shard_map/pallas_call | solution.py:337
  26.7 1.2 %collective-permute-done.7.three = bf16[3,112,128]{2,1,0:T(8,128)(2,1)S(1)} collective-permute-done((bf16[3,112,128]{2,1,0:T(8,128)(2,1)S(1)}, bf16[3,112,128]{2,1,0:T(8,128)(2,1)S(1)}, u32[]{:S(2)}, u32[]{:S(2)}) %collective-permute-start.7) | collective-permute-done | bytes 86048 | tf_op jit(solution)/shard_map/ppermute | solution.py:28
  27.9 0.0 collective-permute-done.8.bundle
  27.9 1.1 %shard_map.126 = bf16[180,384]{1,0:T(8,128)(2,1)} custom-call(bf16[3,112,128]{2,1,0:T(8,128)(2,1)S(1)} %collective-permute-done.7.three, bf16[240,384]{1,0:T(8,128)(2,1)S(1)} %collective-permute-done.8.bundle, bf16[180,144]{1,0:T(8,128)(2,1)S(1)} %get-tuple-element.40.table), custom_call_target="tpu_custom_call" | custom-call | flops 100000000 | bytes 1000000 | tf_op jit(solution)/shard_map/pallas_call | solution.py:337
  (2 shorter events, 0.0 us)
Async XLA Ops:
  2.3 7.5 %collective-permute-start = (bf16[72,384]{1,0:T(8,128)(2,1)S(1)}, bf16[72,384]{1,0:T(8,128)(2,1)S(1)}, u32[]{:S(2)}, u32[]{:S(2)}) collective-permute-start(bf16[72,384]{1,0:T(8,128)(2,1)S(1)} %get-tuple-element.28), channel_id=1, source_target_pairs={{0,6},{1,7},{2,4},{3,5},{4,2},{5,3},{6,0},{7,1},{8,14},{9,15},{10,... | collective-permute-start | bytes 165896 | tf_op jit(solution)/shard_map/ppermute | solution.py:372
  7.5 5.1 %collective-permute-start.1 = (bf16[72,384]{1,0:T(8,128)(2,1)S(1)}, bf16[72,384]{1,0:T(8,128)(2,1)S(1)}, u32[]{:S(2)}, u32[]{:S(2)}) collective-permute-start(bf16[72,384]{1,0:T(8,128)(2,1)S(1)} %get-tuple-element.29), channel_id=1, source_target_pairs={{0,4},{1,5},{2,6},{3,7},{4,0},{5,1},{6,2},{7,3},{8,12},{9,13},{10,... | collective-permute-start | bytes 165896 | tf_op jit(solution)/shard_map/ppermute | solution.py:372
  7.5 5.1 %collective-permute-start.2 = (bf16[72,384]{1,0:T(8,128)(2,1)S(1)}, bf16[72,384]{1,0:T(8,128)(2,1)S(1)}, u32[]{:S(2)}, u32[]{:S(2)}) collective-permute-start(bf16[72,384]{1,0:T(8,128)(2,1)S(1)} %get-tuple-element.30), channel_id=1, source_target_pairs={{0,2},{1,3},{2,0},{3,1},{4,6},{5,7},{6,4},{7,5},{8,10},{9,11},{10,... | collective-permute-start | bytes 165896 | tf_op jit(solution)/shard_map/ppermute | solution.py:372
  12.5 1.5 %collective-permute-start.3 = (bf16[4,72,384]{2,1,0:T(8,128)(2,1)S(1)}, bf16[4,72,384]{2,1,0:T(8,128)(2,1)S(1)}, u32[]{:S(2)}, u32[]{:S(2)}) collective-permute-start(bf16[4,72,384]{2,1,0:T(8,128)(2,1)S(1)} %shard_map.122), channel_id=1, source_target_pairs={{0,1},{1,0},{2,3},{3,2},{4,5},{5,4},{6,7},{7,6},{8,9},{9,8},{10,11... | collective-permute-start | bytes 663560 | tf_op jit(solution)/shard_map/ppermute | solution.py:411
  15.7 6.9 %collective-permute-start.4 = (bf16[112,128]{1,0:T(8,128)(2,1)S(1)}, bf16[112,128]{1,0:T(8,128)(2,1)S(1)}, u32[]{:S(2)}, u32[]{:S(2)}) collective-permute-start(bf16[112,128]{1,0:T(8,128)(2,1)S(1)} %get-tuple-element.36), channel_id=1, source_target_pairs={{0,6},{1,7},{2,4},{3,5},{4,2},{5,3},{6,0},{7,1},{8,14},{9,15},{10,... | collective-permute-start | bytes 86024 | tf_op jit(solution)/shard_map/ppermute | solution.py:372
  18.3 4.8 %collective-permute-start.5 = (bf16[112,128]{1,0:T(8,128)(2,1)S(1)}, bf16[112,128]{1,0:T(8,128)(2,1)S(1)}, u32[]{:S(2)}, u32[]{:S(2)}) collective-permute-start(bf16[112,128]{1,0:T(8,128)(2,1)S(1)} %get-tuple-element.37), channel_id=1, source_target_pairs={{0,4},{1,5},{2,6},{3,7},{4,0},{5,1},{6,2},{7,3},{8,12},{9,13},{10,... | collective-permute-start | bytes 86024 | tf_op jit(solution)/shard_map/ppermute | solution.py:372
  18.3 4.8 %collective-permute-start.6 = (bf16[112,128]{1,0:T(8,128)(2,1)S(1)}, bf16[112,128]{1,0:T(8,128)(2,1)S(1)}, u32[]{:S(2)}, u32[]{:S(2)}) collective-permute-start(bf16[112,128]{1,0:T(8,128)(2,1)S(1)} %get-tuple-element.38), channel_id=1, source_target_pairs={{0,2},{1,3},{2,0},{3,1},{4,6},{5,7},{6,4},{7,5},{8,10},{9,11},{10,... | collective-permute-start | bytes 86024 | tf_op jit(solution)/shard_map/ppermute | solution.py:372
  20.2 7.7 %collective-permute-start.8 = (bf16[240,384]{1,0:T(8,128)(2,1)S(1)}, bf16[240,384]{1,0:T(8,128)(2,1)S(1)}, u32[]{:S(2)}, u32[]{:S(2)}) collective-permute-start(bf16[240,384]{1,0:T(8,128)(2,1)S(1)} %get-tuple-element.39), channel_id=1, source_target_pairs={{0,24},{8,0},{16,8},{24,16},{1,25},{9,1},{17,9},{25,17},{2,26},{10... | collective-permute-start | bytes 552968 | tf_op jit(solution)/shard_map/ppermute | solution.py:28
  23.1 4.8 %collective-permute-start.7 = (bf16[3,112,128]{2,1,0:T(8,128)(2,1)S(1)}, bf16[3,112,128]{2,1,0:T(8,128)(2,1)S(1)}, u32[]{:S(2)}, u32[]{:S(2)}) collective-permute-start(bf16[3,112,128]{2,1,0:T(8,128)(2,1)S(1)} %shard_map.125), channel_id=1, source_target_pairs={{0,24},{8,0},{16,8},{24,16},{1,25},{9,1},{17,9},{25,17},{2,26},{10... | collective-permute-start | bytes 258056 | tf_op jit(solution)/shard_map/ppermute | solution.py:28

commit v16 on v15

--- a/solution.py
+++ b/solution.py
@@ -139,11 +139,19 @@
 
 
 def analyse_kernel(q, *refs):
-    hbm, outs, held, (by_block, sems) = refs[:5], refs[5:9], refs[9:14], refs[14:]
+    hbm, outs, held, (lines, by_block, sems) = refs[:5], refs[5:9], refs[9:14], refs[14:]
     counts, assign, field, table, saved = held
     copies = fetch(sems, hbm, held)
     wait(copies[4:])
-    parts = [saved[:, c, :].astype(F32) for c in range(2)]
+    n_rows, _, columns = saved.shape
+    both = saved[...].reshape(2 * n_rows, columns).astype(F32)
+    tiles = range(columns // LANES)
+    for i in tiles:
+        lines[i] = both[:, i * LANES : (i + 1) * LANES]
+    parts = [
+        jnp.concatenate([lines[i, pl.ds(c, n_rows, stride=2), :] for i in tiles], axis=1)
+        for c in range(2)
+    ]
     points = [
         [
             jnp.concatenate([window(part, (mm * NB + n) * BS) for mm in range(q)], axis=0)
@@ -238,25 +246,30 @@
     slope[...] = sig * (1.0 + pre * (1.0 - sig))
 
 
+def row_spectrum(chunk):
+    return jnp.concatenate([window(chunk, j * BS) for j in range(2)], axis=1)
+
+
 def own_kernel(*refs):
-    mat1, bias, points, hidden, slope, by_pair = refs[NB:]
+    mat1, bias, points, hidden, slope, spectra, by_pair = refs[NB:]
     chunks = [refs[i][...].astype(F32) for i in ORDER]
     silu_points(chunks, mat1, bias, by_pair, points, hidden, slope)
+    for d, chunk in enumerate(chunks):
+        spectra[d] = row_spectrum(chunk)
 
 
 def filter_kernel(*refs):
-    owns, (other, slope_own, mat1, mat2, bias, own_field, assign_hbm) = refs[:4], refs[4:11]
-    outs, (bundle, points, hidden, grad_pre, grad_y) = refs[11:14], refs[14:19]
-    assign, by_lat, by_pair, slope, real, imag, sems = refs[19:]
+    spectra, other, slope_own, mat1, mat2, bias, own_field, assign_hbm = refs[:8]
+    outs, (bundle, points, hidden, grad_pre, grad_y) = refs[8:11], refs[11:16]
+    assign, by_lat, by_pair, slope, real, imag, sems = refs[16:]
     copies = fetch(sems, (assign_hbm,), (assign,))
     core = lax.rem(lax.axis_index("lat"), 2)
-    sides = [[owns[i][...].astype(F32) for i in ORDER], [other[i].astype(F32) for i in ORDER]]
-    silu_points(sides[1], mat1, bias, by_pair, points, hidden, slope)
+    chunks = [other[i].astype(F32) for i in ORDER]
+    silu_points(chunks, mat1, bias, by_pair, points, hidden, slope)
     wait(copies)
-    for side, chunks in zip((core, 1 - core), sides):
-        for d, chunk in enumerate(chunks):
-            parts = [window(chunk, j * BS) for j in range(2)]
-            by_lat[assign[2 * partner(d) + side]] = jnp.concatenate(parts, axis=1)
+    for d, chunk in enumerate(chunks):
+        by_lat[assign[2 * partner(d) + core]] = spectra[d]
+        by_lat[assign[2 * partner(d) + 1 - core]] = row_spectrum(chunk)
     n_rows, rows, _ = by_lat.shape
     half = rows * n_rows // 2
     waves = eight_points([(by_lat[r][:, :LANES], by_lat[r][:, LANES:]) for r in range(n_rows)], -1)
@@ -375,6 +388,7 @@
     shape = jax.ShapeDtypeStruct
     far = (mode_counts, assignment, field, inverse, spec_saved[0])
     scratch, sems = scratch_for(*far)
+    scratch.append(pltpu.VMEM((spec_saved.shape[3] // LANES, 2 * n_rows, LANES), F32))
     sent = call(
         functools.partial(analyse_kernel, q),
         (shape((rows, width), BF16),) * NB,
@@ -412,9 +426,9 @@
     vectors = shape((NB * rows, wide), BF16)
     slopes = shape((NB * rows, wide), F32)
     by_pair = pltpu.VMEM((NB, rows, wide), F32)
-    points0, hidden0, slope0 = call(
+    points0, hidden0, slope0, spectra = call(
         own_kernel,
-        (vectors, vectors, slopes),
+        (vectors, vectors, slopes, shape((NB, rows, wide), F32)),
         [by_pair],
         (*received, mat1, bias),
         (),
@@ -437,7 +451,7 @@
             pltpu.VMEM((n_rows * rows, LANES), F32),
             sems,
         ],
-        (*received, other, slope0, mat1, mat2, bias, field),
+        (spectra, other, slope0, mat1, mat2, bias, field),
         (assignment,),
     )
     backs = swap(chunks)

time: 29.1 us -> 29.2 us (level)
  no operation moved by 1% of the time
where the time goes in v16:
time: 29.2 us; the launch traced here: 29 us
  starting transfers between devices  15.2 us (52%)
  Pallas kernels  7.39 us (25%)
  waiting for transfers between devices  5.73 us (20%)
  between operations  0.69 us (2%)
    ppermute x6, starting transfers between devices, swap(): return [lax.ppermute(chunk, 'lat', p) for chunk, p in zip(chunks, pairs)]  10.2 us
    pallas_call x8, Pallas kernels, call(): pl.pallas_call(kernel, out_shape=outs, in_specs=[VMEM] * len(near) + [HBM...  7.39 us
    ppermute x2, starting transfers between devices, turn(): lax.ppermute(value, axis, [(i, (i - 1) % length) for i in range(length)])  4.94 us
    ppermute x6, waiting for transfers between devices, swap(): return [lax.ppermute(chunk, 'lat', p) for chunk, p in zip(chunks, pairs)]  3.45 us
    ppermute x2, waiting for transfers between devices, turn(): lax.ppermute(value, axis, [(i, (i - 1) % length) for i in range(length)])  1.18 us
    ppermute x1, waiting for transfers between devices, paired_blocks(): other = lax.ppermute(own, 'lat', [(i, i ^ 1) for i in range(2 * NB)])  1.1 us
  transfers between devices with their start and end apart: 9, of which 5 were waited for; matrix products, arithmetic and copies ran while one was open for 0% of the time, Pallas kernels for 10%

profile of v16, /device:TPU:0, one launch (start us, length us, event | category | flops | bytes accessed | tf_op | source)
XLA Modules:
  0.0 29.0 jit_solution(17589365586346167354)
XLA Ops:
  0.6 1.7 %shard_map.120 = (bf16[72,384]{1,0:T(8,128)(2,1)S(1)}, bf16[72,384]{1,0:T(8,128)(2,1)S(1)}, bf16[72,384]{1,0:T(8,128)(2,1)S(1)}, bf16[72,384]{1,0:T(8,128)(2,1)S(1)}) custom-call(s32[8]{0:T(128)} %refs_0_.3, s32[8]{0:T(128)} %refs_7_.1, bf16[180,384]{1,0:T(8,128)(2,1)} %bitcast.16, bf16[144,180]{1,0:T(8,128)(2,1)} %constant.4.clone.refs_3_, ...), custom_call_target="tpu_custom_call" | custom-call | flops 100000000 | bytes 1000000 | tf_op jit(solution)/shard_map/pallas_call | solution.py:350
  2.4 5.1 %collective-permute-start = (bf16[72,384]{1,0:T(8,128)(2,1)S(1)}, bf16[72,384]{1,0:T(8,128)(2,1)S(1)}, u32[]{:S(2)}, u32[]{:S(2)}) collective-permute-start(bf16[72,384]{1,0:T(8,128)(2,1)S(1)} %get-tuple-element.29), channel_id=1, source_target_pairs={{0,6},{1,7},{2,4},{3,5},{4,2},{5,3},{6,0},{7,1},{8,14},{9,15},{10,... | collective-permute-start | bytes 165896 | tf_op jit(solution)/shard_map/ppermute | solution.py:385
  7.5 0.0 collective-permute-start.1
  7.5 0.6 %collective-permute-start.2 = (bf16[72,384]{1,0:T(8,128)(2,1)S(1)}, bf16[72,384]{1,0:T(8,128)(2,1)S(1)}, u32[]{:S(2)}, u32[]{:S(2)}) collective-permute-start(bf16[72,384]{1,0:T(8,128)(2,1)S(1)} %get-tuple-element.31), channel_id=1, source_target_pairs={{0,2},{1,3},{2,0},{3,1},{4,6},{5,7},{6,4},{7,5},{8,10},{9,11},{10,... | collective-permute-start | bytes 165896 | tf_op jit(solution)/shard_map/ppermute | solution.py:385
  8.1 1.4 %shard_map.121 = (bf16[256,256]{1,0:T(8,128)(2,1)S(1)}, bf16[256,256]{1,0:T(8,128)(2,1)S(1)}, f32[1,256]{1,0:T(1,128)S(1)}, bf16[180,384]{1,0:T(8,128)(2,1)S(1)}, bf16[180,144]{1,0:T(8,128)(2,1)S(1)}) custom-call(s32[8]{0:T(128)} %refs_0_.3, s32[8]{0:T(128)} %refs_7_.1, bf16[2,96,384]{2,1,0:T(8,128)(2,1)} %bitcast.14, bf16[2,96,384]{2,1,0:T(8,128)(2,1)} %bitcast.15, ...), custom_call_target="tpu_custom_call" | custom-call | flops 2000000000 | bytes 1000000 | tf_op jit(solution)/shard_map/pallas_call | solution.py:350
  9.5 0.3 %collective-permute-done.refs_1_ = bf16[72,384]{1,0:T(8,128)(2,1)S(1)} collective-permute-done((bf16[72,384]{1,0:T(8,128)(2,1)S(1)}, bf16[72,384]{1,0:T(8,128)(2,1)S(1)}, u32[]{:S(2)}, u32[]{:S(2)}) %collective-permute-start) | collective-permute-done | bytes 55328 | tf_op jit(solution)/shard_map/ppermute | solution.py:385
  9.8 2.7 %collective-permute-done.1.refs_2_ = bf16[72,384]{1,0:T(8,128)(2,1)S(1)} collective-permute-done((bf16[72,384]{1,0:T(8,128)(2,1)S(1)}, bf16[72,384]{1,0:T(8,128)(2,1)S(1)}, u32[]{:S(2)}, u32[]{:S(2)}) %collective-permute-start.1) | collective-permute-done | bytes 55328 | tf_op jit(solution)/shard_map/ppermute | solution.py:385
  12.5 0.0 collective-permute-done.2.refs_3_
  12.6 0.1 collective-permute-start.3
  12.6 0.4 %shard_map.122 = (bf16[288,256]{1,0:T(8,128)(2,1)S(1)}, bf16[288,256]{1,0:T(8,128)(2,1)S(1)}, f32[288,256]{1,0:T(8,128)S(1)}, f32[4,72,256]{2,1,0:T(8,128)S(1)}) custom-call(bf16[72,384]{1,0:T(8,128)(2,1)S(1)} %get-tuple-element.28.refs_0_, bf16[72,384]{1,0:T(8,128)(2,1)S(1)} %collective-permute-done.refs_1_, ...), custom_call_target="tpu_custom_call" | custom-call | flops 2000000000 | bytes 1000000 | tf_op jit(solution)/shard_map/pallas_call | solution.py:350
  13.0 1.1 %collective-permute-done.3.refs_1_ = bf16[4,72,384]{2,1,0:T(8,128)(2,1)S(1)} collective-permute-done((bf16[4,72,384]{2,1,0:T(8,128)(2,1)S(1)}, bf16[4,72,384]{2,1,0:T(8,128)(2,1)S(1)}, u32[]{:S(2)}, u32[]{:S(2)}) %collective-permute-start.3) | collective-permute-done | bytes 221216 | tf_op jit(solution)/shard_map/ppermute | solution.py:425
  14.1 1.7 %shard_map.124 = (bf16[112,128]{1,0:T(8,128)(2,1)S(1)}, bf16[112,128]{1,0:T(8,128)(2,1)S(1)}, bf16[112,128]{1,0:T(8,128)(2,1)S(1)}, bf16[240,384]{1,0:T(8,128)(2...) custom-call(f32[4,72,256]{2,1,0:T(8,128)S(1)} %get-tuple-element.34., ...), custom_call_target="tpu_custom_call" | custom-call | flops 100000000 | bytes 1000000 | tf_op jit(solution)/shard_map/pallas_call | solution.py:350
  15.8 2.6 %collective-permute-start.4 = (bf16[112,128]{1,0:T(8,128)(2,1)S(1)}, bf16[112,128]{1,0:T(8,128)(2,1)S(1)}, u32[]{:S(2)}, u32[]{:S(2)}) collective-permute-start(bf16[112,128]{1,0:T(8,128)(2,1)S(1)} %get-tuple-element.38), channel_id=1, source_target_pairs={{0,6},{1,7},{2,4},{3,5},{4,2},{5,3},{6,0},{7,1},{8,14},{9,15},{10,... | collective-permute-start | bytes 86024 | tf_op jit(solution)/shard_map/ppermute | solution.py:385
  18.3 0.0 collective-permute-start.5
  18.3 1.9 %collective-permute-start.6 = (bf16[112,128]{1,0:T(8,128)(2,1)S(1)}, bf16[112,128]{1,0:T(8,128)(2,1)S(1)}, u32[]{:S(2)}, u32[]{:S(2)}) collective-permute-start(bf16[112,128]{1,0:T(8,128)(2,1)S(1)} %get-tuple-element.40), channel_id=1, source_target_pairs={{0,2},{1,3},{2,0},{3,1},{4,6},{5,7},{6,4},{7,5},{8,10},{9,11},{10,... | collective-permute-start | bytes 86024 | tf_op jit(solution)/shard_map/ppermute | solution.py:385
  20.2 2.4 %collective-permute-start.8 = (bf16[240,384]{1,0:T(8,128)(2,1)S(1)}, bf16[240,384]{1,0:T(8,128)(2,1)S(1)}, u32[]{:S(2)}, u32[]{:S(2)}) collective-permute-start(bf16[240,384]{1,0:T(8,128)(2,1)S(1)} %get-tuple-element.41), channel_id=1, source_target_pairs={{0,24},{8,0},{16,8},{24,16},{1,25},{9,1},{17,9},{25,17},{2,26},{10... | collective-permute-start | bytes 552968 | tf_op jit(solution)/shard_map/ppermute | solution.py:28
  22.7 0.0 collective-permute-done.4.refs_0_
  22.7 0.4 %collective-permute-done.5.refs_1_ = bf16[112,128]{1,0:T(8,128)(2,1)S(1)} collective-permute-done((bf16[112,128]{1,0:T(8,128)(2,1)S(1)}, bf16[112,128]{1,0:T(8,128)(2,1)S(1)}, u32[]{:S(2)}, u32[]{:S(2)}) %collective-permute-start.5) | collective-permute-done | bytes 28704 | tf_op jit(solution)/shard_map/ppermute | solution.py:385
  23.1 0.0 collective-permute-done.6.refs_2_
  23.1 2.5 %collective-permute-start.7 = (bf16[3,112,128]{2,1,0:T(8,128)(2,1)S(1)}, bf16[3,112,128]{2,1,0:T(8,128)(2,1)S(1)}, u32[]{:S(2)}, u32[]{:S(2)}) collective-permute-start(bf16[3,112,128]{2,1,0:T(8,128)(2,1)S(1)} %shard_map.125), channel_id=1, source_target_pairs={{0,24},{8,0},{16,8},{24,16},{1,25},{9,1},{17,9},{25,17},{2,26},{10... | collective-permute-start | bytes 258056 | tf_op jit(solution)/shard_map/ppermute | solution.py:28
  25.6 1.1 %shard_map.127 = (f32[2,48,96]{2,1,0:T(8,128)}, f32[2,48,96]{2,1,0:T(8,128)}, f32[2,48]{1,0:T(2,128)}) custom-call(bf16[288,256]{1,0:T(8,128)(2,1)S(1)} %get-tuple-element.43.points0, bf16[288,256]{1,0:T(8,128)(2,1)S(1)} %get-tuple-element.44.hidden0, bf16[288,256]{1,0:T(8,128)(2,1)S(1)} %get-tuple-element.45.points1, ...), custom_call_target="tpu_custom_call" | custom-call | flops 2000000000 | bytes 1000000 | tf_op jit(solution)/shard_map/pallas_call | solution.py:350
  26.7 1.2 %collective-permute-done.7.three = bf16[3,112,128]{2,1,0:T(8,128)(2,1)S(1)} collective-permute-done((bf16[3,112,128]{2,1,0:T(8,128)(2,1)S(1)}, bf16[3,112,128]{2,1,0:T(8,128)(2,1)S(1)}, u32[]{:S(2)}, u32[]{:S(2)}) %collective-permute-start.7) | collective-permute-done | bytes 86048 | tf_op jit(solution)/shard_map/ppermute | solution.py:28
  27.9 0.0 collective-permute-done.8.bundle
  27.9 1.1 %shard_map.126 = bf16[180,384]{1,0:T(8,128)(2,1)} custom-call(bf16[3,112,128]{2,1,0:T(8,128)(2,1)S(1)} %collective-permute-done.7.three, bf16[240,384]{1,0:T(8,128)(2,1)S(1)} %collective-permute-done.8.bundle, bf16[180,144]{1,0:T(8,128)(2,1)S(1)} %get-tuple-element.42.table), custom_call_target="tpu_custom_call" | custom-call | flops 100000000 | bytes 1000000 | tf_op jit(solution)/shard_map/pallas_call | solution.py:350
  (2 shorter events, 0.0 us)
Async XLA Ops:
  2.4 7.5 %collective-permute-start = (bf16[72,384]{1,0:T(8,128)(2,1)S(1)}, bf16[72,384]{1,0:T(8,128)(2,1)S(1)}, u32[]{:S(2)}, u32[]{:S(2)}) collective-permute-start(bf16[72,384]{1,0:T(8,128)(2,1)S(1)} %get-tuple-element.29), channel_id=1, source_target_pairs={{0,6},{1,7},{2,4},{3,5},{4,2},{5,3},{6,0},{7,1},{8,14},{9,15},{10,... | collective-permute-start | bytes 165896 | tf_op jit(solution)/shard_map/ppermute | solution.py:385
  7.5 5.1 %collective-permute-start.1 = (bf16[72,384]{1,0:T(8,128)(2,1)S(1)}, bf16[72,384]{1,0:T(8,128)(2,1)S(1)}, u32[]{:S(2)}, u32[]{:S(2)}) collective-permute-start(bf16[72,384]{1,0:T(8,128)(2,1)S(1)} %get-tuple-element.30), channel_id=1, source_target_pairs={{0,4},{1,5},{2,6},{3,7},{4,0},{5,1},{6,2},{7,3},{8,12},{9,13},{10,... | collective-permute-start | bytes 165896 | tf_op jit(solution)/shard_map/ppermute | solution.py:385
  7.5 5.1 %collective-permute-start.2 = (bf16[72,384]{1,0:T(8,128)(2,1)S(1)}, bf16[72,384]{1,0:T(8,128)(2,1)S(1)}, u32[]{:S(2)}, u32[]{:S(2)}) collective-permute-start(bf16[72,384]{1,0:T(8,128)(2,1)S(1)} %get-tuple-element.31), channel_id=1, source_target_pairs={{0,2},{1,3},{2,0},{3,1},{4,6},{5,7},{6,4},{7,5},{8,10},{9,11},{10,... | collective-permute-start | bytes 165896 | tf_op jit(solution)/shard_map/ppermute | solution.py:385
  12.6 1.5 %collective-permute-start.3 = (bf16[4,72,384]{2,1,0:T(8,128)(2,1)S(1)}, bf16[4,72,384]{2,1,0:T(8,128)(2,1)S(1)}, u32[]{:S(2)}, u32[]{:S(2)}) collective-permute-start(bf16[4,72,384]{2,1,0:T(8,128)(2,1)S(1)} %shard_map.123), channel_id=1, source_target_pairs={{0,1},{1,0},{2,3},{3,2},{4,5},{5,4},{6,7},{7,6},{8,9},{9,8},{10,11... | collective-permute-start | bytes 663560 | tf_op jit(solution)/shard_map/ppermute | solution.py:425
  15.8 6.9 %collective-permute-start.4 = (bf16[112,128]{1,0:T(8,128)(2,1)S(1)}, bf16[112,128]{1,0:T(8,128)(2,1)S(1)}, u32[]{:S(2)}, u32[]{:S(2)}) collective-permute-start(bf16[112,128]{1,0:T(8,128)(2,1)S(1)} %get-tuple-element.38), channel_id=1, source_target_pairs={{0,6},{1,7},{2,4},{3,5},{4,2},{5,3},{6,0},{7,1},{8,14},{9,15},{10,... | collective-permute-start | bytes 86024 | tf_op jit(solution)/shard_map/ppermute | solution.py:385
  18.3 4.8 %collective-permute-start.5 = (bf16[112,128]{1,0:T(8,128)(2,1)S(1)}, bf16[112,128]{1,0:T(8,128)(2,1)S(1)}, u32[]{:S(2)}, u32[]{:S(2)}) collective-permute-start(bf16[112,128]{1,0:T(8,128)(2,1)S(1)} %get-tuple-element.39), channel_id=1, source_target_pairs={{0,4},{1,5},{2,6},{3,7},{4,0},{5,1},{6,2},{7,3},{8,12},{9,13},{10,... | collective-permute-start | bytes 86024 | tf_op jit(solution)/shard_map/ppermute | solution.py:385
  18.3 4.8 %collective-permute-start.6 = (bf16[112,128]{1,0:T(8,128)(2,1)S(1)}, bf16[112,128]{1,0:T(8,128)(2,1)S(1)}, u32[]{:S(2)}, u32[]{:S(2)}) collective-permute-start(bf16[112,128]{1,0:T(8,128)(2,1)S(1)} %get-tuple-element.40), channel_id=1, source_target_pairs={{0,2},{1,3},{2,0},{3,1},{4,6},{5,7},{6,4},{7,5},{8,10},{9,11},{10,... | collective-permute-start | bytes 86024 | tf_op jit(solution)/shard_map/ppermute | solution.py:385
  20.2 7.7 %collective-permute-start.8 = (bf16[240,384]{1,0:T(8,128)(2,1)S(1)}, bf16[240,384]{1,0:T(8,128)(2,1)S(1)}, u32[]{:S(2)}, u32[]{:S(2)}) collective-permute-start(bf16[240,384]{1,0:T(8,128)(2,1)S(1)} %get-tuple-element.41), channel_id=1, source_target_pairs={{0,24},{8,0},{16,8},{24,16},{1,25},{9,1},{17,9},{25,17},{2,26},{10... | collective-permute-start | bytes 552968 | tf_op jit(solution)/shard_map/ppermute | solution.py:28
  23.1 4.8 %collective-permute-start.7 = (bf16[3,112,128]{2,1,0:T(8,128)(2,1)S(1)}, bf16[3,112,128]{2,1,0:T(8,128)(2,1)S(1)}, u32[]{:S(2)}, u32[]{:S(2)}) collective-permute-start(bf16[3,112,128]{2,1,0:T(8,128)(2,1)S(1)} %shard_map.125), channel_id=1, source_target_pairs={{0,24},{8,0},{16,8},{24,16},{1,25},{9,1},{17,9},{25,17},{2,26},{10... | collective-permute-start | bytes 258056 | tf_op jit(solution)/shard_map/ppermute | solution.py:28

commit v17 on v15

--- a/solution.py
+++ b/solution.py
@@ -129,6 +129,14 @@
     return copies
 
 
+def fetch_parts(sems, source, target, parts):
+    return fetch(sems, [source.at[part] for part in parts], [target.at[part] for part in parts])
+
+
+def columns(width):
+    return [(slice(None), pl.ds(i, LANES)) for i in range(0, width, LANES)]
+
+
 def wait(copies):
     for copy in copies:
         copy.wait()
@@ -139,10 +147,13 @@
 
 
 def analyse_kernel(q, *refs):
-    hbm, outs, held, (by_block, sems) = refs[:5], refs[5:9], refs[9:14], refs[14:]
+    hbm, outs, held = refs[:5], refs[5:9], refs[9:14]
+    by_block, few, sems = refs[14:]
     counts, assign, field, table, saved = held
-    copies = fetch(sems, hbm, held)
-    wait(copies[4:])
+    early = fetch_parts(sems.at[0], hbm[4], saved, [pl.ds(k, 2) for k in range(0, 2 * NB, 2)])
+    late = fetch_parts(sems.at[1], hbm[2], field, columns(field.shape[1]))
+    late += fetch(few, hbm[:2] + hbm[3:4], held[:2] + held[3:4])
+    wait(early)
     parts = [saved[:, c, :].astype(F32) for c in range(2)]
     points = [
         [
@@ -151,7 +162,7 @@
         ]
         for n in range(NB)
     ]
-    wait(copies[:4])
+    wait(late)
     rows = by_block.shape[1]
     spectral = jnp.dot(table[...], field[...], preferred_element_type=F32)
     active = counts[assign[lax.axis_index("lat")]]
@@ -165,8 +176,8 @@
 
 
 def ready_kernel(q, *refs):
-    hbm, (mat1, mat2, bias, own_field, own_table) = refs[:7], refs[7:12]
-    counts, assign, w1, w2, b1, table, sems = refs[12:]
+    hbm, (mat1, turned1, turned2, bias, own_field, own_table) = refs[:7], refs[7:13]
+    counts, assign, w1, w2, b1, table, sems = refs[13:]
     copies = fetch(sems, hbm, (counts, assign, w1, w2, b1, table, own_field))
     wait(copies[:6])
     active = counts[assign[lax.axis_index("lat")]]
@@ -184,13 +195,19 @@
         lane = lax.broadcasted_iota(jnp.int32, value.shape, 1)
         return jnp.where(lane < BS, value, 0.0)
 
-    gap = jnp.zeros((LANES - BS, 2 * LANES), BF16)
-    for source, mat in ((w1, mat1), (w2, mat2)):
+    gap = jnp.zeros((LANES - BS, 2 * LANES), F32)
+    for source, mat, turned in ((w1, mat1, turned1), (w2, None, turned2)):
         real, imag = (pick(source[c].astype(F32)) for c in range(2))
-        mat[0:BS] = jnp.concatenate([real, imag], axis=1).astype(BF16)
-        mat[BS:LANES] = gap
-        mat[LANES : LANES + BS] = jnp.concatenate([-imag, real], axis=1).astype(BF16)
-        mat[LANES + BS : 2 * LANES] = gap
+        whole = [
+            jnp.concatenate([real, imag], axis=1),
+            gap,
+            jnp.concatenate([-imag, real], axis=1),
+            gap,
+        ]
+        whole = jnp.concatenate(whole, axis=0)
+        turned[...] = whole.T.astype(BF16)
+        if mat is not None:
+            mat[...] = whole.astype(BF16)
     shift_b = pick(b1[...].astype(F32))
     bias[...] = jnp.concatenate([shift_b[0:1], shift_b[1:2]], axis=1)
     wait(copies[6:])
@@ -245,9 +262,9 @@
 
 
 def filter_kernel(*refs):
-    owns, (other, slope_own, mat1, mat2, bias, own_field, assign_hbm) = refs[:4], refs[4:11]
-    outs, (bundle, points, hidden, grad_pre, grad_y) = refs[11:14], refs[14:19]
-    assign, by_lat, by_pair, slope, real, imag, sems = refs[19:]
+    owns, (other, slope_own, mat1, turned1, turned2, bias, own_field) = refs[:4], refs[4:11]
+    assign_hbm, outs, (bundle, points, hidden, grad_pre, grad_y) = refs[11], refs[12:15], refs[15:20]
+    assign, by_lat, by_pair, slope, real, imag, sems = refs[20:]
     copies = fetch(sems, (assign_hbm,), (assign,))
     core = lax.rem(lax.axis_index("lat"), 2)
     sides = [[owns[i][...].astype(F32) for i in ORDER], [other[i].astype(F32) for i in ORDER]]
@@ -269,9 +286,9 @@
     ]
     dy = jnp.concatenate(dy, axis=1).astype(BF16)
     dy = [jnp.where(core == side, dy[:half], dy[half:]) for side in range(2)]
-    dh = dot(jnp.concatenate(dy, axis=0), mat2[...], (1, 1))
+    dh = dot(jnp.concatenate(dy, axis=0), turned2[...], (1, 0))
     dp = [(dh[:half] * slope_own[...]).astype(BF16), (dh[half:] * slope[...]).astype(BF16)]
-    dv = dot(jnp.concatenate(dp, axis=0), mat1[...], (1, 1)).astype(BF16).astype(F32)
+    dv = dot(jnp.concatenate(dp, axis=0), turned1[...], (1, 0)).astype(BF16).astype(F32)
     for side in range(2):
         grad_y[side] = dy[side]
         grad_pre[side] = dp[side]
@@ -311,34 +328,40 @@
         gb1[c : c + 1] = jnp.where(core == 0, line[:, :half], line[:, half:BS])
 
 
-def compose_kernel(last, three, bundle, table, out, by_block):
+def compose_kernel(last, three, bundle, table, out, by_block, result, sems):
     rows = by_block.shape[1]
     own = bundle[FIELD_ROWS:].astype(F32)
     own = jnp.concatenate([own[:, i * LANES : (i + 1) * LANES] for i in range(3)], axis=0)
     chunks = [own[: three.shape[1]]] + [three[i].astype(F32) for i in range(3)]
     for d, chunk in zip(ORDER, chunks):
         by_block[partner(d)] = jnp.concatenate(unpack(chunk, rows), axis=1)
-    groups = [
-        dense([by_block[n, :, g * LANES : (g + 1) * LANES] for n in range(NB)]) for g in range(2)
+    parts = [
+        dense([by_block[n, :, c * LANES : (c + 1) * LANES] for n in range(NB)]) for c in range(2)
     ]
-    groups = jnp.concatenate(groups, axis=0).astype(BF16)
-    mixed = jnp.dot(table[...], groups, preferred_element_type=F32).astype(BF16)
-    whole = bundle[0 : out.shape[0]].astype(F32) + mixed.astype(F32)
-    out[...] = jnp.where(lax.axis_index("section") == last, 0.0, whole).astype(BF16)
+    parts = jnp.concatenate(parts, axis=0).astype(BF16)
+    none = lax.axis_index("section") == last
+    copies = []
+    for i, (_, tile) in enumerate(columns(out.shape[1])):
+        mixed = jnp.dot(table[...], parts[:, i * LANES : (i + 1) * LANES], preferred_element_type=F32)
+        whole = bundle[0 : out.shape[0], tile].astype(F32) + mixed.astype(BF16).astype(F32)
+        result[:, tile] = jnp.where(none, 0.0, whole).astype(BF16)
+        copies.append(pltpu.make_async_copy(result.at[:, tile], out.at[:, tile], sems.at[i]))
+        copies[-1].start()
+    wait(copies)
 
 
 VMEM = pl.BlockSpec(memory_space=pltpu.VMEM)
 HBM = pl.BlockSpec(memory_space=pltpu.HBM)
 
 
-def call(kernel, outs, scratch, near, far, flops=10**8):
-    many = isinstance(outs, tuple)
+def call(kernel, outs, scratch, near, far, flops=10**8, out_specs=None):
+    out_specs = out_specs or (tuple([VMEM] * len(outs)) if isinstance(outs, tuple) else VMEM)
     many = isinstance(outs, tuple)
     return pl.pallas_call(
         kernel,
         out_shape=outs,
         in_specs=[VMEM] * len(near) + [HBM] * len(far),
-        out_specs=tuple([VMEM] * len(outs)) if many else VMEM,
+        out_specs=out_specs,
         scratch_shapes=scratch,
         cost_estimate=pl.CostEstimate(flops=flops, bytes_accessed=10**6, transcendentals=0),
         compiler_params=pltpu.CompilerParams(vmem_limit_bytes=32 * 2**20),
@@ -378,7 +401,7 @@
     sent = call(
         functools.partial(analyse_kernel, q),
         (shape((rows, width), BF16),) * NB,
-        scratch + [pltpu.VMEM((NB, rows, width), BF16), sems],
+        scratch + [pltpu.VMEM((NB, rows, width), BF16), sems, pltpu.SemaphoreType.DMA((2, 4))],
         (),
         far,
     )
@@ -387,9 +410,10 @@
     scratch, _ = scratch_for(*far)
     far = (*far, field)
     wide = 2 * LANES
-    mat1, mat2, bias, field, forward = call(
+    mat1, turned1, turned2, bias, field, forward = call(
         functools.partial(ready_kernel, q),
         (
+            shape((wide, wide), BF16),
             shape((wide, wide), BF16),
             shape((wide, wide), BF16),
             shape((1, wide), F32),
@@ -437,7 +461,7 @@
             pltpu.VMEM((n_rows * rows, LANES), F32),
             sems,
         ],
-        (*received, other, slope0, mat1, mat2, bias, field),
+        (*received, other, slope0, mat1, turned1, turned2, bias, field),
         (assignment,),
     )
     backs = swap(chunks)
@@ -456,9 +480,14 @@
     shifted = call(
         functools.partial(compose_kernel, lax.axis_size("section") - 1),
         shape((length, width), BF16),
-        [by_pair],
+        [
+            by_pair,
+            pltpu.VMEM((length, width), BF16),
+            pltpu.SemaphoreType.DMA((width // LANES,)),
+        ],
         (three, bundle, forward),
         (),
+        out_specs=HBM,
     )
     shifted = shifted[None, None]
     return shifted, gw1.swapaxes(1, 2)[None], gw2.swapaxes(1, 2)[None], gb1[None]

time: 29.1 us -> 29.1 us (level)
  no operation moved by 1% of the time
where the time goes in v17:
time: 29.1 us; the launch traced here: 28.9 us
  starting transfers between devices  15.2 us (52%)
  Pallas kernels  7.33 us (25%)
  waiting for transfers between devices  5.64 us (19%)
  between operations  0.69 us (2%)
    ppermute x6, starting transfers between devices, swap(): return [lax.ppermute(chunk, 'lat', p) for chunk, p in zip(chunks, pairs)]  10.2 us
    pallas_call x8, Pallas kernels, call(): pl.pallas_call(kernel, out_shape=outs, in_specs=[VMEM] * len(near) + [HBM...  7.33 us
    ppermute x2, starting transfers between devices, turn(): lax.ppermute(value, axis, [(i, (i - 1) % length) for i in range(length)])  4.94 us
    ppermute x6, waiting for transfers between devices, swap(): return [lax.ppermute(chunk, 'lat', p) for chunk, p in zip(chunks, pairs)]  3.36 us
    ppermute x2, waiting for transfers between devices, turn(): lax.ppermute(value, axis, [(i, (i - 1) % length) for i in range(length)])  1.18 us
    ppermute x1, waiting for transfers between devices, paired_blocks(): other = lax.ppermute(own, 'lat', [(i, i ^ 1) for i in range(2 * NB)])  1.1 us
  transfers between devices with their start and end apart: 9, of which 5 were waited for; matrix products, arithmetic and copies ran while one was open for 0% of the time, Pallas kernels for 10%

profile of v17, /device:TPU:0, one launch (start us, length us, event | category | flops | bytes accessed | tf_op | source)
XLA Modules:
  0.0 28.9 jit_solution(3589380106969703086)
XLA Ops:
  0.6 1.6 %shard_map.120 = (bf16[72,384]{1,0:T(8,128)(2,1)S(1)}, bf16[72,384]{1,0:T(8,128)(2,1)S(1)}, bf16[72,384]{1,0:T(8,128)(2,1)S(1)}, bf16[72,384]{1,0:T(8,128)(2,1)S(1)}) custom-call(s32[8]{0:T(128)} %refs_0_.3, s32[8]{0:T(128)} %refs_11_.1, bf16[180,384]{1,0:T(8,128)(2,1)} %bitcast.16, bf16[144,180]{1,0:T(8,128)(2,1)} %constant.4.clone.refs_3_, ...), custom_call_target="tpu_custom_call" | custom-call | flops 100000000 | bytes 1000000 | tf_op jit(solution)/shard_map/pallas_call | solution.py:360
  2.2 5.1 %collective-permute-start = (bf16[72,384]{1,0:T(8,128)(2,1)S(1)}, bf16[72,384]{1,0:T(8,128)(2,1)S(1)}, u32[]{:S(2)}, u32[]{:S(2)}) collective-permute-start(bf16[72,384]{1,0:T(8,128)(2,1)S(1)} %get-tuple-element.29), channel_id=1, source_target_pairs={{0,6},{1,7},{2,4},{3,5},{4,2},{5,3},{6,0},{7,1},{8,14},{9,15},{10,... | collective-permute-start | bytes 165896 | tf_op jit(solution)/shard_map/ppermute | solution.py:395
  7.3 0.0 collective-permute-start.1
  7.3 0.6 %collective-permute-start.2 = (bf16[72,384]{1,0:T(8,128)(2,1)S(1)}, bf16[72,384]{1,0:T(8,128)(2,1)S(1)}, u32[]{:S(2)}, u32[]{:S(2)}) collective-permute-start(bf16[72,384]{1,0:T(8,128)(2,1)S(1)} %get-tuple-element.31), channel_id=1, source_target_pairs={{0,2},{1,3},{2,0},{3,1},{4,6},{5,7},{6,4},{7,5},{8,10},{9,11},{10,... | collective-permute-start | bytes 165896 | tf_op jit(solution)/shard_map/ppermute | solution.py:395
  8.0 1.5 %shard_map.121 = (bf16[256,256]{1,0:T(8,128)(2,1)S(1)}, bf16[256,256]{1,0:T(8,128)(2,1)S(1)}, bf16[256,256]{1,0:T(8,128)(2,1)S(1)}, f32[1,256]{1,0:T(1,128)S(1)}...) custom-call(s32[8]{0:T(128)} %refs_0_.3, s32[8]{0:T(128)} %refs_11_.1, bf16[2,96,384]{2,1,0:T(8,128)(2,1)} %bitcast.14, ...), custom_call_target="tpu_custom_call" | custom-call | flops 2000000000 | bytes 1000000 | tf_op jit(solution)/shard_map/pallas_call | solution.py:360
  9.5 0.2 collective-permute-done.refs_1_
  9.7 2.7 %collective-permute-done.1.refs_2_ = bf16[72,384]{1,0:T(8,128)(2,1)S(1)} collective-permute-done((bf16[72,384]{1,0:T(8,128)(2,1)S(1)}, bf16[72,384]{1,0:T(8,128)(2,1)S(1)}, u32[]{:S(2)}, u32[]{:S(2)}) %collective-permute-start.1) | collective-permute-done | bytes 55328 | tf_op jit(solution)/shard_map/ppermute | solution.py:395
  12.4 0.0 collective-permute-done.2.refs_3_
  12.4 0.1 collective-permute-start.3
  12.5 0.4 %shard_map.123 = (bf16[288,256]{1,0:T(8,128)(2,1)S(1)}, bf16[288,256]{1,0:T(8,128)(2,1)S(1)}, f32[288,256]{1,0:T(8,128)S(1)}) custom-call(bf16[72,384]{1,0:T(8,128)(2,1)S(1)} %get-tuple-element.28.refs_0_, bf16[72,384]{1,0:T(8,128)(2,1)S(1)} %collective-permute-done.refs_1_, bf16[72,384]{1,0:T(8,128)(2,1)S(1)} %collective-permute-done.1.refs_2_, ...), custom_call_target="tpu_custom_call" | custom-call | flops 2000000000 | bytes 1000000 | tf_op jit(solution)/shard_map/pallas_call | solution.py:360
  12.9 1.1 %collective-permute-done.3.refs_4_ = bf16[4,72,384]{2,1,0:T(8,128)(2,1)S(1)} collective-permute-done((bf16[4,72,384]{2,1,0:T(8,128)(2,1)S(1)}, bf16[4,72,384]{2,1,0:T(8,128)(2,1)S(1)}, u32[]{:S(2)}, u32[]{:S(2)}) %collective-permute-start.3) | collective-permute-done | bytes 221216 | tf_op jit(solution)/shard_map/ppermute | solution.py:435
  14.0 1.6 %shard_map.124 = (bf16[112,128]{1,0:T(8,128)(2,1)S(1)}, bf16[112,128]{1,0:T(8,128)(2,1)S(1)}, bf16[112,128]{1,0:T(8,128)(2,1)S(1)}, bf16[240,384]{1,0:T(8,128)(2...) custom-call(bf16[72,384]{1,0:T(8,128)(2,1)S(1)} %get-tuple-element.2, ...), custom_call_target="tpu_custom_call" | custom-call | flops 100000000 | bytes 1000000 | tf_op jit(solution)/shard_map/pallas_call | solution.py:360
  15.6 2.6 %collective-permute-start.4 = (bf16[112,128]{1,0:T(8,128)(2,1)S(1)}, bf16[112,128]{1,0:T(8,128)(2,1)S(1)}, u32[]{:S(2)}, u32[]{:S(2)}) collective-permute-start(bf16[112,128]{1,0:T(8,128)(2,1)S(1)} %get-tuple-element.38), channel_id=1, source_target_pairs={{0,6},{1,7},{2,4},{3,5},{4,2},{5,3},{6,0},{7,1},{8,14},{9,15},{10,... | collective-permute-start | bytes 86024 | tf_op jit(solution)/shard_map/ppermute | solution.py:395
  18.2 0.0 collective-permute-start.5
  18.2 1.9 %collective-permute-start.6 = (bf16[112,128]{1,0:T(8,128)(2,1)S(1)}, bf16[112,128]{1,0:T(8,128)(2,1)S(1)}, u32[]{:S(2)}, u32[]{:S(2)}) collective-permute-start(bf16[112,128]{1,0:T(8,128)(2,1)S(1)} %get-tuple-element.40), channel_id=1, source_target_pairs={{0,2},{1,3},{2,0},{3,1},{4,6},{5,7},{6,4},{7,5},{8,10},{9,11},{10,... | collective-permute-start | bytes 86024 | tf_op jit(solution)/shard_map/ppermute | solution.py:395
  20.1 2.4 %collective-permute-start.8 = (bf16[240,384]{1,0:T(8,128)(2,1)S(1)}, bf16[240,384]{1,0:T(8,128)(2,1)S(1)}, u32[]{:S(2)}, u32[]{:S(2)}) collective-permute-start(bf16[240,384]{1,0:T(8,128)(2,1)S(1)} %get-tuple-element.41), channel_id=1, source_target_pairs={{0,24},{8,0},{16,8},{24,16},{1,25},{9,1},{17,9},{25,17},{2,26},{10... | collective-permute-start | bytes 552968 | tf_op jit(solution)/shard_map/ppermute | solution.py:28
  22.5 0.0 collective-permute-done.4.refs_0_
  22.5 0.4 %collective-permute-done.5.refs_1_ = bf16[112,128]{1,0:T(8,128)(2,1)S(1)} collective-permute-done((bf16[112,128]{1,0:T(8,128)(2,1)S(1)}, bf16[112,128]{1,0:T(8,128)(2,1)S(1)}, u32[]{:S(2)}, u32[]{:S(2)}) %collective-permute-start.5) | collective-permute-done | bytes 28704 | tf_op jit(solution)/shard_map/ppermute | solution.py:395
  23.0 0.0 collective-permute-done.6.refs_2_
  23.0 2.5 %collective-permute-start.7 = (bf16[3,112,128]{2,1,0:T(8,128)(2,1)S(1)}, bf16[3,112,128]{2,1,0:T(8,128)(2,1)S(1)}, u32[]{:S(2)}, u32[]{:S(2)}) collective-permute-start(bf16[3,112,128]{2,1,0:T(8,128)(2,1)S(1)} %shard_map.125), channel_id=1, source_target_pairs={{0,24},{8,0},{16,8},{24,16},{1,25},{9,1},{17,9},{25,17},{2,26},{10... | collective-permute-start | bytes 258056 | tf_op jit(solution)/shard_map/ppermute | solution.py:28
  25.5 1.1 %shard_map.127 = (f32[2,48,96]{2,1,0:T(8,128)}, f32[2,48,96]{2,1,0:T(8,128)}, f32[2,48]{1,0:T(2,128)}) custom-call(bf16[288,256]{1,0:T(8,128)(2,1)S(1)} %get-tuple-element.43.points0, bf16[288,256]{1,0:T(8,128)(2,1)S(1)} %get-tuple-element.44.hidden0, bf16[288,256]{1,0:T(8,128)(2,1)S(1)} %get-tuple-element.45.points1, ...), custom_call_target="tpu_custom_call" | custom-call | flops 2000000000 | bytes 1000000 | tf_op jit(solution)/shard_map/pallas_call | solution.py:360
  26.6 1.2 %collective-permute-done.7.three = bf16[3,112,128]{2,1,0:T(8,128)(2,1)S(1)} collective-permute-done((bf16[3,112,128]{2,1,0:T(8,128)(2,1)S(1)}, bf16[3,112,128]{2,1,0:T(8,128)(2,1)S(1)}, u32[]{:S(2)}, u32[]{:S(2)}) %collective-permute-start.7) | collective-permute-done | bytes 86048 | tf_op jit(solution)/shard_map/ppermute | solution.py:28
  27.8 0.0 collective-permute-done.8.bundle
  27.8 1.1 %shard_map.126 = bf16[180,384]{1,0:T(8,128)(2,1)} custom-call(bf16[3,112,128]{2,1,0:T(8,128)(2,1)S(1)} %collective-permute-done.7.three, bf16[240,384]{1,0:T(8,128)(2,1)S(1)} %collective-permute-done.8.bundle, bf16[180,144]{1,0:T(8,128)(2,1)S(1)} %get-tuple-element.42.table), custom_call_target="tpu_custom_call" | custom-call | flops 100000000 | bytes 1000000 | tf_op jit(solution)/shard_map/pallas_call | solution.py:360
  (2 shorter events, 0.0 us)
Async XLA Ops:
  2.2 7.5 %collective-permute-start = (bf16[72,384]{1,0:T(8,128)(2,1)S(1)}, bf16[72,384]{1,0:T(8,128)(2,1)S(1)}, u32[]{:S(2)}, u32[]{:S(2)}) collective-permute-start(bf16[72,384]{1,0:T(8,128)(2,1)S(1)} %get-tuple-element.29), channel_id=1, source_target_pairs={{0,6},{1,7},{2,4},{3,5},{4,2},{5,3},{6,0},{7,1},{8,14},{9,15},{10,... | collective-permute-start | bytes 165896 | tf_op jit(solution)/shard_map/ppermute | solution.py:395
  7.3 5.1 %collective-permute-start.1 = (bf16[72,384]{1,0:T(8,128)(2,1)S(1)}, bf16[72,384]{1,0:T(8,128)(2,1)S(1)}, u32[]{:S(2)}, u32[]{:S(2)}) collective-permute-start(bf16[72,384]{1,0:T(8,128)(2,1)S(1)} %get-tuple-element.30), channel_id=1, source_target_pairs={{0,4},{1,5},{2,6},{3,7},{4,0},{5,1},{6,2},{7,3},{8,12},{9,13},{10,... | collective-permute-start | bytes 165896 | tf_op jit(solution)/shard_map/ppermute | solution.py:395
  7.3 5.1 %collective-permute-start.2 = (bf16[72,384]{1,0:T(8,128)(2,1)S(1)}, bf16[72,384]{1,0:T(8,128)(2,1)S(1)}, u32[]{:S(2)}, u32[]{:S(2)}) collective-permute-start(bf16[72,384]{1,0:T(8,128)(2,1)S(1)} %get-tuple-element.31), channel_id=1, source_target_pairs={{0,2},{1,3},{2,0},{3,1},{4,6},{5,7},{6,4},{7,5},{8,10},{9,11},{10,... | collective-permute-start | bytes 165896 | tf_op jit(solution)/shard_map/ppermute | solution.py:395
  12.4 1.5 %collective-permute-start.3 = (bf16[4,72,384]{2,1,0:T(8,128)(2,1)S(1)}, bf16[4,72,384]{2,1,0:T(8,128)(2,1)S(1)}, u32[]{:S(2)}, u32[]{:S(2)}) collective-permute-start(bf16[4,72,384]{2,1,0:T(8,128)(2,1)S(1)} %shard_map.122), channel_id=1, source_target_pairs={{0,1},{1,0},{2,3},{3,2},{4,5},{5,4},{6,7},{7,6},{8,9},{9,8},{10,11... | collective-permute-start | bytes 663560 | tf_op jit(solution)/shard_map/ppermute | solution.py:435
  15.6 6.9 %collective-permute-start.4 = (bf16[112,128]{1,0:T(8,128)(2,1)S(1)}, bf16[112,128]{1,0:T(8,128)(2,1)S(1)}, u32[]{:S(2)}, u32[]{:S(2)}) collective-permute-start(bf16[112,128]{1,0:T(8,128)(2,1)S(1)} %get-tuple-element.38), channel_id=1, source_target_pairs={{0,6},{1,7},{2,4},{3,5},{4,2},{5,3},{6,0},{7,1},{8,14},{9,15},{10,... | collective-permute-start | bytes 86024 | tf_op jit(solution)/shard_map/ppermute | solution.py:395
  18.2 4.8 %collective-permute-start.5 = (bf16[112,128]{1,0:T(8,128)(2,1)S(1)}, bf16[112,128]{1,0:T(8,128)(2,1)S(1)}, u32[]{:S(2)}, u32[]{:S(2)}) collective-permute-start(bf16[112,128]{1,0:T(8,128)(2,1)S(1)} %get-tuple-element.39), channel_id=1, source_target_pairs={{0,4},{1,5},{2,6},{3,7},{4,0},{5,1},{6,2},{7,3},{8,12},{9,13},{10,... | collective-permute-start | bytes 86024 | tf_op jit(solution)/shard_map/ppermute | solution.py:395
  18.2 4.8 %collective-permute-start.6 = (bf16[112,128]{1,0:T(8,128)(2,1)S(1)}, bf16[112,128]{1,0:T(8,128)(2,1)S(1)}, u32[]{:S(2)}, u32[]{:S(2)}) collective-permute-start(bf16[112,128]{1,0:T(8,128)(2,1)S(1)} %get-tuple-element.40), channel_id=1, source_target_pairs={{0,2},{1,3},{2,0},{3,1},{4,6},{5,7},{6,4},{7,5},{8,10},{9,11},{10,... | collective-permute-start | bytes 86024 | tf_op jit(solution)/shard_map/ppermute | solution.py:395
  20.1 7.7 %collective-permute-start.8 = (bf16[240,384]{1,0:T(8,128)(2,1)S(1)}, bf16[240,384]{1,0:T(8,128)(2,1)S(1)}, u32[]{:S(2)}, u32[]{:S(2)}) collective-permute-start(bf16[240,384]{1,0:T(8,128)(2,1)S(1)} %get-tuple-element.41), channel_id=1, source_target_pairs={{0,24},{8,0},{16,8},{24,16},{1,25},{9,1},{17,9},{25,17},{2,26},{10... | collective-permute-start | bytes 552968 | tf_op jit(solution)/shard_map/ppermute | solution.py:28
  23.0 4.8 %collective-permute-start.7 = (bf16[3,112,128]{2,1,0:T(8,128)(2,1)S(1)}, bf16[3,112,128]{2,1,0:T(8,128)(2,1)S(1)}, u32[]{:S(2)}, u32[]{:S(2)}) collective-permute-start(bf16[3,112,128]{2,1,0:T(8,128)(2,1)S(1)} %shard_map.125), channel_id=1, source_target_pairs={{0,24},{8,0},{16,8},{24,16},{1,25},{9,1},{17,9},{25,17},{2,26},{10... | collective-permute-start | bytes 258056 | tf_op jit(solution)/shard_map/ppermute | solution.py:28

commit v18 on v17

--- a/solution.py
+++ b/solution.py
@@ -223,6 +223,11 @@
         out[i] = refs[i][...]
 
 
+def others_kernel(backs, out):
+    for i, d in enumerate(ORDER[1:]):
+        out[i] = backs[partner(d)]
+
+
 def pack(band):
     rows = band.shape[0]
     tail = rows // 2 + 4
@@ -263,8 +268,8 @@
 
 def filter_kernel(*refs):
     owns, (other, slope_own, mat1, turned1, turned2, bias, own_field) = refs[:4], refs[4:11]
-    assign_hbm, outs, (bundle, points, hidden, grad_pre, grad_y) = refs[11], refs[12:15], refs[15:20]
-    assign, by_lat, by_pair, slope, real, imag, sems = refs[20:]
+    assign_hbm, outs, bundle, points, hidden, grad_pre, grad_y = refs[11:18]
+    assign, by_lat, by_pair, slope, real, imag, sems = refs[18:]
     copies = fetch(sems, (assign_hbm,), (assign,))
     core = lax.rem(lax.axis_index("lat"), 2)
     sides = [[owns[i][...].astype(F32) for i in ORDER], [other[i].astype(F32) for i in ORDER]]
@@ -302,11 +307,10 @@
         by_lat[r] = jnp.concatenate(band, axis=1)
     length = own_field.shape[0]
     bundle[0:length] = own_field[...]
-    for i, d in enumerate(ORDER):
+    for d in ORDER:
         band = pack(by_lat[assign[2 * partner(d) + core]])
-        if d:
-            outs[i - 1][...] = band.astype(BF16)
-        else:
+        outs[partner(d)] = band.astype(BF16)
+        if not d:
             tail = bundle.shape[0] - FIELD_ROWS
             band = jnp.concatenate([band, jnp.zeros((3 * tail - band.shape[0], LANES), F32)], axis=0)
             band = [band[i * tail : (i + 1) * tail] for i in range(3)]
@@ -449,9 +453,9 @@
     both = shape((2, NB * rows, wide), BF16)
     tail = -(-packed.shape[0] // 48) * 16
     bundle = shape((FIELD_ROWS + tail, width), BF16)
-    *chunks, bundle, points1, hidden1, grad_pre, grad_y = call(
+    chunks, bundle, points1, hidden1, grad_pre, grad_y = call(
         filter_kernel,
-        (packed,) * (NB - 1) + (bundle, vectors, vectors, both, both),
+        (shape((NB, *packed.shape), BF16), bundle, vectors, vectors, both, both),
         scratch
         + [
             pltpu.VMEM((n_rows, rows, wide), F32),
@@ -464,7 +468,14 @@
         (*received, other, slope0, mat1, turned1, turned2, bias, field),
         (assignment,),
     )
-    backs = swap(chunks)
+    backs = lax.all_to_all(
+        chunks,
+        "lat",
+        split_axis=0,
+        concat_axis=0,
+        axis_index_groups=[[2 * z + c for z in range(NB)] for c in range(2)],
+        tiled=True,
+    )
     matrix = shape((2, BS // 2, BS), F32)
     gw1, gw2, gb1 = call(
         products_kernel,
@@ -474,7 +485,7 @@
         (),
         2 * 10**9,
     )
-    three = call(join_kernel, shape((NB - 1, *packed.shape), BF16), [], backs, ())
+    three = call(others_kernel, shape((NB - 1, *packed.shape), BF16), [], (backs,), ())
     three = turn(three, "section")
     bundle = turn(bundle, "section")
     shifted = call(

time: 29.1 us -> 32 us (1.100)
  waiting for transfers between devices: 5.64 us -> 8.55 us
  starting transfers between devices: 15.2 us -> 14.5 us
  Pallas kernels: 7.33 us -> 7.97 us
    ppermute x6 -> x3, starting transfers between devices: 10.2 us -> 5.76 us  [swap(): return [lax.ppermute(chunk, 'lat', p) for chunk, p in zip(chunks, pairs)]]
    all_to_all x0 -> x1, starting transfers between devices: none -> 3.78 us  [paired_blocks(): lax.all_to_all(chunks, 'lat', split_axis=0, concat_axis=0, axis_index_gro...]
    all_to_all x0 -> x1, waiting for transfers between devices: none -> 3.55 us  [paired_blocks(): lax.all_to_all(chunks, 'lat', split_axis=0, concat_axis=0, axis_index_gro...]
    pallas_call x8, Pallas kernels: 7.33 us -> 7.97 us  [call(): pl.pallas_call(kernel, out_shape=outs, in_specs=[VMEM] * len(near) + [HBM...]
    ppermute x6 -> x3, waiting for transfers between devices: 3.36 us -> 2.93 us  [swap(): return [lax.ppermute(chunk, 'lat', p) for chunk, p in zip(chunks, pairs)]]
  transfers between devices with their start and end apart: 9 -> 7, of which waited for: 5 -> 5; matrix products, arithmetic and copies ran while one was open for 0% -> 0% of each run, Pallas kernels for 10% -> 9%
where the time goes in v18:
time: 32 us; the launch traced here: 31.8 us
  starting transfers between devices  14.5 us (45%)
  waiting for transfers between devices  8.55 us (27%)
  Pallas kernels  7.97 us (25%)
  between operations  0.68 us (2%)
    pallas_call x8, Pallas kernels, call(): pl.pallas_call(kernel, out_shape=outs, in_specs=[VMEM] * len(near) + [HBM...  7.97 us
    ppermute x3, starting transfers between devices, swap(): return [lax.ppermute(chunk, 'lat', p) for chunk, p in zip(chunks, pairs)]  5.76 us
    ppermute x2, starting transfers between devices, turn(): lax.ppermute(value, axis, [(i, (i - 1) % length) for i in range(length)])  4.93 us
    all_to_all x1, starting transfers between devices, paired_blocks(): lax.all_to_all(chunks, 'lat', split_axis=0, concat_axis=0, axis_index_gro...  3.78 us
    all_to_all x1, waiting for transfers between devices, paired_blocks(): lax.all_to_all(chunks, 'lat', split_axis=0, concat_axis=0, axis_index_gro...  3.55 us
    ppermute x3, waiting for transfers between devices, swap(): return [lax.ppermute(chunk, 'lat', p) for chunk, p in zip(chunks, pairs)]  2.93 us
    ppermute x1, waiting for transfers between devices, paired_blocks(): other = lax.ppermute(own, 'lat', [(i, i ^ 1) for i in range(2 * NB)])  1.1 us
    ppermute x2, waiting for transfers between devices, turn(): lax.ppermute(value, axis, [(i, (i - 1) % length) for i in range(length)])  0.98 us
  transfers between devices with their start and end apart: 7, of which 5 were waited for; matrix products, arithmetic and copies ran while one was open for 0% of the time, Pallas kernels for 9%

profile of v18, /device:TPU:0, one launch (start us, length us, event | category | flops | bytes accessed | tf_op | source)
XLA Modules:
  0.0 31.8 jit_solution(18366595452512164445)
XLA Ops:
  0.6 1.6 %shard_map.120 = (bf16[72,384]{1,0:T(8,128)(2,1)S(1)}, bf16[72,384]{1,0:T(8,128)(2,1)S(1)}, bf16[72,384]{1,0:T(8,128)(2,1)S(1)}, bf16[72,384]{1,0:T(8,128)(2,1)S(1)}) custom-call(s32[8]{0:T(128)} %refs_0_.3, s32[8]{0:T(128)} %refs_11_.1, bf16[180,384]{1,0:T(8,128)(2,1)} %bitcast.16, bf16[144,180]{1,0:T(8,128)(2,1)} %constant.4.clone.refs_3_, ...), custom_call_target="tpu_custom_call" | custom-call | flops 100000000 | bytes 1000000 | tf_op jit(solution)/shard_map/pallas_call | solution.py:364
  2.2 5.1 %collective-permute-start = (bf16[72,384]{1,0:T(8,128)(2,1)S(1)}, bf16[72,384]{1,0:T(8,128)(2,1)S(1)}, u32[]{:S(2)}, u32[]{:S(2)}) collective-permute-start(bf16[72,384]{1,0:T(8,128)(2,1)S(1)} %get-tuple-element.27), channel_id=1, source_target_pairs={{0,6},{1,7},{2,4},{3,5},{4,2},{5,3},{6,0},{7,1},{8,14},{9,15},{10,... | collective-permute-start | bytes 165896 | tf_op jit(solution)/shard_map/ppermute | solution.py:399
  7.3 0.0 collective-permute-start.1
  7.3 0.6 %collective-permute-start.2 = (bf16[72,384]{1,0:T(8,128)(2,1)S(1)}, bf16[72,384]{1,0:T(8,128)(2,1)S(1)}, u32[]{:S(2)}, u32[]{:S(2)}) collective-permute-start(bf16[72,384]{1,0:T(8,128)(2,1)S(1)} %get-tuple-element.29), channel_id=1, source_target_pairs={{0,2},{1,3},{2,0},{3,1},{4,6},{5,7},{6,4},{7,5},{8,10},{9,11},{10,... | collective-permute-start | bytes 165896 | tf_op jit(solution)/shard_map/ppermute | solution.py:399
  8.0 1.5 %shard_map.121 = (bf16[256,256]{1,0:T(8,128)(2,1)S(1)}, bf16[256,256]{1,0:T(8,128)(2,1)S(1)}, bf16[256,256]{1,0:T(8,128)(2,1)S(1)}, f32[1,256]{1,0:T(1,128)S(1)}...) custom-call(s32[8]{0:T(128)} %refs_0_.3, s32[8]{0:T(128)} %refs_11_.1, bf16[2,96,384]{2,1,0:T(8,128)(2,1)} %bitcast.14, ...), custom_call_target="tpu_custom_call" | custom-call | flops 2000000000 | bytes 1000000 | tf_op jit(solution)/shard_map/pallas_call | solution.py:364
  9.5 0.2 collective-permute-done.refs_1_
  9.7 2.7 %collective-permute-done.1.refs_2_ = bf16[72,384]{1,0:T(8,128)(2,1)S(1)} collective-permute-done((bf16[72,384]{1,0:T(8,128)(2,1)S(1)}, bf16[72,384]{1,0:T(8,128)(2,1)S(1)}, u32[]{:S(2)}, u32[]{:S(2)}) %collective-permute-start.1) | collective-permute-done | bytes 55328 | tf_op jit(solution)/shard_map/ppermute | solution.py:399
  12.4 0.0 collective-permute-done.2.refs_3_
  12.4 0.1 collective-permute-start.3
  12.5 0.4 %shard_map.123 = (bf16[288,256]{1,0:T(8,128)(2,1)S(1)}, bf16[288,256]{1,0:T(8,128)(2,1)S(1)}, f32[288,256]{1,0:T(8,128)S(1)}) custom-call(bf16[72,384]{1,0:T(8,128)(2,1)S(1)} %get-tuple-element.26.refs_0_, bf16[72,384]{1,0:T(8,128)(2,1)S(1)} %collective-permute-done.refs_1_, bf16[72,384]{1,0:T(8,128)(2,1)S(1)} %collective-permute-done.1.refs_2_, ...), custom_call_target="tpu_custom_call" | custom-call | flops 2000000000 | bytes 1000000 | tf_op jit(solution)/shard_map/pallas_call | solution.py:364
  12.9 1.1 %collective-permute-done.3.refs_4_ = bf16[4,72,384]{2,1,0:T(8,128)(2,1)S(1)} collective-permute-done((bf16[4,72,384]{2,1,0:T(8,128)(2,1)S(1)}, bf16[4,72,384]{2,1,0:T(8,128)(2,1)S(1)}, u32[]{:S(2)}, u32[]{:S(2)}) %collective-permute-start.3) | collective-permute-done | bytes 221216 | tf_op jit(solution)/shard_map/ppermute | solution.py:439
  14.0 2.3 %shard_map.124 = (bf16[4,112,128]{2,1,0:T(8,128)(2,1)}, bf16[240,384]{1,0:T(8,128)(2,1)S(1)}, bf16[288,256]{1,0:T(8,128)(2,1)S(1)}, bf16[288,256]{1,0:T(8,128)(2...) custom-call(bf16[72,384]{1,0:T(8,128)(2,1)S(1)} %get-tuple-element.26.refs_0_, ...), custom_call_target="tpu_custom_call" | custom-call | flops 100000000 | bytes 1000000 | tf_op jit(solution)/shard_map/pallas_call | solution.py:364
  16.3 3.8 %all-to-all-start = ((bf16[4,112,128]{2,1,0:T(8,128)(2,1)}), bf16[4,112,128]{2,1,0:T(8,128)(2,1)S(1)}, u32[]{:S(2)}, u32[]{:S(2)}) async-start(bf16[4,112,128]{2,1,0:T(8,128)(2,1)} %get-tuple-element.36), calls=%async_computation | async-start | bytes 229376 | tf_op jit(solution)/shard_map/all_to_all | solution.py:471
  20.0 2.4 %collective-permute-start.5 = (bf16[240,384]{1,0:T(8,128)(2,1)S(1)}, bf16[240,384]{1,0:T(8,128)(2,1)S(1)}, u32[]{:S(2)}, u32[]{:S(2)}) collective-permute-start(bf16[240,384]{1,0:T(8,128)(2,1)S(1)} %get-tuple-element.37), channel_id=1, source_target_pairs={{0,24},{8,0},{16,8},{24,16},{1,25},{9,1},{17,9},{25,17},{2,26},{10... | collective-permute-start | bytes 552968 | tf_op jit(solution)/shard_map/ppermute | solution.py:28
  22.5 3.5 %all-to-all-done.backs = bf16[4,112,128]{2,1,0:T(8,128)(2,1)S(1)} async-done(((bf16[4,112,128]{2,1,0:T(8,128)(2,1)}), bf16[4,112,128]{2,1,0:T(8,128)(2,1)S(1)}, u32[]{:S(2)}, u32[]{:S(2)}) %all-to-all-start) | async-done | bytes 114720 | tf_op jit(solution)/shard_map/all_to_all | solution.py:471
  26.0 2.5 %collective-permute-start.4 = (bf16[3,112,128]{2,1,0:T(8,128)(2,1)S(1)}, bf16[3,112,128]{2,1,0:T(8,128)(2,1)S(1)}, u32[]{:S(2)}, u32[]{:S(2)}) collective-permute-start(bf16[3,112,128]{2,1,0:T(8,128)(2,1)S(1)} %shard_map.125), channel_id=1, source_target_pairs={{0,24},{8,0},{16,8},{24,16},{1,25},{9,1},{17,9},{25,17},{2,26},{10... | collective-permute-start | bytes 258056 | tf_op jit(solution)/shard_map/ppermute | solution.py:28
  28.5 1.1 %shard_map.127 = (f32[2,48,96]{2,1,0:T(8,128)}, f32[2,48,96]{2,1,0:T(8,128)}, f32[2,48]{1,0:T(2,128)}) custom-call(bf16[288,256]{1,0:T(8,128)(2,1)S(1)} %get-tuple-element.39.points0, bf16[288,256]{1,0:T(8,128)(2,1)S(1)} %get-tuple-element.40.hidden0, bf16[288,256]{1,0:T(8,128)(2,1)S(1)} %get-tuple-element.41.points1, ...), custom_call_target="tpu_custom_call" | custom-call | flops 2000000000 | bytes 1000000 | tf_op jit(solution)/shard_map/pallas_call | solution.py:364
  29.7 0.0 collective-permute-done.5.bundle
  29.7 1.0 %collective-permute-done.4.three = bf16[3,112,128]{2,1,0:T(8,128)(2,1)S(1)} collective-permute-done((bf16[3,112,128]{2,1,0:T(8,128)(2,1)S(1)}, bf16[3,112,128]{2,1,0:T(8,128)(2,1)S(1)}, u32[]{:S(2)}, u32[]{:S(2)}) %collective-permute-start.4) | collective-permute-done | bytes 86048 | tf_op jit(solution)/shard_map/ppermute | solution.py:28
  30.6 1.1 %shard_map.126 = bf16[180,384]{1,0:T(8,128)(2,1)} custom-call(bf16[3,112,128]{2,1,0:T(8,128)(2,1)S(1)} %collective-permute-done.4.three, bf16[240,384]{1,0:T(8,128)(2,1)S(1)} %collective-permute-done.5.bundle, bf16[180,144]{1,0:T(8,128)(2,1)S(1)} %get-tuple-element.38.table), custom_call_target="tpu_custom_call" | custom-call | flops 100000000 | bytes 1000000 | tf_op jit(solution)/shard_map/pallas_call | solution.py:364
  (2 shorter events, 0.0 us)
Async XLA Ops:
  2.2 7.5 %collective-permute-start = (bf16[72,384]{1,0:T(8,128)(2,1)S(1)}, bf16[72,384]{1,0:T(8,128)(2,1)S(1)}, u32[]{:S(2)}, u32[]{:S(2)}) collective-permute-start(bf16[72,384]{1,0:T(8,128)(2,1)S(1)} %get-tuple-element.27), channel_id=1, source_target_pairs={{0,6},{1,7},{2,4},{3,5},{4,2},{5,3},{6,0},{7,1},{8,14},{9,15},{10,... | collective-permute-start | bytes 165896 | tf_op jit(solution)/shard_map/ppermute | solution.py:399
  7.3 5.1 %collective-permute-start.1 = (bf16[72,384]{1,0:T(8,128)(2,1)S(1)}, bf16[72,384]{1,0:T(8,128)(2,1)S(1)}, u32[]{:S(2)}, u32[]{:S(2)}) collective-permute-start(bf16[72,384]{1,0:T(8,128)(2,1)S(1)} %get-tuple-element.28), channel_id=1, source_target_pairs={{0,4},{1,5},{2,6},{3,7},{4,0},{5,1},{6,2},{7,3},{8,12},{9,13},{10,... | collective-permute-start | bytes 165896 | tf_op jit(solution)/shard_map/ppermute | solution.py:399
  7.3 5.1 %collective-permute-start.2 = (bf16[72,384]{1,0:T(8,128)(2,1)S(1)}, bf16[72,384]{1,0:T(8,128)(2,1)S(1)}, u32[]{:S(2)}, u32[]{:S(2)}) collective-permute-start(bf16[72,384]{1,0:T(8,128)(2,1)S(1)} %get-tuple-element.29), channel_id=1, source_target_pairs={{0,2},{1,3},{2,0},{3,1},{4,6},{5,7},{6,4},{7,5},{8,10},{9,11},{10,... | collective-permute-start | bytes 165896 | tf_op jit(solution)/shard_map/ppermute | solution.py:399
  12.4 1.5 %collective-permute-start.3 = (bf16[4,72,384]{2,1,0:T(8,128)(2,1)S(1)}, bf16[4,72,384]{2,1,0:T(8,128)(2,1)S(1)}, u32[]{:S(2)}, u32[]{:S(2)}) collective-permute-start(bf16[4,72,384]{2,1,0:T(8,128)(2,1)S(1)} %shard_map.122), channel_id=1, source_target_pairs={{0,1},{1,0},{2,3},{3,2},{4,5},{5,4},{6,7},{7,6},{8,9},{9,8},{10,11... | collective-permute-start | bytes 663560 | tf_op jit(solution)/shard_map/ppermute | solution.py:439
  16.3 9.8 %all-to-all-start = ((bf16[4,112,128]{2,1,0:T(8,128)(2,1)}), bf16[4,112,128]{2,1,0:T(8,128)(2,1)S(1)}, u32[]{:S(2)}, u32[]{:S(2)}) async-start(bf16[4,112,128]{2,1,0:T(8,128)(2,1)} %get-tuple-element.36), calls=%async_computation | async-start | bytes 229376 | tf_op jit(solution)/shard_map/all_to_all | solution.py:471
  20.0 9.6 %collective-permute-start.5 = (bf16[240,384]{1,0:T(8,128)(2,1)S(1)}, bf16[240,384]{1,0:T(8,128)(2,1)S(1)}, u32[]{:S(2)}, u32[]{:S(2)}) collective-permute-start(bf16[240,384]{1,0:T(8,128)(2,1)S(1)} %get-tuple-element.37), channel_id=1, source_target_pairs={{0,24},{8,0},{16,8},{24,16},{1,25},{9,1},{17,9},{25,17},{2,26},{10... | collective-permute-start | bytes 552968 | tf_op jit(solution)/shard_map/ppermute | solution.py:28
  26.0 4.6 %collective-permute-start.4 = (bf16[3,112,128]{2,1,0:T(8,128)(2,1)S(1)}, bf16[3,112,128]{2,1,0:T(8,128)(2,1)S(1)}, u32[]{:S(2)}, u32[]{:S(2)}) collective-permute-start(bf16[3,112,128]{2,1,0:T(8,128)(2,1)S(1)} %shard_map.125), channel_id=1, source_target_pairs={{0,24},{8,0},{16,8},{24,16},{1,25},{9,1},{17,9},{25,17},{2,26},{10... | collective-permute-start | bytes 258056 | tf_op jit(solution)/shard_map/ppermute | solution.py:28

commit v19 on v17

--- a/solution.py
+++ b/solution.py
@@ -153,7 +153,7 @@
     early = fetch_parts(sems.at[0], hbm[4], saved, [pl.ds(k, 2) for k in range(0, 2 * NB, 2)])
     late = fetch_parts(sems.at[1], hbm[2], field, columns(field.shape[1]))
     late += fetch(few, hbm[:2] + hbm[3:4], held[:2] + held[3:4])
-    wait(early)
+    wait(early + late)
     parts = [saved[:, c, :].astype(F32) for c in range(2)]
     points = [
         [
@@ -162,7 +162,6 @@
         ]
         for n in range(NB)
     ]
-    wait(late)
     rows = by_block.shape[1]
     spectral = jnp.dot(table[...], field[...], preferred_element_type=F32)
     active = counts[assign[lax.axis_index("lat")]]
@@ -176,10 +175,15 @@
 
 
 def ready_kernel(q, *refs):
-    hbm, (mat1, turned1, turned2, bias, own_field, own_table) = refs[:7], refs[7:13]
-    counts, assign, w1, w2, b1, table, sems = refs[13:]
+    hbm, (mat1, turned1, turned2, bias, own_field, own_table, latitudes) = refs[:7], refs[7:14]
+    counts, assign, w1, w2, b1, table, sems = refs[14:]
     copies = fetch(sems, hbm, (counts, assign, w1, w2, b1, table, own_field))
     wait(copies[:6])
+    lane = lax.broadcasted_iota(jnp.int32, latitudes.shape, 1)
+    line = jnp.zeros(latitudes.shape, jnp.int32)
+    for r in range(2 * NB):
+        line = jnp.where(lane == r, assign[r], line)
+    latitudes[...] = line
     active = counts[assign[lax.axis_index("lat")]]
     rows = table.shape[1] // 2
     held_modes = mode_numbers((table.shape[0], rows), 1, q) < active
@@ -263,17 +267,20 @@
 
 def filter_kernel(*refs):
     owns, (other, slope_own, mat1, turned1, turned2, bias, own_field) = refs[:4], refs[4:11]
-    assign_hbm, outs, (bundle, points, hidden, grad_pre, grad_y) = refs[11], refs[12:15], refs[15:20]
+    latitudes, outs, (bundle, points, hidden, grad_pre, grad_y) = refs[11], refs[12:15], refs[15:20]
     assign, by_lat, by_pair, slope, real, imag, sems = refs[20:]
-    copies = fetch(sems, (assign_hbm,), (assign,))
+    copies = fetch(sems, (latitudes,), (assign,))
     core = lax.rem(lax.axis_index("lat"), 2)
     sides = [[owns[i][...].astype(F32) for i in ORDER], [other[i].astype(F32) for i in ORDER]]
     silu_points(sides[1], mat1, bias, by_pair, points, hidden, slope)
+    spectra = [
+        [jnp.concatenate([window(chunk, j * BS) for j in range(2)], axis=1) for chunk in chunks]
+        for chunks in sides
+    ]
     wait(copies)
-    for side, chunks in zip((core, 1 - core), sides):
-        for d, chunk in enumerate(chunks):
-            parts = [window(chunk, j * BS) for j in range(2)]
-            by_lat[assign[2 * partner(d) + side]] = jnp.concatenate(parts, axis=1)
+    for side, rows in zip((core, 1 - core), spectra):
+        for d, row in enumerate(rows):
+            by_lat[assign[0, 2 * partner(d) + side]] = row
     n_rows, rows, _ = by_lat.shape
     half = rows * n_rows // 2
     waves = eight_points([(by_lat[r][:, :LANES], by_lat[r][:, LANES:]) for r in range(n_rows)], -1)
@@ -303,7 +310,7 @@
     length = own_field.shape[0]
     bundle[0:length] = own_field[...]
     for i, d in enumerate(ORDER):
-        band = pack(by_lat[assign[2 * partner(d) + core]])
+        band = pack(by_lat[assign[0, 2 * partner(d) + core]])
         if d:
             outs[i - 1][...] = band.astype(BF16)
         else:
@@ -410,7 +417,7 @@
     scratch, _ = scratch_for(*far)
     far = (*far, field)
     wide = 2 * LANES
-    mat1, turned1, turned2, bias, field, forward = call(
+    mat1, turned1, turned2, bias, field, forward, latitudes = call(
         functools.partial(ready_kernel, q),
         (
             shape((wide, wide), BF16),
@@ -419,6 +426,7 @@
             shape((1, wide), F32),
             shape(field.shape, BF16),
             shape(forward.shape, BF16),
+            shape((1, LANES), jnp.int32),
         ),
         scratch + [pltpu.SemaphoreType.DMA((len(far),))],
         (),
@@ -445,7 +453,7 @@
         2 * 10**9,
     )
     packed = shape((rows + rows // 2 + 4, LANES), BF16)
-    scratch, sems = scratch_for(assignment)
+    scratch, sems = scratch_for(latitudes)
     both = shape((2, NB * rows, wide), BF16)
     tail = -(-packed.shape[0] // 48) * 16
     bundle = shape((FIELD_ROWS + tail, width), BF16)
@@ -461,8 +469,8 @@
             pltpu.VMEM((n_rows * rows, LANES), F32),
             sems,
         ],
-        (*received, other, slope0, mat1, turned1, turned2, bias, field),
-        (assignment,),
+        (*received, other, slope0, mat1, turned1, turned2, bias, field, latitudes),
+        (),
     )
     backs = swap(chunks)
     matrix = shape((2, BS // 2, BS), F32)

time: 29.1 us -> 28.9 us (level)
  no operation moved by 1% of the time
where the time goes in v19:
time: 28.9 us; the launch traced here: 28.7 us
  starting transfers between devices  15.2 us (53%)
  Pallas kernels  7.2 us (25%)
  waiting for transfers between devices  5.63 us (19%)
  between operations  0.69 us (2%)
    ppermute x6, starting transfers between devices, swap(): return [lax.ppermute(chunk, 'lat', p) for chunk, p in zip(chunks, pairs)]  10.2 us
    pallas_call x8, Pallas kernels, call(): pl.pallas_call(kernel, out_shape=outs, in_specs=[VMEM] * len(near) + [HBM...  7.2 us
    ppermute x2, starting transfers between devices, turn(): lax.ppermute(value, axis, [(i, (i - 1) % length) for i in range(length)])  4.94 us
    ppermute x6, waiting for transfers between devices, swap(): return [lax.ppermute(chunk, 'lat', p) for chunk, p in zip(chunks, pairs)]  3.36 us
    ppermute x2, waiting for transfers between devices, turn(): lax.ppermute(value, axis, [(i, (i - 1) % length) for i in range(length)])  1.17 us
    ppermute x1, waiting for transfers between devices, paired_blocks(): other = lax.ppermute(own, 'lat', [(i, i ^ 1) for i in range(2 * NB)])  1.1 us
  transfers between devices with their start and end apart: 9, of which 5 were waited for; matrix products, arithmetic and copies ran while one was open for 0% of the time, Pallas kernels for 10%

profile of v19, /device:TPU:0, one launch (start us, length us, event | category | flops | bytes accessed | tf_op | source)
XLA Modules:
  0.0 28.7 jit_solution(8778845628809050059)
XLA Ops:
  0.6 1.6 %shard_map.120 = (bf16[72,384]{1,0:T(8,128)(2,1)S(1)}, bf16[72,384]{1,0:T(8,128)(2,1)S(1)}, bf16[72,384]{1,0:T(8,128)(2,1)S(1)}, bf16[72,384]{1,0:T(8,128)(2,1)S(1)}) custom-call(s32[8]{0:T(128)} %refs_0_.3, s32[8]{0:T(128)} %refs_1_.3, bf16[180,384]{1,0:T(8,128)(2,1)} %bitcast.16, bf16[144,180]{1,0:T(8,128)(2,1)} %constant.4.clone.refs_3_, ...), custom_call_target="tpu_custom_call" | custom-call | flops 100000000 | bytes 1000000 | tf_op jit(solution)/shard_map/pallas_call | solution.py:367
  2.2 5.1 %collective-permute-start = (bf16[72,384]{1,0:T(8,128)(2,1)S(1)}, bf16[72,384]{1,0:T(8,128)(2,1)S(1)}, u32[]{:S(2)}, u32[]{:S(2)}) collective-permute-start(bf16[72,384]{1,0:T(8,128)(2,1)S(1)} %get-tuple-element.30), channel_id=1, source_target_pairs={{0,6},{1,7},{2,4},{3,5},{4,2},{5,3},{6,0},{7,1},{8,14},{9,15},{10,... | collective-permute-start | bytes 165896 | tf_op jit(solution)/shard_map/ppermute | solution.py:402
  7.3 0.0 collective-permute-start.1
  7.4 0.6 %collective-permute-start.2 = (bf16[72,384]{1,0:T(8,128)(2,1)S(1)}, bf16[72,384]{1,0:T(8,128)(2,1)S(1)}, u32[]{:S(2)}, u32[]{:S(2)}) collective-permute-start(bf16[72,384]{1,0:T(8,128)(2,1)S(1)} %get-tuple-element.32), channel_id=1, source_target_pairs={{0,2},{1,3},{2,0},{3,1},{4,6},{5,7},{6,4},{7,5},{8,10},{9,11},{10,... | collective-permute-start | bytes 165896 | tf_op jit(solution)/shard_map/ppermute | solution.py:402
  8.0 1.5 %shard_map.121 = (bf16[256,256]{1,0:T(8,128)(2,1)S(1)}, bf16[256,256]{1,0:T(8,128)(2,1)S(1)}, bf16[256,256]{1,0:T(8,128)(2,1)S(1)}, f32[1,256]{1,0:T(1,128)S(1)}...) custom-call(s32[8]{0:T(128)} %refs_0_.3, s32[8]{0:T(128)} %refs_1_.3, ...), custom_call_target="tpu_custom_call" | custom-call | flops 2000000000 | bytes 1000000 | tf_op jit(solution)/shard_map/pallas_call | solution.py:367
  9.5 0.2 collective-permute-done.refs_1_
  9.7 2.7 %collective-permute-done.1.refs_2_ = bf16[72,384]{1,0:T(8,128)(2,1)S(1)} collective-permute-done((bf16[72,384]{1,0:T(8,128)(2,1)S(1)}, bf16[72,384]{1,0:T(8,128)(2,1)S(1)}, u32[]{:S(2)}, u32[]{:S(2)}) %collective-permute-start.1) | collective-permute-done | bytes 55328 | tf_op jit(solution)/shard_map/ppermute | solution.py:402
  12.4 0.0 collective-permute-done.2.refs_3_
  12.4 0.1 collective-permute-start.3
  12.5 0.4 %shard_map.123 = (bf16[288,256]{1,0:T(8,128)(2,1)S(1)}, bf16[288,256]{1,0:T(8,128)(2,1)S(1)}, f32[288,256]{1,0:T(8,128)S(1)}) custom-call(bf16[72,384]{1,0:T(8,128)(2,1)S(1)} %get-tuple-element.29.refs_0_, bf16[72,384]{1,0:T(8,128)(2,1)S(1)} %collective-permute-done.refs_1_, bf16[72,384]{1,0:T(8,128)(2,1)S(1)} %collective-permute-done.1.refs_2_, ...), custom_call_target="tpu_custom_call" | custom-call | flops 2000000000 | bytes 1000000 | tf_op jit(solution)/shard_map/pallas_call | solution.py:367
  12.9 1.1 %collective-permute-done.3.refs_4_ = bf16[4,72,384]{2,1,0:T(8,128)(2,1)S(1)} collective-permute-done((bf16[4,72,384]{2,1,0:T(8,128)(2,1)S(1)}, bf16[4,72,384]{2,1,0:T(8,128)(2,1)S(1)}, u32[]{:S(2)}, u32[]{:S(2)}) %collective-permute-start.3) | collective-permute-done | bytes 221216 | tf_op jit(solution)/shard_map/ppermute | solution.py:443
  14.0 1.5 %shard_map.124 = (bf16[112,128]{1,0:T(8,128)(2,1)S(1)}, bf16[112,128]{1,0:T(8,128)(2,1)S(1)}, bf16[112,128]{1,0:T(8,128)(2,1)S(1)}, bf16[240,384]{1,0:T(8,128)(2...) custom-call(bf16[72,384]{1,0:T(8,128)(2,1)S(1)} %get-tuple-element.2, ...), custom_call_target="tpu_custom_call" | custom-call | flops 100000000 | bytes 1000000 | tf_op jit(solution)/shard_map/pallas_call | solution.py:367
  15.5 2.6 %collective-permute-start.4 = (bf16[112,128]{1,0:T(8,128)(2,1)S(1)}, bf16[112,128]{1,0:T(8,128)(2,1)S(1)}, u32[]{:S(2)}, u32[]{:S(2)}) collective-permute-start(bf16[112,128]{1,0:T(8,128)(2,1)S(1)} %get-tuple-element.40), channel_id=1, source_target_pairs={{0,6},{1,7},{2,4},{3,5},{4,2},{5,3},{6,0},{7,1},{8,14},{9,15},{10,... | collective-permute-start | bytes 86024 | tf_op jit(solution)/shard_map/ppermute | solution.py:402
  18.1 0.0 collective-permute-start.5
  18.1 1.9 %collective-permute-start.6 = (bf16[112,128]{1,0:T(8,128)(2,1)S(1)}, bf16[112,128]{1,0:T(8,128)(2,1)S(1)}, u32[]{:S(2)}, u32[]{:S(2)}) collective-permute-start(bf16[112,128]{1,0:T(8,128)(2,1)S(1)} %get-tuple-element.42), channel_id=1, source_target_pairs={{0,2},{1,3},{2,0},{3,1},{4,6},{5,7},{6,4},{7,5},{8,10},{9,11},{10,... | collective-permute-start | bytes 86024 | tf_op jit(solution)/shard_map/ppermute | solution.py:402
  19.9 2.4 %collective-permute-start.8 = (bf16[240,384]{1,0:T(8,128)(2,1)S(1)}, bf16[240,384]{1,0:T(8,128)(2,1)S(1)}, u32[]{:S(2)}, u32[]{:S(2)}) collective-permute-start(bf16[240,384]{1,0:T(8,128)(2,1)S(1)} %get-tuple-element.43), channel_id=1, source_target_pairs={{0,24},{8,0},{16,8},{24,16},{1,25},{9,1},{17,9},{25,17},{2,26},{10... | collective-permute-start | bytes 552968 | tf_op jit(solution)/shard_map/ppermute | solution.py:28
  22.4 0.0 collective-permute-done.4.refs_0_
  22.4 0.4 %collective-permute-done.5.refs_1_ = bf16[112,128]{1,0:T(8,128)(2,1)S(1)} collective-permute-done((bf16[112,128]{1,0:T(8,128)(2,1)S(1)}, bf16[112,128]{1,0:T(8,128)(2,1)S(1)}, u32[]{:S(2)}, u32[]{:S(2)}) %collective-permute-start.5) | collective-permute-done | bytes 28704 | tf_op jit(solution)/shard_map/ppermute | solution.py:402
  22.8 0.0 collective-permute-done.6.refs_2_
  22.8 2.5 %collective-permute-start.7 = (bf16[3,112,128]{2,1,0:T(8,128)(2,1)S(1)}, bf16[3,112,128]{2,1,0:T(8,128)(2,1)S(1)}, u32[]{:S(2)}, u32[]{:S(2)}) collective-permute-start(bf16[3,112,128]{2,1,0:T(8,128)(2,1)S(1)} %shard_map.125), channel_id=1, source_target_pairs={{0,24},{8,0},{16,8},{24,16},{1,25},{9,1},{17,9},{25,17},{2,26},{10... | collective-permute-start | bytes 258056 | tf_op jit(solution)/shard_map/ppermute | solution.py:28
  25.3 1.1 %shard_map.127 = (f32[2,48,96]{2,1,0:T(8,128)}, f32[2,48,96]{2,1,0:T(8,128)}, f32[2,48]{1,0:T(2,128)}) custom-call(bf16[288,256]{1,0:T(8,128)(2,1)S(1)} %get-tuple-element.45.points0, bf16[288,256]{1,0:T(8,128)(2,1)S(1)} %get-tuple-element.46.hidden0, bf16[288,256]{1,0:T(8,128)(2,1)S(1)} %get-tuple-element.47.points1, ...), custom_call_target="tpu_custom_call" | custom-call | flops 2000000000 | bytes 1000000 | tf_op jit(solution)/shard_map/pallas_call | solution.py:367
  26.5 1.2 %collective-permute-done.7.three = bf16[3,112,128]{2,1,0:T(8,128)(2,1)S(1)} collective-permute-done((bf16[3,112,128]{2,1,0:T(8,128)(2,1)S(1)}, bf16[3,112,128]{2,1,0:T(8,128)(2,1)S(1)}, u32[]{:S(2)}, u32[]{:S(2)}) %collective-permute-start.7) | collective-permute-done | bytes 86048 | tf_op jit(solution)/shard_map/ppermute | solution.py:28
  27.6 0.0 collective-permute-done.8.bundle
  27.6 1.1 %shard_map.126 = bf16[180,384]{1,0:T(8,128)(2,1)} custom-call(bf16[3,112,128]{2,1,0:T(8,128)(2,1)S(1)} %collective-permute-done.7.three, bf16[240,384]{1,0:T(8,128)(2,1)S(1)} %collective-permute-done.8.bundle, bf16[180,144]{1,0:T(8,128)(2,1)S(1)} %get-tuple-element.44.table), custom_call_target="tpu_custom_call" | custom-call | flops 100000000 | bytes 1000000 | tf_op jit(solution)/shard_map/pallas_call | solution.py:367
  (2 shorter events, 0.0 us)
Async XLA Ops:
  2.2 7.5 %collective-permute-start = (bf16[72,384]{1,0:T(8,128)(2,1)S(1)}, bf16[72,384]{1,0:T(8,128)(2,1)S(1)}, u32[]{:S(2)}, u32[]{:S(2)}) collective-permute-start(bf16[72,384]{1,0:T(8,128)(2,1)S(1)} %get-tuple-element.30), channel_id=1, source_target_pairs={{0,6},{1,7},{2,4},{3,5},{4,2},{5,3},{6,0},{7,1},{8,14},{9,15},{10,... | collective-permute-start | bytes 165896 | tf_op jit(solution)/shard_map/ppermute | solution.py:402
  7.3 5.1 %collective-permute-start.1 = (bf16[72,384]{1,0:T(8,128)(2,1)S(1)}, bf16[72,384]{1,0:T(8,128)(2,1)S(1)}, u32[]{:S(2)}, u32[]{:S(2)}) collective-permute-start(bf16[72,384]{1,0:T(8,128)(2,1)S(1)} %get-tuple-element.31), channel_id=1, source_target_pairs={{0,4},{1,5},{2,6},{3,7},{4,0},{5,1},{6,2},{7,3},{8,12},{9,13},{10,... | collective-permute-start | bytes 165896 | tf_op jit(solution)/shard_map/ppermute | solution.py:402
  7.4 5.1 %collective-permute-start.2 = (bf16[72,384]{1,0:T(8,128)(2,1)S(1)}, bf16[72,384]{1,0:T(8,128)(2,1)S(1)}, u32[]{:S(2)}, u32[]{:S(2)}) collective-permute-start(bf16[72,384]{1,0:T(8,128)(2,1)S(1)} %get-tuple-element.32), channel_id=1, source_target_pairs={{0,2},{1,3},{2,0},{3,1},{4,6},{5,7},{6,4},{7,5},{8,10},{9,11},{10,... | collective-permute-start | bytes 165896 | tf_op jit(solution)/shard_map/ppermute | solution.py:402
  12.4 1.5 %collective-permute-start.3 = (bf16[4,72,384]{2,1,0:T(8,128)(2,1)S(1)}, bf16[4,72,384]{2,1,0:T(8,128)(2,1)S(1)}, u32[]{:S(2)}, u32[]{:S(2)}) collective-permute-start(bf16[4,72,384]{2,1,0:T(8,128)(2,1)S(1)} %shard_map.122), channel_id=1, source_target_pairs={{0,1},{1,0},{2,3},{3,2},{4,5},{5,4},{6,7},{7,6},{8,9},{9,8},{10,11... | collective-permute-start | bytes 663560 | tf_op jit(solution)/shard_map/ppermute | solution.py:443
  15.5 6.9 %collective-permute-start.4 = (bf16[112,128]{1,0:T(8,128)(2,1)S(1)}, bf16[112,128]{1,0:T(8,128)(2,1)S(1)}, u32[]{:S(2)}, u32[]{:S(2)}) collective-permute-start(bf16[112,128]{1,0:T(8,128)(2,1)S(1)} %get-tuple-element.40), channel_id=1, source_target_pairs={{0,6},{1,7},{2,4},{3,5},{4,2},{5,3},{6,0},{7,1},{8,14},{9,15},{10,... | collective-permute-start | bytes 86024 | tf_op jit(solution)/shard_map/ppermute | solution.py:402
  18.1 4.8 %collective-permute-start.5 = (bf16[112,128]{1,0:T(8,128)(2,1)S(1)}, bf16[112,128]{1,0:T(8,128)(2,1)S(1)}, u32[]{:S(2)}, u32[]{:S(2)}) collective-permute-start(bf16[112,128]{1,0:T(8,128)(2,1)S(1)} %get-tuple-element.41), channel_id=1, source_target_pairs={{0,4},{1,5},{2,6},{3,7},{4,0},{5,1},{6,2},{7,3},{8,12},{9,13},{10,... | collective-permute-start | bytes 86024 | tf_op jit(solution)/shard_map/ppermute | solution.py:402
  18.1 4.8 %collective-permute-start.6 = (bf16[112,128]{1,0:T(8,128)(2,1)S(1)}, bf16[112,128]{1,0:T(8,128)(2,1)S(1)}, u32[]{:S(2)}, u32[]{:S(2)}) collective-permute-start(bf16[112,128]{1,0:T(8,128)(2,1)S(1)} %get-tuple-element.42), channel_id=1, source_target_pairs={{0,2},{1,3},{2,0},{3,1},{4,6},{5,7},{6,4},{7,5},{8,10},{9,11},{10,... | collective-permute-start | bytes 86024 | tf_op jit(solution)/shard_map/ppermute | solution.py:402
  19.9 7.7 %collective-permute-start.8 = (bf16[240,384]{1,0:T(8,128)(2,1)S(1)}, bf16[240,384]{1,0:T(8,128)(2,1)S(1)}, u32[]{:S(2)}, u32[]{:S(2)}) collective-permute-start(bf16[240,384]{1,0:T(8,128)(2,1)S(1)} %get-tuple-element.43), channel_id=1, source_target_pairs={{0,24},{8,0},{16,8},{24,16},{1,25},{9,1},{17,9},{25,17},{2,26},{10... | collective-permute-start | bytes 552968 | tf_op jit(solution)/shard_map/ppermute | solution.py:28
  22.8 4.8 %collective-permute-start.7 = (bf16[3,112,128]{2,1,0:T(8,128)(2,1)S(1)}, bf16[3,112,128]{2,1,0:T(8,128)(2,1)S(1)}, u32[]{:S(2)}, u32[]{:S(2)}) collective-permute-start(bf16[3,112,128]{2,1,0:T(8,128)(2,1)S(1)} %shard_map.125), channel_id=1, source_target_pairs={{0,24},{8,0},{16,8},{24,16},{1,25},{9,1},{17,9},{25,17},{2,26},{10... | collective-permute-start | bytes 258056 | tf_op jit(solution)/shard_map/ppermute | solution.py:28

commit v20 on v19

--- a/solution.py
+++ b/solution.py
@@ -218,7 +218,7 @@
 
 
 ORDER = (0, 3, 2, 1)
-FIELD_ROWS = 192
+FIELD_ROWS = 184
 
 
 def join_kernel(*refs):
@@ -307,8 +307,6 @@
     ]
     for r, band in enumerate(eight_points(inner, 1)):
         by_lat[r] = jnp.concatenate(band, axis=1)
-    length = own_field.shape[0]
-    bundle[0:length] = own_field[...]
     for i, d in enumerate(ORDER):
         band = pack(by_lat[assign[0, 2 * partner(d) + core]])
         if d:
@@ -316,8 +314,10 @@
         else:
             tail = bundle.shape[0] - FIELD_ROWS
             band = jnp.concatenate([band, jnp.zeros((3 * tail - band.shape[0], LANES), F32)], axis=0)
-            band = [band[i * tail : (i + 1) * tail] for i in range(3)]
-            bundle[FIELD_ROWS:] = jnp.concatenate(band, axis=1).astype(BF16)
+            band = jnp.concatenate([band[j * tail : (j + 1) * tail] for j in range(3)], axis=1)
+            lines = own_field[...].astype(F32)
+            gap = jnp.zeros((FIELD_ROWS - lines.shape[0], lines.shape[1]), F32)
+            bundle[...] = jnp.concatenate([lines, gap, band], axis=0).astype(BF16)
 
 
 def products_kernel(points0, hidden0, points1, hidden1, grad_pre, grad_y, gw1, gw2, gb1):
@@ -337,7 +337,8 @@
 
 def compose_kernel(last, three, bundle, table, out, by_block, result, sems):
     rows = by_block.shape[1]
-    own = bundle[FIELD_ROWS:].astype(F32)
+    lines = bundle[...].astype(F32)
+    own = lines[FIELD_ROWS:]
     own = jnp.concatenate([own[:, i * LANES : (i + 1) * LANES] for i in range(3)], axis=0)
     chunks = [own[: three.shape[1]]] + [three[i].astype(F32) for i in range(3)]
     for d, chunk in zip(ORDER, chunks):
@@ -350,7 +351,8 @@
     copies = []
     for i, (_, tile) in enumerate(columns(out.shape[1])):
         mixed = jnp.dot(table[...], parts[:, i * LANES : (i + 1) * LANES], preferred_element_type=F32)
-        whole = bundle[0 : out.shape[0], tile].astype(F32) + mixed.astype(BF16).astype(F32)
+        field = lines[: out.shape[0], i * LANES : (i + 1) * LANES]
+        whole = field + mixed.astype(BF16).astype(F32)
         result[:, tile] = jnp.where(none, 0.0, whole).astype(BF16)
         copies.append(pltpu.make_async_copy(result.at[:, tile], out.at[:, tile], sems.at[i]))
         copies[-1].start()
@@ -455,7 +457,7 @@
     packed = shape((rows + rows // 2 + 4, LANES), BF16)
     scratch, sems = scratch_for(latitudes)
     both = shape((2, NB * rows, wide), BF16)
-    tail = -(-packed.shape[0] // 48) * 16
+    tail = -(-packed.shape[0] // 24) * 8
     bundle = shape((FIELD_ROWS + tail, width), BF16)
     *chunks, bundle, points1, hidden1, grad_pre, grad_y = call(
         filter_kernel,

time: 28.9 us -> 28.7 us (level)
  no operation moved by 1% of the time
where the time goes in v20:
time: 28.7 us; the launch traced here: 28.6 us
  starting transfers between devices  15.2 us (53%)
  Pallas kernels  7.2 us (25%)
  waiting for transfers between devices  5.44 us (19%)
  between operations  0.69 us (2%)
    ppermute x6, starting transfers between devices, swap(): return [lax.ppermute(chunk, 'lat', p) for chunk, p in zip(chunks, pairs)]  10.2 us
    pallas_call x8, Pallas kernels, call(): pl.pallas_call(kernel, out_shape=outs, in_specs=[VMEM] * len(near) + [HBM...  7.2 us
    ppermute x2, starting transfers between devices, turn(): lax.ppermute(value, axis, [(i, (i - 1) % length) for i in range(length)])  4.94 us
    ppermute x6, waiting for transfers between devices, swap(): return [lax.ppermute(chunk, 'lat', p) for chunk, p in zip(chunks, pairs)]  3.36 us
    ppermute x1, waiting for transfers between devices, paired_blocks(): other = lax.ppermute(own, 'lat', [(i, i ^ 1) for i in range(2 * NB)])  1.1 us
    ppermute x2, waiting for transfers between devices, turn(): lax.ppermute(value, axis, [(i, (i - 1) % length) for i in range(length)])  0.98 us
  transfers between devices with their start and end apart: 9, of which 5 were waited for; matrix products, arithmetic and copies ran while one was open for 0% of the time, Pallas kernels for 10%

profile of v20, /device:TPU:0, one launch (start us, length us, event | category | flops | bytes accessed | tf_op | source)
XLA Modules:
  0.0 28.6 jit_solution(18004739391776941756)
XLA Ops:
  0.6 1.6 %shard_map.120 = (bf16[72,384]{1,0:T(8,128)(2,1)S(1)}, bf16[72,384]{1,0:T(8,128)(2,1)S(1)}, bf16[72,384]{1,0:T(8,128)(2,1)S(1)}, bf16[72,384]{1,0:T(8,128)(2,1)S(1)}) custom-call(s32[8]{0:T(128)} %refs_0_.3, s32[8]{0:T(128)} %refs_1_.3, bf16[180,384]{1,0:T(8,128)(2,1)} %bitcast.16, bf16[144,180]{1,0:T(8,128)(2,1)} %constant.4.clone.refs_3_, ...), custom_call_target="tpu_custom_call" | custom-call | flops 100000000 | bytes 1000000 | tf_op jit(solution)/shard_map/pallas_call | solution.py:369
  2.2 5.1 %collective-permute-start = (bf16[72,384]{1,0:T(8,128)(2,1)S(1)}, bf16[72,384]{1,0:T(8,128)(2,1)S(1)}, u32[]{:S(2)}, u32[]{:S(2)}) collective-permute-start(bf16[72,384]{1,0:T(8,128)(2,1)S(1)} %get-tuple-element.30), channel_id=1, source_target_pairs={{0,6},{1,7},{2,4},{3,5},{4,2},{5,3},{6,0},{7,1},{8,14},{9,15},{10,... | collective-permute-start | bytes 165896 | tf_op jit(solution)/shard_map/ppermute | solution.py:404
  7.3 0.0 collective-permute-start.1
  7.4 0.6 %collective-permute-start.2 = (bf16[72,384]{1,0:T(8,128)(2,1)S(1)}, bf16[72,384]{1,0:T(8,128)(2,1)S(1)}, u32[]{:S(2)}, u32[]{:S(2)}) collective-permute-start(bf16[72,384]{1,0:T(8,128)(2,1)S(1)} %get-tuple-element.32), channel_id=1, source_target_pairs={{0,2},{1,3},{2,0},{3,1},{4,6},{5,7},{6,4},{7,5},{8,10},{9,11},{10,... | collective-permute-start | bytes 165896 | tf_op jit(solution)/shard_map/ppermute | solution.py:404
  8.0 1.5 %shard_map.121 = (bf16[256,256]{1,0:T(8,128)(2,1)S(1)}, bf16[256,256]{1,0:T(8,128)(2,1)S(1)}, bf16[256,256]{1,0:T(8,128)(2,1)S(1)}, f32[1,256]{1,0:T(1,128)S(1)}...) custom-call(s32[8]{0:T(128)} %refs_0_.3, s32[8]{0:T(128)} %refs_1_.3, ...), custom_call_target="tpu_custom_call" | custom-call | flops 2000000000 | bytes 1000000 | tf_op jit(solution)/shard_map/pallas_call | solution.py:369
  9.5 0.2 collective-permute-done.refs_1_
  9.7 2.7 %collective-permute-done.1.refs_2_ = bf16[72,384]{1,0:T(8,128)(2,1)S(1)} collective-permute-done((bf16[72,384]{1,0:T(8,128)(2,1)S(1)}, bf16[72,384]{1,0:T(8,128)(2,1)S(1)}, u32[]{:S(2)}, u32[]{:S(2)}) %collective-permute-start.1) | collective-permute-done | bytes 55328 | tf_op jit(solution)/shard_map/ppermute | solution.py:404
  12.4 0.0 collective-permute-done.2.refs_3_
  12.4 0.1 collective-permute-start.3
  12.5 0.4 %shard_map.123 = (bf16[288,256]{1,0:T(8,128)(2,1)S(1)}, bf16[288,256]{1,0:T(8,128)(2,1)S(1)}, f32[288,256]{1,0:T(8,128)S(1)}) custom-call(bf16[72,384]{1,0:T(8,128)(2,1)S(1)} %get-tuple-element.29.refs_0_, bf16[72,384]{1,0:T(8,128)(2,1)S(1)} %collective-permute-done.refs_1_, bf16[72,384]{1,0:T(8,128)(2,1)S(1)} %collective-permute-done.1.refs_2_, ...), custom_call_target="tpu_custom_call" | custom-call | flops 2000000000 | bytes 1000000 | tf_op jit(solution)/shard_map/pallas_call | solution.py:369
  12.9 1.1 %collective-permute-done.3.refs_4_ = bf16[4,72,384]{2,1,0:T(8,128)(2,1)S(1)} collective-permute-done((bf16[4,72,384]{2,1,0:T(8,128)(2,1)S(1)}, bf16[4,72,384]{2,1,0:T(8,128)(2,1)S(1)}, u32[]{:S(2)}, u32[]{:S(2)}) %collective-permute-start.3) | collective-permute-done | bytes 221216 | tf_op jit(solution)/shard_map/ppermute | solution.py:445
  14.0 1.5 %shard_map.124 = (bf16[112,128]{1,0:T(8,128)(2,1)S(1)}, bf16[112,128]{1,0:T(8,128)(2,1)S(1)}, bf16[112,128]{1,0:T(8,128)(2,1)S(1)}, bf16[224,384]{1,0:T(8,128)(2...) custom-call(bf16[72,384]{1,0:T(8,128)(2,1)S(1)} %get-tuple-element.2, ...), custom_call_target="tpu_custom_call" | custom-call | flops 100000000 | bytes 1000000 | tf_op jit(solution)/shard_map/pallas_call | solution.py:369
  15.5 2.6 %collective-permute-start.4 = (bf16[112,128]{1,0:T(8,128)(2,1)S(1)}, bf16[112,128]{1,0:T(8,128)(2,1)S(1)}, u32[]{:S(2)}, u32[]{:S(2)}) collective-permute-start(bf16[112,128]{1,0:T(8,128)(2,1)S(1)} %get-tuple-element.40), channel_id=1, source_target_pairs={{0,6},{1,7},{2,4},{3,5},{4,2},{5,3},{6,0},{7,1},{8,14},{9,15},{10,... | collective-permute-start | bytes 86024 | tf_op jit(solution)/shard_map/ppermute | solution.py:404
  18.1 0.0 collective-permute-start.5
  18.1 1.9 %collective-permute-start.6 = (bf16[112,128]{1,0:T(8,128)(2,1)S(1)}, bf16[112,128]{1,0:T(8,128)(2,1)S(1)}, u32[]{:S(2)}, u32[]{:S(2)}) collective-permute-start(bf16[112,128]{1,0:T(8,128)(2,1)S(1)} %get-tuple-element.42), channel_id=1, source_target_pairs={{0,2},{1,3},{2,0},{3,1},{4,6},{5,7},{6,4},{7,5},{8,10},{9,11},{10,... | collective-permute-start | bytes 86024 | tf_op jit(solution)/shard_map/ppermute | solution.py:404
  19.9 2.4 %collective-permute-start.8 = (bf16[224,384]{1,0:T(8,128)(2,1)S(1)}, bf16[224,384]{1,0:T(8,128)(2,1)S(1)}, u32[]{:S(2)}, u32[]{:S(2)}) collective-permute-start(bf16[224,384]{1,0:T(8,128)(2,1)S(1)} %get-tuple-element.43), channel_id=1, source_target_pairs={{0,24},{8,0},{16,8},{24,16},{1,25},{9,1},{17,9},{25,17},{2,26},{10... | collective-permute-start | bytes 516104 | tf_op jit(solution)/shard_map/ppermute | solution.py:28
  22.4 0.0 collective-permute-done.4.refs_0_
  22.4 0.4 %collective-permute-done.5.refs_1_ = bf16[112,128]{1,0:T(8,128)(2,1)S(1)} collective-permute-done((bf16[112,128]{1,0:T(8,128)(2,1)S(1)}, bf16[112,128]{1,0:T(8,128)(2,1)S(1)}, u32[]{:S(2)}, u32[]{:S(2)}) %collective-permute-start.5) | collective-permute-done | bytes 28704 | tf_op jit(solution)/shard_map/ppermute | solution.py:404
  22.8 0.0 collective-permute-done.6.refs_2_
  22.8 2.5 %collective-permute-start.7 = (bf16[3,112,128]{2,1,0:T(8,128)(2,1)S(1)}, bf16[3,112,128]{2,1,0:T(8,128)(2,1)S(1)}, u32[]{:S(2)}, u32[]{:S(2)}) collective-permute-start(bf16[3,112,128]{2,1,0:T(8,128)(2,1)S(1)} %shard_map.125), channel_id=1, source_target_pairs={{0,24},{8,0},{16,8},{24,16},{1,25},{9,1},{17,9},{25,17},{2,26},{10... | collective-permute-start | bytes 258056 | tf_op jit(solution)/shard_map/ppermute | solution.py:28
  25.3 1.1 %shard_map.127 = (f32[2,48,96]{2,1,0:T(8,128)}, f32[2,48,96]{2,1,0:T(8,128)}, f32[2,48]{1,0:T(2,128)}) custom-call(bf16[288,256]{1,0:T(8,128)(2,1)S(1)} %get-tuple-element.45.points0, bf16[288,256]{1,0:T(8,128)(2,1)S(1)} %get-tuple-element.46.hidden0, bf16[288,256]{1,0:T(8,128)(2,1)S(1)} %get-tuple-element.47.points1, ...), custom_call_target="tpu_custom_call" | custom-call | flops 2000000000 | bytes 1000000 | tf_op jit(solution)/shard_map/pallas_call | solution.py:369
  26.5 1.0 %collective-permute-done.7.three = bf16[3,112,128]{2,1,0:T(8,128)(2,1)S(1)} collective-permute-done((bf16[3,112,128]{2,1,0:T(8,128)(2,1)S(1)}, bf16[3,112,128]{2,1,0:T(8,128)(2,1)S(1)}, u32[]{:S(2)}, u32[]{:S(2)}) %collective-permute-start.7) | collective-permute-done | bytes 86048 | tf_op jit(solution)/shard_map/ppermute | solution.py:28
  27.4 0.0 collective-permute-done.8.bundle
  27.4 1.1 %shard_map.126 = bf16[180,384]{1,0:T(8,128)(2,1)} custom-call(bf16[3,112,128]{2,1,0:T(8,128)(2,1)S(1)} %collective-permute-done.7.three, bf16[224,384]{1,0:T(8,128)(2,1)S(1)} %collective-permute-done.8.bundle, bf16[180,144]{1,0:T(8,128)(2,1)S(1)} %get-tuple-element.44.table), custom_call_target="tpu_custom_call" | custom-call | flops 100000000 | bytes 1000000 | tf_op jit(solution)/shard_map/pallas_call | solution.py:369
  (2 shorter events, 0.0 us)
Async XLA Ops:
  2.2 7.5 %collective-permute-start = (bf16[72,384]{1,0:T(8,128)(2,1)S(1)}, bf16[72,384]{1,0:T(8,128)(2,1)S(1)}, u32[]{:S(2)}, u32[]{:S(2)}) collective-permute-start(bf16[72,384]{1,0:T(8,128)(2,1)S(1)} %get-tuple-element.30), channel_id=1, source_target_pairs={{0,6},{1,7},{2,4},{3,5},{4,2},{5,3},{6,0},{7,1},{8,14},{9,15},{10,... | collective-permute-start | bytes 165896 | tf_op jit(solution)/shard_map/ppermute | solution.py:404
  7.3 5.1 %collective-permute-start.1 = (bf16[72,384]{1,0:T(8,128)(2,1)S(1)}, bf16[72,384]{1,0:T(8,128)(2,1)S(1)}, u32[]{:S(2)}, u32[]{:S(2)}) collective-permute-start(bf16[72,384]{1,0:T(8,128)(2,1)S(1)} %get-tuple-element.31), channel_id=1, source_target_pairs={{0,4},{1,5},{2,6},{3,7},{4,0},{5,1},{6,2},{7,3},{8,12},{9,13},{10,... | collective-permute-start | bytes 165896 | tf_op jit(solution)/shard_map/ppermute | solution.py:404
  7.4 5.1 %collective-permute-start.2 = (bf16[72,384]{1,0:T(8,128)(2,1)S(1)}, bf16[72,384]{1,0:T(8,128)(2,1)S(1)}, u32[]{:S(2)}, u32[]{:S(2)}) collective-permute-start(bf16[72,384]{1,0:T(8,128)(2,1)S(1)} %get-tuple-element.32), channel_id=1, source_target_pairs={{0,2},{1,3},{2,0},{3,1},{4,6},{5,7},{6,4},{7,5},{8,10},{9,11},{10,... | collective-permute-start | bytes 165896 | tf_op jit(solution)/shard_map/ppermute | solution.py:404
  12.4 1.5 %collective-permute-start.3 = (bf16[4,72,384]{2,1,0:T(8,128)(2,1)S(1)}, bf16[4,72,384]{2,1,0:T(8,128)(2,1)S(1)}, u32[]{:S(2)}, u32[]{:S(2)}) collective-permute-start(bf16[4,72,384]{2,1,0:T(8,128)(2,1)S(1)} %shard_map.122), channel_id=1, source_target_pairs={{0,1},{1,0},{2,3},{3,2},{4,5},{5,4},{6,7},{7,6},{8,9},{9,8},{10,11... | collective-permute-start | bytes 663560 | tf_op jit(solution)/shard_map/ppermute | solution.py:445
  15.5 6.9 %collective-permute-start.4 = (bf16[112,128]{1,0:T(8,128)(2,1)S(1)}, bf16[112,128]{1,0:T(8,128)(2,1)S(1)}, u32[]{:S(2)}, u32[]{:S(2)}) collective-permute-start(bf16[112,128]{1,0:T(8,128)(2,1)S(1)} %get-tuple-element.40), channel_id=1, source_target_pairs={{0,6},{1,7},{2,4},{3,5},{4,2},{5,3},{6,0},{7,1},{8,14},{9,15},{10,... | collective-permute-start | bytes 86024 | tf_op jit(solution)/shard_map/ppermute | solution.py:404
  18.1 4.8 %collective-permute-start.5 = (bf16[112,128]{1,0:T(8,128)(2,1)S(1)}, bf16[112,128]{1,0:T(8,128)(2,1)S(1)}, u32[]{:S(2)}, u32[]{:S(2)}) collective-permute-start(bf16[112,128]{1,0:T(8,128)(2,1)S(1)} %get-tuple-element.41), channel_id=1, source_target_pairs={{0,4},{1,5},{2,6},{3,7},{4,0},{5,1},{6,2},{7,3},{8,12},{9,13},{10,... | collective-permute-start | bytes 86024 | tf_op jit(solution)/shard_map/ppermute | solution.py:404
  18.1 4.8 %collective-permute-start.6 = (bf16[112,128]{1,0:T(8,128)(2,1)S(1)}, bf16[112,128]{1,0:T(8,128)(2,1)S(1)}, u32[]{:S(2)}, u32[]{:S(2)}) collective-permute-start(bf16[112,128]{1,0:T(8,128)(2,1)S(1)} %get-tuple-element.42), channel_id=1, source_target_pairs={{0,2},{1,3},{2,0},{3,1},{4,6},{5,7},{6,4},{7,5},{8,10},{9,11},{10,... | collective-permute-start | bytes 86024 | tf_op jit(solution)/shard_map/ppermute | solution.py:404
  19.9 7.5 %collective-permute-start.8 = (bf16[224,384]{1,0:T(8,128)(2,1)S(1)}, bf16[224,384]{1,0:T(8,128)(2,1)S(1)}, u32[]{:S(2)}, u32[]{:S(2)}) collective-permute-start(bf16[224,384]{1,0:T(8,128)(2,1)S(1)} %get-tuple-element.43), channel_id=1, source_target_pairs={{0,24},{8,0},{16,8},{24,16},{1,25},{9,1},{17,9},{25,17},{2,26},{10... | collective-permute-start | bytes 516104 | tf_op jit(solution)/shard_map/ppermute | solution.py:28
  22.8 4.6 %collective-permute-start.7 = (bf16[3,112,128]{2,1,0:T(8,128)(2,1)S(1)}, bf16[3,112,128]{2,1,0:T(8,128)(2,1)S(1)}, u32[]{:S(2)}, u32[]{:S(2)}) collective-permute-start(bf16[3,112,128]{2,1,0:T(8,128)(2,1)S(1)} %shard_map.125), channel_id=1, source_target_pairs={{0,24},{8,0},{16,8},{24,16},{1,25},{9,1},{17,9},{25,17},{2,26},{10... | collective-permute-start | bytes 258056 | tf_op jit(solution)/shard_map/ppermute | solution.py:28

commit v21 on v20

--- a/solution.py
+++ b/solution.py
@@ -284,11 +284,12 @@
     n_rows, rows, _ = by_lat.shape
     half = rows * n_rows // 2
     waves = eight_points([(by_lat[r][:, :LANES], by_lat[r][:, LANES:]) for r in range(n_rows)], -1)
+    step = rows + 1
     for k, wave in enumerate(waves):
-        real[k * rows : (k + 1) * rows] = wave[0]
-        imag[k * rows : (k + 1) * rows] = wave[1]
+        real[k * step : k * step + rows] = wave[0]
+        imag[k * step : k * step + rows] = wave[1]
     dy = [
-        jnp.concatenate([ref[pl.ds(m, n_rows, stride=rows), :] for m in range(rows)], axis=0)
+        jnp.concatenate([ref[pl.ds(m, n_rows, stride=step), :] for m in range(rows)], axis=0)
         for ref in (real, imag)
     ]
     dy = jnp.concatenate(dy, axis=1).astype(BF16)
@@ -299,12 +300,14 @@
     for side in range(2):
         grad_y[side] = dy[side]
         grad_pre[side] = dp[side]
-        place = pl.ds(pl.multiple_of((core if side == 0 else 1 - core) * half, 8), half)
-        real[place] = dv[side * half : (side + 1) * half, :LANES]
-        imag[place] = dv[side * half : (side + 1) * half, LANES:]
-    inner = [
-        tuple(ref[pl.ds(k, rows, stride=n_rows), :] for ref in (real, imag)) for k in range(n_rows)
-    ]
+    step = n_rows + 1
+    dv = [jnp.where(core == g, dv[:half], dv[half:]) for g in range(2)]
+    for g in range(2):
+        for i in range(rows // 2):
+            m = g * rows // 2 + i
+            real[m * step : m * step + n_rows] = dv[g][i * n_rows : (i + 1) * n_rows, :LANES]
+            imag[m * step : m * step + n_rows] = dv[g][i * n_rows : (i + 1) * n_rows, LANES:]
+    inner = [tuple(ref[pl.ds(k, rows, stride=step), :] for ref in (real, imag)) for k in range(n_rows)]
     for r, band in enumerate(eight_points(inner, 1)):
         by_lat[r] = jnp.concatenate(band, axis=1)
     for i, d in enumerate(ORDER):
@@ -467,8 +470,8 @@
             pltpu.VMEM((n_rows, rows, wide), F32),
             by_pair,
             pltpu.VMEM((NB * rows, wide), F32),
-            pltpu.VMEM((n_rows * rows, LANES), F32),
-            pltpu.VMEM((n_rows * rows, LANES), F32),
+            pltpu.VMEM(((n_rows + 1) * rows, LANES), F32),
+            pltpu.VMEM(((n_rows + 1) * rows, LANES), F32),
             sems,
         ],
         (*received, other, slope0, mat1, turned1, turned2, bias, field, latitudes),

time: 28.7 us -> 28.7 us (level)
  no operation moved by 1% of the time
where the time goes in v21:
time: 28.7 us; the launch traced here: 28.5 us
  starting transfers between devices  15.2 us (53%)
  Pallas kernels  7.15 us (25%)
  waiting for transfers between devices  5.44 us (19%)
  between operations  0.69 us (2%)
    ppermute x6, starting transfers between devices, swap(): return [lax.ppermute(chunk, 'lat', p) for chunk, p in zip(chunks, pairs)]  10.2 us
    pallas_call x8, Pallas kernels, call(): pl.pallas_call(kernel, out_shape=outs, in_specs=[VMEM] * len(near) + [HBM...  7.15 us
    ppermute x2, starting transfers between devices, turn(): lax.ppermute(value, axis, [(i, (i - 1) % length) for i in range(length)])  4.94 us
    ppermute x6, waiting for transfers between devices, swap(): return [lax.ppermute(chunk, 'lat', p) for chunk, p in zip(chunks, pairs)]  3.36 us
    ppermute x1, waiting for transfers between devices, paired_blocks(): other = lax.ppermute(own, 'lat', [(i, i ^ 1) for i in range(2 * NB)])  1.1 us
    ppermute x2, waiting for transfers between devices, turn(): lax.ppermute(value, axis, [(i, (i - 1) % length) for i in range(length)])  0.98 us
  transfers between devices with their start and end apart: 9, of which 5 were waited for; matrix products, arithmetic and copies ran while one was open for 0% of the time, Pallas kernels for 10%

profile of v21, /device:TPU:0, one launch (start us, length us, event | category | flops | bytes accessed | tf_op | source)
XLA Modules:
  0.0 28.5 jit_solution(6952670696180260209)
XLA Ops:
  0.6 1.6 %shard_map.120 = (bf16[72,384]{1,0:T(8,128)(2,1)S(1)}, bf16[72,384]{1,0:T(8,128)(2,1)S(1)}, bf16[72,384]{1,0:T(8,128)(2,1)S(1)}, bf16[72,384]{1,0:T(8,128)(2,1)S(1)}) custom-call(s32[8]{0:T(128)} %refs_0_.3, s32[8]{0:T(128)} %refs_1_.3, bf16[180,384]{1,0:T(8,128)(2,1)} %bitcast.16, bf16[144,180]{1,0:T(8,128)(2,1)} %constant.4.clone.refs_3_, ...), custom_call_target="tpu_custom_call" | custom-call | flops 100000000 | bytes 1000000 | tf_op jit(solution)/shard_map/pallas_call | solution.py:372
  2.2 5.1 %collective-permute-start = (bf16[72,384]{1,0:T(8,128)(2,1)S(1)}, bf16[72,384]{1,0:T(8,128)(2,1)S(1)}, u32[]{:S(2)}, u32[]{:S(2)}) collective-permute-start(bf16[72,384]{1,0:T(8,128)(2,1)S(1)} %get-tuple-element.30), channel_id=1, source_target_pairs={{0,6},{1,7},{2,4},{3,5},{4,2},{5,3},{6,0},{7,1},{8,14},{9,15},{10,... | collective-permute-start | bytes 165896 | tf_op jit(solution)/shard_map/ppermute | solution.py:407
  7.3 0.0 collective-permute-start.1
  7.4 0.6 %collective-permute-start.2 = (bf16[72,384]{1,0:T(8,128)(2,1)S(1)}, bf16[72,384]{1,0:T(8,128)(2,1)S(1)}, u32[]{:S(2)}, u32[]{:S(2)}) collective-permute-start(bf16[72,384]{1,0:T(8,128)(2,1)S(1)} %get-tuple-element.32), channel_id=1, source_target_pairs={{0,2},{1,3},{2,0},{3,1},{4,6},{5,7},{6,4},{7,5},{8,10},{9,11},{10,... | collective-permute-start | bytes 165896 | tf_op jit(solution)/shard_map/ppermute | solution.py:407
  8.0 1.5 %shard_map.121 = (bf16[256,256]{1,0:T(8,128)(2,1)S(1)}, bf16[256,256]{1,0:T(8,128)(2,1)S(1)}, bf16[256,256]{1,0:T(8,128)(2,1)S(1)}, f32[1,256]{1,0:T(1,128)S(1)}...) custom-call(s32[8]{0:T(128)} %refs_0_.3, s32[8]{0:T(128)} %refs_1_.3, ...), custom_call_target="tpu_custom_call" | custom-call | flops 2000000000 | bytes 1000000 | tf_op jit(solution)/shard_map/pallas_call | solution.py:372
  9.5 0.2 collective-permute-done.refs_1_
  9.7 2.7 %collective-permute-done.1.refs_2_ = bf16[72,384]{1,0:T(8,128)(2,1)S(1)} collective-permute-done((bf16[72,384]{1,0:T(8,128)(2,1)S(1)}, bf16[72,384]{1,0:T(8,128)(2,1)S(1)}, u32[]{:S(2)}, u32[]{:S(2)}) %collective-permute-start.1) | collective-permute-done | bytes 55328 | tf_op jit(solution)/shard_map/ppermute | solution.py:407
  12.4 0.0 collective-permute-done.2.refs_3_
  12.4 0.1 collective-permute-start.3
  12.5 0.4 %shard_map.123 = (bf16[288,256]{1,0:T(8,128)(2,1)S(1)}, bf16[288,256]{1,0:T(8,128)(2,1)S(1)}, f32[288,256]{1,0:T(8,128)S(1)}) custom-call(bf16[72,384]{1,0:T(8,128)(2,1)S(1)} %get-tuple-element.29.refs_0_, bf16[72,384]{1,0:T(8,128)(2,1)S(1)} %collective-permute-done.refs_1_, bf16[72,384]{1,0:T(8,128)(2,1)S(1)} %collective-permute-done.1.refs_2_, ...), custom_call_target="tpu_custom_call" | custom-call | flops 2000000000 | bytes 1000000 | tf_op jit(solution)/shard_map/pallas_call | solution.py:372
  12.9 1.1 %collective-permute-done.3.refs_4_ = bf16[4,72,384]{2,1,0:T(8,128)(2,1)S(1)} collective-permute-done((bf16[4,72,384]{2,1,0:T(8,128)(2,1)S(1)}, bf16[4,72,384]{2,1,0:T(8,128)(2,1)S(1)}, u32[]{:S(2)}, u32[]{:S(2)}) %collective-permute-start.3) | collective-permute-done | bytes 221216 | tf_op jit(solution)/shard_map/ppermute | solution.py:448
  14.0 1.5 %shard_map.124 = (bf16[112,128]{1,0:T(8,128)(2,1)S(1)}, bf16[112,128]{1,0:T(8,128)(2,1)S(1)}, bf16[112,128]{1,0:T(8,128)(2,1)S(1)}, bf16[224,384]{1,0:T(8,128)(2...) custom-call(bf16[72,384]{1,0:T(8,128)(2,1)S(1)} %get-tuple-element.2, ...), custom_call_target="tpu_custom_call" | custom-call | flops 100000000 | bytes 1000000 | tf_op jit(solution)/shard_map/pallas_call | solution.py:372
  15.4 2.6 %collective-permute-start.4 = (bf16[112,128]{1,0:T(8,128)(2,1)S(1)}, bf16[112,128]{1,0:T(8,128)(2,1)S(1)}, u32[]{:S(2)}, u32[]{:S(2)}) collective-permute-start(bf16[112,128]{1,0:T(8,128)(2,1)S(1)} %get-tuple-element.40), channel_id=1, source_target_pairs={{0,6},{1,7},{2,4},{3,5},{4,2},{5,3},{6,0},{7,1},{8,14},{9,15},{10,... | collective-permute-start | bytes 86024 | tf_op jit(solution)/shard_map/ppermute | solution.py:407
  18.0 0.0 collective-permute-start.5
  18.0 1.9 %collective-permute-start.6 = (bf16[112,128]{1,0:T(8,128)(2,1)S(1)}, bf16[112,128]{1,0:T(8,128)(2,1)S(1)}, u32[]{:S(2)}, u32[]{:S(2)}) collective-permute-start(bf16[112,128]{1,0:T(8,128)(2,1)S(1)} %get-tuple-element.42), channel_id=1, source_target_pairs={{0,2},{1,3},{2,0},{3,1},{4,6},{5,7},{6,4},{7,5},{8,10},{9,11},{10,... | collective-permute-start | bytes 86024 | tf_op jit(solution)/shard_map/ppermute | solution.py:407
  19.9 2.4 %collective-permute-start.8 = (bf16[224,384]{1,0:T(8,128)(2,1)S(1)}, bf16[224,384]{1,0:T(8,128)(2,1)S(1)}, u32[]{:S(2)}, u32[]{:S(2)}) collective-permute-start(bf16[224,384]{1,0:T(8,128)(2,1)S(1)} %get-tuple-element.43), channel_id=1, source_target_pairs={{0,24},{8,0},{16,8},{24,16},{1,25},{9,1},{17,9},{25,17},{2,26},{10... | collective-permute-start | bytes 516104 | tf_op jit(solution)/shard_map/ppermute | solution.py:28
  22.3 0.0 collective-permute-done.4.refs_0_
  22.3 0.4 %collective-permute-done.5.refs_1_ = bf16[112,128]{1,0:T(8,128)(2,1)S(1)} collective-permute-done((bf16[112,128]{1,0:T(8,128)(2,1)S(1)}, bf16[112,128]{1,0:T(8,128)(2,1)S(1)}, u32[]{:S(2)}, u32[]{:S(2)}) %collective-permute-start.5) | collective-permute-done | bytes 28704 | tf_op jit(solution)/shard_map/ppermute | solution.py:407
  22.8 0.0 collective-permute-done.6.refs_2_
  22.8 2.5 %collective-permute-start.7 = (bf16[3,112,128]{2,1,0:T(8,128)(2,1)S(1)}, bf16[3,112,128]{2,1,0:T(8,128)(2,1)S(1)}, u32[]{:S(2)}, u32[]{:S(2)}) collective-permute-start(bf16[3,112,128]{2,1,0:T(8,128)(2,1)S(1)} %shard_map.125), channel_id=1, source_target_pairs={{0,24},{8,0},{16,8},{24,16},{1,25},{9,1},{17,9},{25,17},{2,26},{10... | collective-permute-start | bytes 258056 | tf_op jit(solution)/shard_map/ppermute | solution.py:28
  25.3 1.1 %shard_map.127 = (f32[2,48,96]{2,1,0:T(8,128)}, f32[2,48,96]{2,1,0:T(8,128)}, f32[2,48]{1,0:T(2,128)}) custom-call(bf16[288,256]{1,0:T(8,128)(2,1)S(1)} %get-tuple-element.45.points0, bf16[288,256]{1,0:T(8,128)(2,1)S(1)} %get-tuple-element.46.hidden0, bf16[288,256]{1,0:T(8,128)(2,1)S(1)} %get-tuple-element.47.points1, ...), custom_call_target="tpu_custom_call" | custom-call | flops 2000000000 | bytes 1000000 | tf_op jit(solution)/shard_map/pallas_call | solution.py:372
  26.4 1.0 %collective-permute-done.7.three = bf16[3,112,128]{2,1,0:T(8,128)(2,1)S(1)} collective-permute-done((bf16[3,112,128]{2,1,0:T(8,128)(2,1)S(1)}, bf16[3,112,128]{2,1,0:T(8,128)(2,1)S(1)}, u32[]{:S(2)}, u32[]{:S(2)}) %collective-permute-start.7) | collective-permute-done | bytes 86048 | tf_op jit(solution)/shard_map/ppermute | solution.py:28
  27.4 0.0 collective-permute-done.8.bundle
  27.4 1.1 %shard_map.126 = bf16[180,384]{1,0:T(8,128)(2,1)} custom-call(bf16[3,112,128]{2,1,0:T(8,128)(2,1)S(1)} %collective-permute-done.7.three, bf16[224,384]{1,0:T(8,128)(2,1)S(1)} %collective-permute-done.8.bundle, bf16[180,144]{1,0:T(8,128)(2,1)S(1)} %get-tuple-element.44.table), custom_call_target="tpu_custom_call" | custom-call | flops 100000000 | bytes 1000000 | tf_op jit(solution)/shard_map/pallas_call | solution.py:372
  (2 shorter events, 0.0 us)
Async XLA Ops:
  2.2 7.5 %collective-permute-start = (bf16[72,384]{1,0:T(8,128)(2,1)S(1)}, bf16[72,384]{1,0:T(8,128)(2,1)S(1)}, u32[]{:S(2)}, u32[]{:S(2)}) collective-permute-start(bf16[72,384]{1,0:T(8,128)(2,1)S(1)} %get-tuple-element.30), channel_id=1, source_target_pairs={{0,6},{1,7},{2,4},{3,5},{4,2},{5,3},{6,0},{7,1},{8,14},{9,15},{10,... | collective-permute-start | bytes 165896 | tf_op jit(solution)/shard_map/ppermute | solution.py:407
  7.3 5.1 %collective-permute-start.1 = (bf16[72,384]{1,0:T(8,128)(2,1)S(1)}, bf16[72,384]{1,0:T(8,128)(2,1)S(1)}, u32[]{:S(2)}, u32[]{:S(2)}) collective-permute-start(bf16[72,384]{1,0:T(8,128)(2,1)S(1)} %get-tuple-element.31), channel_id=1, source_target_pairs={{0,4},{1,5},{2,6},{3,7},{4,0},{5,1},{6,2},{7,3},{8,12},{9,13},{10,... | collective-permute-start | bytes 165896 | tf_op jit(solution)/shard_map/ppermute | solution.py:407
  7.4 5.1 %collective-permute-start.2 = (bf16[72,384]{1,0:T(8,128)(2,1)S(1)}, bf16[72,384]{1,0:T(8,128)(2,1)S(1)}, u32[]{:S(2)}, u32[]{:S(2)}) collective-permute-start(bf16[72,384]{1,0:T(8,128)(2,1)S(1)} %get-tuple-element.32), channel_id=1, source_target_pairs={{0,2},{1,3},{2,0},{3,1},{4,6},{5,7},{6,4},{7,5},{8,10},{9,11},{10,... | collective-permute-start | bytes 165896 | tf_op jit(solution)/shard_map/ppermute | solution.py:407
  12.4 1.5 %collective-permute-start.3 = (bf16[4,72,384]{2,1,0:T(8,128)(2,1)S(1)}, bf16[4,72,384]{2,1,0:T(8,128)(2,1)S(1)}, u32[]{:S(2)}, u32[]{:S(2)}) collective-permute-start(bf16[4,72,384]{2,1,0:T(8,128)(2,1)S(1)} %shard_map.122), channel_id=1, source_target_pairs={{0,1},{1,0},{2,3},{3,2},{4,5},{5,4},{6,7},{7,6},{8,9},{9,8},{10,11... | collective-permute-start | bytes 663560 | tf_op jit(solution)/shard_map/ppermute | solution.py:448
  15.4 6.9 %collective-permute-start.4 = (bf16[112,128]{1,0:T(8,128)(2,1)S(1)}, bf16[112,128]{1,0:T(8,128)(2,1)S(1)}, u32[]{:S(2)}, u32[]{:S(2)}) collective-permute-start(bf16[112,128]{1,0:T(8,128)(2,1)S(1)} %get-tuple-element.40), channel_id=1, source_target_pairs={{0,6},{1,7},{2,4},{3,5},{4,2},{5,3},{6,0},{7,1},{8,14},{9,15},{10,... | collective-permute-start | bytes 86024 | tf_op jit(solution)/shard_map/ppermute | solution.py:407
  18.0 4.8 %collective-permute-start.5 = (bf16[112,128]{1,0:T(8,128)(2,1)S(1)}, bf16[112,128]{1,0:T(8,128)(2,1)S(1)}, u32[]{:S(2)}, u32[]{:S(2)}) collective-permute-start(bf16[112,128]{1,0:T(8,128)(2,1)S(1)} %get-tuple-element.41), channel_id=1, source_target_pairs={{0,4},{1,5},{2,6},{3,7},{4,0},{5,1},{6,2},{7,3},{8,12},{9,13},{10,... | collective-permute-start | bytes 86024 | tf_op jit(solution)/shard_map/ppermute | solution.py:407
  18.0 4.8 %collective-permute-start.6 = (bf16[112,128]{1,0:T(8,128)(2,1)S(1)}, bf16[112,128]{1,0:T(8,128)(2,1)S(1)}, u32[]{:S(2)}, u32[]{:S(2)}) collective-permute-start(bf16[112,128]{1,0:T(8,128)(2,1)S(1)} %get-tuple-element.42), channel_id=1, source_target_pairs={{0,2},{1,3},{2,0},{3,1},{4,6},{5,7},{6,4},{7,5},{8,10},{9,11},{10,... | collective-permute-start | bytes 86024 | tf_op jit(solution)/shard_map/ppermute | solution.py:407
  19.9 7.5 %collective-permute-start.8 = (bf16[224,384]{1,0:T(8,128)(2,1)S(1)}, bf16[224,384]{1,0:T(8,128)(2,1)S(1)}, u32[]{:S(2)}, u32[]{:S(2)}) collective-permute-start(bf16[224,384]{1,0:T(8,128)(2,1)S(1)} %get-tuple-element.43), channel_id=1, source_target_pairs={{0,24},{8,0},{16,8},{24,16},{1,25},{9,1},{17,9},{25,17},{2,26},{10... | collective-permute-start | bytes 516104 | tf_op jit(solution)/shard_map/ppermute | solution.py:28
  22.8 4.6 %collective-permute-start.7 = (bf16[3,112,128]{2,1,0:T(8,128)(2,1)S(1)}, bf16[3,112,128]{2,1,0:T(8,128)(2,1)S(1)}, u32[]{:S(2)}, u32[]{:S(2)}) collective-permute-start(bf16[3,112,128]{2,1,0:T(8,128)(2,1)S(1)} %shard_map.125), channel_id=1, source_target_pairs={{0,24},{8,0},{16,8},{24,16},{1,25},{9,1},{17,9},{25,17},{2,26},{10... | collective-permute-start | bytes 258056 | tf_op jit(solution)/shard_map/ppermute | solution.py:28

commit v22 on v21

--- a/solution.py
+++ b/solution.py
@@ -170,8 +170,9 @@
     for n in range(NB):
         pieces = [window(spectrum, n * BS) for spectrum in spectra]
         by_block[n] = dense(pieces + points[n]).astype(BF16)
-    for d, out in enumerate(outs):
-        out[...] = by_block[partner(d)]
+    core = lax.rem(lax.axis_index("lat"), 2)
+    for step, out in enumerate(outs):
+        out[...] = by_block[partner(swap_at(step, core))]
 
 
 def ready_kernel(q, *refs):
@@ -217,7 +218,10 @@
     wait(copies[6:])
 
 
-ORDER = (0, 3, 2, 1)
+def swap_at(step, core):
+    return (0, 3, 2 - core, 1 + core)[step]
+
+
 FIELD_ROWS = 184
 
 
@@ -247,10 +251,10 @@
     return [upper, right]
 
 
-def silu_points(chunks, mat, bias, by_pair, points, hidden, slope):
-    for d, chunk in enumerate(chunks):
+def silu_points(core, chunks, mat, bias, by_pair, points, hidden, slope):
+    for step, chunk in enumerate(chunks):
         parts = [window(chunk, j * BS) for j in (2, 3)]
-        by_pair[partner(d)] = jnp.concatenate(parts, axis=1)
+        by_pair[partner(swap_at(step, core))] = jnp.concatenate(parts, axis=1)
     v = by_pair[...].reshape(points.shape).astype(BF16)
     pre = dot(v, mat[...], (1, 0)) + bias[...]
     sig = jax.nn.sigmoid(pre)
@@ -260,9 +264,11 @@
 
 
 def own_kernel(*refs):
-    mat1, bias, points, hidden, slope, by_pair = refs[NB:]
-    chunks = [refs[i][...].astype(F32) for i in ORDER]
-    silu_points(chunks, mat1, bias, by_pair, points, hidden, slope)
+    chunks, rest = refs[:NB], refs[NB:]
+    mat1, bias, points, hidden, slope, by_pair = rest
+    core = lax.rem(lax.axis_index("lat"), 2)
+    chunks = [chunk[...].astype(F32) for chunk in chunks]
+    silu_points(core, chunks, mat1, bias, by_pair, points, hidden, slope)
 
 
 def filter_kernel(*refs):
@@ -271,16 +277,17 @@
     assign, by_lat, by_pair, slope, real, imag, sems = refs[20:]
     copies = fetch(sems, (latitudes,), (assign,))
     core = lax.rem(lax.axis_index("lat"), 2)
-    sides = [[owns[i][...].astype(F32) for i in ORDER], [other[i].astype(F32) for i in ORDER]]
-    silu_points(sides[1], mat1, bias, by_pair, points, hidden, slope)
+    steps = range(NB)
+    sides = [[owns[i][...].astype(F32) for i in steps], [other[i].astype(F32) for i in steps]]
+    silu_points(1 - core, sides[1], mat1, bias, by_pair, points, hidden, slope)
     spectra = [
         [jnp.concatenate([window(chunk, j * BS) for j in range(2)], axis=1) for chunk in chunks]
         for chunks in sides
     ]
     wait(copies)
     for side, rows in zip((core, 1 - core), spectra):
-        for d, row in enumerate(rows):
-            by_lat[assign[0, 2 * partner(d) + side]] = row
+        for i, row in enumerate(rows):
+            by_lat[assign[0, 2 * partner(swap_at(i, side)) + side]] = row
     n_rows, rows, _ = by_lat.shape
     half = rows * n_rows // 2
     waves = eight_points([(by_lat[r][:, :LANES], by_lat[r][:, LANES:]) for r in range(n_rows)], -1)
@@ -310,9 +317,9 @@
     inner = [tuple(ref[pl.ds(k, rows, stride=step), :] for ref in (real, imag)) for k in range(n_rows)]
     for r, band in enumerate(eight_points(inner, 1)):
         by_lat[r] = jnp.concatenate(band, axis=1)
-    for i, d in enumerate(ORDER):
-        band = pack(by_lat[assign[0, 2 * partner(d) + core]])
-        if d:
+    for i in steps:
+        band = pack(by_lat[assign[0, 2 * partner(swap_at(i, core)) + core]])
+        if i:
             outs[i - 1][...] = band.astype(BF16)
         else:
             tail = bundle.shape[0] - FIELD_ROWS
@@ -344,8 +351,9 @@
     own = lines[FIELD_ROWS:]
     own = jnp.concatenate([own[:, i * LANES : (i + 1) * LANES] for i in range(3)], axis=0)
     chunks = [own[: three.shape[1]]] + [three[i].astype(F32) for i in range(3)]
-    for d, chunk in zip(ORDER, chunks):
-        by_block[partner(d)] = jnp.concatenate(unpack(chunk, rows), axis=1)
+    core = lax.rem(lax.axis_index("lat"), 2)
+    for i, chunk in enumerate(chunks):
+        by_block[partner(swap_at(i, core))] = jnp.concatenate(unpack(chunk, rows), axis=1)
     parts = [
         dense([by_block[n, :, c * LANES : (c + 1) * LANES] for n in range(NB)]) for c in range(2)
     ]
@@ -403,7 +411,7 @@
     forward = jnp.asarray(by_part(forward).T)
 
     def swap(chunks):
-        pairs = [[(i, i ^ (2 * d)) for i in range(2 * NB)] for d in ORDER[1:]]
+        pairs = [[(i, i ^ (2 * swap_at(j, i % 2))) for i in range(2 * NB)] for j in range(1, NB)]
         return [lax.ppermute(chunk, "lat", p) for chunk, p in zip(chunks, pairs)]
 
     field = grad_out.reshape(length, width)
@@ -417,7 +425,7 @@
         (),
         far,
     )
-    received = [sent[0], *swap([sent[d] for d in ORDER[1:]])]
+    received = [sent[0], *swap(sent[1:])]
     far = (mode_counts, assignment, w1[0], w2[0], b1[0], forward)
     scratch, _ = scratch_for(*far)
     far = (*far, field)

time: 28.7 us -> 29.2 us (1.017)
  waiting for transfers between devices: 5.44 us -> 5.97 us
    ppermute x6, waiting for transfers between devices: 3.36 us -> 3.89 us  [swap(): return [lax.ppermute(chunk, 'lat', p) for chunk, p in zip(chunks, pairs)]]
where the time goes in v22:
time: 29.2 us; the launch traced here: 29 us
  starting transfers between devices  15.2 us (52%)
  Pallas kernels  7.1 us (24%)
  waiting for transfers between devices  5.97 us (20%)
  between operations  0.69 us (2%)
    ppermute x6, starting transfers between devices, swap(): return [lax.ppermute(chunk, 'lat', p) for chunk, p in zip(chunks, pairs)]  10.2 us
    pallas_call x8, Pallas kernels, call(): pl.pallas_call(kernel, out_shape=outs, in_specs=[VMEM] * len(near) + [HBM...  7.1 us
    ppermute x2, starting transfers between devices, turn(): lax.ppermute(value, axis, [(i, (i - 1) % length) for i in range(length)])  4.95 us
    ppermute x6, waiting for transfers between devices, swap(): return [lax.ppermute(chunk, 'lat', p) for chunk, p in zip(chunks, pairs)]  3.89 us
    ppermute x1, waiting for transfers between devices, paired_blocks(): other = lax.ppermute(own, 'lat', [(i, i ^ 1) for i in range(2 * NB)])  1.1 us
    ppermute x2, waiting for transfers between devices, turn(): lax.ppermute(value, axis, [(i, (i - 1) % length) for i in range(length)])  0.98 us
  transfers between devices with their start and end apart: 9, of which 5 were waited for; matrix products, arithmetic and copies ran while one was open for 0% of the time, Pallas kernels for 10%

profile of v22, /device:TPU:0, one launch (start us, length us, event | category | flops | bytes accessed | tf_op | source)
XLA Modules:
  0.0 29.0 jit_solution(5606850856607210675)
XLA Ops:
  0.6 1.6 %shard_map.120 = (bf16[72,384]{1,0:T(8,128)(2,1)S(1)}, bf16[72,384]{1,0:T(8,128)(2,1)S(1)}, bf16[72,384]{1,0:T(8,128)(2,1)S(1)}, bf16[72,384]{1,0:T(8,128)(2,1)S(1)}) custom-call(s32[8]{0:T(128)} %refs_0_.3, s32[8]{0:T(128)} %refs_1_.3, bf16[180,384]{1,0:T(8,128)(2,1)} %bitcast.16, bf16[144,180]{1,0:T(8,128)(2,1)} %constant.4.clone.refs_3_, ...), custom_call_target="tpu_custom_call" | custom-call | flops 100000000 | bytes 1000000 | tf_op jit(solution)/shard_map/pallas_call | solution.py:380
  2.2 5.1 %collective-permute-start = (bf16[72,384]{1,0:T(8,128)(2,1)S(1)}, bf16[72,384]{1,0:T(8,128)(2,1)S(1)}, u32[]{:S(2)}, u32[]{:S(2)}) collective-permute-start(bf16[72,384]{1,0:T(8,128)(2,1)S(1)} %get-tuple-element.30), channel_id=1, source_target_pairs={{0,6},{1,7},{2,4},{3,5},{4,2},{5,3},{6,0},{7,1},{8,14},{9,15},{10,... | collective-permute-start | bytes 165896 | tf_op jit(solution)/shard_map/ppermute | solution.py:415
  7.3 0.0 collective-permute-start.1
  7.4 0.6 %collective-permute-start.2 = (bf16[72,384]{1,0:T(8,128)(2,1)S(1)}, bf16[72,384]{1,0:T(8,128)(2,1)S(1)}, u32[]{:S(2)}, u32[]{:S(2)}) collective-permute-start(bf16[72,384]{1,0:T(8,128)(2,1)S(1)} %get-tuple-element.32), channel_id=1, source_target_pairs={{0,2},{1,5},{2,0},{3,7},{4,6},{5,1},{6,4},{7,3},{8,10},{9,13},{10,... | collective-permute-start | bytes 165896 | tf_op jit(solution)/shard_map/ppermute | solution.py:415
  8.0 1.5 %shard_map.121 = (bf16[256,256]{1,0:T(8,128)(2,1)S(1)}, bf16[256,256]{1,0:T(8,128)(2,1)S(1)}, bf16[256,256]{1,0:T(8,128)(2,1)S(1)}, f32[1,256]{1,0:T(1,128)S(1)}...) custom-call(s32[8]{0:T(128)} %refs_0_.3, s32[8]{0:T(128)} %refs_1_.3, ...), custom_call_target="tpu_custom_call" | custom-call | flops 2000000000 | bytes 1000000 | tf_op jit(solution)/shard_map/pallas_call | solution.py:380
  9.5 0.4 %collective-permute-done.refs_1_ = bf16[72,384]{1,0:T(8,128)(2,1)S(1)} collective-permute-done((bf16[72,384]{1,0:T(8,128)(2,1)S(1)}, bf16[72,384]{1,0:T(8,128)(2,1)S(1)}, u32[]{:S(2)}, u32[]{:S(2)}) %collective-permute-start) | collective-permute-done | bytes 55328 | tf_op jit(solution)/shard_map/ppermute | solution.py:415
  9.9 2.9 %collective-permute-done.1.refs_2_ = bf16[72,384]{1,0:T(8,128)(2,1)S(1)} collective-permute-done((bf16[72,384]{1,0:T(8,128)(2,1)S(1)}, bf16[72,384]{1,0:T(8,128)(2,1)S(1)}, u32[]{:S(2)}, u32[]{:S(2)}) %collective-permute-start.1) | collective-permute-done | bytes 55328 | tf_op jit(solution)/shard_map/ppermute | solution.py:415
  12.8 0.0 collective-permute-done.2.refs_3_
  12.8 0.1 collective-permute-start.3
  12.9 0.4 %shard_map.123 = (bf16[288,256]{1,0:T(8,128)(2,1)S(1)}, bf16[288,256]{1,0:T(8,128)(2,1)S(1)}, f32[288,256]{1,0:T(8,128)S(1)}) custom-call(bf16[72,384]{1,0:T(8,128)(2,1)S(1)} %get-tuple-element.29.refs_0_, bf16[72,384]{1,0:T(8,128)(2,1)S(1)} %collective-permute-done.refs_1_, bf16[72,384]{1,0:T(8,128)(2,1)S(1)} %collective-permute-done.1.refs_2_, ...), custom_call_target="tpu_custom_call" | custom-call | flops 2000000000 | bytes 1000000 | tf_op jit(solution)/shard_map/pallas_call | solution.py:380
  13.2 1.1 %collective-permute-done.3.refs_4_ = bf16[4,72,384]{2,1,0:T(8,128)(2,1)S(1)} collective-permute-done((bf16[4,72,384]{2,1,0:T(8,128)(2,1)S(1)}, bf16[4,72,384]{2,1,0:T(8,128)(2,1)S(1)}, u32[]{:S(2)}, u32[]{:S(2)}) %collective-permute-start.3) | collective-permute-done | bytes 221216 | tf_op jit(solution)/shard_map/ppermute | solution.py:456
  14.3 1.4 %shard_map.124 = (bf16[112,128]{1,0:T(8,128)(2,1)S(1)}, bf16[112,128]{1,0:T(8,128)(2,1)S(1)}, bf16[112,128]{1,0:T(8,128)(2,1)S(1)}, bf16[224,384]{1,0:T(8,128)(2...) custom-call(bf16[72,384]{1,0:T(8,128)(2,1)S(1)} %get-tuple-element.2, ...), custom_call_target="tpu_custom_call" | custom-call | flops 100000000 | bytes 1000000 | tf_op jit(solution)/shard_map/pallas_call | solution.py:380
  15.8 2.4 %collective-permute-start.4 = (bf16[112,128]{1,0:T(8,128)(2,1)S(1)}, bf16[112,128]{1,0:T(8,128)(2,1)S(1)}, u32[]{:S(2)}, u32[]{:S(2)}) collective-permute-start(bf16[112,128]{1,0:T(8,128)(2,1)S(1)} %get-tuple-element.40), channel_id=1, source_target_pairs={{0,6},{1,7},{2,4},{3,5},{4,2},{5,3},{6,0},{7,1},{8,14},{9,15},{10,... | collective-permute-start | bytes 86024 | tf_op jit(solution)/shard_map/ppermute | solution.py:415
  18.2 0.0 collective-permute-start.5
  18.2 2.0 %collective-permute-start.6 = (bf16[112,128]{1,0:T(8,128)(2,1)S(1)}, bf16[112,128]{1,0:T(8,128)(2,1)S(1)}, u32[]{:S(2)}, u32[]{:S(2)}) collective-permute-start(bf16[112,128]{1,0:T(8,128)(2,1)S(1)} %get-tuple-element.42), channel_id=1, source_target_pairs={{0,2},{1,5},{2,0},{3,7},{4,6},{5,1},{6,4},{7,3},{8,10},{9,13},{10,... | collective-permute-start | bytes 86024 | tf_op jit(solution)/shard_map/ppermute | solution.py:415
  20.2 2.4 %collective-permute-start.8 = (bf16[224,384]{1,0:T(8,128)(2,1)S(1)}, bf16[224,384]{1,0:T(8,128)(2,1)S(1)}, u32[]{:S(2)}, u32[]{:S(2)}) collective-permute-start(bf16[224,384]{1,0:T(8,128)(2,1)S(1)} %get-tuple-element.43), channel_id=1, source_target_pairs={{0,24},{8,0},{16,8},{24,16},{1,25},{9,1},{17,9},{25,17},{2,26},{10... | collective-permute-start | bytes 516104 | tf_op jit(solution)/shard_map/ppermute | solution.py:28
  22.7 0.0 collective-permute-done.4.refs_0_
  22.7 0.6 %collective-permute-done.5.refs_1_ = bf16[112,128]{1,0:T(8,128)(2,1)S(1)} collective-permute-done((bf16[112,128]{1,0:T(8,128)(2,1)S(1)}, bf16[112,128]{1,0:T(8,128)(2,1)S(1)}, u32[]{:S(2)}, u32[]{:S(2)}) %collective-permute-start.5) | collective-permute-done | bytes 28704 | tf_op jit(solution)/shard_map/ppermute | solution.py:415
  23.2 0.0 collective-permute-done.6.refs_2_
  23.3 2.5 %collective-permute-start.7 = (bf16[3,112,128]{2,1,0:T(8,128)(2,1)S(1)}, bf16[3,112,128]{2,1,0:T(8,128)(2,1)S(1)}, u32[]{:S(2)}, u32[]{:S(2)}) collective-permute-start(bf16[3,112,128]{2,1,0:T(8,128)(2,1)S(1)} %shard_map.125), channel_id=1, source_target_pairs={{0,24},{8,0},{16,8},{24,16},{1,25},{9,1},{17,9},{25,17},{2,26},{10... | collective-permute-start | bytes 258056 | tf_op jit(solution)/shard_map/ppermute | solution.py:28
  25.8 1.1 %shard_map.127 = (f32[2,48,96]{2,1,0:T(8,128)}, f32[2,48,96]{2,1,0:T(8,128)}, f32[2,48]{1,0:T(2,128)}) custom-call(bf16[288,256]{1,0:T(8,128)(2,1)S(1)} %get-tuple-element.45.points0, bf16[288,256]{1,0:T(8,128)(2,1)S(1)} %get-tuple-element.46.hidden0, bf16[288,256]{1,0:T(8,128)(2,1)S(1)} %get-tuple-element.47.points1, ...), custom_call_target="tpu_custom_call" | custom-call | flops 2000000000 | bytes 1000000 | tf_op jit(solution)/shard_map/pallas_call | solution.py:380
  26.9 1.0 %collective-permute-done.7.three = bf16[3,112,128]{2,1,0:T(8,128)(2,1)S(1)} collective-permute-done((bf16[3,112,128]{2,1,0:T(8,128)(2,1)S(1)}, bf16[3,112,128]{2,1,0:T(8,128)(2,1)S(1)}, u32[]{:S(2)}, u32[]{:S(2)}) %collective-permute-start.7) | collective-permute-done | bytes 86048 | tf_op jit(solution)/shard_map/ppermute | solution.py:28
  27.9 0.0 collective-permute-done.8.bundle
  27.9 1.1 %shard_map.126 = bf16[180,384]{1,0:T(8,128)(2,1)} custom-call(bf16[3,112,128]{2,1,0:T(8,128)(2,1)S(1)} %collective-permute-done.7.three, bf16[224,384]{1,0:T(8,128)(2,1)S(1)} %collective-permute-done.8.bundle, bf16[180,144]{1,0:T(8,128)(2,1)S(1)} %get-tuple-element.44.table), custom_call_target="tpu_custom_call" | custom-call | flops 100000000 | bytes 1000000 | tf_op jit(solution)/shard_map/pallas_call | solution.py:380
  (2 shorter events, 0.0 us)
Async XLA Ops:
  2.2 7.7 %collective-permute-start = (bf16[72,384]{1,0:T(8,128)(2,1)S(1)}, bf16[72,384]{1,0:T(8,128)(2,1)S(1)}, u32[]{:S(2)}, u32[]{:S(2)}) collective-permute-start(bf16[72,384]{1,0:T(8,128)(2,1)S(1)} %get-tuple-element.30), channel_id=1, source_target_pairs={{0,6},{1,7},{2,4},{3,5},{4,2},{5,3},{6,0},{7,1},{8,14},{9,15},{10,... | collective-permute-start | bytes 165896 | tf_op jit(solution)/shard_map/ppermute | solution.py:415
  7.3 5.4 %collective-permute-start.1 = (bf16[72,384]{1,0:T(8,128)(2,1)S(1)}, bf16[72,384]{1,0:T(8,128)(2,1)S(1)}, u32[]{:S(2)}, u32[]{:S(2)}) collective-permute-start(bf16[72,384]{1,0:T(8,128)(2,1)S(1)} %get-tuple-element.31), channel_id=1, source_target_pairs={{0,4},{1,3},{2,6},{3,1},{4,0},{5,7},{6,2},{7,5},{8,12},{9,11},{10,... | collective-permute-start | bytes 165896 | tf_op jit(solution)/shard_map/ppermute | solution.py:415
  7.4 5.4 %collective-permute-start.2 = (bf16[72,384]{1,0:T(8,128)(2,1)S(1)}, bf16[72,384]{1,0:T(8,128)(2,1)S(1)}, u32[]{:S(2)}, u32[]{:S(2)}) collective-permute-start(bf16[72,384]{1,0:T(8,128)(2,1)S(1)} %get-tuple-element.32), channel_id=1, source_target_pairs={{0,2},{1,5},{2,0},{3,7},{4,6},{5,1},{6,4},{7,3},{8,10},{9,13},{10,... | collective-permute-start | bytes 165896 | tf_op jit(solution)/shard_map/ppermute | solution.py:415
  12.8 1.5 %collective-permute-start.3 = (bf16[4,72,384]{2,1,0:T(8,128)(2,1)S(1)}, bf16[4,72,384]{2,1,0:T(8,128)(2,1)S(1)}, u32[]{:S(2)}, u32[]{:S(2)}) collective-permute-start(bf16[4,72,384]{2,1,0:T(8,128)(2,1)S(1)} %shard_map.122), channel_id=1, source_target_pairs={{0,1},{1,0},{2,3},{3,2},{4,5},{5,4},{6,7},{7,6},{8,9},{9,8},{10,11... | collective-permute-start | bytes 663560 | tf_op jit(solution)/shard_map/ppermute | solution.py:456
  15.8 6.9 %collective-permute-start.4 = (bf16[112,128]{1,0:T(8,128)(2,1)S(1)}, bf16[112,128]{1,0:T(8,128)(2,1)S(1)}, u32[]{:S(2)}, u32[]{:S(2)}) collective-permute-start(bf16[112,128]{1,0:T(8,128)(2,1)S(1)} %get-tuple-element.40), channel_id=1, source_target_pairs={{0,6},{1,7},{2,4},{3,5},{4,2},{5,3},{6,0},{7,1},{8,14},{9,15},{10,... | collective-permute-start | bytes 86024 | tf_op jit(solution)/shard_map/ppermute | solution.py:415
  18.2 5.1 %collective-permute-start.5 = (bf16[112,128]{1,0:T(8,128)(2,1)S(1)}, bf16[112,128]{1,0:T(8,128)(2,1)S(1)}, u32[]{:S(2)}, u32[]{:S(2)}) collective-permute-start(bf16[112,128]{1,0:T(8,128)(2,1)S(1)} %get-tuple-element.41), channel_id=1, source_target_pairs={{0,4},{1,3},{2,6},{3,1},{4,0},{5,7},{6,2},{7,5},{8,12},{9,11},{10,... | collective-permute-start | bytes 86024 | tf_op jit(solution)/shard_map/ppermute | solution.py:415
  18.2 5.1 %collective-permute-start.6 = (bf16[112,128]{1,0:T(8,128)(2,1)S(1)}, bf16[112,128]{1,0:T(8,128)(2,1)S(1)}, u32[]{:S(2)}, u32[]{:S(2)}) collective-permute-start(bf16[112,128]{1,0:T(8,128)(2,1)S(1)} %get-tuple-element.42), channel_id=1, source_target_pairs={{0,2},{1,5},{2,0},{3,7},{4,6},{5,1},{6,4},{7,3},{8,10},{9,13},{10,... | collective-permute-start | bytes 86024 | tf_op jit(solution)/shard_map/ppermute | solution.py:415
  20.2 7.7 %collective-permute-start.8 = (bf16[224,384]{1,0:T(8,128)(2,1)S(1)}, bf16[224,384]{1,0:T(8,128)(2,1)S(1)}, u32[]{:S(2)}, u32[]{:S(2)}) collective-permute-start(bf16[224,384]{1,0:T(8,128)(2,1)S(1)} %get-tuple-element.43), channel_id=1, source_target_pairs={{0,24},{8,0},{16,8},{24,16},{1,25},{9,1},{17,9},{25,17},{2,26},{10... | collective-permute-start | bytes 516104 | tf_op jit(solution)/shard_map/ppermute | solution.py:28
  23.3 4.6 %collective-permute-start.7 = (bf16[3,112,128]{2,1,0:T(8,128)(2,1)S(1)}, bf16[3,112,128]{2,1,0:T(8,128)(2,1)S(1)}, u32[]{:S(2)}, u32[]{:S(2)}) collective-permute-start(bf16[3,112,128]{2,1,0:T(8,128)(2,1)S(1)} %shard_map.125), channel_id=1, source_target_pairs={{0,24},{8,0},{16,8},{24,16},{1,25},{9,1},{17,9},{25,17},{2,26},{10... | collective-permute-start | bytes 258056 | tf_op jit(solution)/shard_map/ppermute | solution.py:28

commit v23 on v22

--- a/solution.py
+++ b/solution.py
@@ -219,7 +219,7 @@
 
 
 def swap_at(step, core):
-    return (0, 3, 2 - core, 1 + core)[step]
+    return (0, 3 - core, 2 + core, 1)[step]
 
 
 FIELD_ROWS = 184

time: 29.2 us -> 29.1 us (level)
  no operation moved by 1% of the time
where the time goes in v23:
time: 29.1 us; the launch traced here: 28.9 us
  starting transfers between devices  15.2 us (52%)
  Pallas kernels  7.15 us (25%)
  waiting for transfers between devices  5.84 us (20%)
  between operations  0.69 us (2%)
    ppermute x6, starting transfers between devices, swap(): return [lax.ppermute(chunk, 'lat', p) for chunk, p in zip(chunks, pairs)]  10.2 us
    pallas_call x8, Pallas kernels, call(): pl.pallas_call(kernel, out_shape=outs, in_specs=[VMEM] * len(near) + [HBM...  7.15 us
    ppermute x2, starting transfers between devices, turn(): lax.ppermute(value, axis, [(i, (i - 1) % length) for i in range(length)])  4.94 us
    ppermute x6, waiting for transfers between devices, swap(): return [lax.ppermute(chunk, 'lat', p) for chunk, p in zip(chunks, pairs)]  3.76 us
    ppermute x1, waiting for transfers between devices, paired_blocks(): other = lax.ppermute(own, 'lat', [(i, i ^ 1) for i in range(2 * NB)])  1.1 us
    ppermute x2, waiting for transfers between devices, turn(): lax.ppermute(value, axis, [(i, (i - 1) % length) for i in range(length)])  0.98 us
  transfers between devices with their start and end apart: 9, of which 5 were waited for; matrix products, arithmetic and copies ran while one was open for 0% of the time, Pallas kernels for 10%

profile of v23, /device:TPU:0, one launch (start us, length us, event | category | flops | bytes accessed | tf_op | source)
XLA Modules:
  0.0 28.9 jit_solution(10056113419827557585)
XLA Ops:
  0.6 1.6 %shard_map.120 = (bf16[72,384]{1,0:T(8,128)(2,1)S(1)}, bf16[72,384]{1,0:T(8,128)(2,1)S(1)}, bf16[72,384]{1,0:T(8,128)(2,1)S(1)}, bf16[72,384]{1,0:T(8,128)(2,1)S(1)}) custom-call(s32[8]{0:T(128)} %refs_0_.3, s32[8]{0:T(128)} %refs_1_.3, bf16[180,384]{1,0:T(8,128)(2,1)} %bitcast.16, bf16[144,180]{1,0:T(8,128)(2,1)} %constant.4.clone.refs_3_, ...), custom_call_target="tpu_custom_call" | custom-call | flops 100000000 | bytes 1000000 | tf_op jit(solution)/shard_map/pallas_call | solution.py:380
  2.2 5.1 %collective-permute-start = (bf16[72,384]{1,0:T(8,128)(2,1)S(1)}, bf16[72,384]{1,0:T(8,128)(2,1)S(1)}, u32[]{:S(2)}, u32[]{:S(2)}) collective-permute-start(bf16[72,384]{1,0:T(8,128)(2,1)S(1)} %get-tuple-element.30), channel_id=1, source_target_pairs={{0,6},{1,5},{2,4},{3,7},{4,2},{5,1},{6,0},{7,3},{8,14},{9,13},{10,... | collective-permute-start | bytes 165896 | tf_op jit(solution)/shard_map/ppermute | solution.py:415
  7.3 0.0 collective-permute-start.1
  7.4 0.6 %collective-permute-start.2 = (bf16[72,384]{1,0:T(8,128)(2,1)S(1)}, bf16[72,384]{1,0:T(8,128)(2,1)S(1)}, u32[]{:S(2)}, u32[]{:S(2)}) collective-permute-start(bf16[72,384]{1,0:T(8,128)(2,1)S(1)} %get-tuple-element.32), channel_id=1, source_target_pairs={{0,2},{1,3},{2,0},{3,1},{4,6},{5,7},{6,4},{7,5},{8,10},{9,11},{10,... | collective-permute-start | bytes 165896 | tf_op jit(solution)/shard_map/ppermute | solution.py:415
  8.0 1.5 %shard_map.121 = (bf16[256,256]{1,0:T(8,128)(2,1)S(1)}, bf16[256,256]{1,0:T(8,128)(2,1)S(1)}, bf16[256,256]{1,0:T(8,128)(2,1)S(1)}, f32[1,256]{1,0:T(1,128)S(1)}...) custom-call(s32[8]{0:T(128)} %refs_0_.3, s32[8]{0:T(128)} %refs_1_.3, ...), custom_call_target="tpu_custom_call" | custom-call | flops 2000000000 | bytes 1000000 | tf_op jit(solution)/shard_map/pallas_call | solution.py:380
  9.5 0.1 collective-permute-done.refs_1_
  9.5 2.9 %collective-permute-done.1.refs_2_ = bf16[72,384]{1,0:T(8,128)(2,1)S(1)} collective-permute-done((bf16[72,384]{1,0:T(8,128)(2,1)S(1)}, bf16[72,384]{1,0:T(8,128)(2,1)S(1)}, u32[]{:S(2)}, u32[]{:S(2)}) %collective-permute-start.1) | collective-permute-done | bytes 55328 | tf_op jit(solution)/shard_map/ppermute | solution.py:415
  12.5 0.0 collective-permute-done.2.refs_3_
  12.5 0.1 collective-permute-start.3
  12.6 0.4 %shard_map.123 = (bf16[288,256]{1,0:T(8,128)(2,1)S(1)}, bf16[288,256]{1,0:T(8,128)(2,1)S(1)}, f32[288,256]{1,0:T(8,128)S(1)}) custom-call(bf16[72,384]{1,0:T(8,128)(2,1)S(1)} %get-tuple-element.29.refs_0_, bf16[72,384]{1,0:T(8,128)(2,1)S(1)} %collective-permute-done.refs_1_, bf16[72,384]{1,0:T(8,128)(2,1)S(1)} %collective-permute-done.1.refs_2_, ...), custom_call_target="tpu_custom_call" | custom-call | flops 2000000000 | bytes 1000000 | tf_op jit(solution)/shard_map/pallas_call | solution.py:380
  12.9 1.1 %collective-permute-done.3.refs_4_ = bf16[4,72,384]{2,1,0:T(8,128)(2,1)S(1)} collective-permute-done((bf16[4,72,384]{2,1,0:T(8,128)(2,1)S(1)}, bf16[4,72,384]{2,1,0:T(8,128)(2,1)S(1)}, u32[]{:S(2)}, u32[]{:S(2)}) %collective-permute-start.3) | collective-permute-done | bytes 221216 | tf_op jit(solution)/shard_map/ppermute | solution.py:456
  14.0 1.5 %shard_map.124 = (bf16[112,128]{1,0:T(8,128)(2,1)S(1)}, bf16[112,128]{1,0:T(8,128)(2,1)S(1)}, bf16[112,128]{1,0:T(8,128)(2,1)S(1)}, bf16[224,384]{1,0:T(8,128)(2...) custom-call(bf16[72,384]{1,0:T(8,128)(2,1)S(1)} %get-tuple-element.2, ...), custom_call_target="tpu_custom_call" | custom-call | flops 100000000 | bytes 1000000 | tf_op jit(solution)/shard_map/pallas_call | solution.py:380
  15.5 2.9 %collective-permute-start.4 = (bf16[112,128]{1,0:T(8,128)(2,1)S(1)}, bf16[112,128]{1,0:T(8,128)(2,1)S(1)}, u32[]{:S(2)}, u32[]{:S(2)}) collective-permute-start(bf16[112,128]{1,0:T(8,128)(2,1)S(1)} %get-tuple-element.40), channel_id=1, source_target_pairs={{0,6},{1,5},{2,4},{3,7},{4,2},{5,1},{6,0},{7,3},{8,14},{9,13},{10,... | collective-permute-start | bytes 86024 | tf_op jit(solution)/shard_map/ppermute | solution.py:415
  18.4 0.0 collective-permute-start.5
  18.4 1.5 %collective-permute-start.6 = (bf16[112,128]{1,0:T(8,128)(2,1)S(1)}, bf16[112,128]{1,0:T(8,128)(2,1)S(1)}, u32[]{:S(2)}, u32[]{:S(2)}) collective-permute-start(bf16[112,128]{1,0:T(8,128)(2,1)S(1)} %get-tuple-element.42), channel_id=1, source_target_pairs={{0,2},{1,3},{2,0},{3,1},{4,6},{5,7},{6,4},{7,5},{8,10},{9,11},{10,... | collective-permute-start | bytes 86024 | tf_op jit(solution)/shard_map/ppermute | solution.py:415
  19.9 2.4 %collective-permute-start.8 = (bf16[224,384]{1,0:T(8,128)(2,1)S(1)}, bf16[224,384]{1,0:T(8,128)(2,1)S(1)}, u32[]{:S(2)}, u32[]{:S(2)}) collective-permute-start(bf16[224,384]{1,0:T(8,128)(2,1)S(1)} %get-tuple-element.43), channel_id=1, source_target_pairs={{0,24},{8,0},{16,8},{24,16},{1,25},{9,1},{17,9},{25,17},{2,26},{10... | collective-permute-start | bytes 516104 | tf_op jit(solution)/shard_map/ppermute | solution.py:28
  22.4 0.0 collective-permute-done.4.refs_0_
  22.4 0.8 %collective-permute-done.5.refs_1_ = bf16[112,128]{1,0:T(8,128)(2,1)S(1)} collective-permute-done((bf16[112,128]{1,0:T(8,128)(2,1)S(1)}, bf16[112,128]{1,0:T(8,128)(2,1)S(1)}, u32[]{:S(2)}, u32[]{:S(2)}) %collective-permute-start.5) | collective-permute-done | bytes 28704 | tf_op jit(solution)/shard_map/ppermute | solution.py:415
  23.2 0.0 collective-permute-done.6.refs_2_
  23.2 2.5 %collective-permute-start.7 = (bf16[3,112,128]{2,1,0:T(8,128)(2,1)S(1)}, bf16[3,112,128]{2,1,0:T(8,128)(2,1)S(1)}, u32[]{:S(2)}, u32[]{:S(2)}) collective-permute-start(bf16[3,112,128]{2,1,0:T(8,128)(2,1)S(1)} %shard_map.125), channel_id=1, source_target_pairs={{0,24},{8,0},{16,8},{24,16},{1,25},{9,1},{17,9},{25,17},{2,26},{10... | collective-permute-start | bytes 258056 | tf_op jit(solution)/shard_map/ppermute | solution.py:28
  25.7 1.1 %shard_map.127 = (f32[2,48,96]{2,1,0:T(8,128)}, f32[2,48,96]{2,1,0:T(8,128)}, f32[2,48]{1,0:T(2,128)}) custom-call(bf16[288,256]{1,0:T(8,128)(2,1)S(1)} %get-tuple-element.45.points0, bf16[288,256]{1,0:T(8,128)(2,1)S(1)} %get-tuple-element.46.hidden0, bf16[288,256]{1,0:T(8,128)(2,1)S(1)} %get-tuple-element.47.points1, ...), custom_call_target="tpu_custom_call" | custom-call | flops 2000000000 | bytes 1000000 | tf_op jit(solution)/shard_map/pallas_call | solution.py:380
  26.8 1.0 %collective-permute-done.7.three = bf16[3,112,128]{2,1,0:T(8,128)(2,1)S(1)} collective-permute-done((bf16[3,112,128]{2,1,0:T(8,128)(2,1)S(1)}, bf16[3,112,128]{2,1,0:T(8,128)(2,1)S(1)}, u32[]{:S(2)}, u32[]{:S(2)}) %collective-permute-start.7) | collective-permute-done | bytes 86048 | tf_op jit(solution)/shard_map/ppermute | solution.py:28
  27.8 0.0 collective-permute-done.8.bundle
  27.8 1.1 %shard_map.126 = bf16[180,384]{1,0:T(8,128)(2,1)} custom-call(bf16[3,112,128]{2,1,0:T(8,128)(2,1)S(1)} %collective-permute-done.7.three, bf16[224,384]{1,0:T(8,128)(2,1)S(1)} %collective-permute-done.8.bundle, bf16[180,144]{1,0:T(8,128)(2,1)S(1)} %get-tuple-element.44.table), custom_call_target="tpu_custom_call" | custom-call | flops 100000000 | bytes 1000000 | tf_op jit(solution)/shard_map/pallas_call | solution.py:380
  (2 shorter events, 0.0 us)
Async XLA Ops:
  2.2 7.3 %collective-permute-start = (bf16[72,384]{1,0:T(8,128)(2,1)S(1)}, bf16[72,384]{1,0:T(8,128)(2,1)S(1)}, u32[]{:S(2)}, u32[]{:S(2)}) collective-permute-start(bf16[72,384]{1,0:T(8,128)(2,1)S(1)} %get-tuple-element.30), channel_id=1, source_target_pairs={{0,6},{1,5},{2,4},{3,7},{4,2},{5,1},{6,0},{7,3},{8,14},{9,13},{10,... | collective-permute-start | bytes 165896 | tf_op jit(solution)/shard_map/ppermute | solution.py:415
  7.3 5.1 %collective-permute-start.1 = (bf16[72,384]{1,0:T(8,128)(2,1)S(1)}, bf16[72,384]{1,0:T(8,128)(2,1)S(1)}, u32[]{:S(2)}, u32[]{:S(2)}) collective-permute-start(bf16[72,384]{1,0:T(8,128)(2,1)S(1)} %get-tuple-element.31), channel_id=1, source_target_pairs={{0,4},{1,7},{2,6},{3,5},{4,0},{5,3},{6,2},{7,1},{8,12},{9,15},{10,... | collective-permute-start | bytes 165896 | tf_op jit(solution)/shard_map/ppermute | solution.py:415
  7.4 5.1 %collective-permute-start.2 = (bf16[72,384]{1,0:T(8,128)(2,1)S(1)}, bf16[72,384]{1,0:T(8,128)(2,1)S(1)}, u32[]{:S(2)}, u32[]{:S(2)}) collective-permute-start(bf16[72,384]{1,0:T(8,128)(2,1)S(1)} %get-tuple-element.32), channel_id=1, source_target_pairs={{0,2},{1,3},{2,0},{3,1},{4,6},{5,7},{6,4},{7,5},{8,10},{9,11},{10,... | collective-permute-start | bytes 165896 | tf_op jit(solution)/shard_map/ppermute | solution.py:415
  12.5 1.5 %collective-permute-start.3 = (bf16[4,72,384]{2,1,0:T(8,128)(2,1)S(1)}, bf16[4,72,384]{2,1,0:T(8,128)(2,1)S(1)}, u32[]{:S(2)}, u32[]{:S(2)}) collective-permute-start(bf16[4,72,384]{2,1,0:T(8,128)(2,1)S(1)} %shard_map.122), channel_id=1, source_target_pairs={{0,1},{1,0},{2,3},{3,2},{4,5},{5,4},{6,7},{7,6},{8,9},{9,8},{10,11... | collective-permute-start | bytes 663560 | tf_op jit(solution)/shard_map/ppermute | solution.py:456
  15.5 6.9 %collective-permute-start.4 = (bf16[112,128]{1,0:T(8,128)(2,1)S(1)}, bf16[112,128]{1,0:T(8,128)(2,1)S(1)}, u32[]{:S(2)}, u32[]{:S(2)}) collective-permute-start(bf16[112,128]{1,0:T(8,128)(2,1)S(1)} %get-tuple-element.40), channel_id=1, source_target_pairs={{0,6},{1,5},{2,4},{3,7},{4,2},{5,1},{6,0},{7,3},{8,14},{9,13},{10,... | collective-permute-start | bytes 86024 | tf_op jit(solution)/shard_map/ppermute | solution.py:415
  18.4 4.8 %collective-permute-start.5 = (bf16[112,128]{1,0:T(8,128)(2,1)S(1)}, bf16[112,128]{1,0:T(8,128)(2,1)S(1)}, u32[]{:S(2)}, u32[]{:S(2)}) collective-permute-start(bf16[112,128]{1,0:T(8,128)(2,1)S(1)} %get-tuple-element.41), channel_id=1, source_target_pairs={{0,4},{1,7},{2,6},{3,5},{4,0},{5,3},{6,2},{7,1},{8,12},{9,15},{10,... | collective-permute-start | bytes 86024 | tf_op jit(solution)/shard_map/ppermute | solution.py:415
  18.4 4.8 %collective-permute-start.6 = (bf16[112,128]{1,0:T(8,128)(2,1)S(1)}, bf16[112,128]{1,0:T(8,128)(2,1)S(1)}, u32[]{:S(2)}, u32[]{:S(2)}) collective-permute-start(bf16[112,128]{1,0:T(8,128)(2,1)S(1)} %get-tuple-element.42), channel_id=1, source_target_pairs={{0,2},{1,3},{2,0},{3,1},{4,6},{5,7},{6,4},{7,5},{8,10},{9,11},{10,... | collective-permute-start | bytes 86024 | tf_op jit(solution)/shard_map/ppermute | solution.py:415
  19.9 7.8 %collective-permute-start.8 = (bf16[224,384]{1,0:T(8,128)(2,1)S(1)}, bf16[224,384]{1,0:T(8,128)(2,1)S(1)}, u32[]{:S(2)}, u32[]{:S(2)}) collective-permute-start(bf16[224,384]{1,0:T(8,128)(2,1)S(1)} %get-tuple-element.43), channel_id=1, source_target_pairs={{0,24},{8,0},{16,8},{24,16},{1,25},{9,1},{17,9},{25,17},{2,26},{10... | collective-permute-start | bytes 516104 | tf_op jit(solution)/shard_map/ppermute | solution.py:28
  23.2 4.6 %collective-permute-start.7 = (bf16[3,112,128]{2,1,0:T(8,128)(2,1)S(1)}, bf16[3,112,128]{2,1,0:T(8,128)(2,1)S(1)}, u32[]{:S(2)}, u32[]{:S(2)}) collective-permute-start(bf16[3,112,128]{2,1,0:T(8,128)(2,1)S(1)} %shard_map.125), channel_id=1, source_target_pairs={{0,24},{8,0},{16,8},{24,16},{1,25},{9,1},{17,9},{25,17},{2,26},{10... | collective-permute-start | bytes 258056 | tf_op jit(solution)/shard_map/ppermute | solution.py:28

commit v24 on v21

--- a/solution.py
+++ b/solution.py
@@ -26,6 +26,15 @@
 def turn(value, axis):
     length = lax.axis_size(axis)
     return lax.ppermute(value, axis, [(i, (i - 1) % length) for i in range(length)])
+
+
+def halves_of_turn(value, axis):
+    length = lax.axis_size(axis)
+    if length % 2:
+        return [turn(value, axis)] * 2
+    to_even = [(i, i ^ 1) for i in range(length)]
+    to_odd = [(i, i - 1) for i in range(2, length)] + [(0, 0), (1, length - 1)]
+    return [lax.ppermute(value, axis, pairs) for pairs in (to_even, to_odd)]
 
 
 def lon_tables(n_modes, length):
@@ -175,10 +184,10 @@
 
 
 def ready_kernel(q, *refs):
-    hbm, (mat1, turned1, turned2, bias, own_field, own_table, latitudes) = refs[:7], refs[7:14]
-    counts, assign, w1, w2, b1, table, sems = refs[14:]
-    copies = fetch(sems, hbm, (counts, assign, w1, w2, b1, table, own_field))
-    wait(copies[:6])
+    hbm, (mat1, turned1, turned2, bias, own_table, latitudes) = refs[:6], refs[6:12]
+    counts, assign, w1, w2, b1, table, sems = refs[12:]
+    copies = fetch(sems, hbm, (counts, assign, w1, w2, b1, table))
+    wait(copies)
     lane = lax.broadcasted_iota(jnp.int32, latitudes.shape, 1)
     line = jnp.zeros(latitudes.shape, jnp.int32)
     for r in range(2 * NB):
@@ -214,11 +223,9 @@
             mat[...] = whole.astype(BF16)
     shift_b = pick(b1[...].astype(F32))
     bias[...] = jnp.concatenate([shift_b[0:1], shift_b[1:2]], axis=1)
-    wait(copies[6:])
 
 
 ORDER = (0, 3, 2, 1)
-FIELD_ROWS = 184
 
 
 def join_kernel(*refs):
@@ -260,15 +267,15 @@
 
 
 def own_kernel(*refs):
-    mat1, bias, points, hidden, slope, by_pair = refs[NB:]
+    mat1, bias, _, points, hidden, slope, by_pair = refs[NB:]
     chunks = [refs[i][...].astype(F32) for i in ORDER]
     silu_points(chunks, mat1, bias, by_pair, points, hidden, slope)
 
 
 def filter_kernel(*refs):
-    owns, (other, slope_own, mat1, turned1, turned2, bias, own_field) = refs[:4], refs[4:11]
-    latitudes, outs, (bundle, points, hidden, grad_pre, grad_y) = refs[11], refs[12:15], refs[15:20]
-    assign, by_lat, by_pair, slope, real, imag, sems = refs[20:]
+    owns, (other, slope_own, mat1, turned1, turned2, bias, latitudes) = refs[:4], refs[4:11]
+    outs, (points, hidden, grad_pre, grad_y) = refs[11:15], refs[15:19]
+    assign, by_lat, by_pair, slope, real, imag, sems = refs[19:]
     copies = fetch(sems, (latitudes,), (assign,))
     core = lax.rem(lax.axis_index("lat"), 2)
     sides = [[owns[i][...].astype(F32) for i in ORDER], [other[i].astype(F32) for i in ORDER]]
@@ -310,17 +317,8 @@
     inner = [tuple(ref[pl.ds(k, rows, stride=step), :] for ref in (real, imag)) for k in range(n_rows)]
     for r, band in enumerate(eight_points(inner, 1)):
         by_lat[r] = jnp.concatenate(band, axis=1)
-    for i, d in enumerate(ORDER):
-        band = pack(by_lat[assign[0, 2 * partner(d) + core]])
-        if d:
-            outs[i - 1][...] = band.astype(BF16)
-        else:
-            tail = bundle.shape[0] - FIELD_ROWS
-            band = jnp.concatenate([band, jnp.zeros((3 * tail - band.shape[0], LANES), F32)], axis=0)
-            band = jnp.concatenate([band[j * tail : (j + 1) * tail] for j in range(3)], axis=1)
-            lines = own_field[...].astype(F32)
-            gap = jnp.zeros((FIELD_ROWS - lines.shape[0], lines.shape[1]), F32)
-            bundle[...] = jnp.concatenate([lines, gap, band], axis=0).astype(BF16)
+    for out, d in zip(outs, ORDER):
+        out[...] = pack(by_lat[assign[0, 2 * partner(d) + core]]).astype(BF16)
 
 
 def products_kernel(points0, hidden0, points1, hidden1, grad_pre, grad_y, gw1, gw2, gb1):
@@ -338,12 +336,9 @@
         gb1[c : c + 1] = jnp.where(core == 0, line[:, :half], line[:, half:BS])
 
 
-def compose_kernel(last, three, bundle, table, out, by_block, result, sems):
+def compose_kernel(last, three, one, even, odd, table, out, by_block, result, sems):
     rows = by_block.shape[1]
-    lines = bundle[...].astype(F32)
-    own = lines[FIELD_ROWS:]
-    own = jnp.concatenate([own[:, i * LANES : (i + 1) * LANES] for i in range(3)], axis=0)
-    chunks = [own[: three.shape[1]]] + [three[i].astype(F32) for i in range(3)]
+    chunks = [one[...].astype(F32)] + [three[i].astype(F32) for i in range(3)]
     for d, chunk in zip(ORDER, chunks):
         by_block[partner(d)] = jnp.concatenate(unpack(chunk, rows), axis=1)
     parts = [
@@ -354,8 +349,8 @@
     copies = []
     for i, (_, tile) in enumerate(columns(out.shape[1])):
         mixed = jnp.dot(table[...], parts[:, i * LANES : (i + 1) * LANES], preferred_element_type=F32)
-        field = lines[: out.shape[0], i * LANES : (i + 1) * LANES]
-        whole = field + mixed.astype(BF16).astype(F32)
+        field = jnp.where(lax.axis_index("section") % 2 == 1, odd[:, tile], even[:, tile])
+        whole = field.astype(F32) + mixed.astype(BF16).astype(F32)
         result[:, tile] = jnp.where(none, 0.0, whole).astype(BF16)
         copies.append(pltpu.make_async_copy(result.at[:, tile], out.at[:, tile], sems.at[i]))
         copies[-1].start()
@@ -366,7 +361,7 @@
 HBM = pl.BlockSpec(memory_space=pltpu.HBM)
 
 
-def call(kernel, outs, scratch, near, far, flops=10**8, out_specs=None):
+def call(kernel, outs, scratch, near, far, flops=10**5, out_specs=None):
     out_specs = out_specs or (tuple([VMEM] * len(outs)) if isinstance(outs, tuple) else VMEM)
     many = isinstance(outs, tuple)
     return pl.pallas_call(
@@ -375,7 +370,7 @@
         in_specs=[VMEM] * len(near) + [HBM] * len(far),
         out_specs=out_specs,
         scratch_shapes=scratch,
-        cost_estimate=pl.CostEstimate(flops=flops, bytes_accessed=10**6, transcendentals=0),
+        cost_estimate=pl.CostEstimate(flops=flops, bytes_accessed=10**3, transcendentals=0),
         compiler_params=pltpu.CompilerParams(vmem_limit_bytes=32 * 2**20),
     )(*near, *(pltpu.with_memory_space_constraint(x, pltpu.HBM) for x in far))
 
@@ -417,19 +412,18 @@
         (),
         far,
     )
+    even_field, odd_field = halves_of_turn(field, "section")
     received = [sent[0], *swap([sent[d] for d in ORDER[1:]])]
     far = (mode_counts, assignment, w1[0], w2[0], b1[0], forward)
     scratch, _ = scratch_for(*far)
-    far = (*far, field)
     wide = 2 * LANES
-    mat1, turned1, turned2, bias, field, forward, latitudes = call(
+    mat1, turned1, turned2, bias, forward, latitudes = call(
         functools.partial(ready_kernel, q),
         (
             shape((wide, wide), BF16),
             shape((wide, wide), BF16),
             shape((wide, wide), BF16),
             shape((1, wide), F32),
-            shape(field.shape, BF16),
             shape(forward.shape, BF16),
             shape((1, LANES), jnp.int32),
         ),
@@ -453,18 +447,15 @@
         own_kernel,
         (vectors, vectors, slopes),
         [by_pair],
-        (*received, mat1, bias),
+        (*received, mat1, bias, own),
         (),
-        2 * 10**9,
     )
     packed = shape((rows + rows // 2 + 4, LANES), BF16)
     scratch, sems = scratch_for(latitudes)
     both = shape((2, NB * rows, wide), BF16)
-    tail = -(-packed.shape[0] // 24) * 8
-    bundle = shape((FIELD_ROWS + tail, width), BF16)
-    *chunks, bundle, points1, hidden1, grad_pre, grad_y = call(
+    own_chunk, *chunks, points1, hidden1, grad_pre, grad_y = call(
         filter_kernel,
-        (packed,) * (NB - 1) + (bundle, vectors, vectors, both, both),
+        (packed,) * NB + (vectors, vectors, both, both),
         scratch
         + [
             pltpu.VMEM((n_rows, rows, wide), F32),
@@ -474,7 +465,7 @@
             pltpu.VMEM(((n_rows + 1) * rows, LANES), F32),
             sems,
         ],
-        (*received, other, slope0, mat1, turned1, turned2, bias, field, latitudes),
+        (*received, other, slope0, mat1, turned1, turned2, bias, latitudes),
         (),
     )
     backs = swap(chunks)
@@ -487,9 +478,9 @@
         (),
         2 * 10**9,
     )
-    three = call(join_kernel, shape((NB - 1, *packed.shape), BF16), [], backs, ())
+    three = call(join_kernel, shape((NB - 1, *packed.shape), BF16), [], (*backs, even_field), ())
     three = turn(three, "section")
-    bundle = turn(bundle, "section")
+    one = turn(own_chunk, "section")
     shifted = call(
         functools.partial(compose_kernel, lax.axis_size("section") - 1),
         shape((length, width), BF16),
@@ -498,7 +489,7 @@
             pltpu.VMEM((length, width), BF16),
             pltpu.SemaphoreType.DMA((width // LANES,)),
         ],
-        (three, bundle, forward),
+        (three, one, even_field, odd_field, forward),
         (),
         out_specs=HBM,
     )

time: 28.7 us -> 32 us (1.11)
  starting transfers between devices: 15.2 us -> 17.2 us
  local copies, waits for them, and re-layouts: 0 us -> 0.8 us
  waiting for transfers between devices: 5.44 us -> 5.83 us
    ppermute x0 -> x2, starting transfers between devices: none -> 2.15 us  [halves_of_turn(): return [lax.ppermute(value, axis, pairs) for pairs in (to_even, to_odd)]]
    ppermute x2, waiting for transfers between devices: 0.98 us -> 2.88 us  [turn(): lax.ppermute(value, axis, [(i, (i - 1) % length) for i in range(length)])]
    ppermute x1, waiting for transfers between devices: 1.1 us -> 0.01 us  [paired_blocks(): other = lax.ppermute(own, 'lat', [(i, i ^ 1) for i in range(2 * NB)])]
    unnamed x0 -> x2, local copies, waits for them, and re-layouts: none -> 0.8 us
    ppermute x6, waiting for transfers between devices: 3.36 us -> 2.95 us  [swap(): return [lax.ppermute(chunk, 'lat', p) for chunk, p in zip(chunks, pairs)]]
  transfers between devices with their start and end apart: 9 -> 11, of which waited for: 5 -> 3; matrix products, arithmetic and copies ran while one was open for 0% -> 0% of each run, Pallas kernels for 10% -> 14%
where the time goes in v24:
time: 32 us; the launch traced here: 31.7 us
  starting transfers between devices  17.2 us (54%)
  Pallas kernels  7.15 us (22%)
  waiting for transfers between devices  5.83 us (18%)
  local copies, waits for them, and re-layouts  0.8 us (2%)
  between operations  0.72 us (2%)
    ppermute x6, starting transfers between devices, swap(): return [lax.ppermute(chunk, 'lat', p) for chunk, p in zip(chunks, pairs)]  10.2 us
    pallas_call x8, Pallas kernels, call(): pl.pallas_call(kernel, out_shape=outs, in_specs=[VMEM] * len(near) + [HBM...  7.15 us
    ppermute x2, starting transfers between devices, turn(): lax.ppermute(value, axis, [(i, (i - 1) % length) for i in range(length)])  4.8 us
    ppermute x6, waiting for transfers between devices, swap(): return [lax.ppermute(chunk, 'lat', p) for chunk, p in zip(chunks, pairs)]  2.95 us
    ppermute x2, waiting for transfers between devices, turn(): lax.ppermute(value, axis, [(i, (i - 1) % length) for i in range(length)])  2.88 us
    ppermute x2, starting transfers between devices, halves_of_turn(): return [lax.ppermute(value, axis, pairs) for pairs in (to_even, to_odd)]  2.15 us
    unnamed x2, local copies, waits for them, and re-layouts  0.8 us
  transfers between devices with their start and end apart: 11, of which 3 were waited for; matrix products, arithmetic and copies ran while one was open for 0% of the time, Pallas kernels for 14%

profile of v24, /device:TPU:0, one launch (start us, length us, event | category | flops | bytes accessed | tf_op | source)
XLA Modules:
  0.0 31.7 jit_solution(15563088186004079554)
XLA Ops:
  0.6 1.6 %shard_map.120 = (bf16[72,384]{1,0:T(8,128)(2,1)S(1)}, bf16[72,384]{1,0:T(8,128)(2,1)S(1)}, bf16[72,384]{1,0:T(8,128)(2,1)S(1)}, bf16[72,384]{1,0:T(8,128)(2,1)S(1)}) custom-call(s32[8]{0:T(128)} %refs_0_.3, s32[8]{0:T(128)} %refs_1_.3, bf16[180,384]{1,0:T(8,128)(2,1)} %bitcast.14, bf16[144,180]{1,0:T(8,128)(2,1)} %constant.4.clone.refs_3_, ...), custom_call_target="tpu_custom_call" | custom-call | flops 100000 | bytes 1000 | tf_op jit(solution)/shard_map/pallas_call | solution.py:367
  2.2 5.1 %collective-permute-start = (bf16[72,384]{1,0:T(8,128)(2,1)S(1)}, bf16[72,384]{1,0:T(8,128)(2,1)S(1)}, u32[]{:S(2)}, u32[]{:S(2)}) collective-permute-start(bf16[72,384]{1,0:T(8,128)(2,1)S(1)} %get-tuple-element.29), channel_id=1, source_target_pairs={{0,6},{1,7},{2,4},{3,5},{4,2},{5,3},{6,0},{7,1},{8,14},{9,15},{10,... | collective-permute-start | bytes 165896 | tf_op jit(solution)/shard_map/ppermute | solution.py:402
  7.4 0.6 %collective-permute-start.2 = (bf16[72,384]{1,0:T(8,128)(2,1)S(1)}, bf16[72,384]{1,0:T(8,128)(2,1)S(1)}, u32[]{:S(2)}, u32[]{:S(2)}) collective-permute-start(bf16[72,384]{1,0:T(8,128)(2,1)S(1)} %get-tuple-element.31), channel_id=1, source_target_pairs={{0,2},{1,3},{2,0},{3,1},{4,6},{5,7},{6,4},{7,5},{8,10},{9,11},{10,... | collective-permute-start | bytes 165896 | tf_op jit(solution)/shard_map/ppermute | solution.py:402
  8.0 1.5 %shard_map.121 = (bf16[256,256]{1,0:T(8,128)(2,1)S(1)}, bf16[256,256]{1,0:T(8,128)(2,1)S(1)}, bf16[256,256]{1,0:T(8,128)(2,1)S(1)}, f32[1,256]{1,0:T(1,128)S(1)}...) custom-call(s32[8]{0:T(128)} %refs_0_.3, s32[8]{0:T(128)} %refs_1_.3, bf16[2,96,384]{2,1,0:T(8,128)(2,1)} %bitcast.18, ...), custom_call_target="tpu_custom_call" | custom-call | flops 2000000000 | bytes 1000 | tf_op jit(solution)/shard_map/pallas_call | solution.py:367
  9.5 0.2 collective-permute-done.refs_1_
  9.7 2.7 %collective-permute-done.1.refs_2_ = bf16[72,384]{1,0:T(8,128)(2,1)S(1)} collective-permute-done((bf16[72,384]{1,0:T(8,128)(2,1)S(1)}, bf16[72,384]{1,0:T(8,128)(2,1)S(1)}, u32[]{:S(2)}, u32[]{:S(2)}) %collective-permute-start.1) | collective-permute-done | bytes 55328 | tf_op jit(solution)/shard_map/ppermute | solution.py:402
  12.4 0.0 collective-permute-done.2.refs_3_
  12.4 0.1 collective-permute-start.3
  12.5 0.8 %copy-done = bf16[1,1,180,384]{3,2,1,0:T(8,128)(2,1)S(1)} copy-done((bf16[1,1,180,384]{3,2,1,0:T(8,128)(2,1)S(1)}, bf16[1,1,180,384]{3,2,1,0:T(8,128)(2,1)}, u32[]{:S(2)}) %copy-start) | copy-done | bytes 138264
  13.3 1.5 %collective-permute-start.7 = (bf16[180,384]{1,0:T(8,128)(2,1)S(1)}, bf16[180,384]{1,0:T(8,128)(2,1)S(1)}, u32[]{:S(2)}, u32[]{:S(2)}) collective-permute-start(bf16[180,384]{1,0:T(8,128)(2,1)S(1)} %bitcast.15), channel_id=1, source_target_pairs={{0,8},{8,0},{16,24},{24,16},{1,9},{9,1},{17,25},{25,17},{2,10},{10... | collective-permute-start | bytes 414728 | tf_op jit(solution)/shard_map/ppermute | solution.py:37
  14.8 0.4 %shard_map.123 = (bf16[288,256]{1,0:T(8,128)(2,1)S(1)}, bf16[288,256]{1,0:T(8,128)(2,1)S(1)}, f32[288,256]{1,0:T(8,128)S(1)}) custom-call(bf16[72,384]{1,0:T(8,128)(2,1)S(1)} %get-tuple-element.28.refs_0_, bf16[72,384]{1,0:T(8,128)(2,1)S(1)} %collective-permute-done.refs_1_, bf16[72,384]{1,0:T(8,128)(2,1)S(1)} %collective-permute-done.1.refs_2_, ...), custom_call_target="tpu_custom_call" | custom-call | flops 100000 | bytes 1000 | tf_op jit(solution)/shard_map/pallas_call | solution.py:367
  15.2 0.0 collective-permute-done.3.refs_4_
  15.2 1.5 %shard_map.124 = (bf16[112,128]{1,0:T(8,128)(2,1)S(1)}, bf16[112,128]{1,0:T(8,128)(2,1)S(1)}, bf16[112,128]{1,0:T(8,128)(2,1)S(1)}, bf16[112,128]{1,0:T(8,128)(2...) custom-call(bf16[72,384]{1,0:T(8,128)(2,1)S(1)} %get-tuple-element.2, ...), custom_call_target="tpu_custom_call" | custom-call | flops 100000 | bytes 1000 | tf_op jit(solution)/shard_map/pallas_call | solution.py:367
  16.7 2.6 %collective-permute-start.4 = (bf16[112,128]{1,0:T(8,128)(2,1)S(1)}, bf16[112,128]{1,0:T(8,128)(2,1)S(1)}, u32[]{:S(2)}, u32[]{:S(2)}) collective-permute-start(bf16[112,128]{1,0:T(8,128)(2,1)S(1)} %get-tuple-element.38), channel_id=1, source_target_pairs={{0,6},{1,7},{2,4},{3,5},{4,2},{5,3},{6,0},{7,1},{8,14},{9,15},{10,... | collective-permute-start | bytes 86024 | tf_op jit(solution)/shard_map/ppermute | solution.py:402
  19.2 1.9 %collective-permute-start.6 = (bf16[112,128]{1,0:T(8,128)(2,1)S(1)}, bf16[112,128]{1,0:T(8,128)(2,1)S(1)}, u32[]{:S(2)}, u32[]{:S(2)}) collective-permute-start(bf16[112,128]{1,0:T(8,128)(2,1)S(1)} %get-tuple-element.40), channel_id=1, source_target_pairs={{0,2},{1,3},{2,0},{3,1},{4,6},{5,7},{6,4},{7,5},{8,10},{9,11},{10,... | collective-permute-start | bytes 86024 | tf_op jit(solution)/shard_map/ppermute | solution.py:402
  21.1 0.7 %collective-permute-start.10 = (bf16[180,384]{1,0:T(8,128)(2,1)S(1)}, bf16[180,384]{1,0:T(8,128)(2,1)S(1)}, u32[]{:S(2)}, u32[]{:S(2)}) collective-permute-start(bf16[180,384]{1,0:T(8,128)(2,1)S(1)} %bitcast.16), channel_id=1, source_target_pairs={{16,8},{24,16},{0,0},{8,24},{17,9},{25,17},{1,1},{9,25},{18,10},{2... | collective-permute-start | bytes 414728 | tf_op jit(solution)/shard_map/ppermute | solution.py:37
  21.8 0.0 collective-permute-done.7.refs_3_.even
  21.8 4.3 %collective-permute-start.9 = (bf16[112,128]{1,0:T(8,128)(2,1)S(1)}, bf16[112,128]{1,0:T(8,128)(2,1)S(1)}, u32[]{:S(2)}, u32[]{:S(2)}) collective-permute-start(bf16[112,128]{1,0:T(8,128)(2,1)S(1)} %get-tuple-element.41), channel_id=1, source_target_pairs={{0,24},{8,0},{16,8},{24,16},{1,25},{9,1},{17,9},{25,17},{2,26},{10... | collective-permute-start | bytes 86024 | tf_op jit(solution)/shard_map/ppermute | solution.py:28
  26.1 0.0 collective-permute-done.4.refs_0_
  26.1 0.0 collective-permute-done.5.refs_1_
  26.1 0.5 %collective-permute-start.8 = (bf16[3,112,128]{2,1,0:T(8,128)(2,1)S(1)}, bf16[3,112,128]{2,1,0:T(8,128)(2,1)S(1)}, u32[]{:S(2)}, u32[]{:S(2)}) collective-permute-start(bf16[3,112,128]{2,1,0:T(8,128)(2,1)S(1)} %shard_map.125), channel_id=1, source_target_pairs={{0,24},{8,0},{16,8},{24,16},{1,25},{9,1},{17,9},{25,17},{2,26},{10... | collective-permute-start | bytes 258056 | tf_op jit(solution)/shard_map/ppermute | solution.py:28
  26.6 1.1 %shard_map.127 = (f32[2,48,96]{2,1,0:T(8,128)}, f32[2,48,96]{2,1,0:T(8,128)}, f32[2,48]{1,0:T(2,128)}) custom-call(bf16[288,256]{1,0:T(8,128)(2,1)S(1)} %get-tuple-element.43.points0, bf16[288,256]{1,0:T(8,128)(2,1)S(1)} %get-tuple-element.44.hidden0, bf16[288,256]{1,0:T(8,128)(2,1)S(1)} %get-tuple-element.45.points1, ...), custom_call_target="tpu_custom_call" | custom-call | flops 2000000000 | bytes 1000 | tf_op jit(solution)/shard_map/pallas_call | solution.py:367
  27.7 2.9 %collective-permute-done.8.three = bf16[3,112,128]{2,1,0:T(8,128)(2,1)S(1)} collective-permute-done((bf16[3,112,128]{2,1,0:T(8,128)(2,1)S(1)}, bf16[3,112,128]{2,1,0:T(8,128)(2,1)S(1)}, u32[]{:S(2)}, u32[]{:S(2)}) %collective-permute-start.8) | collective-permute-done | bytes 86048 | tf_op jit(solution)/shard_map/ppermute | solution.py:28
  30.6 1.1 %shard_map.126 = bf16[180,384]{1,0:T(8,128)(2,1)} custom-call(bf16[3,112,128]{2,1,0:T(8,128)(2,1)S(1)} %collective-permute-done.8.three, bf16[112,128]{1,0:T(8,128)(2,1)S(1)} %collective-permute-done.9.one, bf16[180,384]{1,0:T(8,128)(2,1)S(1)} %collective-permute-done.7.refs_3_.even, bf16[180,384]{1,0:T(8,128)(2,1)S(1)} %collective-permute-done.10.odd, ...), custom_call_target="tpu_custom_call" | custom-call | flops 100000 | bytes 1000 | tf_op jit(solution)/shard_map/pallas_call | solution.py:367
  (8 shorter events, 0.0 us)
Async XLA Ops:
  2.2 7.5 %collective-permute-start = (bf16[72,384]{1,0:T(8,128)(2,1)S(1)}, bf16[72,384]{1,0:T(8,128)(2,1)S(1)}, u32[]{:S(2)}, u32[]{:S(2)}) collective-permute-start(bf16[72,384]{1,0:T(8,128)(2,1)S(1)} %get-tuple-element.29), channel_id=1, source_target_pairs={{0,6},{1,7},{2,4},{3,5},{4,2},{5,3},{6,0},{7,1},{8,14},{9,15},{10,... | collective-permute-start | bytes 165896 | tf_op jit(solution)/shard_map/ppermute | solution.py:402
  7.3 5.1 %collective-permute-start.1 = (bf16[72,384]{1,0:T(8,128)(2,1)S(1)}, bf16[72,384]{1,0:T(8,128)(2,1)S(1)}, u32[]{:S(2)}, u32[]{:S(2)}) collective-permute-start(bf16[72,384]{1,0:T(8,128)(2,1)S(1)} %get-tuple-element.30), channel_id=1, source_target_pairs={{0,4},{1,5},{2,6},{3,7},{4,0},{5,1},{6,2},{7,3},{8,12},{9,13},{10,... | collective-permute-start | bytes 165896 | tf_op jit(solution)/shard_map/ppermute | solution.py:402
  7.4 5.1 %collective-permute-start.2 = (bf16[72,384]{1,0:T(8,128)(2,1)S(1)}, bf16[72,384]{1,0:T(8,128)(2,1)S(1)}, u32[]{:S(2)}, u32[]{:S(2)}) collective-permute-start(bf16[72,384]{1,0:T(8,128)(2,1)S(1)} %get-tuple-element.31), channel_id=1, source_target_pairs={{0,2},{1,3},{2,0},{3,1},{4,6},{5,7},{6,4},{7,5},{8,10},{9,11},{10,... | collective-permute-start | bytes 165896 | tf_op jit(solution)/shard_map/ppermute | solution.py:402
  12.4 0.9 %copy-start = (bf16[1,1,180,384]{3,2,1,0:T(8,128)(2,1)S(1)}, bf16[1,1,180,384]{3,2,1,0:T(8,128)(2,1)}, u32[]{:S(2)}) copy-start(bf16[1,1,180,384]{3,2,1,0:T(8,128)(2,1)} %param.9) | copy-start | bytes 414724
  12.4 2.7 %collective-permute-start.3 = (bf16[4,72,384]{2,1,0:T(8,128)(2,1)S(1)}, bf16[4,72,384]{2,1,0:T(8,128)(2,1)S(1)}, u32[]{:S(2)}, u32[]{:S(2)}) collective-permute-start(bf16[4,72,384]{2,1,0:T(8,128)(2,1)S(1)} %shard_map.122.refs_6_), channel_id=1, source_target_pairs={{0,1},{1,0},{2,3},{3,2},{4,5},{5,4},{6,7},{7,6},{8,9},{9,8},{10,11... | collective-permute-start | bytes 663560 | tf_op jit(solution)/shard_map/ppermute | solution.py:442
  13.3 8.5 %collective-permute-start.7 = (bf16[180,384]{1,0:T(8,128)(2,1)S(1)}, bf16[180,384]{1,0:T(8,128)(2,1)S(1)}, u32[]{:S(2)}, u32[]{:S(2)}) collective-permute-start(bf16[180,384]{1,0:T(8,128)(2,1)S(1)} %bitcast.15), channel_id=1, source_target_pairs={{0,8},{8,0},{16,24},{24,16},{1,9},{9,1},{17,25},{25,17},{2,10},{10... | collective-permute-start | bytes 414728 | tf_op jit(solution)/shard_map/ppermute | solution.py:37
  16.7 9.4 %collective-permute-start.4 = (bf16[112,128]{1,0:T(8,128)(2,1)S(1)}, bf16[112,128]{1,0:T(8,128)(2,1)S(1)}, u32[]{:S(2)}, u32[]{:S(2)}) collective-permute-start(bf16[112,128]{1,0:T(8,128)(2,1)S(1)} %get-tuple-element.38), channel_id=1, source_target_pairs={{0,6},{1,7},{2,4},{3,5},{4,2},{5,3},{6,0},{7,1},{8,14},{9,15},{10,... | collective-permute-start | bytes 86024 | tf_op jit(solution)/shard_map/ppermute | solution.py:402
  19.2 6.8 %collective-permute-start.5 = (bf16[112,128]{1,0:T(8,128)(2,1)S(1)}, bf16[112,128]{1,0:T(8,128)(2,1)S(1)}, u32[]{:S(2)}, u32[]{:S(2)}) collective-permute-start(bf16[112,128]{1,0:T(8,128)(2,1)S(1)} %get-tuple-element.39), channel_id=1, source_target_pairs={{0,4},{1,5},{2,6},{3,7},{4,0},{5,1},{6,2},{7,3},{8,12},{9,13},{10,... | collective-permute-start | bytes 86024 | tf_op jit(solution)/shard_map/ppermute | solution.py:402
  19.2 6.8 %collective-permute-start.6 = (bf16[112,128]{1,0:T(8,128)(2,1)S(1)}, bf16[112,128]{1,0:T(8,128)(2,1)S(1)}, u32[]{:S(2)}, u32[]{:S(2)}) collective-permute-start(bf16[112,128]{1,0:T(8,128)(2,1)S(1)} %get-tuple-element.40), channel_id=1, source_target_pairs={{0,2},{1,3},{2,0},{3,1},{4,6},{5,7},{6,4},{7,5},{8,10},{9,11},{10,... | collective-permute-start | bytes 86024 | tf_op jit(solution)/shard_map/ppermute | solution.py:402
  21.1 6.6 %collective-permute-start.10 = (bf16[180,384]{1,0:T(8,128)(2,1)S(1)}, bf16[180,384]{1,0:T(8,128)(2,1)S(1)}, u32[]{:S(2)}, u32[]{:S(2)}) collective-permute-start(bf16[180,384]{1,0:T(8,128)(2,1)S(1)} %bitcast.16), channel_id=1, source_target_pairs={{16,8},{24,16},{0,0},{8,24},{17,9},{25,17},{1,1},{9,25},{18,10},{2... | collective-permute-start | bytes 414728 | tf_op jit(solution)/shard_map/ppermute | solution.py:37
  21.8 6.0 %collective-permute-start.9 = (bf16[112,128]{1,0:T(8,128)(2,1)S(1)}, bf16[112,128]{1,0:T(8,128)(2,1)S(1)}, u32[]{:S(2)}, u32[]{:S(2)}) collective-permute-start(bf16[112,128]{1,0:T(8,128)(2,1)S(1)} %get-tuple-element.41), channel_id=1, source_target_pairs={{0,24},{8,0},{16,8},{24,16},{1,25},{9,1},{17,9},{25,17},{2,26},{10... | collective-permute-start | bytes 86024 | tf_op jit(solution)/shard_map/ppermute | solution.py:28
  26.1 4.5 %collective-permute-start.8 = (bf16[3,112,128]{2,1,0:T(8,128)(2,1)S(1)}, bf16[3,112,128]{2,1,0:T(8,128)(2,1)S(1)}, u32[]{:S(2)}, u32[]{:S(2)}) collective-permute-start(bf16[3,112,128]{2,1,0:T(8,128)(2,1)S(1)} %shard_map.125), channel_id=1, source_target_pairs={{0,24},{8,0},{16,8},{24,16},{1,25},{9,1},{17,9},{25,17},{2,26},{10... | collective-permute-start | bytes 258056 | tf_op jit(solution)/shard_map/ppermute | solution.py:28

commit v25 on v21

--- a/solution.py
+++ b/solution.py
@@ -155,21 +155,28 @@
     late += fetch(few, hbm[:2] + hbm[3:4], held[:2] + held[3:4])
     wait(early + late)
     parts = [saved[:, c, :].astype(F32) for c in range(2)]
+    width = field.shape[1]
     points = [
-        [
-            jnp.concatenate([window(part, (mm * NB + n) * BS) for mm in range(q)], axis=0)
-            for part in parts
-        ]
-        for n in range(NB)
+        jnp.concatenate([part[:, i : i + width] for i in range(0, part.shape[1], width)], axis=0)
+        for part in parts
     ]
     rows = by_block.shape[1]
     spectral = jnp.dot(table[...], field[...], preferred_element_type=F32)
     active = counts[assign[lax.axis_index("lat")]]
-    held_modes = mode_numbers((rows, spectral.shape[1]), 0, q) < active
-    spectra = [jnp.where(held_modes, spectral[c * rows : (c + 1) * rows], 0.0) for c in range(2)]
+    held_modes = mode_numbers((rows, LANES), 0, q) < active
+    spectra = [
+        jnp.concatenate(
+            [
+                jnp.where(held_modes, spectral[c * rows : (c + 1) * rows, i : i + LANES], 0.0)
+                for i in range(0, width, LANES)
+            ],
+            axis=1,
+        )
+        for c in range(2)
+    ]
+    arrays = [array.astype(BF16) for array in spectra + points]
     for n in range(NB):
-        pieces = [window(spectrum, n * BS) for spectrum in spectra]
-        by_block[n] = dense(pieces + points[n]).astype(BF16)
+        by_block[n] = dense([window(array, n * BS) for array in arrays]).astype(BF16)
     for d, out in enumerate(outs):
         out[...] = by_block[partner(d)]
 

time: 28.7 us -> 28.7 us (level)
  no operation moved by 1% of the time
where the time goes in v25:
time: 28.7 us; the launch traced here: 28.5 us
  starting transfers between devices  15.2 us (53%)
  Pallas kernels  7.11 us (25%)
  waiting for transfers between devices  5.44 us (19%)
  between operations  0.69 us (2%)
    ppermute x6, starting transfers between devices, swap(): return [lax.ppermute(chunk, 'lat', p) for chunk, p in zip(chunks, pairs)]  10.2 us
    pallas_call x8, Pallas kernels, call(): pl.pallas_call(kernel, out_shape=outs, in_specs=[VMEM] * len(near) + [HBM...  7.11 us
    ppermute x2, starting transfers between devices, turn(): lax.ppermute(value, axis, [(i, (i - 1) % length) for i in range(length)])  4.94 us
    ppermute x6, waiting for transfers between devices, swap(): return [lax.ppermute(chunk, 'lat', p) for chunk, p in zip(chunks, pairs)]  3.36 us
    ppermute x1, waiting for transfers between devices, paired_blocks(): other = lax.ppermute(own, 'lat', [(i, i ^ 1) for i in range(2 * NB)])  1.1 us
    ppermute x2, waiting for transfers between devices, turn(): lax.ppermute(value, axis, [(i, (i - 1) % length) for i in range(length)])  0.98 us
  transfers between devices with their start and end apart: 9, of which 5 were waited for; matrix products, arithmetic and copies ran while one was open for 0% of the time, Pallas kernels for 10%

profile of v25, /device:TPU:0, one launch (start us, length us, event | category | flops | bytes accessed | tf_op | source)
XLA Modules:
  0.0 28.5 jit_solution(792738293734541299)
XLA Ops:
  0.6 1.6 %shard_map.120 = (bf16[72,384]{1,0:T(8,128)(2,1)S(1)}, bf16[72,384]{1,0:T(8,128)(2,1)S(1)}, bf16[72,384]{1,0:T(8,128)(2,1)S(1)}, bf16[72,384]{1,0:T(8,128)(2,1)S(1)}) custom-call(s32[8]{0:T(128)} %refs_0_.3, s32[8]{0:T(128)} %refs_1_.3, bf16[180,384]{1,0:T(8,128)(2,1)} %bitcast.16, bf16[144,180]{1,0:T(8,128)(2,1)} %constant.4.clone.refs_3_, ...), custom_call_target="tpu_custom_call" | custom-call | flops 100000000 | bytes 1000000 | tf_op jit(solution)/shard_map/pallas_call | solution.py:379
  2.2 5.1 %collective-permute-start = (bf16[72,384]{1,0:T(8,128)(2,1)S(1)}, bf16[72,384]{1,0:T(8,128)(2,1)S(1)}, u32[]{:S(2)}, u32[]{:S(2)}) collective-permute-start(bf16[72,384]{1,0:T(8,128)(2,1)S(1)} %get-tuple-element.30), channel_id=1, source_target_pairs={{0,6},{1,7},{2,4},{3,5},{4,2},{5,3},{6,0},{7,1},{8,14},{9,15},{10,... | collective-permute-start | bytes 165896 | tf_op jit(solution)/shard_map/ppermute | solution.py:414
  7.3 0.0 collective-permute-start.1
  7.3 0.6 %collective-permute-start.2 = (bf16[72,384]{1,0:T(8,128)(2,1)S(1)}, bf16[72,384]{1,0:T(8,128)(2,1)S(1)}, u32[]{:S(2)}, u32[]{:S(2)}) collective-permute-start(bf16[72,384]{1,0:T(8,128)(2,1)S(1)} %get-tuple-element.32), channel_id=1, source_target_pairs={{0,2},{1,3},{2,0},{3,1},{4,6},{5,7},{6,4},{7,5},{8,10},{9,11},{10,... | collective-permute-start | bytes 165896 | tf_op jit(solution)/shard_map/ppermute | solution.py:414
  7.9 1.5 %shard_map.121 = (bf16[256,256]{1,0:T(8,128)(2,1)S(1)}, bf16[256,256]{1,0:T(8,128)(2,1)S(1)}, bf16[256,256]{1,0:T(8,128)(2,1)S(1)}, f32[1,256]{1,0:T(1,128)S(1)}...) custom-call(s32[8]{0:T(128)} %refs_0_.3, s32[8]{0:T(128)} %refs_1_.3, ...), custom_call_target="tpu_custom_call" | custom-call | flops 2000000000 | bytes 1000000 | tf_op jit(solution)/shard_map/pallas_call | solution.py:379
  9.4 0.2 collective-permute-done.refs_1_
  9.7 2.7 %collective-permute-done.1.refs_2_ = bf16[72,384]{1,0:T(8,128)(2,1)S(1)} collective-permute-done((bf16[72,384]{1,0:T(8,128)(2,1)S(1)}, bf16[72,384]{1,0:T(8,128)(2,1)S(1)}, u32[]{:S(2)}, u32[]{:S(2)}) %collective-permute-start.1) | collective-permute-done | bytes 55328 | tf_op jit(solution)/shard_map/ppermute | solution.py:414
  12.4 0.0 collective-permute-done.2.refs_3_
  12.4 0.1 collective-permute-start.3
  12.5 0.4 %shard_map.123 = (bf16[288,256]{1,0:T(8,128)(2,1)S(1)}, bf16[288,256]{1,0:T(8,128)(2,1)S(1)}, f32[288,256]{1,0:T(8,128)S(1)}) custom-call(bf16[72,384]{1,0:T(8,128)(2,1)S(1)} %get-tuple-element.29.refs_0_, bf16[72,384]{1,0:T(8,128)(2,1)S(1)} %collective-permute-done.refs_1_, bf16[72,384]{1,0:T(8,128)(2,1)S(1)} %collective-permute-done.1.refs_2_, ...), custom_call_target="tpu_custom_call" | custom-call | flops 2000000000 | bytes 1000000 | tf_op jit(solution)/shard_map/pallas_call | solution.py:379
  12.8 1.1 %collective-permute-done.3.refs_4_ = bf16[4,72,384]{2,1,0:T(8,128)(2,1)S(1)} collective-permute-done((bf16[4,72,384]{2,1,0:T(8,128)(2,1)S(1)}, bf16[4,72,384]{2,1,0:T(8,128)(2,1)S(1)}, u32[]{:S(2)}, u32[]{:S(2)}) %collective-permute-start.3) | collective-permute-done | bytes 221216 | tf_op jit(solution)/shard_map/ppermute | solution.py:455
  13.9 1.5 %shard_map.124 = (bf16[112,128]{1,0:T(8,128)(2,1)S(1)}, bf16[112,128]{1,0:T(8,128)(2,1)S(1)}, bf16[112,128]{1,0:T(8,128)(2,1)S(1)}, bf16[224,384]{1,0:T(8,128)(2...) custom-call(bf16[72,384]{1,0:T(8,128)(2,1)S(1)} %get-tuple-element.2, ...), custom_call_target="tpu_custom_call" | custom-call | flops 100000000 | bytes 1000000 | tf_op jit(solution)/shard_map/pallas_call | solution.py:379
  15.4 2.6 %collective-permute-start.4 = (bf16[112,128]{1,0:T(8,128)(2,1)S(1)}, bf16[112,128]{1,0:T(8,128)(2,1)S(1)}, u32[]{:S(2)}, u32[]{:S(2)}) collective-permute-start(bf16[112,128]{1,0:T(8,128)(2,1)S(1)} %get-tuple-element.40), channel_id=1, source_target_pairs={{0,6},{1,7},{2,4},{3,5},{4,2},{5,3},{6,0},{7,1},{8,14},{9,15},{10,... | collective-permute-start | bytes 86024 | tf_op jit(solution)/shard_map/ppermute | solution.py:414
  18.0 0.0 collective-permute-start.5
  18.0 1.9 %collective-permute-start.6 = (bf16[112,128]{1,0:T(8,128)(2,1)S(1)}, bf16[112,128]{1,0:T(8,128)(2,1)S(1)}, u32[]{:S(2)}, u32[]{:S(2)}) collective-permute-start(bf16[112,128]{1,0:T(8,128)(2,1)S(1)} %get-tuple-element.42), channel_id=1, source_target_pairs={{0,2},{1,3},{2,0},{3,1},{4,6},{5,7},{6,4},{7,5},{8,10},{9,11},{10,... | collective-permute-start | bytes 86024 | tf_op jit(solution)/shard_map/ppermute | solution.py:414
  19.9 2.4 %collective-permute-start.8 = (bf16[224,384]{1,0:T(8,128)(2,1)S(1)}, bf16[224,384]{1,0:T(8,128)(2,1)S(1)}, u32[]{:S(2)}, u32[]{:S(2)}) collective-permute-start(bf16[224,384]{1,0:T(8,128)(2,1)S(1)} %get-tuple-element.43), channel_id=1, source_target_pairs={{0,24},{8,0},{16,8},{24,16},{1,25},{9,1},{17,9},{25,17},{2,26},{10... | collective-permute-start | bytes 516104 | tf_op jit(solution)/shard_map/ppermute | solution.py:28
  22.3 0.0 collective-permute-done.4.refs_0_
  22.3 0.4 %collective-permute-done.5.refs_1_ = bf16[112,128]{1,0:T(8,128)(2,1)S(1)} collective-permute-done((bf16[112,128]{1,0:T(8,128)(2,1)S(1)}, bf16[112,128]{1,0:T(8,128)(2,1)S(1)}, u32[]{:S(2)}, u32[]{:S(2)}) %collective-permute-start.5) | collective-permute-done | bytes 28704 | tf_op jit(solution)/shard_map/ppermute | solution.py:414
  22.7 0.0 collective-permute-done.6.refs_2_
  22.7 2.5 %collective-permute-start.7 = (bf16[3,112,128]{2,1,0:T(8,128)(2,1)S(1)}, bf16[3,112,128]{2,1,0:T(8,128)(2,1)S(1)}, u32[]{:S(2)}, u32[]{:S(2)}) collective-permute-start(bf16[3,112,128]{2,1,0:T(8,128)(2,1)S(1)} %shard_map.125), channel_id=1, source_target_pairs={{0,24},{8,0},{16,8},{24,16},{1,25},{9,1},{17,9},{25,17},{2,26},{10... | collective-permute-start | bytes 258056 | tf_op jit(solution)/shard_map/ppermute | solution.py:28
  25.2 1.1 %shard_map.127 = (f32[2,48,96]{2,1,0:T(8,128)}, f32[2,48,96]{2,1,0:T(8,128)}, f32[2,48]{1,0:T(2,128)}) custom-call(bf16[288,256]{1,0:T(8,128)(2,1)S(1)} %get-tuple-element.45.points0, bf16[288,256]{1,0:T(8,128)(2,1)S(1)} %get-tuple-element.46.hidden0, bf16[288,256]{1,0:T(8,128)(2,1)S(1)} %get-tuple-element.47.points1, ...), custom_call_target="tpu_custom_call" | custom-call | flops 2000000000 | bytes 1000000 | tf_op jit(solution)/shard_map/pallas_call | solution.py:379
  26.4 1.0 %collective-permute-done.7.three = bf16[3,112,128]{2,1,0:T(8,128)(2,1)S(1)} collective-permute-done((bf16[3,112,128]{2,1,0:T(8,128)(2,1)S(1)}, bf16[3,112,128]{2,1,0:T(8,128)(2,1)S(1)}, u32[]{:S(2)}, u32[]{:S(2)}) %collective-permute-start.7) | collective-permute-done | bytes 86048 | tf_op jit(solution)/shard_map/ppermute | solution.py:28
  27.3 0.0 collective-permute-done.8.bundle
  27.3 1.1 %shard_map.126 = bf16[180,384]{1,0:T(8,128)(2,1)} custom-call(bf16[3,112,128]{2,1,0:T(8,128)(2,1)S(1)} %collective-permute-done.7.three, bf16[224,384]{1,0:T(8,128)(2,1)S(1)} %collective-permute-done.8.bundle, bf16[180,144]{1,0:T(8,128)(2,1)S(1)} %get-tuple-element.44.table), custom_call_target="tpu_custom_call" | custom-call | flops 100000000 | bytes 1000000 | tf_op jit(solution)/shard_map/pallas_call | solution.py:379
  (2 shorter events, 0.0 us)
Async XLA Ops:
  2.2 7.5 %collective-permute-start = (bf16[72,384]{1,0:T(8,128)(2,1)S(1)}, bf16[72,384]{1,0:T(8,128)(2,1)S(1)}, u32[]{:S(2)}, u32[]{:S(2)}) collective-permute-start(bf16[72,384]{1,0:T(8,128)(2,1)S(1)} %get-tuple-element.30), channel_id=1, source_target_pairs={{0,6},{1,7},{2,4},{3,5},{4,2},{5,3},{6,0},{7,1},{8,14},{9,15},{10,... | collective-permute-start | bytes 165896 | tf_op jit(solution)/shard_map/ppermute | solution.py:414
  7.3 5.1 %collective-permute-start.1 = (bf16[72,384]{1,0:T(8,128)(2,1)S(1)}, bf16[72,384]{1,0:T(8,128)(2,1)S(1)}, u32[]{:S(2)}, u32[]{:S(2)}) collective-permute-start(bf16[72,384]{1,0:T(8,128)(2,1)S(1)} %get-tuple-element.31), channel_id=1, source_target_pairs={{0,4},{1,5},{2,6},{3,7},{4,0},{5,1},{6,2},{7,3},{8,12},{9,13},{10,... | collective-permute-start | bytes 165896 | tf_op jit(solution)/shard_map/ppermute | solution.py:414
  7.3 5.1 %collective-permute-start.2 = (bf16[72,384]{1,0:T(8,128)(2,1)S(1)}, bf16[72,384]{1,0:T(8,128)(2,1)S(1)}, u32[]{:S(2)}, u32[]{:S(2)}) collective-permute-start(bf16[72,384]{1,0:T(8,128)(2,1)S(1)} %get-tuple-element.32), channel_id=1, source_target_pairs={{0,2},{1,3},{2,0},{3,1},{4,6},{5,7},{6,4},{7,5},{8,10},{9,11},{10,... | collective-permute-start | bytes 165896 | tf_op jit(solution)/shard_map/ppermute | solution.py:414
  12.4 1.5 %collective-permute-start.3 = (bf16[4,72,384]{2,1,0:T(8,128)(2,1)S(1)}, bf16[4,72,384]{2,1,0:T(8,128)(2,1)S(1)}, u32[]{:S(2)}, u32[]{:S(2)}) collective-permute-start(bf16[4,72,384]{2,1,0:T(8,128)(2,1)S(1)} %shard_map.122), channel_id=1, source_target_pairs={{0,1},{1,0},{2,3},{3,2},{4,5},{5,4},{6,7},{7,6},{8,9},{9,8},{10,11... | collective-permute-start | bytes 663560 | tf_op jit(solution)/shard_map/ppermute | solution.py:455
  15.4 6.9 %collective-permute-start.4 = (bf16[112,128]{1,0:T(8,128)(2,1)S(1)}, bf16[112,128]{1,0:T(8,128)(2,1)S(1)}, u32[]{:S(2)}, u32[]{:S(2)}) collective-permute-start(bf16[112,128]{1,0:T(8,128)(2,1)S(1)} %get-tuple-element.40), channel_id=1, source_target_pairs={{0,6},{1,7},{2,4},{3,5},{4,2},{5,3},{6,0},{7,1},{8,14},{9,15},{10,... | collective-permute-start | bytes 86024 | tf_op jit(solution)/shard_map/ppermute | solution.py:414
  18.0 4.8 %collective-permute-start.5 = (bf16[112,128]{1,0:T(8,128)(2,1)S(1)}, bf16[112,128]{1,0:T(8,128)(2,1)S(1)}, u32[]{:S(2)}, u32[]{:S(2)}) collective-permute-start(bf16[112,128]{1,0:T(8,128)(2,1)S(1)} %get-tuple-element.41), channel_id=1, source_target_pairs={{0,4},{1,5},{2,6},{3,7},{4,0},{5,1},{6,2},{7,3},{8,12},{9,13},{10,... | collective-permute-start | bytes 86024 | tf_op jit(solution)/shard_map/ppermute | solution.py:414
  18.0 4.8 %collective-permute-start.6 = (bf16[112,128]{1,0:T(8,128)(2,1)S(1)}, bf16[112,128]{1,0:T(8,128)(2,1)S(1)}, u32[]{:S(2)}, u32[]{:S(2)}) collective-permute-start(bf16[112,128]{1,0:T(8,128)(2,1)S(1)} %get-tuple-element.42), channel_id=1, source_target_pairs={{0,2},{1,3},{2,0},{3,1},{4,6},{5,7},{6,4},{7,5},{8,10},{9,11},{10,... | collective-permute-start | bytes 86024 | tf_op jit(solution)/shard_map/ppermute | solution.py:414
  19.9 7.5 %collective-permute-start.8 = (bf16[224,384]{1,0:T(8,128)(2,1)S(1)}, bf16[224,384]{1,0:T(8,128)(2,1)S(1)}, u32[]{:S(2)}, u32[]{:S(2)}) collective-permute-start(bf16[224,384]{1,0:T(8,128)(2,1)S(1)} %get-tuple-element.43), channel_id=1, source_target_pairs={{0,24},{8,0},{16,8},{24,16},{1,25},{9,1},{17,9},{25,17},{2,26},{10... | collective-permute-start | bytes 516104 | tf_op jit(solution)/shard_map/ppermute | solution.py:28
  22.7 4.6 %collective-permute-start.7 = (bf16[3,112,128]{2,1,0:T(8,128)(2,1)S(1)}, bf16[3,112,128]{2,1,0:T(8,128)(2,1)S(1)}, u32[]{:S(2)}, u32[]{:S(2)}) collective-permute-start(bf16[3,112,128]{2,1,0:T(8,128)(2,1)S(1)} %shard_map.125), channel_id=1, source_target_pairs={{0,24},{8,0},{16,8},{24,16},{1,25},{9,1},{17,9},{25,17},{2,26},{10... | collective-permute-start | bytes 258056 | tf_op jit(solution)/shard_map/ppermute | solution.py:28

commit v26 on v25

--- a/solution.py
+++ b/solution.py
@@ -353,8 +353,10 @@
     chunks = [own[: three.shape[1]]] + [three[i].astype(F32) for i in range(3)]
     for d, chunk in zip(ORDER, chunks):
         by_block[partner(d)] = jnp.concatenate(unpack(chunk, rows), axis=1)
+    blocks = [by_block[n].astype(BF16) for n in range(NB)]
     parts = [
-        dense([by_block[n, :, c * LANES : (c + 1) * LANES] for n in range(NB)]) for c in range(2)
+        dense([block[:, c * LANES : (c + 1) * LANES] for block in blocks]).astype(F32)
+        for c in range(2)
     ]
     parts = jnp.concatenate(parts, axis=0).astype(BF16)
     none = lax.axis_index("section") == last

time: 28.7 us -> 28.7 us (level)
  no operation moved by 1% of the time
where the time goes in v26:
time: 28.7 us; the launch traced here: 28.5 us
  starting transfers between devices  15.2 us (53%)
  Pallas kernels  7.11 us (25%)
  waiting for transfers between devices  5.44 us (19%)
  between operations  0.69 us (2%)
    ppermute x6, starting transfers between devices, swap(): return [lax.ppermute(chunk, 'lat', p) for chunk, p in zip(chunks, pairs)]  10.2 us
    pallas_call x8, Pallas kernels, call(): pl.pallas_call(kernel, out_shape=outs, in_specs=[VMEM] * len(near) + [HBM...  7.11 us
    ppermute x2, starting transfers between devices, turn(): lax.ppermute(value, axis, [(i, (i - 1) % length) for i in range(length)])  4.94 us
    ppermute x6, waiting for transfers between devices, swap(): return [lax.ppermute(chunk, 'lat', p) for chunk, p in zip(chunks, pairs)]  3.36 us
    ppermute x1, waiting for transfers between devices, paired_blocks(): other = lax.ppermute(own, 'lat', [(i, i ^ 1) for i in range(2 * NB)])  1.1 us
    ppermute x2, waiting for transfers between devices, turn(): lax.ppermute(value, axis, [(i, (i - 1) % length) for i in range(length)])  0.98 us
  transfers between devices with their start and end apart: 9, of which 5 were waited for; matrix products, arithmetic and copies ran while one was open for 0% of the time, Pallas kernels for 10%

profile of v26, /device:TPU:0, one launch (start us, length us, event | category | flops | bytes accessed | tf_op | source)
XLA Modules:
  0.0 28.5 jit_solution(2019347712662490526)
XLA Ops:
  0.6 1.6 %shard_map.120 = (bf16[72,384]{1,0:T(8,128)(2,1)S(1)}, bf16[72,384]{1,0:T(8,128)(2,1)S(1)}, bf16[72,384]{1,0:T(8,128)(2,1)S(1)}, bf16[72,384]{1,0:T(8,128)(2,1)S(1)}) custom-call(s32[8]{0:T(128)} %refs_0_.3, s32[8]{0:T(128)} %refs_1_.3, bf16[180,384]{1,0:T(8,128)(2,1)} %bitcast.16, bf16[144,180]{1,0:T(8,128)(2,1)} %constant.4.clone.refs_3_, ...), custom_call_target="tpu_custom_call" | custom-call | flops 100000000 | bytes 1000000 | tf_op jit(solution)/shard_map/pallas_call | solution.py:381
  2.2 5.1 %collective-permute-start = (bf16[72,384]{1,0:T(8,128)(2,1)S(1)}, bf16[72,384]{1,0:T(8,128)(2,1)S(1)}, u32[]{:S(2)}, u32[]{:S(2)}) collective-permute-start(bf16[72,384]{1,0:T(8,128)(2,1)S(1)} %get-tuple-element.30), channel_id=1, source_target_pairs={{0,6},{1,7},{2,4},{3,5},{4,2},{5,3},{6,0},{7,1},{8,14},{9,15},{10,... | collective-permute-start | bytes 165896 | tf_op jit(solution)/shard_map/ppermute | solution.py:416
  7.3 0.0 collective-permute-start.1
  7.3 0.6 %collective-permute-start.2 = (bf16[72,384]{1,0:T(8,128)(2,1)S(1)}, bf16[72,384]{1,0:T(8,128)(2,1)S(1)}, u32[]{:S(2)}, u32[]{:S(2)}) collective-permute-start(bf16[72,384]{1,0:T(8,128)(2,1)S(1)} %get-tuple-element.32), channel_id=1, source_target_pairs={{0,2},{1,3},{2,0},{3,1},{4,6},{5,7},{6,4},{7,5},{8,10},{9,11},{10,... | collective-permute-start | bytes 165896 | tf_op jit(solution)/shard_map/ppermute | solution.py:416
  7.9 1.5 %shard_map.121 = (bf16[256,256]{1,0:T(8,128)(2,1)S(1)}, bf16[256,256]{1,0:T(8,128)(2,1)S(1)}, bf16[256,256]{1,0:T(8,128)(2,1)S(1)}, f32[1,256]{1,0:T(1,128)S(1)}...) custom-call(s32[8]{0:T(128)} %refs_0_.3, s32[8]{0:T(128)} %refs_1_.3, ...), custom_call_target="tpu_custom_call" | custom-call | flops 2000000000 | bytes 1000000 | tf_op jit(solution)/shard_map/pallas_call | solution.py:381
  9.4 0.2 collective-permute-done.refs_1_
  9.7 2.7 %collective-permute-done.1.refs_2_ = bf16[72,384]{1,0:T(8,128)(2,1)S(1)} collective-permute-done((bf16[72,384]{1,0:T(8,128)(2,1)S(1)}, bf16[72,384]{1,0:T(8,128)(2,1)S(1)}, u32[]{:S(2)}, u32[]{:S(2)}) %collective-permute-start.1) | collective-permute-done | bytes 55328 | tf_op jit(solution)/shard_map/ppermute | solution.py:416
  12.4 0.0 collective-permute-done.2.refs_3_
  12.4 0.1 collective-permute-start.3
  12.5 0.4 %shard_map.123 = (bf16[288,256]{1,0:T(8,128)(2,1)S(1)}, bf16[288,256]{1,0:T(8,128)(2,1)S(1)}, f32[288,256]{1,0:T(8,128)S(1)}) custom-call(bf16[72,384]{1,0:T(8,128)(2,1)S(1)} %get-tuple-element.29.refs_0_, bf16[72,384]{1,0:T(8,128)(2,1)S(1)} %collective-permute-done.refs_1_, bf16[72,384]{1,0:T(8,128)(2,1)S(1)} %collective-permute-done.1.refs_2_, ...), custom_call_target="tpu_custom_call" | custom-call | flops 2000000000 | bytes 1000000 | tf_op jit(solution)/shard_map/pallas_call | solution.py:381
  12.8 1.1 %collective-permute-done.3.refs_4_ = bf16[4,72,384]{2,1,0:T(8,128)(2,1)S(1)} collective-permute-done((bf16[4,72,384]{2,1,0:T(8,128)(2,1)S(1)}, bf16[4,72,384]{2,1,0:T(8,128)(2,1)S(1)}, u32[]{:S(2)}, u32[]{:S(2)}) %collective-permute-start.3) | collective-permute-done | bytes 221216 | tf_op jit(solution)/shard_map/ppermute | solution.py:457
  13.9 1.5 %shard_map.124 = (bf16[112,128]{1,0:T(8,128)(2,1)S(1)}, bf16[112,128]{1,0:T(8,128)(2,1)S(1)}, bf16[112,128]{1,0:T(8,128)(2,1)S(1)}, bf16[224,384]{1,0:T(8,128)(2...) custom-call(bf16[72,384]{1,0:T(8,128)(2,1)S(1)} %get-tuple-element.2, ...), custom_call_target="tpu_custom_call" | custom-call | flops 100000000 | bytes 1000000 | tf_op jit(solution)/shard_map/pallas_call | solution.py:381
  15.4 2.6 %collective-permute-start.4 = (bf16[112,128]{1,0:T(8,128)(2,1)S(1)}, bf16[112,128]{1,0:T(8,128)(2,1)S(1)}, u32[]{:S(2)}, u32[]{:S(2)}) collective-permute-start(bf16[112,128]{1,0:T(8,128)(2,1)S(1)} %get-tuple-element.40), channel_id=1, source_target_pairs={{0,6},{1,7},{2,4},{3,5},{4,2},{5,3},{6,0},{7,1},{8,14},{9,15},{10,... | collective-permute-start | bytes 86024 | tf_op jit(solution)/shard_map/ppermute | solution.py:416
  18.0 0.0 collective-permute-start.5
  18.0 1.9 %collective-permute-start.6 = (bf16[112,128]{1,0:T(8,128)(2,1)S(1)}, bf16[112,128]{1,0:T(8,128)(2,1)S(1)}, u32[]{:S(2)}, u32[]{:S(2)}) collective-permute-start(bf16[112,128]{1,0:T(8,128)(2,1)S(1)} %get-tuple-element.42), channel_id=1, source_target_pairs={{0,2},{1,3},{2,0},{3,1},{4,6},{5,7},{6,4},{7,5},{8,10},{9,11},{10,... | collective-permute-start | bytes 86024 | tf_op jit(solution)/shard_map/ppermute | solution.py:416
  19.8 2.4 %collective-permute-start.8 = (bf16[224,384]{1,0:T(8,128)(2,1)S(1)}, bf16[224,384]{1,0:T(8,128)(2,1)S(1)}, u32[]{:S(2)}, u32[]{:S(2)}) collective-permute-start(bf16[224,384]{1,0:T(8,128)(2,1)S(1)} %get-tuple-element.43), channel_id=1, source_target_pairs={{0,24},{8,0},{16,8},{24,16},{1,25},{9,1},{17,9},{25,17},{2,26},{10... | collective-permute-start | bytes 516104 | tf_op jit(solution)/shard_map/ppermute | solution.py:28
  22.3 0.0 collective-permute-done.4.refs_0_
  22.3 0.4 %collective-permute-done.5.refs_1_ = bf16[112,128]{1,0:T(8,128)(2,1)S(1)} collective-permute-done((bf16[112,128]{1,0:T(8,128)(2,1)S(1)}, bf16[112,128]{1,0:T(8,128)(2,1)S(1)}, u32[]{:S(2)}, u32[]{:S(2)}) %collective-permute-start.5) | collective-permute-done | bytes 28704 | tf_op jit(solution)/shard_map/ppermute | solution.py:416
  22.7 0.0 collective-permute-done.6.refs_2_
  22.7 2.5 %collective-permute-start.7 = (bf16[3,112,128]{2,1,0:T(8,128)(2,1)S(1)}, bf16[3,112,128]{2,1,0:T(8,128)(2,1)S(1)}, u32[]{:S(2)}, u32[]{:S(2)}) collective-permute-start(bf16[3,112,128]{2,1,0:T(8,128)(2,1)S(1)} %shard_map.125), channel_id=1, source_target_pairs={{0,24},{8,0},{16,8},{24,16},{1,25},{9,1},{17,9},{25,17},{2,26},{10... | collective-permute-start | bytes 258056 | tf_op jit(solution)/shard_map/ppermute | solution.py:28
  25.2 1.1 %shard_map.127 = (f32[2,48,96]{2,1,0:T(8,128)}, f32[2,48,96]{2,1,0:T(8,128)}, f32[2,48]{1,0:T(2,128)}) custom-call(bf16[288,256]{1,0:T(8,128)(2,1)S(1)} %get-tuple-element.45.points0, bf16[288,256]{1,0:T(8,128)(2,1)S(1)} %get-tuple-element.46.hidden0, bf16[288,256]{1,0:T(8,128)(2,1)S(1)} %get-tuple-element.47.points1, ...), custom_call_target="tpu_custom_call" | custom-call | flops 2000000000 | bytes 1000000 | tf_op jit(solution)/shard_map/pallas_call | solution.py:381
  26.4 1.0 %collective-permute-done.7.three = bf16[3,112,128]{2,1,0:T(8,128)(2,1)S(1)} collective-permute-done((bf16[3,112,128]{2,1,0:T(8,128)(2,1)S(1)}, bf16[3,112,128]{2,1,0:T(8,128)(2,1)S(1)}, u32[]{:S(2)}, u32[]{:S(2)}) %collective-permute-start.7) | collective-permute-done | bytes 86048 | tf_op jit(solution)/shard_map/ppermute | solution.py:28
  27.3 0.0 collective-permute-done.8.bundle
  27.3 1.1 %shard_map.126 = bf16[180,384]{1,0:T(8,128)(2,1)} custom-call(bf16[3,112,128]{2,1,0:T(8,128)(2,1)S(1)} %collective-permute-done.7.three, bf16[224,384]{1,0:T(8,128)(2,1)S(1)} %collective-permute-done.8.bundle, bf16[180,144]{1,0:T(8,128)(2,1)S(1)} %get-tuple-element.44.table), custom_call_target="tpu_custom_call" | custom-call | flops 100000000 | bytes 1000000 | tf_op jit(solution)/shard_map/pallas_call | solution.py:381
  (2 shorter events, 0.0 us)
Async XLA Ops:
  2.2 7.5 %collective-permute-start = (bf16[72,384]{1,0:T(8,128)(2,1)S(1)}, bf16[72,384]{1,0:T(8,128)(2,1)S(1)}, u32[]{:S(2)}, u32[]{:S(2)}) collective-permute-start(bf16[72,384]{1,0:T(8,128)(2,1)S(1)} %get-tuple-element.30), channel_id=1, source_target_pairs={{0,6},{1,7},{2,4},{3,5},{4,2},{5,3},{6,0},{7,1},{8,14},{9,15},{10,... | collective-permute-start | bytes 165896 | tf_op jit(solution)/shard_map/ppermute | solution.py:416
  7.3 5.1 %collective-permute-start.1 = (bf16[72,384]{1,0:T(8,128)(2,1)S(1)}, bf16[72,384]{1,0:T(8,128)(2,1)S(1)}, u32[]{:S(2)}, u32[]{:S(2)}) collective-permute-start(bf16[72,384]{1,0:T(8,128)(2,1)S(1)} %get-tuple-element.31), channel_id=1, source_target_pairs={{0,4},{1,5},{2,6},{3,7},{4,0},{5,1},{6,2},{7,3},{8,12},{9,13},{10,... | collective-permute-start | bytes 165896 | tf_op jit(solution)/shard_map/ppermute | solution.py:416
  7.3 5.1 %collective-permute-start.2 = (bf16[72,384]{1,0:T(8,128)(2,1)S(1)}, bf16[72,384]{1,0:T(8,128)(2,1)S(1)}, u32[]{:S(2)}, u32[]{:S(2)}) collective-permute-start(bf16[72,384]{1,0:T(8,128)(2,1)S(1)} %get-tuple-element.32), channel_id=1, source_target_pairs={{0,2},{1,3},{2,0},{3,1},{4,6},{5,7},{6,4},{7,5},{8,10},{9,11},{10,... | collective-permute-start | bytes 165896 | tf_op jit(solution)/shard_map/ppermute | solution.py:416
  12.4 1.5 %collective-permute-start.3 = (bf16[4,72,384]{2,1,0:T(8,128)(2,1)S(1)}, bf16[4,72,384]{2,1,0:T(8,128)(2,1)S(1)}, u32[]{:S(2)}, u32[]{:S(2)}) collective-permute-start(bf16[4,72,384]{2,1,0:T(8,128)(2,1)S(1)} %shard_map.122), channel_id=1, source_target_pairs={{0,1},{1,0},{2,3},{3,2},{4,5},{5,4},{6,7},{7,6},{8,9},{9,8},{10,11... | collective-permute-start | bytes 663560 | tf_op jit(solution)/shard_map/ppermute | solution.py:457
  15.4 6.9 %collective-permute-start.4 = (bf16[112,128]{1,0:T(8,128)(2,1)S(1)}, bf16[112,128]{1,0:T(8,128)(2,1)S(1)}, u32[]{:S(2)}, u32[]{:S(2)}) collective-permute-start(bf16[112,128]{1,0:T(8,128)(2,1)S(1)} %get-tuple-element.40), channel_id=1, source_target_pairs={{0,6},{1,7},{2,4},{3,5},{4,2},{5,3},{6,0},{7,1},{8,14},{9,15},{10,... | collective-permute-start | bytes 86024 | tf_op jit(solution)/shard_map/ppermute | solution.py:416
  18.0 4.8 %collective-permute-start.5 = (bf16[112,128]{1,0:T(8,128)(2,1)S(1)}, bf16[112,128]{1,0:T(8,128)(2,1)S(1)}, u32[]{:S(2)}, u32[]{:S(2)}) collective-permute-start(bf16[112,128]{1,0:T(8,128)(2,1)S(1)} %get-tuple-element.41), channel_id=1, source_target_pairs={{0,4},{1,5},{2,6},{3,7},{4,0},{5,1},{6,2},{7,3},{8,12},{9,13},{10,... | collective-permute-start | bytes 86024 | tf_op jit(solution)/shard_map/ppermute | solution.py:416
  18.0 4.8 %collective-permute-start.6 = (bf16[112,128]{1,0:T(8,128)(2,1)S(1)}, bf16[112,128]{1,0:T(8,128)(2,1)S(1)}, u32[]{:S(2)}, u32[]{:S(2)}) collective-permute-start(bf16[112,128]{1,0:T(8,128)(2,1)S(1)} %get-tuple-element.42), channel_id=1, source_target_pairs={{0,2},{1,3},{2,0},{3,1},{4,6},{5,7},{6,4},{7,5},{8,10},{9,11},{10,... | collective-permute-start | bytes 86024 | tf_op jit(solution)/shard_map/ppermute | solution.py:416
  19.8 7.5 %collective-permute-start.8 = (bf16[224,384]{1,0:T(8,128)(2,1)S(1)}, bf16[224,384]{1,0:T(8,128)(2,1)S(1)}, u32[]{:S(2)}, u32[]{:S(2)}) collective-permute-start(bf16[224,384]{1,0:T(8,128)(2,1)S(1)} %get-tuple-element.43), channel_id=1, source_target_pairs={{0,24},{8,0},{16,8},{24,16},{1,25},{9,1},{17,9},{25,17},{2,26},{10... | collective-permute-start | bytes 516104 | tf_op jit(solution)/shard_map/ppermute | solution.py:28
  22.7 4.6 %collective-permute-start.7 = (bf16[3,112,128]{2,1,0:T(8,128)(2,1)S(1)}, bf16[3,112,128]{2,1,0:T(8,128)(2,1)S(1)}, u32[]{:S(2)}, u32[]{:S(2)}) collective-permute-start(bf16[3,112,128]{2,1,0:T(8,128)(2,1)S(1)} %shard_map.125), channel_id=1, source_target_pairs={{0,24},{8,0},{16,8},{24,16},{1,25},{9,1},{17,9},{25,17},{2,26},{10... | collective-permute-start | bytes 258056 | tf_op jit(solution)/shard_map/ppermute | solution.py:28

commit v27 on v25

--- a/solution.py
+++ b/solution.py
@@ -272,6 +272,10 @@
     silu_points(chunks, mat1, bias, by_pair, points, hidden, slope)
 
 
+def row_spectrum(chunk):
+    return jnp.concatenate([window(chunk, j * BS) for j in range(2)], axis=1)
+
+
 def filter_kernel(*refs):
     owns, (other, slope_own, mat1, turned1, turned2, bias, own_field) = refs[:4], refs[4:11]
     latitudes, outs, (bundle, points, hidden, grad_pre, grad_y) = refs[11], refs[12:15], refs[15:20]
@@ -281,13 +285,13 @@
     sides = [[owns[i][...].astype(F32) for i in ORDER], [other[i].astype(F32) for i in ORDER]]
     silu_points(sides[1], mat1, bias, by_pair, points, hidden, slope)
     spectra = [
-        [jnp.concatenate([window(chunk, j * BS) for j in range(2)], axis=1) for chunk in chunks]
+        [row_spectrum((chunk * 1.0).astype(BF16)) for chunk in chunks]
         for chunks in sides
     ]
     wait(copies)
     for side, rows in zip((core, 1 - core), spectra):
         for d, row in enumerate(rows):
-            by_lat[assign[0, 2 * partner(d) + side]] = row
+            by_lat[assign[0, 2 * partner(d) + side]] = row.astype(F32)
     n_rows, rows, _ = by_lat.shape
     half = rows * n_rows // 2
     waves = eight_points([(by_lat[r][:, :LANES], by_lat[r][:, LANES:]) for r in range(n_rows)], -1)

time: 28.7 us -> 28.7 us (level)
  no operation moved by 1% of the time
where the time goes in v27:
time: 28.7 us; the launch traced here: 28.5 us
  starting transfers between devices  15.2 us (53%)
  Pallas kernels  7.14 us (25%)
  waiting for transfers between devices  5.44 us (19%)
  between operations  0.69 us (2%)
    ppermute x6, starting transfers between devices, swap(): return [lax.ppermute(chunk, 'lat', p) for chunk, p in zip(chunks, pairs)]  10.2 us
    pallas_call x8, Pallas kernels, call(): pl.pallas_call(kernel, out_shape=outs, in_specs=[VMEM] * len(near) + [HBM...  7.14 us
    ppermute x2, starting transfers between devices, turn(): lax.ppermute(value, axis, [(i, (i - 1) % length) for i in range(length)])  4.95 us
    ppermute x6, waiting for transfers between devices, swap(): return [lax.ppermute(chunk, 'lat', p) for chunk, p in zip(chunks, pairs)]  3.36 us
    ppermute x1, waiting for transfers between devices, paired_blocks(): other = lax.ppermute(own, 'lat', [(i, i ^ 1) for i in range(2 * NB)])  1.1 us
    ppermute x2, waiting for transfers between devices, turn(): lax.ppermute(value, axis, [(i, (i - 1) % length) for i in range(length)])  0.98 us
  transfers between devices with their start and end apart: 9, of which 5 were waited for; matrix products, arithmetic and copies ran while one was open for 0% of the time, Pallas kernels for 10%

profile of v27, /device:TPU:0, one launch (start us, length us, event | category | flops | bytes accessed | tf_op | source)
XLA Modules:
  0.0 28.5 jit_solution(12597346794609203041)
XLA Ops:
  0.6 1.6 %shard_map.120 = (bf16[72,384]{1,0:T(8,128)(2,1)S(1)}, bf16[72,384]{1,0:T(8,128)(2,1)S(1)}, bf16[72,384]{1,0:T(8,128)(2,1)S(1)}, bf16[72,384]{1,0:T(8,128)(2,1)S(1)}) custom-call(s32[8]{0:T(128)} %refs_0_.3, s32[8]{0:T(128)} %refs_1_.3, bf16[180,384]{1,0:T(8,128)(2,1)} %bitcast.16, bf16[144,180]{1,0:T(8,128)(2,1)} %constant.4.clone.refs_3_, ...), custom_call_target="tpu_custom_call" | custom-call | flops 100000000 | bytes 1000000 | tf_op jit(solution)/shard_map/pallas_call | solution.py:383
  2.2 5.1 %collective-permute-start = (bf16[72,384]{1,0:T(8,128)(2,1)S(1)}, bf16[72,384]{1,0:T(8,128)(2,1)S(1)}, u32[]{:S(2)}, u32[]{:S(2)}) collective-permute-start(bf16[72,384]{1,0:T(8,128)(2,1)S(1)} %get-tuple-element.30), channel_id=1, source_target_pairs={{0,6},{1,7},{2,4},{3,5},{4,2},{5,3},{6,0},{7,1},{8,14},{9,15},{10,... | collective-permute-start | bytes 165896 | tf_op jit(solution)/shard_map/ppermute | solution.py:418
  7.3 0.0 collective-permute-start.1
  7.3 0.6 %collective-permute-start.2 = (bf16[72,384]{1,0:T(8,128)(2,1)S(1)}, bf16[72,384]{1,0:T(8,128)(2,1)S(1)}, u32[]{:S(2)}, u32[]{:S(2)}) collective-permute-start(bf16[72,384]{1,0:T(8,128)(2,1)S(1)} %get-tuple-element.32), channel_id=1, source_target_pairs={{0,2},{1,3},{2,0},{3,1},{4,6},{5,7},{6,4},{7,5},{8,10},{9,11},{10,... | collective-permute-start | bytes 165896 | tf_op jit(solution)/shard_map/ppermute | solution.py:418
  7.9 1.5 %shard_map.121 = (bf16[256,256]{1,0:T(8,128)(2,1)S(1)}, bf16[256,256]{1,0:T(8,128)(2,1)S(1)}, bf16[256,256]{1,0:T(8,128)(2,1)S(1)}, f32[1,256]{1,0:T(1,128)S(1)}...) custom-call(s32[8]{0:T(128)} %refs_0_.3, s32[8]{0:T(128)} %refs_1_.3, ...), custom_call_target="tpu_custom_call" | custom-call | flops 2000000000 | bytes 1000000 | tf_op jit(solution)/shard_map/pallas_call | solution.py:383
  9.4 0.2 collective-permute-done.refs_1_
  9.7 2.7 %collective-permute-done.1.refs_2_ = bf16[72,384]{1,0:T(8,128)(2,1)S(1)} collective-permute-done((bf16[72,384]{1,0:T(8,128)(2,1)S(1)}, bf16[72,384]{1,0:T(8,128)(2,1)S(1)}, u32[]{:S(2)}, u32[]{:S(2)}) %collective-permute-start.1) | collective-permute-done | bytes 55328 | tf_op jit(solution)/shard_map/ppermute | solution.py:418
  12.4 0.0 collective-permute-done.2.refs_3_
  12.4 0.1 collective-permute-start.3
  12.5 0.4 %shard_map.123 = (bf16[288,256]{1,0:T(8,128)(2,1)S(1)}, bf16[288,256]{1,0:T(8,128)(2,1)S(1)}, f32[288,256]{1,0:T(8,128)S(1)}) custom-call(bf16[72,384]{1,0:T(8,128)(2,1)S(1)} %get-tuple-element.29.refs_0_, bf16[72,384]{1,0:T(8,128)(2,1)S(1)} %collective-permute-done.refs_1_, bf16[72,384]{1,0:T(8,128)(2,1)S(1)} %collective-permute-done.1.refs_2_, ...), custom_call_target="tpu_custom_call" | custom-call | flops 2000000000 | bytes 1000000 | tf_op jit(solution)/shard_map/pallas_call | solution.py:383
  12.8 1.1 %collective-permute-done.3.refs_4_ = bf16[4,72,384]{2,1,0:T(8,128)(2,1)S(1)} collective-permute-done((bf16[4,72,384]{2,1,0:T(8,128)(2,1)S(1)}, bf16[4,72,384]{2,1,0:T(8,128)(2,1)S(1)}, u32[]{:S(2)}, u32[]{:S(2)}) %collective-permute-start.3) | collective-permute-done | bytes 221216 | tf_op jit(solution)/shard_map/ppermute | solution.py:459
  13.9 1.5 %shard_map.124 = (bf16[112,128]{1,0:T(8,128)(2,1)S(1)}, bf16[112,128]{1,0:T(8,128)(2,1)S(1)}, bf16[112,128]{1,0:T(8,128)(2,1)S(1)}, bf16[224,384]{1,0:T(8,128)(2...) custom-call(bf16[72,384]{1,0:T(8,128)(2,1)S(1)} %get-tuple-element.2, ...), custom_call_target="tpu_custom_call" | custom-call | flops 100000000 | bytes 1000000 | tf_op jit(solution)/shard_map/pallas_call | solution.py:383
  15.4 2.6 %collective-permute-start.4 = (bf16[112,128]{1,0:T(8,128)(2,1)S(1)}, bf16[112,128]{1,0:T(8,128)(2,1)S(1)}, u32[]{:S(2)}, u32[]{:S(2)}) collective-permute-start(bf16[112,128]{1,0:T(8,128)(2,1)S(1)} %get-tuple-element.40), channel_id=1, source_target_pairs={{0,6},{1,7},{2,4},{3,5},{4,2},{5,3},{6,0},{7,1},{8,14},{9,15},{10,... | collective-permute-start | bytes 86024 | tf_op jit(solution)/shard_map/ppermute | solution.py:418
  18.0 0.0 collective-permute-start.5
  18.0 1.9 %collective-permute-start.6 = (bf16[112,128]{1,0:T(8,128)(2,1)S(1)}, bf16[112,128]{1,0:T(8,128)(2,1)S(1)}, u32[]{:S(2)}, u32[]{:S(2)}) collective-permute-start(bf16[112,128]{1,0:T(8,128)(2,1)S(1)} %get-tuple-element.42), channel_id=1, source_target_pairs={{0,2},{1,3},{2,0},{3,1},{4,6},{5,7},{6,4},{7,5},{8,10},{9,11},{10,... | collective-permute-start | bytes 86024 | tf_op jit(solution)/shard_map/ppermute | solution.py:418
  19.9 2.4 %collective-permute-start.8 = (bf16[224,384]{1,0:T(8,128)(2,1)S(1)}, bf16[224,384]{1,0:T(8,128)(2,1)S(1)}, u32[]{:S(2)}, u32[]{:S(2)}) collective-permute-start(bf16[224,384]{1,0:T(8,128)(2,1)S(1)} %get-tuple-element.43), channel_id=1, source_target_pairs={{0,24},{8,0},{16,8},{24,16},{1,25},{9,1},{17,9},{25,17},{2,26},{10... | collective-permute-start | bytes 516104 | tf_op jit(solution)/shard_map/ppermute | solution.py:28
  22.3 0.0 collective-permute-done.4.refs_0_
  22.3 0.4 %collective-permute-done.5.refs_1_ = bf16[112,128]{1,0:T(8,128)(2,1)S(1)} collective-permute-done((bf16[112,128]{1,0:T(8,128)(2,1)S(1)}, bf16[112,128]{1,0:T(8,128)(2,1)S(1)}, u32[]{:S(2)}, u32[]{:S(2)}) %collective-permute-start.5) | collective-permute-done | bytes 28704 | tf_op jit(solution)/shard_map/ppermute | solution.py:418
  22.8 0.0 collective-permute-done.6.refs_2_
  22.8 2.5 %collective-permute-start.7 = (bf16[3,112,128]{2,1,0:T(8,128)(2,1)S(1)}, bf16[3,112,128]{2,1,0:T(8,128)(2,1)S(1)}, u32[]{:S(2)}, u32[]{:S(2)}) collective-permute-start(bf16[3,112,128]{2,1,0:T(8,128)(2,1)S(1)} %shard_map.125), channel_id=1, source_target_pairs={{0,24},{8,0},{16,8},{24,16},{1,25},{9,1},{17,9},{25,17},{2,26},{10... | collective-permute-start | bytes 258056 | tf_op jit(solution)/shard_map/ppermute | solution.py:28
  25.3 1.1 %shard_map.127 = (f32[2,48,96]{2,1,0:T(8,128)}, f32[2,48,96]{2,1,0:T(8,128)}, f32[2,48]{1,0:T(2,128)}) custom-call(bf16[288,256]{1,0:T(8,128)(2,1)S(1)} %get-tuple-element.45.points0, bf16[288,256]{1,0:T(8,128)(2,1)S(1)} %get-tuple-element.46.hidden0, bf16[288,256]{1,0:T(8,128)(2,1)S(1)} %get-tuple-element.47.points1, ...), custom_call_target="tpu_custom_call" | custom-call | flops 2000000000 | bytes 1000000 | tf_op jit(solution)/shard_map/pallas_call | solution.py:383
  26.4 1.0 %collective-permute-done.7.three = bf16[3,112,128]{2,1,0:T(8,128)(2,1)S(1)} collective-permute-done((bf16[3,112,128]{2,1,0:T(8,128)(2,1)S(1)}, bf16[3,112,128]{2,1,0:T(8,128)(2,1)S(1)}, u32[]{:S(2)}, u32[]{:S(2)}) %collective-permute-start.7) | collective-permute-done | bytes 86048 | tf_op jit(solution)/shard_map/ppermute | solution.py:28
  27.4 0.0 collective-permute-done.8.bundle
  27.4 1.1 %shard_map.126 = bf16[180,384]{1,0:T(8,128)(2,1)} custom-call(bf16[3,112,128]{2,1,0:T(8,128)(2,1)S(1)} %collective-permute-done.7.three, bf16[224,384]{1,0:T(8,128)(2,1)S(1)} %collective-permute-done.8.bundle, bf16[180,144]{1,0:T(8,128)(2,1)S(1)} %get-tuple-element.44.table), custom_call_target="tpu_custom_call" | custom-call | flops 100000000 | bytes 1000000 | tf_op jit(solution)/shard_map/pallas_call | solution.py:383
  (2 shorter events, 0.0 us)
Async XLA Ops:
  2.2 7.5 %collective-permute-start = (bf16[72,384]{1,0:T(8,128)(2,1)S(1)}, bf16[72,384]{1,0:T(8,128)(2,1)S(1)}, u32[]{:S(2)}, u32[]{:S(2)}) collective-permute-start(bf16[72,384]{1,0:T(8,128)(2,1)S(1)} %get-tuple-element.30), channel_id=1, source_target_pairs={{0,6},{1,7},{2,4},{3,5},{4,2},{5,3},{6,0},{7,1},{8,14},{9,15},{10,... | collective-permute-start | bytes 165896 | tf_op jit(solution)/shard_map/ppermute | solution.py:418
  7.3 5.1 %collective-permute-start.1 = (bf16[72,384]{1,0:T(8,128)(2,1)S(1)}, bf16[72,384]{1,0:T(8,128)(2,1)S(1)}, u32[]{:S(2)}, u32[]{:S(2)}) collective-permute-start(bf16[72,384]{1,0:T(8,128)(2,1)S(1)} %get-tuple-element.31), channel_id=1, source_target_pairs={{0,4},{1,5},{2,6},{3,7},{4,0},{5,1},{6,2},{7,3},{8,12},{9,13},{10,... | collective-permute-start | bytes 165896 | tf_op jit(solution)/shard_map/ppermute | solution.py:418
  7.3 5.1 %collective-permute-start.2 = (bf16[72,384]{1,0:T(8,128)(2,1)S(1)}, bf16[72,384]{1,0:T(8,128)(2,1)S(1)}, u32[]{:S(2)}, u32[]{:S(2)}) collective-permute-start(bf16[72,384]{1,0:T(8,128)(2,1)S(1)} %get-tuple-element.32), channel_id=1, source_target_pairs={{0,2},{1,3},{2,0},{3,1},{4,6},{5,7},{6,4},{7,5},{8,10},{9,11},{10,... | collective-permute-start | bytes 165896 | tf_op jit(solution)/shard_map/ppermute | solution.py:418
  12.4 1.5 %collective-permute-start.3 = (bf16[4,72,384]{2,1,0:T(8,128)(2,1)S(1)}, bf16[4,72,384]{2,1,0:T(8,128)(2,1)S(1)}, u32[]{:S(2)}, u32[]{:S(2)}) collective-permute-start(bf16[4,72,384]{2,1,0:T(8,128)(2,1)S(1)} %shard_map.122), channel_id=1, source_target_pairs={{0,1},{1,0},{2,3},{3,2},{4,5},{5,4},{6,7},{7,6},{8,9},{9,8},{10,11... | collective-permute-start | bytes 663560 | tf_op jit(solution)/shard_map/ppermute | solution.py:459
  15.4 6.9 %collective-permute-start.4 = (bf16[112,128]{1,0:T(8,128)(2,1)S(1)}, bf16[112,128]{1,0:T(8,128)(2,1)S(1)}, u32[]{:S(2)}, u32[]{:S(2)}) collective-permute-start(bf16[112,128]{1,0:T(8,128)(2,1)S(1)} %get-tuple-element.40), channel_id=1, source_target_pairs={{0,6},{1,7},{2,4},{3,5},{4,2},{5,3},{6,0},{7,1},{8,14},{9,15},{10,... | collective-permute-start | bytes 86024 | tf_op jit(solution)/shard_map/ppermute | solution.py:418
  18.0 4.8 %collective-permute-start.5 = (bf16[112,128]{1,0:T(8,128)(2,1)S(1)}, bf16[112,128]{1,0:T(8,128)(2,1)S(1)}, u32[]{:S(2)}, u32[]{:S(2)}) collective-permute-start(bf16[112,128]{1,0:T(8,128)(2,1)S(1)} %get-tuple-element.41), channel_id=1, source_target_pairs={{0,4},{1,5},{2,6},{3,7},{4,0},{5,1},{6,2},{7,3},{8,12},{9,13},{10,... | collective-permute-start | bytes 86024 | tf_op jit(solution)/shard_map/ppermute | solution.py:418
  18.0 4.8 %collective-permute-start.6 = (bf16[112,128]{1,0:T(8,128)(2,1)S(1)}, bf16[112,128]{1,0:T(8,128)(2,1)S(1)}, u32[]{:S(2)}, u32[]{:S(2)}) collective-permute-start(bf16[112,128]{1,0:T(8,128)(2,1)S(1)} %get-tuple-element.42), channel_id=1, source_target_pairs={{0,2},{1,3},{2,0},{3,1},{4,6},{5,7},{6,4},{7,5},{8,10},{9,11},{10,... | collective-permute-start | bytes 86024 | tf_op jit(solution)/shard_map/ppermute | solution.py:418
  19.9 7.5 %collective-permute-start.8 = (bf16[224,384]{1,0:T(8,128)(2,1)S(1)}, bf16[224,384]{1,0:T(8,128)(2,1)S(1)}, u32[]{:S(2)}, u32[]{:S(2)}) collective-permute-start(bf16[224,384]{1,0:T(8,128)(2,1)S(1)} %get-tuple-element.43), channel_id=1, source_target_pairs={{0,24},{8,0},{16,8},{24,16},{1,25},{9,1},{17,9},{25,17},{2,26},{10... | collective-permute-start | bytes 516104 | tf_op jit(solution)/shard_map/ppermute | solution.py:28
  22.8 4.6 %collective-permute-start.7 = (bf16[3,112,128]{2,1,0:T(8,128)(2,1)S(1)}, bf16[3,112,128]{2,1,0:T(8,128)(2,1)S(1)}, u32[]{:S(2)}, u32[]{:S(2)}) collective-permute-start(bf16[3,112,128]{2,1,0:T(8,128)(2,1)S(1)} %shard_map.125), channel_id=1, source_target_pairs={{0,24},{8,0},{16,8},{24,16},{1,25},{9,1},{17,9},{25,17},{2,26},{10... | collective-permute-start | bytes 258056 | tf_op jit(solution)/shard_map/ppermute | solution.py:28
